TPU v7x, 32 devices: a whole 2x2x4 slice. The times are simulated.
32 devices in a mesh: grp: 2 (over x), cell: 16 (over z, y, core).
Axes of the slice: x: 2, y: 2, z: 4, core: 2. Of those that a mesh axis runs over, the one named last changes fastest.
Arguments:
- jac_blocks: bfloat16 [448, 640, 640], P(('grp', 'cell')), parts along dimension 0, may hold values from -0.3125 to 0.3125
- modes: bfloat16 [81920, 256], P(('grp', 'cell')), parts along dimension 0, may hold values from -1.5 to 1.5
- neighbours: int32 [448, 2], P(('grp', 'cell')), parts along dimension 0, may hold values from -1 to 63, as said below
Outputs:
- projected: float32 [512, 256], P(('grp', 'cell')), parts along dimension 0
There are 2 independent parts, one for each index of `grp`. A program takes and returns all parts, laid end to end along the dimension named above; each array names one. Nothing has to cross between parts.
Inputs may be any that keep to these rules, and one draw needn't show every extreme that they name: `neighbours`: slot j < 4 of each device is its diagonal block (j, d * 4 + j). Every other live slot (r, c) of device d has c = d * 4 + r - 1 or c = d * 4 + r + 1, so it couples a block row only to the block just before or after it, which may be the last block of the previous device or the first of the next. Column and row are both -1 or both live. Counts of live slots differ from device to device; some device has all 14 slots live.
All inputs are finite; a program needn't handle non-finite values.
Results may differ from a plain program's by a relative error of at most 0.0003.
Values may be sent and summed in bfloat16 or wider, within the bound.
No kernel may reach another device: no remote copies, remote signals or barrier semaphores. Data moves between devices by JAX's collectives and lax.ppermute only.
A program may use at most 128 MiB of HBM per device.

v0:
```python
import jax
import jax.numpy as jnp
from jax import lax
from jax.sharding import PartitionSpec as P


def padded(cells, sides, width):
    for axis, dim in sides:
        count = lax.axis_size(axis)
        ends = count - 1
        head = lax.slice_in_dim(cells, 0, width, axis=dim)
        tail = lax.slice_in_dim(cells, cells.shape[dim] - width, cells.shape[dim], axis=dim)
        cells = jnp.concatenate(
            [
                lax.ppermute(tail, axis, [(i, (i + 1) % count) for i in range(ends)]),
                cells,
                lax.ppermute(head, axis, [((i + 1) % count, i) for i in range(ends)]),
            ],
            axis=dim,
        )
    return cells


def per_device(jac_blocks, modes, neighbours):
    width = jac_blocks.shape[1]
    n_modes = modes.shape[1]
    n_blocks = modes.shape[0] // width
    device = lax.axis_index("cell")
    extended = padded(modes, (("cell", 0),), width)
    ext_blocks = extended.reshape(n_blocks + 2, width, n_modes)
    slot_rows = neighbours[:, 0]
    position = jnp.clip(neighbours[:, 1] - device * n_blocks + 1, 0, n_blocks + 1)
    picked = ext_blocks[position]
    products = jnp.einsum("sij,sjm->sim", jac_blocks, picked, preferred_element_type=jnp.float32)
    selector = (slot_rows[None, :] == jnp.arange(n_blocks, dtype=jnp.int32)[:, None]).astype(
        jnp.float32
    )
    jv_rows = jnp.einsum("rs,sim->rim", selector, products, precision=lax.Precision.HIGHEST)
    own_modes = modes.reshape(n_blocks, width, n_modes)
    upper_part = lax.optimization_barrier(jv_rows.astype(jnp.bfloat16))
    lower_part = (jv_rows - upper_part.astype(jnp.float32)).astype(jnp.bfloat16)
    partial_value = jnp.einsum(
        "rim,rin->mn", own_modes, upper_part, preferred_element_type=jnp.float32
    )
    partial_value = partial_value + jnp.einsum(
        "rim,rin->mn", own_modes, lower_part, preferred_element_type=jnp.float32
    )
    keep_rows = n_modes // lax.axis_size("cell")
    summed = lax.psum(partial_value, "cell")
    return lax.dynamic_slice_in_dim(summed, device * keep_rows, keep_rows, 0)


def solution(mesh):
    placed = (P(("grp", "cell"), None, None), P(("grp", "cell"), None), P(("grp", "cell"), None))
    return jax.shard_map(
        per_device, mesh=mesh, in_specs=placed, out_specs=P(("grp", "cell"), None), check_vma=False
    )
```

profile of v0, /device:TPU:0, one launch (start us, length us, event | category | flops | bytes accessed | tf_op | source)
XLA Modules:
  0.0 159.5 jit_solution(14258311183006366439)
XLA Ops:
  6.5 0.0 copy-start
  6.5 0.0 all-reduce.2.cloned.1.call-start
  6.5 1.2 fusion.22
  7.8 2.4 %collective-permute-start = (bf16[640,256]{1,0:T(8,128)(2,1)S(1)}, bf16[640,256]{1,0:T(8,128)(2,1)S(1)}, u32[]{:S(2)}, u32[]{:S(2)}) collective-permute-start(bf16[640,256]{1,0:T(8,128)(2,1)S(1)} %get-tuple-element.5), channel_id=1, source_target_pairs={{0,1},{1,2},{2,3},{3,4},{4,5},{5,6},{6,7},{7,8},{8,9},{9,10},{10,1... | collective-permute-start | bytes 983048 | tf_op jit(solution)/shard_map/ppermute | solution.py:15
  10.1 1.3 collective-permute-start.1
  11.4 0.8 slice_bitcast_fusion
  12.2 0.0 collective-permute-done
  12.2 0.0 copy-start.1
  12.2 0.7 copy-done.1
  13.0 3.0 %collective-permute-done.1 = bf16[640,256]{1,0:T(8,128)(2,1)} collective-permute-done((bf16[640,256]{1,0:T(8,128)(2,1)S(1)}, bf16[640,256]{1,0:T(8,128)(2,1)}, u32[]{:S(2)}, u32[]{:S(2)}) %collective-permute-start.1) | collective-permute-done | bytes 327712 | tf_op jit(solution)/shard_map/ppermute | solution.py:17
  15.9 0.0 copy-done
  15.9 1.2 pad_maximum_fusion
  17.1 3.0 %gather_fusion = bf16[14,640,256]{2,1,0:T(8,128)(2,1)} fusion(bf16[6,640,256]{2,1,0:T(8,128)(2,1)S(1)} %bitcast.30, s32[1024]{0:T(1024)S(1)} %pad_clamp_fusion), kind=kCustom, calls=%fused_computation | custom fusion | bytes 9175096 | tf_op jit(solution)/shard_map/gather | solution.py:33
  20.1 13.8 %fusion.24 = f32[14,256,640]{2,1,0:T(8,128)} fusion(bf16[14,640,256]{2,1,0:T(8,128)(2,1)} %gather_fusion, bf16[14,640,640]{2,1,0:T(8,128)(2,1)} %param.3), kind=kOutput, calls=%fused_computation.23 | convolution fusion | flops 2936012800 | bytes 25231360 | tf_op jit(solution)/shard_map/sij,sjm->sim/dot_general | solution.py:34
  33.9 11.0 %copy.7 = f32[14,256,640]{1,0,2:T(8,128)} copy(f32[14,256,640]{2,1,0:T(8,128)} %fusion.24) | data formatting | bytes 18350080 | tf_op jit(solution)/shard_map/sij,sjm->sim/dot_general | solution.py:34
  45.0 8.4 %fusion.23 = (bf16[4,640,256]{2,0,1:T(4,128)(2,1)S(1)}, f32[4,640,256]{2,0,1:T(4,128)S(1)}) fusion(f32[14,256,640]{1,0,2:T(8,128)} %copy.7, s32[14]{0:T(128)S(1)} %get-tuple-element.7), kind=kOutput, calls=%fused_computation.22 | convolution fusion | flops 110755896 | bytes 13107256 | tf_op jit(solution)/shard_map/rs,sim->rim/dot_general | solution.py:38
  53.4 0.7 subtract_convert_fusion
  54.1 0.6 fusion.6
  54.6 1.3 fusion.15
  55.9 0.0 all-reduce.2.cloned.1.call-update
  55.9 95.0 %all-reduce.2.cloned.1.call-done = f32[256,256]{0,1:T(8,128)} async-done(((f32[256,256]{0,1:T(8,128)}), f32[256,256]{0,1:T(8,128)}) %all-reduce.2.cloned.1.call-update) | async-done | bytes 262160 | tf_op jit(solution)/shard_map/psum | solution.py:49
  151.0 1.0 constant_dynamic-slice_fusion
  152.0 0.7 copy.6
  (1 shorter events, 0.0 us)
Async XLA Ops:
  6.5 9.4 %copy-start = (bf16[2560,256]{1,0:T(8,128)(2,1)S(1)}, bf16[2560,256]{1,0:T(8,128)(2,1)}, u32[]{:S(2)}) copy-start(bf16[2560,256]{1,0:T(8,128)(2,1)} %param.4) | copy-start | bytes 3932164
  6.5 144.4 %all-reduce.2.cloned.1.call-start = ((), (), s32[]{:S(2)}) async-start(), calls=%async_computation | async-start | bytes 524288 | tf_op jit(solution)/shard_map/psum | solution.py:49
  7.8 4.5 %collective-permute-start = (bf16[640,256]{1,0:T(8,128)(2,1)S(1)}, bf16[640,256]{1,0:T(8,128)(2,1)S(1)}, u32[]{:S(2)}, u32[]{:S(2)}) collective-permute-start(bf16[640,256]{1,0:T(8,128)(2,1)S(1)} %get-tuple-element.5), channel_id=1, source_target_pairs={{0,1},{1,2},{2,3},{3,4},{4,5},{5,6},{6,7},{7,8},{8,9},{9,10},{10,1... | collective-permute-start | bytes 983048 | tf_op jit(solution)/shard_map/ppermute | solution.py:15
  10.1 5.8 %collective-permute-start.1 = (bf16[640,256]{1,0:T(8,128)(2,1)S(1)}, bf16[640,256]{1,0:T(8,128)(2,1)}, u32[]{:S(2)}, u32[]{:S(2)}) collective-permute-start(bf16[640,256]{1,0:T(8,128)(2,1)S(1)} %get-tuple-element.6), channel_id=1, source_target_pairs={{1,0},{2,1},{3,2},{4,3},{5,4},{6,5},{7,6},{8,7},{9,8},{10,9},{11,1... | collective-permute-start | bytes 983048 | tf_op jit(solution)/shard_map/ppermute | solution.py:17
  12.2 0.7 copy-start.1
Sparse Core Ops, SparseCore 0:
  56.0 94.8 all-reduce.1
where the time goes:
time: 160 us; the launch traced here: 159 us
  waiting for transfers between devices  98 us (61%)
  matrix products  24 us (15%)
  local copies, waits for them, and re-layouts  17.6 us (11%)
  between operations  13.5 us (8%)
  starting transfers between devices  3.67 us (2%)
  other arithmetic  2.65 us (2%)
    psum x1, waiting for transfers between devices, per_device(): summed = lax.psum(partial_value, 'cell')  95 us
    dot_general x1, matrix products, per_device(): jnp.einsum('sij,sjm->sim', jac_blocks, picked, preferred_element_type=jnp...  13.8 us
    dot_general x1, local copies, waits for them, and re-layouts, per_device(): jnp.einsum('sij,sjm->sim', jac_blocks, picked, preferred_element_type=jnp...  11 us
    dot_general x1, matrix products, per_device(): jnp.einsum('rs,sim->rim', selector, products, precision=lax.Precision.HIG...  8.42 us
  transfers between devices with their start and end apart: 3, of which 2 were waited for; matrix products, arithmetic and copies ran while one was open for 0% of the time, Pallas kernels for 0%

commit v1 on v0

v1 whole, which is shorter than its diff:
```python
import functools

import jax
import jax.numpy as jnp
from jax import lax
from jax.experimental import pallas as pl
from jax.experimental.pallas import tpu as pltpu
from jax.sharding import PartitionSpec as P

OWN_VMEM = 54 * 2**20
JOIN_VMEM = 8 * 2**20


def dot(a, b):
    return jnp.dot(a, b, preferred_element_type=jnp.float32)


def halves(value):
    upper = value.astype(jnp.bfloat16)
    return upper, (value - upper.astype(jnp.float32)).astype(jnp.bfloat16)


def own_kernel(blocks, nb_ref, jac_hbm, modes_hbm, p_ref, t_ref, jac, modes, turned, jv, face, sems, mode_sem):
    slots, width, _ = jac_hbm.shape
    load_modes = pltpu.make_async_copy(modes_hbm, modes, mode_sem)
    load_modes.start()
    for s in range(slots):
        pltpu.make_async_copy(jac_hbm.at[s], jac.at[s], sems.at[s]).start()
    face[...] = jnp.zeros_like(face)
    load_modes.wait()
    for k in range(blocks):
        turned[k] = modes[pl.ds(k * width, width), :].T
    base = nb_ref[1, 0]
    for s in range(blocks):
        pltpu.make_async_copy(jac_hbm.at[s], jac.at[s], sems.at[s]).wait()
        jv[s] = dot(jac[s], modes[pl.ds(s * width, width), :])

    def step(s, carry):
        pltpu.make_async_copy(jac_hbm.at[s], jac.at[s], sems.at[s]).wait()
        r = nb_ref[0, s]
        c = nb_ref[1, s] - base
        live = r >= 0

        @pl.when(live & (c >= 0) & (c < blocks))
        def _():
            rows = pl.ds(pl.multiple_of(c * width, width), width)
            jv[r] += dot(jac[s], modes[rows, :])

        @pl.when(live & (c < 0))
        def _():
            face[0] += dot(turned[0], jac[s])

        @pl.when(live & (c >= blocks))
        def _():
            face[1] += dot(turned[blocks - 1], jac[s])

        return carry

    lax.fori_loop(blocks, slots, step, 0)
    total = jnp.zeros(p_ref.shape, jnp.float32)
    for k in range(blocks):
        upper, lower = halves(jv[k])
        total += dot(turned[k], upper) + dot(turned[k], lower)
    p_ref[...] = total
    for side in range(2):
        upper, lower = halves(face[side])
        t_ref[side, 0] = upper
        t_ref[side, 1] = lower


def own_part(neighbours, jac_blocks, modes):
    slots, width, _ = jac_blocks.shape
    rows, n_modes = modes.shape
    blocks = rows // width
    flops = 2 * n_modes * width * width * slots + 4 * rows * n_modes * n_modes
    return pl.pallas_call(
        functools.partial(own_kernel, blocks),
        out_shape=(
            jax.ShapeDtypeStruct((n_modes, n_modes), jnp.float32),
            jax.ShapeDtypeStruct((2, 2, n_modes, width), jnp.bfloat16),
        ),
        in_specs=[
            pl.BlockSpec(memory_space=pltpu.SMEM),
            pl.BlockSpec(memory_space=pl.ANY),
            pl.BlockSpec(memory_space=pl.ANY),
        ],
        out_specs=(pl.BlockSpec(memory_space=pltpu.VMEM), pl.BlockSpec(memory_space=pltpu.VMEM)),
        scratch_shapes=[
            pltpu.VMEM((slots, width, width), jnp.bfloat16),
            pltpu.VMEM((rows, n_modes), jnp.bfloat16),
            pltpu.VMEM((blocks, n_modes, width), jnp.bfloat16),
            pltpu.VMEM((blocks, width, n_modes), jnp.float32),
            pltpu.VMEM((2, n_modes, width), jnp.float32),
            pltpu.SemaphoreType.DMA((slots,)),
            pltpu.SemaphoreType.DMA,
        ],
        compiler_params=pltpu.CompilerParams(vmem_limit_bytes=OWN_VMEM),
        cost_estimate=pl.CostEstimate(
            flops=flops, bytes_accessed=slots * width * width * 2 + rows * n_modes * 2, transcendentals=0
        ),
        name="own_part",
    )(neighbours, jac_blocks, modes)


def join_kernel(p_ref, t_ref, before_ref, after_ref, out_ref):
    total = p_ref[...]
    for side, halo in enumerate((before_ref, after_ref)):
        for part in range(2):
            total += dot(t_ref[side, part], halo[...])
    out_ref[...] = total


def join(p, t, before, after):
    return pl.pallas_call(
        join_kernel,
        out_shape=jax.ShapeDtypeStruct(p.shape, jnp.float32),
        in_specs=[pl.BlockSpec(memory_space=pltpu.VMEM)] * 4,
        out_specs=pl.BlockSpec(memory_space=pltpu.VMEM),
        compiler_params=pltpu.CompilerParams(vmem_limit_bytes=JOIN_VMEM),
        name="join",
    )(p, t, before, after)


def per_device(jac_blocks, modes, neighbours):
    width = jac_blocks.shape[1]
    rows, n_modes = modes.shape
    count = lax.axis_size("cell")
    ends = count - 1
    before = lax.ppermute(modes[rows - width :], "cell", [(i, i + 1) for i in range(ends)])
    after = lax.ppermute(modes[:width], "cell", [(i + 1, i) for i in range(ends)])
    p, t = own_part(neighbours.T, jac_blocks, modes)
    total = join(p, t, before, after)
    parts = lax.all_to_all(total.reshape(count, n_modes // count, n_modes), "cell", 0, 0)
    return jnp.sum(parts, axis=0)


def solution(mesh):
    placed = (P(("grp", "cell"), None, None), P(("grp", "cell"), None), P(("grp", "cell"), None))
    return jax.shard_map(
        per_device, mesh=mesh, in_specs=placed, out_specs=P(("grp", "cell"), None), check_vma=False
    )
```

time: 160 us -> 41.9 us (0.26)
  waiting for transfers between devices: 98 us -> 0.01 us
  matrix products: 24 us -> 0 us
  blocking collectives: 0 us -> 20.4 us
  local copies, waits for them, and re-layouts: 17.6 us -> 3.37 us
  between operations: 13.5 us -> 0.06 us
  Pallas kernels: 0 us -> 13.1 us
  other arithmetic: 2.65 us -> 0.63 us
    psum x1 -> x0, waiting for transfers between devices: 95 us -> none  [per_device(): summed = lax.psum(partial_value, 'cell')]
    dot_general x4 -> x0, matrix products: 24 us -> none  [the longest x1 13.8 us: per_device(): jnp.einsum('sij,sjm->sim', jac_blocks, picked, preferred_element_type=jnp...]
    all_to_all x0 -> x1, blocking collectives: none -> 20.4 us  [per_device(): lax.all_to_all(total.reshape(count, n_modes // count, n_modes), 'cell', 0...]
    pallas_call x0 -> x2, Pallas kernels: none -> 13.1 us  [the longest x1 12.6 us: own_part(): pl.pallas_call(functools.partial(own_kernel, blocks), out_shape=(jax.Shap...]
    dot_general x1 -> x0, local copies, waits for them, and re-layouts: 11 us -> none  [per_device(): jnp.einsum('sij,sjm->sim', jac_blocks, picked, preferred_element_type=jnp...]
    gather x1 -> x0, local copies, waits for them, and re-layouts: 2.99 us -> none  [per_device(): picked = ext_blocks[position]]
    ppermute x2, waiting for transfers between devices: 2.96 us -> 0.01 us  [the longest x1 0.01 us: per_device(): lax.ppermute(modes[:width], 'cell', [(i + 1, i) for i in range(ends)])]
    dynamic_slice x2 -> x0, local copies, waits for them, and re-layouts: 1.67 us -> none  [per_device(): return lax.dynamic_slice_in_dim(summed, device * keep_rows, keep_rows, 0)]
  transfers between devices with their start and end apart: 3 -> 2, of which waited for: 2 -> 0; matrix products, arithmetic and copies ran while one was open for 0% -> 0% of each run, Pallas kernels for 0% -> 30%
where the time goes in v1:
time: 41.9 us
  blocking collectives  20.4 us (49%)
  Pallas kernels  13.1 us (31%)
  starting transfers between devices  4.34 us (10%)
  local copies, waits for them, and re-layouts  3.37 us (8%)
  other arithmetic  0.63 us (2%)
    all_to_all x1, blocking collectives, per_device(): lax.all_to_all(total.reshape(count, n_modes // count, n_modes), 'cell', 0...  20.4 us
    pallas_call x1, Pallas kernels, own_part(): pl.pallas_call(functools.partial(own_kernel, blocks), out_shape=(jax.Shap...  12.6 us
    ppermute x1, starting transfers between devices, per_device(): lax.ppermute(modes[rows - width:], 'cell', [(i, i + 1) for i in range(end...  3.05 us
    unnamed x4, local copies, waits for them, and re-layouts  2.26 us
    ppermute x1, starting transfers between devices, per_device(): lax.ppermute(modes[:width], 'cell', [(i + 1, i) for i in range(ends)])  1.29 us
    slice x1, local copies, waits for them, and re-layouts, per_device(): modes[:width]  1.11 us
  transfers between devices with their start and end apart: 2, of which 0 were waited for; matrix products, arithmetic and copies ran while one was open for 0% of the time, Pallas kernels for 30%

profile of v1, /device:TPU:0, one launch (start us, length us, event | category | flops | bytes accessed | tf_op | source)
XLA Modules:
  0.0 41.9 jit_solution(622472562872977208)
XLA Ops:
  0.0 1.1 %fusion = (bf16[640,256]{1,0:T(8,128)(2,1)S(1)}, bf16[640,256]{1,0:T(8,128)(2,1)S(1)}) fusion(bf16[2560,256]{1,0:T(8,128)(2,1)} %modes_hbm.1), kind=kLoop, calls=%fused_computation | loop fusion | bytes 1310720 | tf_op jit(solution)/shard_map/slice | solution.py:130
  1.1 1.3 %collective-permute-start.1 = (bf16[640,256]{1,0:T(8,128)(2,1)S(1)}, bf16[640,256]{1,0:T(8,128)(2,1)S(1)}, u32[]{:S(2)}, u32[]{:S(2)}) collective-permute-start(bf16[640,256]{1,0:T(8,128)(2,1)S(1)} %get-tuple-element.9), channel_id=1, source_target_pairs={{1,0},{2,1},{3,2},{4,3},{5,4},{6,5},{7,6},{8,7},{9,8},{10,9},{11,1... | collective-permute-start | bytes 983048 | tf_op jit(solution)/shard_map/ppermute | solution.py:130
  2.4 3.1 %collective-permute-start = (bf16[640,256]{1,0:T(8,128)(2,1)S(1)}, bf16[640,256]{1,0:T(8,128)(2,1)S(1)}, u32[]{:S(2)}, u32[]{:S(2)}) collective-permute-start(bf16[640,256]{1,0:T(8,128)(2,1)S(1)} %get-tuple-element.10), channel_id=1, source_target_pairs={{0,1},{1,2},{2,3},{3,4},{4,5},{5,6},{6,7},{7,8},{8,9},{9,10},{10,1... | collective-permute-start | bytes 983048 | tf_op jit(solution)/shard_map/ppermute | solution.py:129
  5.5 12.6 %own_part.1 = (f32[256,256]{1,0:T(8,128)}, bf16[2,2,256,640]{3,2,1,0:T(8,128)(2,1)}) custom-call(s32[2,14]{1,0:T(2,128)} %bitcast.3, bf16[14,640,640]{2,1,0:T(8,128)(2,1)} %jac_hbm.1, bf16[2560,256]{1,0:T(8,128)(2,1)} %modes_hbm.1), custom_call_target="tpu_custom_call" | custom-call | flops 3607101440 | bytes 12779520 | tf_op jit(solution)/shard_map/own_part/pallas_call | solution.py:76
  18.0 0.0 collective-permute-done.1.after_ref
  18.1 0.0 collective-permute-done.before_ref
  18.1 0.0 copy-start
  18.1 1.3 %copy-done = bf16[2,2,256,640]{3,2,1,0:T(8,128)(2,1)S(1)} copy-done((bf16[2,2,256,640]{3,2,1,0:T(8,128)(2,1)S(1)}, bf16[2,2,256,640]{3,2,1,0:T(8,128)(2,1)}, u32[]{:S(2)}) %copy-start) | copy-done | bytes 1310744
  19.4 0.0 copy-start.1
  19.4 0.9 %copy-done.1 = f32[256,256]{1,0:T(8,128)S(1)} copy-done((f32[256,256]{1,0:T(8,128)S(1)}, f32[256,256]{1,0:T(8,128)}, u32[]{:S(2)}) %copy-start.1) | copy-done | bytes 262168
  20.3 0.6 %join.1 = f32[256,256]{1,0:T(8,128)S(1)} custom-call(f32[256,256]{1,0:T(8,128)S(1)} %copy-done.1, bf16[2,2,256,640]{3,2,1,0:T(8,128)(2,1)S(1)} %copy-done, bf16[640,256]{1,0:T(8,128)(2,1)S(1)} %collective-permute-done.before_ref, bf16[640,256]{1,0:T(8,128)(2,1)S(1)} %collective-permute-done.1.after_ref), custom_call_target="tpu_custom_call" | custom-call | tf_op jit(solution)/shard_map/join/pallas_call | solution.py:114
  20.9 20.4 %all_to_all.5 = f32[16,16,256]{2,1,0:T(8,128)S(1)} all-to-all(f32[16,16,256]{2,1,0:T(8,128)S(1)} %bitcast.2), channel_id=1, replica_groups=mesh['grp'=2,'cell'=16] {'cell'}, dimensions={0} | all-to-all | bytes 524288 | tf_op jit(solution)/shard_map/all_to_all | solution.py:133
  41.3 0.6 %reduce_sum.9 = f32[16,256]{1,0:T(8,128)} reduce(f32[16,16,256]{2,1,0:T(8,128)S(1)} %all_to_all.5, f32[]{:T(128)} %constant.0.clone.1), dimensions={0}, to_apply=%region_0.0 | reduce | flops 61440 | bytes 278532 | tf_op jit(solution)/shard_map/reduce_sum | solution.py:134
Async XLA Ops:
  1.1 16.9 %collective-permute-start.1 = (bf16[640,256]{1,0:T(8,128)(2,1)S(1)}, bf16[640,256]{1,0:T(8,128)(2,1)S(1)}, u32[]{:S(2)}, u32[]{:S(2)}) collective-permute-start(bf16[640,256]{1,0:T(8,128)(2,1)S(1)} %get-tuple-element.9), channel_id=1, source_target_pairs={{1,0},{2,1},{3,2},{4,3},{5,4},{6,5},{7,6},{8,7},{9,8},{10,9},{11,1... | collective-permute-start | bytes 983048 | tf_op jit(solution)/shard_map/ppermute | solution.py:130
  2.4 15.6 %collective-permute-start = (bf16[640,256]{1,0:T(8,128)(2,1)S(1)}, bf16[640,256]{1,0:T(8,128)(2,1)S(1)}, u32[]{:S(2)}, u32[]{:S(2)}) collective-permute-start(bf16[640,256]{1,0:T(8,128)(2,1)S(1)} %get-tuple-element.10), channel_id=1, source_target_pairs={{0,1},{1,2},{2,3},{3,4},{4,5},{5,6},{6,7},{7,8},{8,9},{9,10},{10,1... | collective-permute-start | bytes 983048 | tf_op jit(solution)/shard_map/ppermute | solution.py:129
  18.1 1.3 %copy-start = (bf16[2,2,256,640]{3,2,1,0:T(8,128)(2,1)S(1)}, bf16[2,2,256,640]{3,2,1,0:T(8,128)(2,1)}, u32[]{:S(2)}) copy-start(bf16[2,2,256,640]{3,2,1,0:T(8,128)(2,1)} %get-tuple-element.8.t_ref) | copy-start | bytes 3932164
  19.4 0.9 %copy-start.1 = (f32[256,256]{1,0:T(8,128)S(1)}, f32[256,256]{1,0:T(8,128)}, u32[]{:S(2)}) copy-start(f32[256,256]{1,0:T(8,128)} %get-tuple-element.7.p_ref) | copy-start | bytes 786436

commit v2 on v1

--- a/solution.py
+++ b/solution.py
@@ -7,7 +7,7 @@
 from jax.experimental.pallas import tpu as pltpu
 from jax.sharding import PartitionSpec as P
 
-OWN_VMEM = 54 * 2**20
+OWN_VMEM = 48 * 2**20
 JOIN_VMEM = 8 * 2**20
 
 
@@ -20,52 +20,58 @@
     return upper, (value - upper.astype(jnp.float32)).astype(jnp.bfloat16)
 
 
-def own_kernel(blocks, nb_ref, jac_hbm, modes_hbm, p_ref, t_ref, jac, modes, turned, jv, face, sems, mode_sem):
+def own_kernel(blocks, nb_ref, jac_hbm, modes, p_ref, t_ref, jac, turned, jv, parts, face, sems):
     slots, width, _ = jac_hbm.shape
-    load_modes = pltpu.make_async_copy(modes_hbm, modes, mode_sem)
-    load_modes.start()
+    n_modes = modes.shape[1]
+
+    def load(s):
+        return pltpu.make_async_copy(jac_hbm.at[s], jac.at[s], sems.at[s])
+
     for s in range(slots):
-        pltpu.make_async_copy(jac_hbm.at[s], jac.at[s], sems.at[s]).start()
+        load(s).start()
     face[...] = jnp.zeros_like(face)
-    load_modes.wait()
-    for k in range(blocks):
-        turned[k] = modes[pl.ds(k * width, width), :].T
+    for s in range(blocks):
+        rows = pl.ds(s * width, width)
+        load(s).wait()
+        jv[rows, :] = dot(jac[s], modes[rows, :])
+        turned[:, rows] = modes[rows, :].T
     base = nb_ref[1, 0]
-    for s in range(blocks):
-        pltpu.make_async_copy(jac_hbm.at[s], jac.at[s], sems.at[s]).wait()
-        jv[s] = dot(jac[s], modes[pl.ds(s * width, width), :])
+    last = (blocks - 1) * width
 
     def step(s, carry):
-        pltpu.make_async_copy(jac_hbm.at[s], jac.at[s], sems.at[s]).wait()
+        load(s).wait()
         r = nb_ref[0, s]
         c = nb_ref[1, s] - base
         live = r >= 0
 
         @pl.when(live & (c >= 0) & (c < blocks))
         def _():
-            rows = pl.ds(pl.multiple_of(c * width, width), width)
-            jv[r] += dot(jac[s], modes[rows, :])
+            rows = pl.ds(pl.multiple_of(r * width, width), width)
+            picked = pl.ds(pl.multiple_of(c * width, width), width)
+            jv[rows, :] += dot(jac[s], modes[picked, :])
 
         @pl.when(live & (c < 0))
         def _():
-            face[0] += dot(turned[0], jac[s])
+            face[0] += dot(turned[:, :width], jac[s])
 
         @pl.when(live & (c >= blocks))
         def _():
-            face[1] += dot(turned[blocks - 1], jac[s])
+            face[1] += dot(turned[:, last:], jac[s])
 
         return carry
 
     lax.fori_loop(blocks, slots, step, 0)
-    total = jnp.zeros(p_ref.shape, jnp.float32)
-    for k in range(blocks):
-        upper, lower = halves(jv[k])
-        total += dot(turned[k], upper) + dot(turned[k], lower)
-    p_ref[...] = total
     for side in range(2):
         upper, lower = halves(face[side])
         t_ref[side, 0] = upper
         t_ref[side, 1] = lower
+    for s in range(blocks):
+        rows = pl.ds(s * width, width)
+        upper, lower = halves(jv[rows, :])
+        parts[rows, :n_modes] = upper
+        parts[rows, n_modes:] = lower
+    both = dot(turned[...], parts[...])
+    p_ref[...] = both[:, :n_modes] + both[:, n_modes:]
 
 
 def own_part(neighbours, jac_blocks, modes):
@@ -82,17 +88,16 @@
         in_specs=[
             pl.BlockSpec(memory_space=pltpu.SMEM),
             pl.BlockSpec(memory_space=pl.ANY),
-            pl.BlockSpec(memory_space=pl.ANY),
+            pl.BlockSpec(memory_space=pltpu.VMEM),
         ],
         out_specs=(pl.BlockSpec(memory_space=pltpu.VMEM), pl.BlockSpec(memory_space=pltpu.VMEM)),
         scratch_shapes=[
             pltpu.VMEM((slots, width, width), jnp.bfloat16),
-            pltpu.VMEM((rows, n_modes), jnp.bfloat16),
-            pltpu.VMEM((blocks, n_modes, width), jnp.bfloat16),
-            pltpu.VMEM((blocks, width, n_modes), jnp.float32),
+            pltpu.VMEM((n_modes, rows), jnp.bfloat16),
+            pltpu.VMEM((rows, n_modes), jnp.float32),
+            pltpu.VMEM((rows, 2 * n_modes), jnp.bfloat16),
             pltpu.VMEM((2, n_modes, width), jnp.float32),
             pltpu.SemaphoreType.DMA((slots,)),
-            pltpu.SemaphoreType.DMA,
         ],
         compiler_params=pltpu.CompilerParams(vmem_limit_bytes=OWN_VMEM),
         cost_estimate=pl.CostEstimate(

time: 41.9 us -> 34.5 us (0.82)
  Pallas kernels: 13.1 us -> 8.2 us
  local copies, waits for them, and re-layouts: 3.37 us -> 1.23 us
    pallas_call x1, Pallas kernels: 12.6 us -> 7.64 us  [own_part(): pl.pallas_call(functools.partial(own_kernel, blocks), out_shape=(jax.Shap...]
    unnamed x4, local copies, waits for them, and re-layouts: 2.26 us -> 0.01 us
  transfers between devices with their start and end apart: 2 -> 2, of which waited for: 0 -> 0; matrix products, arithmetic and copies ran while one was open for 0% -> 0% of each run, Pallas kernels for 30% -> 22%
where the time goes in v2:
time: 34.5 us; the launch traced here: 34.9 us
  blocking collectives  20.4 us (59%)
  Pallas kernels  8.2 us (24%)
  starting transfers between devices  4.34 us (13%)
  local copies, waits for them, and re-layouts  1.23 us (4%)
  other arithmetic  0.63 us (2%)
    all_to_all x1, blocking collectives, per_device(): lax.all_to_all(total.reshape(count, n_modes // count, n_modes), 'cell', 0...  20.4 us
    pallas_call x1, Pallas kernels, own_part(): pl.pallas_call(functools.partial(own_kernel, blocks), out_shape=(jax.Shap...  7.64 us
    ppermute x1, starting transfers between devices, per_device(): lax.ppermute(modes[rows - width:], 'cell', [(i, i + 1) for i in range(end...  3.05 us
    ppermute x1, starting transfers between devices, per_device(): lax.ppermute(modes[:width], 'cell', [(i + 1, i) for i in range(ends)])  1.29 us
    slice x1, local copies, waits for them, and re-layouts, per_device(): modes[:width]  1.22 us
  transfers between devices with their start and end apart: 2, of which 0 were waited for; matrix products, arithmetic and copies ran while one was open for 0% of the time, Pallas kernels for 22%

profile of v2, /device:TPU:0, one launch (start us, length us, event | category | flops | bytes accessed | tf_op | source)
XLA Modules:
  0.0 34.9 jit_solution(1800260405842954247)
XLA Ops:
  0.0 0.0 copy-start
  0.0 0.0 copy-start.1
  0.0 1.2 %fusion = (bf16[640,256]{1,0:T(8,128)(2,1)S(1)}, bf16[640,256]{1,0:T(8,128)(2,1)S(1)}) fusion(bf16[2560,256]{1,0:T(8,128)(2,1)} %modes.1), kind=kLoop, calls=%fused_computation | loop fusion | bytes 1310720 | tf_op jit(solution)/shard_map/slice | solution.py:135
  1.2 1.3 %collective-permute-start.1 = (bf16[640,256]{1,0:T(8,128)(2,1)S(1)}, bf16[640,256]{1,0:T(8,128)(2,1)S(1)}, u32[]{:S(2)}, u32[]{:S(2)}) collective-permute-start(bf16[640,256]{1,0:T(8,128)(2,1)S(1)} %get-tuple-element.9), channel_id=1, source_target_pairs={{1,0},{2,1},{3,2},{4,3},{5,4},{6,5},{7,6},{8,7},{9,8},{10,9},{11,1... | collective-permute-start | bytes 983048 | tf_op jit(solution)/shard_map/ppermute | solution.py:135
  2.5 3.1 %collective-permute-start = (bf16[640,256]{1,0:T(8,128)(2,1)S(1)}, bf16[640,256]{1,0:T(8,128)(2,1)S(1)}, u32[]{:S(2)}, u32[]{:S(2)}) collective-permute-start(bf16[640,256]{1,0:T(8,128)(2,1)S(1)} %get-tuple-element.10), channel_id=1, source_target_pairs={{0,1},{1,2},{2,3},{3,4},{4,5},{5,6},{6,7},{7,8},{8,9},{9,10},{10,1... | collective-permute-start | bytes 983048 | tf_op jit(solution)/shard_map/ppermute | solution.py:134
  5.6 0.0 copy-done
  5.6 0.0 copy-done.1
  5.6 7.6 %own_part.1 = (f32[256,256]{1,0:T(8,128)S(1)}, bf16[2,2,256,640]{3,2,1,0:T(8,128)(2,1)S(1)}) custom-call(s32[2,14]{1,0:T(2,128)S(1)} %bitcast.3, bf16[14,640,640]{2,1,0:T(8,128)(2,1)} %jac_hbm.1, bf16[2560,256]{1,0:T(8,128)(2,1)S(1)} %copy-done), custom_call_target="tpu_custom_call" | custom-call | flops 3607101440 | bytes 12779520 | tf_op jit(solution)/shard_map/own_part/pallas_call | solution.py:82
  13.2 0.0 collective-permute-done.1.after_ref
  13.3 0.0 collective-permute-done.before_ref
  13.3 0.6 %join.1 = f32[256,256]{1,0:T(8,128)S(1)} custom-call(f32[256,256]{1,0:T(8,128)S(1)} %get-tuple-element.7.p_ref, bf16[2,2,256,640]{3,2,1,0:T(8,128)(2,1)S(1)} %get-tuple-element.8.t_ref, bf16[640,256]{1,0:T(8,128)(2,1)S(1)} %collective-permute-done.before_ref, bf16[640,256]{1,0:T(8,128)(2,1)S(1)} %collective-permute-done.1.after_ref), custom_call_target="tpu_custom_call" | custom-call | tf_op jit(solution)/shard_map/join/pallas_call | solution.py:119
  13.8 20.4 %all_to_all.5 = f32[16,16,256]{2,1,0:T(8,128)S(1)} all-to-all(f32[16,16,256]{2,1,0:T(8,128)S(1)} %bitcast.2), channel_id=1, replica_groups=mesh['grp'=2,'cell'=16] {'cell'}, dimensions={0} | all-to-all | bytes 524288 | tf_op jit(solution)/shard_map/all_to_all | solution.py:138
  34.3 0.6 %reduce_sum.9 = f32[16,256]{1,0:T(8,128)} reduce(f32[16,16,256]{2,1,0:T(8,128)S(1)} %all_to_all.5, f32[]{:T(128)} %constant.0.clone.1), dimensions={0}, to_apply=%region_0.0 | reduce | flops 61440 | bytes 278532 | tf_op jit(solution)/shard_map/reduce_sum | solution.py:139
Async XLA Ops:
  0.0 5.6 %copy-start = (bf16[2560,256]{1,0:T(8,128)(2,1)S(1)}, bf16[2560,256]{1,0:T(8,128)(2,1)}, u32[]{:S(2)}) copy-start(bf16[2560,256]{1,0:T(8,128)(2,1)} %modes.1) | copy-start | bytes 3932164
  0.0 5.6 %copy-start.1 = (s32[14,2]{0,1:T(2,128)S(1)}, s32[14,2]{0,1:T(2,128)}, u32[]{:S(2)}) copy-start(s32[14,2]{0,1:T(2,128)} %param.5) | copy-start | bytes 340
  1.2 12.0 %collective-permute-start.1 = (bf16[640,256]{1,0:T(8,128)(2,1)S(1)}, bf16[640,256]{1,0:T(8,128)(2,1)S(1)}, u32[]{:S(2)}, u32[]{:S(2)}) collective-permute-start(bf16[640,256]{1,0:T(8,128)(2,1)S(1)} %get-tuple-element.9), channel_id=1, source_target_pairs={{1,0},{2,1},{3,2},{4,3},{5,4},{6,5},{7,6},{8,7},{9,8},{10,9},{11,1... | collective-permute-start | bytes 983048 | tf_op jit(solution)/shard_map/ppermute | solution.py:135
  2.5 10.7 %collective-permute-start = (bf16[640,256]{1,0:T(8,128)(2,1)S(1)}, bf16[640,256]{1,0:T(8,128)(2,1)S(1)}, u32[]{:S(2)}, u32[]{:S(2)}) collective-permute-start(bf16[640,256]{1,0:T(8,128)(2,1)S(1)} %get-tuple-element.10), channel_id=1, source_target_pairs={{0,1},{1,2},{2,3},{3,4},{4,5},{5,6},{6,7},{7,8},{8,9},{9,10},{10,1... | collective-permute-start | bytes 983048 | tf_op jit(solution)/shard_map/ppermute | solution.py:134

commit v3 on v2

--- a/solution.py
+++ b/solution.py
@@ -107,20 +107,27 @@
     )(neighbours, jac_blocks, modes)
 
 
-def join_kernel(p_ref, t_ref, before_ref, after_ref, out_ref):
+def join_kernel(rows, p_ref, t_ref, before_ref, after_ref, keep_ref, give_ref):
     total = p_ref[...]
     for side, halo in enumerate((before_ref, after_ref)):
         for part in range(2):
             total += dot(t_ref[side, part], halo[...])
-    out_ref[...] = total
+    first = lax.rem(lax.axis_index("cell"), 2) == 0
+    for chip in range(total.shape[0] // (2 * rows)):
+        even = total[2 * chip * rows : (2 * chip + 1) * rows]
+        odd = total[(2 * chip + 1) * rows : (2 * chip + 2) * rows]
+        place = slice(chip * rows, (chip + 1) * rows)
+        keep_ref[place, :] = jnp.where(first, even, odd)
+        give_ref[place, :] = jnp.where(first, odd, even)
 
 
-def join(p, t, before, after):
+def join(rows, p, t, before, after):
+    half = jax.ShapeDtypeStruct((p.shape[0] // 2, p.shape[1]), jnp.float32)
     return pl.pallas_call(
-        join_kernel,
-        out_shape=jax.ShapeDtypeStruct(p.shape, jnp.float32),
+        functools.partial(join_kernel, rows),
+        out_shape=(half, half),
         in_specs=[pl.BlockSpec(memory_space=pltpu.VMEM)] * 4,
-        out_specs=pl.BlockSpec(memory_space=pltpu.VMEM),
+        out_specs=(pl.BlockSpec(memory_space=pltpu.VMEM),) * 2,
         compiler_params=pltpu.CompilerParams(vmem_limit_bytes=JOIN_VMEM),
         name="join",
     )(p, t, before, after)
@@ -134,8 +141,11 @@
     before = lax.ppermute(modes[rows - width :], "cell", [(i, i + 1) for i in range(ends)])
     after = lax.ppermute(modes[:width], "cell", [(i + 1, i) for i in range(ends)])
     p, t = own_part(neighbours.T, jac_blocks, modes)
-    total = join(p, t, before, after)
-    parts = lax.all_to_all(total.reshape(count, n_modes // count, n_modes), "cell", 0, 0)
+    keep, give = join(n_modes // count, p, t, before, after)
+    got = lax.ppermute(give, "cell", [(i, i ^ 1) for i in range(count)])
+    pair = (keep + got).reshape(count // 2, n_modes // count, n_modes)
+    same_core = [list(range(core, count, 2)) for core in range(2)]
+    parts = lax.all_to_all(pair, "cell", 0, 0, axis_index_groups=same_core)
     return jnp.sum(parts, axis=0)
 
 

time: 34.5 us -> 32.1 us (0.930); the launches traced: 34.9 us -> 31.9 us
  blocking collectives: 20.4 us -> 14.2 us
  starting transfers between devices: 4.34 us -> 7.01 us
  waiting for transfers between devices: 0.01 us -> 0.99 us
  Pallas kernels: 8.2 us -> 7.78 us
    all_to_all x1, blocking collectives: 20.4 us -> 14.2 us  [per_device(): parts = lax.all_to_all(pair, 'cell', 0, 0, axis_index_groups=same_core)]
    ppermute x0 -> x1, starting transfers between devices: none -> 2.66 us  [per_device(): got = lax.ppermute(give, 'cell', [(i, i ^ 1) for i in range(count)])]
    ppermute x0 -> x1, waiting for transfers between devices: none -> 0.99 us  [per_device(): got = lax.ppermute(give, 'cell', [(i, i ^ 1) for i in range(count)])]
    pallas_call x1, Pallas kernels: 7.64 us -> 7.21 us  [own_part(): pl.pallas_call(functools.partial(own_kernel, blocks), out_shape=(jax.Shap...]
  transfers between devices with their start and end apart: 2 -> 3, of which waited for: 0 -> 1; matrix products, arithmetic and copies ran while one was open for 0% -> 0% of each run, Pallas kernels for 22% -> 23%
where the time goes in v3:
time: 32.1 us; the launch traced here: 31.9 us
  blocking collectives  14.2 us (44%)
  Pallas kernels  7.78 us (24%)
  starting transfers between devices  7.01 us (22%)
  local copies, waits for them, and re-layouts  1.23 us (4%)
  waiting for transfers between devices  0.99 us (3%)
  other arithmetic  0.63 us (2%)
    all_to_all x1, blocking collectives, per_device(): parts = lax.all_to_all(pair, 'cell', 0, 0, axis_index_groups=same_core)  14.2 us
    pallas_call x1, Pallas kernels, own_part(): pl.pallas_call(functools.partial(own_kernel, blocks), out_shape=(jax.Shap...  7.21 us
    ppermute x1, starting transfers between devices, per_device(): lax.ppermute(modes[rows - width:], 'cell', [(i, i + 1) for i in range(end...  3.05 us
    ppermute x1, starting transfers between devices, per_device(): got = lax.ppermute(give, 'cell', [(i, i ^ 1) for i in range(count)])  2.66 us
    ppermute x1, starting transfers between devices, per_device(): lax.ppermute(modes[:width], 'cell', [(i + 1, i) for i in range(ends)])  1.29 us
    slice x1, local copies, waits for them, and re-layouts, per_device(): modes[:width]  1.22 us
    ppermute x1, waiting for transfers between devices, per_device(): got = lax.ppermute(give, 'cell', [(i, i ^ 1) for i in range(count)])  0.99 us
  transfers between devices with their start and end apart: 3, of which 1 were waited for; matrix products, arithmetic and copies ran while one was open for 0% of the time, Pallas kernels for 23%

profile of v3, /device:TPU:0, one launch (start us, length us, event | category | flops | bytes accessed | tf_op | source)
XLA Modules:
  0.0 31.9 jit_solution(543625450600728248)
XLA Ops:
  0.0 0.0 copy-start
  0.0 0.0 copy-start.1
  0.0 1.2 %fusion = (bf16[640,256]{1,0:T(8,128)(2,1)S(1)}, bf16[640,256]{1,0:T(8,128)(2,1)S(1)}) fusion(bf16[2560,256]{1,0:T(8,128)(2,1)} %modes.1), kind=kLoop, calls=%fused_computation | loop fusion | bytes 1310720 | tf_op jit(solution)/shard_map/slice | solution.py:142
  1.2 1.3 %collective-permute-start.1 = (bf16[640,256]{1,0:T(8,128)(2,1)S(1)}, bf16[640,256]{1,0:T(8,128)(2,1)S(1)}, u32[]{:S(2)}, u32[]{:S(2)}) collective-permute-start(bf16[640,256]{1,0:T(8,128)(2,1)S(1)} %get-tuple-element.13), channel_id=1, source_target_pairs={{1,0},{2,1},{3,2},{4,3},{5,4},{6,5},{7,6},{8,7},{9,8},{10,9},{11,1... | collective-permute-start | bytes 983048 | tf_op jit(solution)/shard_map/ppermute | solution.py:142
  2.5 3.1 %collective-permute-start = (bf16[640,256]{1,0:T(8,128)(2,1)S(1)}, bf16[640,256]{1,0:T(8,128)(2,1)S(1)}, u32[]{:S(2)}, u32[]{:S(2)}) collective-permute-start(bf16[640,256]{1,0:T(8,128)(2,1)S(1)} %get-tuple-element.14), channel_id=1, source_target_pairs={{0,1},{1,2},{2,3},{3,4},{4,5},{5,6},{6,7},{7,8},{8,9},{9,10},{10,1... | collective-permute-start | bytes 983048 | tf_op jit(solution)/shard_map/ppermute | solution.py:141
  5.6 0.0 copy-done
  5.6 0.0 copy-done.1
  5.6 7.2 %own_part.1 = (f32[256,256]{1,0:T(8,128)S(1)}, bf16[2,2,256,640]{3,2,1,0:T(8,128)(2,1)S(1)}) custom-call(s32[2,14]{1,0:T(2,128)S(1)} %bitcast.2, bf16[14,640,640]{2,1,0:T(8,128)(2,1)} %jac_hbm.1, bf16[2560,256]{1,0:T(8,128)(2,1)S(1)} %copy-done), custom_call_target="tpu_custom_call" | custom-call | flops 3607101440 | bytes 12779520 | tf_op jit(solution)/shard_map/own_part/pallas_call | solution.py:82
  12.8 0.0 collective-permute-done.1.after_ref
  12.8 0.0 collective-permute-done.before_ref
  12.8 0.6 %join.1 = (f32[128,256]{1,0:T(8,128)S(1)}, f32[128,256]{1,0:T(8,128)S(1)}) custom-call(f32[256,256]{1,0:T(8,128)S(1)} %get-tuple-element.9.p_ref, bf16[2,2,256,640]{3,2,1,0:T(8,128)(2,1)S(1)} %get-tuple-element.10.t_ref, bf16[640,256]{1,0:T(8,128)(2,1)S(1)} %collective-permute-done.before_ref, bf16[640,256]{1,0:T(8,128)(2,1)S(1)} %collective-permute-done.1.after_ref), custom_call_target="tpu_custom_call" | custom-call | tf_op jit(solution)/shard_map/join/pallas_call | solution.py:126
  13.4 2.7 %collective-permute-start.2 = (f32[128,256]{1,0:T(8,128)S(1)}, f32[128,256]{1,0:T(8,128)S(1)}, u32[]{:S(2)}, u32[]{:S(2)}) collective-permute-start(f32[128,256]{1,0:T(8,128)S(1)} %get-tuple-element.12), channel_id=1, source_target_pairs={{0,1},{1,0},{2,3},{3,2},{4,5},{5,4},{6,7},{7,6},{8,9},{9,8},{10,11... | collective-permute-start | bytes 393224 | tf_op jit(solution)/shard_map/ppermute | solution.py:145
  16.1 1.0 %collective-permute-done.2 = f32[128,256]{1,0:T(8,128)S(1)} collective-permute-done((f32[128,256]{1,0:T(8,128)S(1)}, f32[128,256]{1,0:T(8,128)S(1)}, u32[]{:S(2)}, u32[]{:S(2)}) %collective-permute-start.2) | collective-permute-done | bytes 131104 | tf_op jit(solution)/shard_map/ppermute | solution.py:145
  17.1 14.2 %all_to_all.5 = f32[8,16,256]{2,1,0:T(8,128)S(1)} all-to-all(f32[8,16,256]{2,1,0:T(8,128)S(1)} %bitcast.3), channel_id=1, replica_groups={{0,2,4,6,8,10,12,14},{1,3,5,7,9,11,13,15},{16,18,20,22,24,26,28,30},{17..., dimensions={0} | all-to-all | bytes 262144 | tf_op jit(solution)/shard_map/all_to_all | solution.py:148
  31.3 0.6 %reduce_sum.9 = f32[16,256]{1,0:T(8,128)} reduce(f32[8,16,256]{2,1,0:T(8,128)S(1)} %all_to_all.5, f32[]{:T(128)} %constant.0.clone.1), dimensions={0}, to_apply=%region_0.0 | reduce | flops 28672 | bytes 147460 | tf_op jit(solution)/shard_map/reduce_sum | solution.py:149
  (1 shorter events, 0.0 us)
Async XLA Ops:
  0.0 5.6 %copy-start = (bf16[2560,256]{1,0:T(8,128)(2,1)S(1)}, bf16[2560,256]{1,0:T(8,128)(2,1)}, u32[]{:S(2)}) copy-start(bf16[2560,256]{1,0:T(8,128)(2,1)} %modes.1) | copy-start | bytes 3932164
  0.0 5.6 %copy-start.1 = (s32[14,2]{0,1:T(2,128)S(1)}, s32[14,2]{0,1:T(2,128)}, u32[]{:S(2)}) copy-start(s32[14,2]{0,1:T(2,128)} %param.5) | copy-start | bytes 340
  1.2 11.6 %collective-permute-start.1 = (bf16[640,256]{1,0:T(8,128)(2,1)S(1)}, bf16[640,256]{1,0:T(8,128)(2,1)S(1)}, u32[]{:S(2)}, u32[]{:S(2)}) collective-permute-start(bf16[640,256]{1,0:T(8,128)(2,1)S(1)} %get-tuple-element.13), channel_id=1, source_target_pairs={{1,0},{2,1},{3,2},{4,3},{5,4},{6,5},{7,6},{8,7},{9,8},{10,9},{11,1... | collective-permute-start | bytes 983048 | tf_op jit(solution)/shard_map/ppermute | solution.py:142
  2.5 10.3 %collective-permute-start = (bf16[640,256]{1,0:T(8,128)(2,1)S(1)}, bf16[640,256]{1,0:T(8,128)(2,1)S(1)}, u32[]{:S(2)}, u32[]{:S(2)}) collective-permute-start(bf16[640,256]{1,0:T(8,128)(2,1)S(1)} %get-tuple-element.14), channel_id=1, source_target_pairs={{0,1},{1,2},{2,3},{3,4},{4,5},{5,6},{6,7},{7,8},{8,9},{9,10},{10,1... | collective-permute-start | bytes 983048 | tf_op jit(solution)/shard_map/ppermute | solution.py:141
  13.4 3.7 %collective-permute-start.2 = (f32[128,256]{1,0:T(8,128)S(1)}, f32[128,256]{1,0:T(8,128)S(1)}, u32[]{:S(2)}, u32[]{:S(2)}) collective-permute-start(f32[128,256]{1,0:T(8,128)S(1)} %get-tuple-element.12), channel_id=1, source_target_pairs={{0,1},{1,0},{2,3},{3,2},{4,5},{5,4},{6,7},{7,6},{8,9},{9,8},{10,11... | collective-permute-start | bytes 393224 | tf_op jit(solution)/shard_map/ppermute | solution.py:145

commit v4 on v3

--- a/solution.py
+++ b/solution.py
@@ -107,12 +107,13 @@
     )(neighbours, jac_blocks, modes)
 
 
-def join_kernel(rows, p_ref, t_ref, before_ref, after_ref, keep_ref, give_ref):
+def join_kernel(rows, p_ref, t_ref, inner_ref, outer_ref, keep_ref, give_ref):
     total = p_ref[...]
-    for side, halo in enumerate((before_ref, after_ref)):
+    core = lax.rem(lax.axis_index("cell"), 2)
+    for side, halo in ((1 - core, inner_ref), (core, outer_ref)):
         for part in range(2):
             total += dot(t_ref[side, part], halo[...])
-    first = lax.rem(lax.axis_index("cell"), 2) == 0
+    first = core == 0
     for chip in range(total.shape[0] // (2 * rows)):
         even = total[2 * chip * rows : (2 * chip + 1) * rows]
         odd = total[(2 * chip + 1) * rows : (2 * chip + 2) * rows]
@@ -121,7 +122,7 @@
         give_ref[place, :] = jnp.where(first, odd, even)
 
 
-def join(rows, p, t, before, after):
+def join(rows, p, t, inner, outer):
     half = jax.ShapeDtypeStruct((p.shape[0] // 2, p.shape[1]), jnp.float32)
     return pl.pallas_call(
         functools.partial(join_kernel, rows),
@@ -130,18 +131,22 @@
         out_specs=(pl.BlockSpec(memory_space=pltpu.VMEM),) * 2,
         compiler_params=pltpu.CompilerParams(vmem_limit_bytes=JOIN_VMEM),
         name="join",
-    )(p, t, before, after)
+    )(p, t, inner, outer)
 
 
 def per_device(jac_blocks, modes, neighbours):
     width = jac_blocks.shape[1]
     rows, n_modes = modes.shape
     count = lax.axis_size("cell")
-    ends = count - 1
-    before = lax.ppermute(modes[rows - width :], "cell", [(i, i + 1) for i in range(ends)])
-    after = lax.ppermute(modes[:width], "cell", [(i + 1, i) for i in range(ends)])
+    core = lax.rem(lax.axis_index("cell"), 2)
+    edge = rows - width
+    across = [(i, min(max(i - 1 + 2 * (i % 2), 0), count - 1)) for i in range(count)]
+    outer = lax.ppermute(lax.dynamic_slice_in_dim(modes, core * edge, width), "cell", across)
+    inner = lax.ppermute(
+        lax.dynamic_slice_in_dim(modes, (1 - core) * edge, width), "cell", [(i, i ^ 1) for i in range(count)]
+    )
     p, t = own_part(neighbours.T, jac_blocks, modes)
-    keep, give = join(n_modes // count, p, t, before, after)
+    keep, give = join(n_modes // count, p, t, inner, outer)
     got = lax.ppermute(give, "cell", [(i, i ^ 1) for i in range(count)])
     pair = (keep + got).reshape(count // 2, n_modes // count, n_modes)
     same_core = [list(range(core, count, 2)) for core in range(2)]

time: 32.1 us -> 30.9 us (0.963); the launches traced: 31.9 us -> 31 us
  Pallas kernels: 7.78 us -> 6.91 us
  starting transfers between devices: 7.01 us -> 6.18 us
  blocking collectives: 14.2 us -> 15 us
    ppermute x1, starting transfers between devices: 2.66 us -> 1.12 us  [per_device(): got = lax.ppermute(give, 'cell', [(i, i ^ 1) for i in range(count)])]
    dynamic_slice x0 -> x1, local copies, waits for them, and re-layouts: none -> 1.22 us  [per_device(): lax.dynamic_slice_in_dim(modes, core * edge, width)]
    slice x1 -> x0, local copies, waits for them, and re-layouts: 1.22 us -> none  [per_device(): modes[:width]]
    all_to_all x1, blocking collectives: 14.2 us -> 15 us  [per_device(): parts = lax.all_to_all(pair, 'cell', 0, 0, axis_index_groups=same_core)]
    pallas_call x1, Pallas kernels: 7.21 us -> 6.35 us  [own_part(): pl.pallas_call(functools.partial(own_kernel, blocks), out_shape=(jax.Shap...]
    ppermute x2, starting transfers between devices: 4.34 us -> 5.06 us  [the longest x1 4.37 us: per_device(): lax.ppermute(lax.dynamic_slice_in_dim(modes, (1 - core) * edge, width), '...]
  transfers between devices with their start and end apart: 3 -> 3, of which waited for: 1 -> 1; matrix products, arithmetic and copies ran while one was open for 0% -> 0% of each run, Pallas kernels for 23% -> 20%
where the time goes in v4:
time: 30.9 us; the launch traced here: 31 us
  blocking collectives  15 us (49%)
  Pallas kernels  6.91 us (22%)
  starting transfers between devices  6.18 us (20%)
  local copies, waits for them, and re-layouts  1.23 us (4%)
  waiting for transfers between devices  0.99 us (3%)
  other arithmetic  0.63 us (2%)
    all_to_all x1, blocking collectives, per_device(): parts = lax.all_to_all(pair, 'cell', 0, 0, axis_index_groups=same_core)  15 us
    pallas_call x1, Pallas kernels, own_part(): pl.pallas_call(functools.partial(own_kernel, blocks), out_shape=(jax.Shap...  6.35 us
    ppermute x1, starting transfers between devices, per_device(): lax.ppermute(lax.dynamic_slice_in_dim(modes, (1 - core) * edge, width), '...  4.37 us
    dynamic_slice x1, local copies, waits for them, and re-layouts, per_device(): lax.dynamic_slice_in_dim(modes, core * edge, width)  1.22 us
    ppermute x1, starting transfers between devices, per_device(): got = lax.ppermute(give, 'cell', [(i, i ^ 1) for i in range(count)])  1.12 us
    ppermute x1, waiting for transfers between devices, per_device(): got = lax.ppermute(give, 'cell', [(i, i ^ 1) for i in range(count)])  0.99 us
    ppermute x1, starting transfers between devices, per_device(): lax.ppermute(lax.dynamic_slice_in_dim(modes, core * edge, width), 'cell',...  0.68 us
  transfers between devices with their start and end apart: 3, of which 1 were waited for; matrix products, arithmetic and copies ran while one was open for 0% of the time, Pallas kernels for 20%

profile of v4, /device:TPU:0, one launch (start us, length us, event | category | flops | bytes accessed | tf_op | source)
XLA Modules:
  0.0 31.0 jit_solution(15224222604516881431)
XLA Ops:
  0.0 0.0 copy-start
  0.0 0.0 copy-start.1
  0.0 1.2 %constant_dynamic-slice_fusion = (bf16[640,256]{1,0:T(8,128)(2,1)S(1)}, bf16[640,256]{1,0:T(8,128)(2,1)S(1)}) fusion(bf16[2560,256]{1,0:T(8,128)(2,1)} %modes.1, s32[]{:T(128)S(6)} %select_n.7, s32[]{:T(128)S(6)} %select_n.6), kind=kLoop, calls=%fused_computation | loop fusion | bytes 1310728 | tf_op jit(solution)/shard_map/dynamic_slice | solution.py:144
  1.2 0.7 %collective-permute-start.1 = (bf16[640,256]{1,0:T(8,128)(2,1)S(1)}, bf16[640,256]{1,0:T(8,128)(2,1)S(1)}, u32[]{:S(2)}, u32[]{:S(2)}) collective-permute-start(bf16[640,256]{1,0:T(8,128)(2,1)S(1)} %get-tuple-element.13), channel_id=1, source_target_pairs={{0,0},{1,2},{2,1},{3,4},{4,3},{5,6},{6,5},{7,8},{8,7},{9,10},{10,9... | collective-permute-start | bytes 983048 | tf_op jit(solution)/shard_map/ppermute | solution.py:144
  1.9 4.4 %collective-permute-start = (bf16[640,256]{1,0:T(8,128)(2,1)S(1)}, bf16[640,256]{1,0:T(8,128)(2,1)S(1)}, u32[]{:S(2)}, u32[]{:S(2)}) collective-permute-start(bf16[640,256]{1,0:T(8,128)(2,1)S(1)} %get-tuple-element.14), channel_id=1, source_target_pairs={{0,1},{1,0},{2,3},{3,2},{4,5},{5,4},{6,7},{7,6},{8,9},{9,8},{10,11... | collective-permute-start | bytes 983048 | tf_op jit(solution)/shard_map/ppermute | solution.py:145
  6.3 0.0 copy-done
  6.3 0.0 copy-done.1
  6.3 6.4 %own_part.1 = (f32[256,256]{1,0:T(8,128)S(1)}, bf16[2,2,256,640]{3,2,1,0:T(8,128)(2,1)S(1)}) custom-call(s32[2,14]{1,0:T(2,128)S(1)} %bitcast.2, bf16[14,640,640]{2,1,0:T(8,128)(2,1)} %jac_hbm.1, bf16[2560,256]{1,0:T(8,128)(2,1)S(1)} %copy-done), custom_call_target="tpu_custom_call" | custom-call | flops 3607101440 | bytes 12779520 | tf_op jit(solution)/shard_map/own_part/pallas_call | solution.py:82
  12.7 0.0 collective-permute-done.1.outer_ref
  12.7 0.0 collective-permute-done.inner_ref
  12.7 0.6 %join.1 = (f32[128,256]{1,0:T(8,128)S(1)}, f32[128,256]{1,0:T(8,128)S(1)}) custom-call(f32[256,256]{1,0:T(8,128)S(1)} %get-tuple-element.9.p_ref, bf16[2,2,256,640]{3,2,1,0:T(8,128)(2,1)S(1)} %get-tuple-element.10.t_ref, bf16[640,256]{1,0:T(8,128)(2,1)S(1)} %collective-permute-done.inner_ref, bf16[640,256]{1,0:T(8,128)(2,1)S(1)} %collective-permute-done.1.outer_ref), custom_call_target="tpu_custom_call" | custom-call | tf_op jit(solution)/shard_map/join/pallas_call | solution.py:127
  13.2 1.1 %collective-permute-start.2 = (f32[128,256]{1,0:T(8,128)S(1)}, f32[128,256]{1,0:T(8,128)S(1)}, u32[]{:S(2)}, u32[]{:S(2)}) collective-permute-start(f32[128,256]{1,0:T(8,128)S(1)} %get-tuple-element.12), channel_id=1, source_target_pairs={{0,1},{1,0},{2,3},{3,2},{4,5},{5,4},{6,7},{7,6},{8,9},{9,8},{10,11... | collective-permute-start | bytes 393224 | tf_op jit(solution)/shard_map/ppermute | solution.py:150
  14.4 1.0 %collective-permute-done.2 = f32[128,256]{1,0:T(8,128)S(1)} collective-permute-done((f32[128,256]{1,0:T(8,128)S(1)}, f32[128,256]{1,0:T(8,128)S(1)}, u32[]{:S(2)}, u32[]{:S(2)}) %collective-permute-start.2) | collective-permute-done | bytes 131104 | tf_op jit(solution)/shard_map/ppermute | solution.py:150
  15.4 15.0 %all_to_all.5 = f32[8,16,256]{2,1,0:T(8,128)S(1)} all-to-all(f32[8,16,256]{2,1,0:T(8,128)S(1)} %bitcast.3), channel_id=1, replica_groups={{0,2,4,6,8,10,12,14},{1,3,5,7,9,11,13,15},{16,18,20,22,24,26,28,30},{17..., dimensions={0} | all-to-all | bytes 262144 | tf_op jit(solution)/shard_map/all_to_all | solution.py:153
  30.4 0.6 %reduce_sum.9 = f32[16,256]{1,0:T(8,128)} reduce(f32[8,16,256]{2,1,0:T(8,128)S(1)} %all_to_all.5, f32[]{:T(128)} %constant.16.clone.1), dimensions={0}, to_apply=%region_0.0 | reduce | flops 28672 | bytes 147460 | tf_op jit(solution)/shard_map/reduce_sum | solution.py:154
  (1 shorter events, 0.0 us)
Async XLA Ops:
  0.0 6.3 %copy-start = (bf16[2560,256]{1,0:T(8,128)(2,1)S(1)}, bf16[2560,256]{1,0:T(8,128)(2,1)}, u32[]{:S(2)}) copy-start(bf16[2560,256]{1,0:T(8,128)(2,1)} %modes.1) | copy-start | bytes 3932164
  0.0 6.3 %copy-start.1 = (s32[14,2]{0,1:T(2,128)S(1)}, s32[14,2]{0,1:T(2,128)}, u32[]{:S(2)}) copy-start(s32[14,2]{0,1:T(2,128)} %param.5) | copy-start | bytes 340
  1.2 11.4 %collective-permute-start.1 = (bf16[640,256]{1,0:T(8,128)(2,1)S(1)}, bf16[640,256]{1,0:T(8,128)(2,1)S(1)}, u32[]{:S(2)}, u32[]{:S(2)}) collective-permute-start(bf16[640,256]{1,0:T(8,128)(2,1)S(1)} %get-tuple-element.13), channel_id=1, source_target_pairs={{0,0},{1,2},{2,1},{3,4},{4,3},{5,6},{6,5},{7,8},{8,7},{9,10},{10,9... | collective-permute-start | bytes 983048 | tf_op jit(solution)/shard_map/ppermute | solution.py:144
  1.9 10.8 %collective-permute-start = (bf16[640,256]{1,0:T(8,128)(2,1)S(1)}, bf16[640,256]{1,0:T(8,128)(2,1)S(1)}, u32[]{:S(2)}, u32[]{:S(2)}) collective-permute-start(bf16[640,256]{1,0:T(8,128)(2,1)S(1)} %get-tuple-element.14), channel_id=1, source_target_pairs={{0,1},{1,0},{2,3},{3,2},{4,5},{5,4},{6,7},{7,6},{8,9},{9,8},{10,11... | collective-permute-start | bytes 983048 | tf_op jit(solution)/shard_map/ppermute | solution.py:145
  13.2 2.1 %collective-permute-start.2 = (f32[128,256]{1,0:T(8,128)S(1)}, f32[128,256]{1,0:T(8,128)S(1)}, u32[]{:S(2)}, u32[]{:S(2)}) collective-permute-start(f32[128,256]{1,0:T(8,128)S(1)} %get-tuple-element.12), channel_id=1, source_target_pairs={{0,1},{1,0},{2,3},{3,2},{4,5},{5,4},{6,7},{7,6},{8,9},{9,8},{10,11... | collective-permute-start | bytes 393224 | tf_op jit(solution)/shard_map/ppermute | solution.py:150

commit v5 on v4

--- a/solution.py
+++ b/solution.py
@@ -7,8 +7,9 @@
 from jax.experimental.pallas import tpu as pltpu
 from jax.sharding import PartitionSpec as P
 
-OWN_VMEM = 48 * 2**20
+OWN_VMEM = 24 * 2**20
 JOIN_VMEM = 8 * 2**20
+STAGE_COST = 10**10
 
 
 def dot(a, b):
@@ -20,26 +21,41 @@
     return upper, (value - upper.astype(jnp.float32)).astype(jnp.bfloat16)
 
 
-def own_kernel(blocks, nb_ref, jac_hbm, modes, p_ref, t_ref, jac, turned, jv, parts, face, sems):
-    slots, width, _ = jac_hbm.shape
+def stage_kernel(modes, outer_ref, inner_ref):
+    width = outer_ref.shape[0]
+    head = modes[:width, :]
+    tail = modes[modes.shape[0] - width :, :]
+    first = lax.rem(lax.axis_index("cell"), 2) == 0
+    outer_ref[...] = jnp.where(first, head, tail)
+    inner_ref[...] = jnp.where(first, tail, head)
+
+
+def stage(modes, width):
+    edge = jax.ShapeDtypeStruct((width, modes.shape[1]), modes.dtype)
+    return pl.pallas_call(
+        stage_kernel,
+        out_shape=(edge, edge),
+        in_specs=[pl.BlockSpec(memory_space=pltpu.VMEM)],
+        out_specs=(pl.BlockSpec(memory_space=pltpu.VMEM),) * 2,
+        compiler_params=pltpu.CompilerParams(vmem_limit_bytes=JOIN_VMEM),
+        cost_estimate=pl.CostEstimate(flops=STAGE_COST, bytes_accessed=4 * edge.size * 2, transcendentals=0),
+        name="stage",
+    )(modes)
+
+
+def own_kernel(blocks, nb_ref, jac, modes, p_ref, t_ref, turned, jv, parts, face):
+    slots, width, _ = jac.shape
     n_modes = modes.shape[1]
 
-    def load(s):
-        return pltpu.make_async_copy(jac_hbm.at[s], jac.at[s], sems.at[s])
-
-    for s in range(slots):
-        load(s).start()
     face[...] = jnp.zeros_like(face)
     for s in range(blocks):
         rows = pl.ds(s * width, width)
-        load(s).wait()
         jv[rows, :] = dot(jac[s], modes[rows, :])
         turned[:, rows] = modes[rows, :].T
     base = nb_ref[1, 0]
     last = (blocks - 1) * width
 
     def step(s, carry):
-        load(s).wait()
         r = nb_ref[0, s]
         c = nb_ref[1, s] - base
         live = r >= 0
@@ -87,17 +103,15 @@
         ),
         in_specs=[
             pl.BlockSpec(memory_space=pltpu.SMEM),
-            pl.BlockSpec(memory_space=pl.ANY),
+            pl.BlockSpec(memory_space=pltpu.VMEM),
             pl.BlockSpec(memory_space=pltpu.VMEM),
         ],
         out_specs=(pl.BlockSpec(memory_space=pltpu.VMEM), pl.BlockSpec(memory_space=pltpu.VMEM)),
         scratch_shapes=[
-            pltpu.VMEM((slots, width, width), jnp.bfloat16),
             pltpu.VMEM((n_modes, rows), jnp.bfloat16),
             pltpu.VMEM((rows, n_modes), jnp.float32),
             pltpu.VMEM((rows, 2 * n_modes), jnp.bfloat16),
             pltpu.VMEM((2, n_modes, width), jnp.float32),
-            pltpu.SemaphoreType.DMA((slots,)),
         ],
         compiler_params=pltpu.CompilerParams(vmem_limit_bytes=OWN_VMEM),
         cost_estimate=pl.CostEstimate(
@@ -138,13 +152,10 @@
     width = jac_blocks.shape[1]
     rows, n_modes = modes.shape
     count = lax.axis_size("cell")
-    core = lax.rem(lax.axis_index("cell"), 2)
-    edge = rows - width
     across = [(i, min(max(i - 1 + 2 * (i % 2), 0), count - 1)) for i in range(count)]
-    outer = lax.ppermute(lax.dynamic_slice_in_dim(modes, core * edge, width), "cell", across)
-    inner = lax.ppermute(
-        lax.dynamic_slice_in_dim(modes, (1 - core) * edge, width), "cell", [(i, i ^ 1) for i in range(count)]
-    )
+    outer, inner = stage(modes, width)
+    outer = lax.ppermute(outer, "cell", across)
+    inner = lax.ppermute(inner, "cell", [(i, i ^ 1) for i in range(count)])
     p, t = own_part(neighbours.T, jac_blocks, modes)
     keep, give = join(n_modes // count, p, t, inner, outer)
     got = lax.ppermute(give, "cell", [(i, i ^ 1) for i in range(count)])

time: 30.9 us -> 30.3 us (0.981)
  local copies, waits for them, and re-layouts: 1.23 us -> 4.49 us
  starting transfers between devices: 6.18 us -> 4.75 us
  blocking collectives: 15 us -> 13.6 us
  Pallas kernels: 6.91 us -> 5.58 us
    unnamed x4 -> x8, local copies, waits for them, and re-layouts: 0.01 us -> 4.49 us
    ppermute x2, starting transfers between devices: 5.06 us -> 1.32 us  [the longest x1 0.8 us: per_device(): outer = lax.ppermute(outer, 'cell', across)]
    ppermute x1, starting transfers between devices: 1.12 us -> 3.44 us  [per_device(): got = lax.ppermute(give, 'cell', [(i, i ^ 1) for i in range(count)])]
    pallas_call x1, Pallas kernels: 6.35 us -> 4.95 us  [own_part(): pl.pallas_call(functools.partial(own_kernel, blocks), out_shape=(jax.Shap...]
    all_to_all x1, blocking collectives: 15 us -> 13.6 us  [per_device(): parts = lax.all_to_all(pair, 'cell', 0, 0, axis_index_groups=same_core)]
    dynamic_slice x1 -> x0, local copies, waits for them, and re-layouts: 1.22 us -> none  [per_device(): lax.dynamic_slice_in_dim(modes, core * edge, width)]
  transfers between devices with their start and end apart: 3 -> 3, of which waited for: 1 -> 1; matrix products, arithmetic and copies ran while one was open for 0% -> 0% of each run, Pallas kernels for 20% -> 16%
where the time goes in v5:
time: 30.3 us; the launch traced here: 30.2 us
  blocking collectives  13.6 us (45%)
  Pallas kernels  5.58 us (18%)
  starting transfers between devices  4.75 us (16%)
  local copies, waits for them, and re-layouts  4.49 us (15%)
  waiting for transfers between devices  0.99 us (3%)
  other arithmetic  0.63 us (2%)
    all_to_all x1, blocking collectives, per_device(): parts = lax.all_to_all(pair, 'cell', 0, 0, axis_index_groups=same_core)  13.6 us
    pallas_call x1, Pallas kernels, own_part(): pl.pallas_call(functools.partial(own_kernel, blocks), out_shape=(jax.Shap...  4.95 us
    unnamed x8, local copies, waits for them, and re-layouts  4.49 us
    ppermute x1, starting transfers between devices, per_device(): got = lax.ppermute(give, 'cell', [(i, i ^ 1) for i in range(count)])  3.44 us
    ppermute x1, waiting for transfers between devices, per_device(): got = lax.ppermute(give, 'cell', [(i, i ^ 1) for i in range(count)])  0.99 us
    ppermute x1, starting transfers between devices, per_device(): outer = lax.ppermute(outer, 'cell', across)  0.8 us
    reduce_sum x1, other arithmetic, per_device(): return jnp.sum(parts, axis=0)  0.62 us
  transfers between devices with their start and end apart: 3, of which 1 were waited for; matrix products, arithmetic and copies ran while one was open for 0% of the time, Pallas kernels for 16%

profile of v5, /device:TPU:0, one launch (start us, length us, event | category | flops | bytes accessed | tf_op | source)
XLA Modules:
  0.0 30.2 jit_solution(15739063911074765585)
XLA Ops:
  0.0 0.0 copy-start.1
  0.0 1.3 %copy-done.1 = bf16[2560,256]{1,0:T(8,128)(2,1)S(1)} copy-done((bf16[2560,256]{1,0:T(8,128)(2,1)S(1)}, bf16[2560,256]{1,0:T(8,128)(2,1)}, u32[]{:S(2)}) %copy-start.1) | copy-done | bytes 1310744
  1.3 0.0 copy-start
  1.3 0.0 copy-start.2
  1.3 0.0 copy-start.3
  1.3 0.1 stage.1
  1.4 0.5 %collective-permute-start = (bf16[640,256]{1,0:T(8,128)(2,1)S(1)}, bf16[640,256]{1,0:T(8,128)(2,1)S(1)}, u32[]{:S(2)}, u32[]{:S(2)}) collective-permute-start(bf16[640,256]{1,0:T(8,128)(2,1)S(1)} %get-tuple-element.13), channel_id=1, source_target_pairs={{0,1},{1,0},{2,3},{3,2},{4,5},{5,4},{6,7},{7,6},{8,9},{9,8},{10,11... | collective-permute-start | bytes 983048 | tf_op jit(solution)/shard_map/ppermute | solution.py:158
  1.9 0.8 %collective-permute-start.1 = (bf16[640,256]{1,0:T(8,128)(2,1)S(1)}, bf16[640,256]{1,0:T(8,128)(2,1)S(1)}, u32[]{:S(2)}, u32[]{:S(2)}) collective-permute-start(bf16[640,256]{1,0:T(8,128)(2,1)S(1)} %get-tuple-element.14), channel_id=1, source_target_pairs={{0,0},{1,2},{2,1},{3,4},{4,3},{5,6},{6,5},{7,8},{8,7},{9,10},{10,9... | collective-permute-start | bytes 983048 | tf_op jit(solution)/shard_map/ppermute | solution.py:157
  2.7 2.9 %copy-done = bf16[14,640,640]{2,1,0:T(8,128)(2,1)S(1)} copy-done((bf16[14,640,640]{2,1,0:T(8,128)(2,1)S(1)}, bf16[14,640,640]{2,1,0:T(8,128)(2,1)}, u32[]{:S(2)}) %copy-start) | copy-done | bytes 11468824
  5.6 0.3 %copy-done.2 = bf16[2560,256]{1,0:T(8,128)(2,1)S(1)} copy-done((bf16[2560,256]{1,0:T(8,128)(2,1)S(1)}, bf16[2560,256]{1,0:T(8,128)(2,1)}, u32[]{:S(2)}) %copy-start.2) | copy-done | bytes 1310744
  5.9 0.0 copy-done.3
  5.9 4.9 %own_part.1 = (f32[256,256]{1,0:T(8,128)S(1)}, bf16[2,2,256,640]{3,2,1,0:T(8,128)(2,1)S(1)}) custom-call(s32[2,14]{1,0:T(2,128)S(1)} %bitcast.2, bf16[14,640,640]{2,1,0:T(8,128)(2,1)S(1)} %copy-done, bf16[2560,256]{1,0:T(8,128)(2,1)S(1)} %copy-done.2), custom_call_target="tpu_custom_call" | custom-call | flops 3607101440 | bytes 12779520 | tf_op jit(solution)/shard_map/own_part/pallas_call | solution.py:98
  10.9 0.0 collective-permute-done.inner_ref
  10.9 0.0 collective-permute-done.1.outer_ref
  10.9 0.6 %join.1 = (f32[128,256]{1,0:T(8,128)S(1)}, f32[128,256]{1,0:T(8,128)S(1)}) custom-call(f32[256,256]{1,0:T(8,128)S(1)} %get-tuple-element.11.p_ref, bf16[2,2,256,640]{3,2,1,0:T(8,128)(2,1)S(1)} %get-tuple-element.12.t_ref, bf16[640,256]{1,0:T(8,128)(2,1)S(1)} %collective-permute-done.inner_ref, bf16[640,256]{1,0:T(8,128)(2,1)S(1)} %collective-permute-done.1.outer_ref), custom_call_target="tpu_custom_call" | custom-call | tf_op jit(solution)/shard_map/join/pallas_call | solution.py:141
  11.4 3.4 %collective-permute-start.2 = (f32[128,256]{1,0:T(8,128)S(1)}, f32[128,256]{1,0:T(8,128)S(1)}, u32[]{:S(2)}, u32[]{:S(2)}) collective-permute-start(f32[128,256]{1,0:T(8,128)S(1)} %get-tuple-element.16), channel_id=1, source_target_pairs={{0,1},{1,0},{2,3},{3,2},{4,5},{5,4},{6,7},{7,6},{8,9},{9,8},{10,11... | collective-permute-start | bytes 393224 | tf_op jit(solution)/shard_map/ppermute | solution.py:161
  14.9 1.0 %collective-permute-done.2 = f32[128,256]{1,0:T(8,128)S(1)} collective-permute-done((f32[128,256]{1,0:T(8,128)S(1)}, f32[128,256]{1,0:T(8,128)S(1)}, u32[]{:S(2)}, u32[]{:S(2)}) %collective-permute-start.2) | collective-permute-done | bytes 131104 | tf_op jit(solution)/shard_map/ppermute | solution.py:161
  15.9 13.6 %all_to_all.5 = f32[8,16,256]{2,1,0:T(8,128)S(1)} all-to-all(f32[8,16,256]{2,1,0:T(8,128)S(1)} %bitcast.3), channel_id=1, replica_groups={{0,2,4,6,8,10,12,14},{1,3,5,7,9,11,13,15},{16,18,20,22,24,26,28,30},{17..., dimensions={0} | all-to-all | bytes 262144 | tf_op jit(solution)/shard_map/all_to_all | solution.py:164
  29.5 0.6 %reduce_sum.9 = f32[16,256]{1,0:T(8,128)} reduce(f32[8,16,256]{2,1,0:T(8,128)S(1)} %all_to_all.5, f32[]{:T(128)} %constant.0.clone.1), dimensions={0}, to_apply=%region_0.0 | reduce | flops 28672 | bytes 147460 | tf_op jit(solution)/shard_map/reduce_sum | solution.py:165
  (1 shorter events, 0.0 us)
Async XLA Ops:
  0.0 1.3 %copy-start.1 = (bf16[2560,256]{1,0:T(8,128)(2,1)S(1)}, bf16[2560,256]{1,0:T(8,128)(2,1)}, u32[]{:S(2)}) copy-start(bf16[2560,256]{1,0:T(8,128)(2,1)} %modes.3) | copy-start | bytes 3932164
  1.3 4.3 %copy-start = (bf16[14,640,640]{2,1,0:T(8,128)(2,1)S(1)}, bf16[14,640,640]{2,1,0:T(8,128)(2,1)}, u32[]{:S(2)}) copy-start(bf16[14,640,640]{2,1,0:T(8,128)(2,1)} %jac.1) | copy-start | bytes 34406404
  1.3 4.6 %copy-start.2 = (bf16[2560,256]{1,0:T(8,128)(2,1)S(1)}, bf16[2560,256]{1,0:T(8,128)(2,1)}, u32[]{:S(2)}) copy-start(bf16[2560,256]{1,0:T(8,128)(2,1)} %modes.3) | copy-start | bytes 3932164
  1.3 4.6 %copy-start.3 = (s32[14,2]{0,1:T(2,128)S(1)}, s32[14,2]{0,1:T(2,128)}, u32[]{:S(2)}) copy-start(s32[14,2]{0,1:T(2,128)} %param.5) | copy-start | bytes 340
  1.4 9.5 %collective-permute-start = (bf16[640,256]{1,0:T(8,128)(2,1)S(1)}, bf16[640,256]{1,0:T(8,128)(2,1)S(1)}, u32[]{:S(2)}, u32[]{:S(2)}) collective-permute-start(bf16[640,256]{1,0:T(8,128)(2,1)S(1)} %get-tuple-element.13), channel_id=1, source_target_pairs={{0,1},{1,0},{2,3},{3,2},{4,5},{5,4},{6,7},{7,6},{8,9},{9,8},{10,11... | collective-permute-start | bytes 983048 | tf_op jit(solution)/shard_map/ppermute | solution.py:158
  1.9 9.0 %collective-permute-start.1 = (bf16[640,256]{1,0:T(8,128)(2,1)S(1)}, bf16[640,256]{1,0:T(8,128)(2,1)S(1)}, u32[]{:S(2)}, u32[]{:S(2)}) collective-permute-start(bf16[640,256]{1,0:T(8,128)(2,1)S(1)} %get-tuple-element.14), channel_id=1, source_target_pairs={{0,0},{1,2},{2,1},{3,4},{4,3},{5,6},{6,5},{7,8},{8,7},{9,10},{10,9... | collective-permute-start | bytes 983048 | tf_op jit(solution)/shard_map/ppermute | solution.py:157
  11.4 4.4 %collective-permute-start.2 = (f32[128,256]{1,0:T(8,128)S(1)}, f32[128,256]{1,0:T(8,128)S(1)}, u32[]{:S(2)}, u32[]{:S(2)}) collective-permute-start(f32[128,256]{1,0:T(8,128)S(1)} %get-tuple-element.16), channel_id=1, source_target_pairs={{0,1},{1,0},{2,3},{3,2},{4,5},{5,4},{6,7},{7,6},{8,9},{9,8},{10,11... | collective-permute-start | bytes 393224 | tf_op jit(solution)/shard_map/ppermute | solution.py:161

commit v6 on v5

--- a/solution.py
+++ b/solution.py
@@ -9,7 +9,7 @@
 
 OWN_VMEM = 24 * 2**20
 JOIN_VMEM = 8 * 2**20
-STAGE_COST = 10**10
+EDGES_COST = 10**10
 
 
 def dot(a, b):
@@ -21,26 +21,32 @@
     return upper, (value - upper.astype(jnp.float32)).astype(jnp.bfloat16)
 
 
-def stage_kernel(modes, outer_ref, inner_ref):
+def edges_kernel(modes_hbm, outer_ref, inner_ref, sems):
     width = outer_ref.shape[0]
-    head = modes[:width, :]
-    tail = modes[modes.shape[0] - width :, :]
-    first = lax.rem(lax.axis_index("cell"), 2) == 0
-    outer_ref[...] = jnp.where(first, head, tail)
-    inner_ref[...] = jnp.where(first, tail, head)
+    last = modes_hbm.shape[0] - width
+    core = lax.rem(lax.axis_index("cell"), 2)
+    copies = []
+    for k, (side, out_ref) in enumerate(((core, outer_ref), (1 - core, inner_ref))):
+        rows = pl.ds(pl.multiple_of(side * last, 128), width)
+        copies.append(pltpu.make_async_copy(modes_hbm.at[rows, :], out_ref, sems.at[k]))
+    for copy in copies:
+        copy.start()
+    for copy in copies:
+        copy.wait()
 
 
-def stage(modes, width):
+def edges(modes, width):
     edge = jax.ShapeDtypeStruct((width, modes.shape[1]), modes.dtype)
     return pl.pallas_call(
-        stage_kernel,
+        edges_kernel,
         out_shape=(edge, edge),
-        in_specs=[pl.BlockSpec(memory_space=pltpu.VMEM)],
+        in_specs=[pl.BlockSpec(memory_space=pltpu.HBM)],
         out_specs=(pl.BlockSpec(memory_space=pltpu.VMEM),) * 2,
+        scratch_shapes=[pltpu.SemaphoreType.DMA((2,))],
         compiler_params=pltpu.CompilerParams(vmem_limit_bytes=JOIN_VMEM),
-        cost_estimate=pl.CostEstimate(flops=STAGE_COST, bytes_accessed=4 * edge.size * 2, transcendentals=0),
-        name="stage",
-    )(modes)
+        cost_estimate=pl.CostEstimate(flops=EDGES_COST, bytes_accessed=4 * edge.size * 2, transcendentals=0),
+        name="edges",
+    )(pltpu.with_memory_space_constraint(modes, pltpu.HBM))
 
 
 def own_kernel(blocks, nb_ref, jac, modes, p_ref, t_ref, turned, jv, parts, face):
@@ -153,7 +159,7 @@
     rows, n_modes = modes.shape
     count = lax.axis_size("cell")
     across = [(i, min(max(i - 1 + 2 * (i % 2), 0), count - 1)) for i in range(count)]
-    outer, inner = stage(modes, width)
+    outer, inner = edges(modes, width)
     outer = lax.ppermute(outer, "cell", across)
     inner = lax.ppermute(inner, "cell", [(i, i ^ 1) for i in range(count)])
     p, t = own_part(neighbours.T, jac_blocks, modes)

time: 30.3 us -> 30.2 us (level)
  local copies, waits for them, and re-layouts: 4.49 us -> 2.28 us
  Pallas kernels: 5.58 us -> 7.62 us
    unnamed x8 -> x6, local copies, waits for them, and re-layouts: 4.49 us -> 2.28 us
    pallas_call x1, Pallas kernels: 0.07 us -> 1.24 us  [edges(): pl.pallas_call(edges_kernel, out_shape=(edge, edge), in_specs=[pl.BlockSp...]
    pallas_call x1, Pallas kernels: 4.95 us -> 5.82 us  [own_part(): pl.pallas_call(functools.partial(own_kernel, blocks), out_shape=(jax.Shap...]
  transfers between devices with their start and end apart: 3 -> 3, of which waited for: 1 -> 1; matrix products, arithmetic and copies ran while one was open for 0% -> 0% of each run, Pallas kernels for 16% -> 19%
where the time goes in v6:
time: 30.2 us; the launch traced here: 30 us
  blocking collectives  13.5 us (45%)
  Pallas kernels  7.62 us (25%)
  starting transfers between devices  4.94 us (16%)
  local copies, waits for them, and re-layouts  2.28 us (8%)
  waiting for transfers between devices  0.99 us (3%)
  other arithmetic  0.63 us (2%)
    all_to_all x1, blocking collectives, per_device(): parts = lax.all_to_all(pair, 'cell', 0, 0, axis_index_groups=same_core)  13.5 us
    pallas_call x1, Pallas kernels, own_part(): pl.pallas_call(functools.partial(own_kernel, blocks), out_shape=(jax.Shap...  5.82 us
    ppermute x1, starting transfers between devices, per_device(): got = lax.ppermute(give, 'cell', [(i, i ^ 1) for i in range(count)])  3.61 us
    unnamed x6, local copies, waits for them, and re-layouts  2.28 us
    pallas_call x1, Pallas kernels, edges(): pl.pallas_call(edges_kernel, out_shape=(edge, edge), in_specs=[pl.BlockSp...  1.24 us
    ppermute x1, waiting for transfers between devices, per_device(): got = lax.ppermute(give, 'cell', [(i, i ^ 1) for i in range(count)])  0.99 us
    ppermute x1, starting transfers between devices, per_device(): outer = lax.ppermute(outer, 'cell', across)  0.8 us
    reduce_sum x1, other arithmetic, per_device(): return jnp.sum(parts, axis=0)  0.62 us
  transfers between devices with their start and end apart: 3, of which 1 were waited for; matrix products, arithmetic and copies ran while one was open for 0% of the time, Pallas kernels for 19%

profile of v6, /device:TPU:0, one launch (start us, length us, event | category | flops | bytes accessed | tf_op | source)
XLA Modules:
  0.0 30.0 jit_solution(17658775315389547559)
XLA Ops:
  0.0 0.0 copy-start.1
  0.0 0.0 copy-start.2
  0.0 0.0 copy-start
  0.0 1.2 %edges.1 = (bf16[640,256]{1,0:T(8,128)(2,1)S(1)}, bf16[640,256]{1,0:T(8,128)(2,1)S(1)}) custom-call(bf16[2560,256]{1,0:T(8,128)(2,1)} %modes_hbm.1), custom_call_target="tpu_custom_call" | custom-call | flops 10000000000 | bytes 1310720 | tf_op jit(solution)/shard_map/edges/pallas_call | solution.py:40
  1.3 0.5 %collective-permute-start = (bf16[640,256]{1,0:T(8,128)(2,1)S(1)}, bf16[640,256]{1,0:T(8,128)(2,1)S(1)}, u32[]{:S(2)}, u32[]{:S(2)}) collective-permute-start(bf16[640,256]{1,0:T(8,128)(2,1)S(1)} %get-tuple-element.13), channel_id=1, source_target_pairs={{0,1},{1,0},{2,3},{3,2},{4,5},{5,4},{6,7},{7,6},{8,9},{9,8},{10,11... | collective-permute-start | bytes 983048 | tf_op jit(solution)/shard_map/ppermute | solution.py:164
  1.8 0.8 %collective-permute-start.1 = (bf16[640,256]{1,0:T(8,128)(2,1)S(1)}, bf16[640,256]{1,0:T(8,128)(2,1)S(1)}, u32[]{:S(2)}, u32[]{:S(2)}) collective-permute-start(bf16[640,256]{1,0:T(8,128)(2,1)S(1)} %get-tuple-element.14), channel_id=1, source_target_pairs={{0,0},{1,2},{2,1},{3,4},{4,3},{5,6},{6,5},{7,8},{8,7},{9,10},{10,9... | collective-permute-start | bytes 983048 | tf_op jit(solution)/shard_map/ppermute | solution.py:163
  2.6 0.0 copy-done.1
  2.6 0.0 copy-done.2
  2.6 2.3 %copy-done = bf16[14,640,640]{2,1,0:T(8,128)(2,1)S(1)} copy-done((bf16[14,640,640]{2,1,0:T(8,128)(2,1)S(1)}, bf16[14,640,640]{2,1,0:T(8,128)(2,1)}, u32[]{:S(2)}) %copy-start) | copy-done | bytes 11468824
  4.9 5.8 %own_part.1 = (f32[256,256]{1,0:T(8,128)S(1)}, bf16[2,2,256,640]{3,2,1,0:T(8,128)(2,1)S(1)}) custom-call(s32[2,14]{1,0:T(2,128)S(1)} %bitcast.2, bf16[14,640,640]{2,1,0:T(8,128)(2,1)S(1)} %copy-done, bf16[2560,256]{1,0:T(8,128)(2,1)S(1)} %copy-done.1), custom_call_target="tpu_custom_call" | custom-call | flops 3607101440 | bytes 12779520 | tf_op jit(solution)/shard_map/own_part/pallas_call | solution.py:104
  10.7 0.0 collective-permute-done.inner_ref
  10.7 0.0 collective-permute-done.1.outer_ref
  10.7 0.6 %join.1 = (f32[128,256]{1,0:T(8,128)S(1)}, f32[128,256]{1,0:T(8,128)S(1)}) custom-call(f32[256,256]{1,0:T(8,128)S(1)} %get-tuple-element.11.p_ref, bf16[2,2,256,640]{3,2,1,0:T(8,128)(2,1)S(1)} %get-tuple-element.12.t_ref, bf16[640,256]{1,0:T(8,128)(2,1)S(1)} %collective-permute-done.inner_ref, bf16[640,256]{1,0:T(8,128)(2,1)S(1)} %collective-permute-done.1.outer_ref), custom_call_target="tpu_custom_call" | custom-call | tf_op jit(solution)/shard_map/join/pallas_call | solution.py:147
  11.3 3.6 %collective-permute-start.2 = (f32[128,256]{1,0:T(8,128)S(1)}, f32[128,256]{1,0:T(8,128)S(1)}, u32[]{:S(2)}, u32[]{:S(2)}) collective-permute-start(f32[128,256]{1,0:T(8,128)S(1)} %get-tuple-element.16), channel_id=1, source_target_pairs={{0,1},{1,0},{2,3},{3,2},{4,5},{5,4},{6,7},{7,6},{8,9},{9,8},{10,11... | collective-permute-start | bytes 393224 | tf_op jit(solution)/shard_map/ppermute | solution.py:167
  14.9 1.0 %collective-permute-done.2 = f32[128,256]{1,0:T(8,128)S(1)} collective-permute-done((f32[128,256]{1,0:T(8,128)S(1)}, f32[128,256]{1,0:T(8,128)S(1)}, u32[]{:S(2)}, u32[]{:S(2)}) %collective-permute-start.2) | collective-permute-done | bytes 131104 | tf_op jit(solution)/shard_map/ppermute | solution.py:167
  15.9 13.5 %all_to_all.5 = f32[8,16,256]{2,1,0:T(8,128)S(1)} all-to-all(f32[8,16,256]{2,1,0:T(8,128)S(1)} %bitcast.3), channel_id=1, replica_groups={{0,2,4,6,8,10,12,14},{1,3,5,7,9,11,13,15},{16,18,20,22,24,26,28,30},{17..., dimensions={0} | all-to-all | bytes 262144 | tf_op jit(solution)/shard_map/all_to_all | solution.py:170
  29.4 0.6 %reduce_sum.9 = f32[16,256]{1,0:T(8,128)} reduce(f32[8,16,256]{2,1,0:T(8,128)S(1)} %all_to_all.5, f32[]{:T(128)} %constant.0.clone.1), dimensions={0}, to_apply=%region_0.0 | reduce | flops 28672 | bytes 147460 | tf_op jit(solution)/shard_map/reduce_sum | solution.py:171
  (1 shorter events, 0.0 us)
Async XLA Ops:
  0.0 2.6 %copy-start.1 = (bf16[2560,256]{1,0:T(8,128)(2,1)S(1)}, bf16[2560,256]{1,0:T(8,128)(2,1)}, u32[]{:S(2)}) copy-start(bf16[2560,256]{1,0:T(8,128)(2,1)} %modes_hbm.1) | copy-start | bytes 3932164
  0.0 2.6 %copy-start.2 = (s32[14,2]{0,1:T(2,128)S(1)}, s32[14,2]{0,1:T(2,128)}, u32[]{:S(2)}) copy-start(s32[14,2]{0,1:T(2,128)} %param.5) | copy-start | bytes 340
  0.0 4.9 %copy-start = (bf16[14,640,640]{2,1,0:T(8,128)(2,1)S(1)}, bf16[14,640,640]{2,1,0:T(8,128)(2,1)}, u32[]{:S(2)}) copy-start(bf16[14,640,640]{2,1,0:T(8,128)(2,1)} %jac.1) | copy-start | bytes 34406404
  1.3 9.5 %collective-permute-start = (bf16[640,256]{1,0:T(8,128)(2,1)S(1)}, bf16[640,256]{1,0:T(8,128)(2,1)S(1)}, u32[]{:S(2)}, u32[]{:S(2)}) collective-permute-start(bf16[640,256]{1,0:T(8,128)(2,1)S(1)} %get-tuple-element.13), channel_id=1, source_target_pairs={{0,1},{1,0},{2,3},{3,2},{4,5},{5,4},{6,7},{7,6},{8,9},{9,8},{10,11... | collective-permute-start | bytes 983048 | tf_op jit(solution)/shard_map/ppermute | solution.py:164
  1.8 8.9 %collective-permute-start.1 = (bf16[640,256]{1,0:T(8,128)(2,1)S(1)}, bf16[640,256]{1,0:T(8,128)(2,1)S(1)}, u32[]{:S(2)}, u32[]{:S(2)}) collective-permute-start(bf16[640,256]{1,0:T(8,128)(2,1)S(1)} %get-tuple-element.14), channel_id=1, source_target_pairs={{0,0},{1,2},{2,1},{3,4},{4,3},{5,6},{6,5},{7,8},{8,7},{9,10},{10,9... | collective-permute-start | bytes 983048 | tf_op jit(solution)/shard_map/ppermute | solution.py:163
  11.3 4.6 %collective-permute-start.2 = (f32[128,256]{1,0:T(8,128)S(1)}, f32[128,256]{1,0:T(8,128)S(1)}, u32[]{:S(2)}, u32[]{:S(2)}) collective-permute-start(f32[128,256]{1,0:T(8,128)S(1)} %get-tuple-element.16), channel_id=1, source_target_pairs={{0,1},{1,0},{2,3},{3,2},{4,5},{5,4},{6,7},{7,6},{8,9},{9,8},{10,11... | collective-permute-start | bytes 393224 | tf_op jit(solution)/shard_map/ppermute | solution.py:167

commit v7 on v6

--- a/solution.py
+++ b/solution.py
@@ -8,8 +8,8 @@
 from jax.sharding import PartitionSpec as P
 
 OWN_VMEM = 24 * 2**20
-JOIN_VMEM = 8 * 2**20
-EDGES_COST = 10**10
+SMALL_VMEM = 8 * 2**20
+LOAD_COST = 5 * 10**9
 
 
 def dot(a, b):
@@ -43,10 +43,24 @@
         in_specs=[pl.BlockSpec(memory_space=pltpu.HBM)],
         out_specs=(pl.BlockSpec(memory_space=pltpu.VMEM),) * 2,
         scratch_shapes=[pltpu.SemaphoreType.DMA((2,))],
-        compiler_params=pltpu.CompilerParams(vmem_limit_bytes=JOIN_VMEM),
-        cost_estimate=pl.CostEstimate(flops=EDGES_COST, bytes_accessed=4 * edge.size * 2, transcendentals=0),
+        compiler_params=pltpu.CompilerParams(vmem_limit_bytes=SMALL_VMEM),
+        cost_estimate=pl.CostEstimate(flops=0, bytes_accessed=4 * edge.size * 2, transcendentals=0),
         name="edges",
     )(pltpu.with_memory_space_constraint(modes, pltpu.HBM))
+
+
+def gate(outer, inner):
+    edge = jax.ShapeDtypeStruct(outer.shape, outer.dtype)
+    return pl.pallas_call(
+        lambda *refs: None,
+        out_shape=(edge, edge),
+        in_specs=[pl.BlockSpec(memory_space=pltpu.VMEM)] * 2,
+        out_specs=(pl.BlockSpec(memory_space=pltpu.VMEM),) * 2,
+        input_output_aliases={0: 0, 1: 1},
+        compiler_params=pltpu.CompilerParams(vmem_limit_bytes=SMALL_VMEM),
+        cost_estimate=pl.CostEstimate(flops=LOAD_COST, bytes_accessed=0, transcendentals=0),
+        name="gate",
+    )(outer, inner)
 
 
 def own_kernel(blocks, nb_ref, jac, modes, p_ref, t_ref, turned, jv, parts, face):
@@ -124,7 +138,7 @@
             flops=flops, bytes_accessed=slots * width * width * 2 + rows * n_modes * 2, transcendentals=0
         ),
         name="own_part",
-    )(neighbours, jac_blocks, modes)
+    )(neighbours, pltpu.with_memory_space_constraint(jac_blocks, pltpu.VMEM), modes)
 
 
 def join_kernel(rows, p_ref, t_ref, inner_ref, outer_ref, keep_ref, give_ref):
@@ -149,7 +163,7 @@
         out_shape=(half, half),
         in_specs=[pl.BlockSpec(memory_space=pltpu.VMEM)] * 4,
         out_specs=(pl.BlockSpec(memory_space=pltpu.VMEM),) * 2,
-        compiler_params=pltpu.CompilerParams(vmem_limit_bytes=JOIN_VMEM),
+        compiler_params=pltpu.CompilerParams(vmem_limit_bytes=SMALL_VMEM),
         name="join",
     )(p, t, inner, outer)
 
@@ -159,7 +173,7 @@
     rows, n_modes = modes.shape
     count = lax.axis_size("cell")
     across = [(i, min(max(i - 1 + 2 * (i % 2), 0), count - 1)) for i in range(count)]
-    outer, inner = edges(modes, width)
+    outer, inner = gate(*edges(modes, width))
     outer = lax.ppermute(outer, "cell", across)
     inner = lax.ppermute(inner, "cell", [(i, i ^ 1) for i in range(count)])
     p, t = own_part(neighbours.T, jac_blocks, modes)

time: 30.2 us -> 30.1 us (level)
  starting transfers between devices: 4.94 us -> 3.78 us
  local copies, waits for them, and re-layouts: 2.28 us -> 3.31 us
    ppermute x1, starting transfers between devices: 3.61 us -> 2.46 us  [per_device(): got = lax.ppermute(give, 'cell', [(i, i ^ 1) for i in range(count)])]
    unnamed x6, local copies, waits for them, and re-layouts: 2.28 us -> 3.31 us
where the time goes in v7:
time: 30.1 us; the launch traced here: 29.9 us
  blocking collectives  13.6 us (45%)
  Pallas kernels  7.44 us (25%)
  starting transfers between devices  3.78 us (13%)
  local copies, waits for them, and re-layouts  3.31 us (11%)
  waiting for transfers between devices  0.99 us (3%)
  other arithmetic  0.63 us (2%)
    all_to_all x1, blocking collectives, per_device(): parts = lax.all_to_all(pair, 'cell', 0, 0, axis_index_groups=same_core)  13.6 us
    pallas_call x1, Pallas kernels, own_part(): pl.pallas_call(functools.partial(own_kernel, blocks), out_shape=(jax.Shap...  5.79 us
    unnamed x6, local copies, waits for them, and re-layouts  3.31 us
    ppermute x1, starting transfers between devices, per_device(): got = lax.ppermute(give, 'cell', [(i, i ^ 1) for i in range(count)])  2.46 us
    pallas_call x1, Pallas kernels, edges(): pl.pallas_call(edges_kernel, out_shape=(edge, edge), in_specs=[pl.BlockSp...  1.09 us
    ppermute x1, waiting for transfers between devices, per_device(): got = lax.ppermute(give, 'cell', [(i, i ^ 1) for i in range(count)])  0.99 us
    ppermute x1, starting transfers between devices, per_device(): outer = lax.ppermute(outer, 'cell', across)  0.8 us
    reduce_sum x1, other arithmetic, per_device(): return jnp.sum(parts, axis=0)  0.62 us
  transfers between devices with their start and end apart: 3, of which 1 were waited for; matrix products, arithmetic and copies ran while one was open for 0% of the time, Pallas kernels for 19%

profile of v7, /device:TPU:0, one launch (start us, length us, event | category | flops | bytes accessed | tf_op | source)
XLA Modules:
  0.0 29.9 jit_solution(16356407745756712898)
XLA Ops:
  0.0 1.1 %edges.1 = (bf16[640,256]{1,0:T(8,128)(2,1)S(1)}, bf16[640,256]{1,0:T(8,128)(2,1)S(1)}) custom-call(bf16[2560,256]{1,0:T(8,128)(2,1)} %modes_hbm.1), custom_call_target="tpu_custom_call" | custom-call | bytes 1310720 | tf_op jit(solution)/shard_map/edges/pallas_call | solution.py:40
  1.1 0.0 copy-start
  1.1 0.0 copy-start.1
  1.1 0.0 copy-start.2
  1.1 0.5 %collective-permute-start = (bf16[640,256]{1,0:T(8,128)(2,1)S(1)}, bf16[640,256]{1,0:T(8,128)(2,1)S(1)}, u32[]{:S(2)}, u32[]{:S(2)}) collective-permute-start(bf16[640,256]{1,0:T(8,128)(2,1)S(1)} %get-tuple-element.17), channel_id=1, source_target_pairs={{0,1},{1,0},{2,3},{3,2},{4,5},{5,4},{6,7},{7,6},{8,9},{9,8},{10,11... | collective-permute-start | bytes 983048 | tf_op jit(solution)/shard_map/ppermute | solution.py:178
  1.7 0.8 %collective-permute-start.1 = (bf16[640,256]{1,0:T(8,128)(2,1)S(1)}, bf16[640,256]{1,0:T(8,128)(2,1)S(1)}, u32[]{:S(2)}, u32[]{:S(2)}) collective-permute-start(bf16[640,256]{1,0:T(8,128)(2,1)S(1)} %get-tuple-element.18), channel_id=1, source_target_pairs={{0,0},{1,2},{2,1},{3,4},{4,3},{5,6},{6,5},{7,8},{8,7},{9,10},{10,9... | collective-permute-start | bytes 983048 | tf_op jit(solution)/shard_map/ppermute | solution.py:177
  2.5 0.0 copy-done
  2.5 3.3 %copy-done.1 = bf16[14,640,640]{2,1,0:T(8,128)(2,1)S(1)} copy-done((bf16[14,640,640]{2,1,0:T(8,128)(2,1)S(1)}, bf16[14,640,640]{2,1,0:T(8,128)(2,1)}, u32[]{:S(2)}) %copy-start.1) | copy-done | bytes 11468824
  5.8 0.0 copy-done.2
  5.8 5.8 %own_part.1 = (f32[256,256]{1,0:T(8,128)S(1)}, bf16[2,2,256,640]{3,2,1,0:T(8,128)(2,1)S(1)}) custom-call(s32[2,14]{1,0:T(2,128)S(1)} %bitcast.2, bf16[14,640,640]{2,1,0:T(8,128)(2,1)S(1)} %copy-done.1, bf16[2560,256]{1,0:T(8,128)(2,1)S(1)} %copy-done), custom_call_target="tpu_custom_call" | custom-call | flops 3607101440 | bytes 12779520 | tf_op jit(solution)/shard_map/own_part/pallas_call | solution.py:118
  11.6 0.0 collective-permute-done.inner_ref
  11.6 0.0 collective-permute-done.1.outer_ref
  11.6 0.6 %join.1 = (f32[128,256]{1,0:T(8,128)S(1)}, f32[128,256]{1,0:T(8,128)S(1)}) custom-call(f32[256,256]{1,0:T(8,128)S(1)} %get-tuple-element.13.p_ref, bf16[2,2,256,640]{3,2,1,0:T(8,128)(2,1)S(1)} %get-tuple-element.14.t_ref, bf16[640,256]{1,0:T(8,128)(2,1)S(1)} %collective-permute-done.inner_ref, bf16[640,256]{1,0:T(8,128)(2,1)S(1)} %collective-permute-done.1.outer_ref), custom_call_target="tpu_custom_call" | custom-call | tf_op jit(solution)/shard_map/join/pallas_call | solution.py:161
  12.2 2.5 %collective-permute-start.2 = (f32[128,256]{1,0:T(8,128)S(1)}, f32[128,256]{1,0:T(8,128)S(1)}, u32[]{:S(2)}, u32[]{:S(2)}) collective-permute-start(f32[128,256]{1,0:T(8,128)S(1)} %get-tuple-element.20), channel_id=1, source_target_pairs={{0,1},{1,0},{2,3},{3,2},{4,5},{5,4},{6,7},{7,6},{8,9},{9,8},{10,11... | collective-permute-start | bytes 393224 | tf_op jit(solution)/shard_map/ppermute | solution.py:181
  14.6 1.0 %collective-permute-done.2 = f32[128,256]{1,0:T(8,128)S(1)} collective-permute-done((f32[128,256]{1,0:T(8,128)S(1)}, f32[128,256]{1,0:T(8,128)S(1)}, u32[]{:S(2)}, u32[]{:S(2)}) %collective-permute-start.2) | collective-permute-done | bytes 131104 | tf_op jit(solution)/shard_map/ppermute | solution.py:181
  15.6 13.6 %all_to_all.5 = f32[8,16,256]{2,1,0:T(8,128)S(1)} all-to-all(f32[8,16,256]{2,1,0:T(8,128)S(1)} %bitcast.3), channel_id=1, replica_groups={{0,2,4,6,8,10,12,14},{1,3,5,7,9,11,13,15},{16,18,20,22,24,26,28,30},{17..., dimensions={0} | all-to-all | bytes 262144 | tf_op jit(solution)/shard_map/all_to_all | solution.py:184
  29.3 0.6 %reduce_sum.9 = f32[16,256]{1,0:T(8,128)} reduce(f32[8,16,256]{2,1,0:T(8,128)S(1)} %all_to_all.5, f32[]{:T(128)} %constant.0.clone.1), dimensions={0}, to_apply=%region_0.0 | reduce | flops 28672 | bytes 147460 | tf_op jit(solution)/shard_map/reduce_sum | solution.py:185
  (2 shorter events, 0.0 us)
Async XLA Ops:
  1.1 1.4 %copy-start = (bf16[2560,256]{1,0:T(8,128)(2,1)S(1)}, bf16[2560,256]{1,0:T(8,128)(2,1)}, u32[]{:S(2)}) copy-start(bf16[2560,256]{1,0:T(8,128)(2,1)} %modes_hbm.1) | copy-start | bytes 3932164
  1.1 4.7 %copy-start.1 = (bf16[14,640,640]{2,1,0:T(8,128)(2,1)S(1)}, bf16[14,640,640]{2,1,0:T(8,128)(2,1)}, u32[]{:S(2)}) copy-start(bf16[14,640,640]{2,1,0:T(8,128)(2,1)} %jac.1) | copy-start | bytes 34406404
  1.1 4.7 %copy-start.2 = (s32[14,2]{0,1:T(2,128)S(1)}, s32[14,2]{0,1:T(2,128)}, u32[]{:S(2)}) copy-start(s32[14,2]{0,1:T(2,128)} %param.5) | copy-start | bytes 340
  1.1 10.4 %collective-permute-start = (bf16[640,256]{1,0:T(8,128)(2,1)S(1)}, bf16[640,256]{1,0:T(8,128)(2,1)S(1)}, u32[]{:S(2)}, u32[]{:S(2)}) collective-permute-start(bf16[640,256]{1,0:T(8,128)(2,1)S(1)} %get-tuple-element.17), channel_id=1, source_target_pairs={{0,1},{1,0},{2,3},{3,2},{4,5},{5,4},{6,7},{7,6},{8,9},{9,8},{10,11... | collective-permute-start | bytes 983048 | tf_op jit(solution)/shard_map/ppermute | solution.py:178
  1.7 9.9 %collective-permute-start.1 = (bf16[640,256]{1,0:T(8,128)(2,1)S(1)}, bf16[640,256]{1,0:T(8,128)(2,1)S(1)}, u32[]{:S(2)}, u32[]{:S(2)}) collective-permute-start(bf16[640,256]{1,0:T(8,128)(2,1)S(1)} %get-tuple-element.18), channel_id=1, source_target_pairs={{0,0},{1,2},{2,1},{3,4},{4,3},{5,6},{6,5},{7,8},{8,7},{9,10},{10,9... | collective-permute-start | bytes 983048 | tf_op jit(solution)/shard_map/ppermute | solution.py:177
  12.2 3.4 %collective-permute-start.2 = (f32[128,256]{1,0:T(8,128)S(1)}, f32[128,256]{1,0:T(8,128)S(1)}, u32[]{:S(2)}, u32[]{:S(2)}) collective-permute-start(f32[128,256]{1,0:T(8,128)S(1)} %get-tuple-element.20), channel_id=1, source_target_pairs={{0,1},{1,0},{2,3},{3,2},{4,5},{5,4},{6,7},{7,6},{8,9},{9,8},{10,11... | collective-permute-start | bytes 393224 | tf_op jit(solution)/shard_map/ppermute | solution.py:181

commit v8 on v6

--- a/solution.py
+++ b/solution.py
@@ -9,6 +9,7 @@
 
 OWN_VMEM = 24 * 2**20
 JOIN_VMEM = 8 * 2**20
+TILE_ROWS = 16
 EDGES_COST = 10**10
 
 
@@ -49,7 +50,7 @@
     )(pltpu.with_memory_space_constraint(modes, pltpu.HBM))
 
 
-def own_kernel(blocks, nb_ref, jac, modes, p_ref, t_ref, turned, jv, parts, face):
+def own_kernel(blocks, keep_rows, nb_ref, jac, modes, p_ref, t_ref, turned, jv, parts, face):
     slots, width, _ = jac.shape
     n_modes = modes.shape[1]
 
@@ -57,7 +58,13 @@
     for s in range(blocks):
         rows = pl.ds(s * width, width)
         jv[rows, :] = dot(jac[s], modes[rows, :])
-        turned[:, rows] = modes[rows, :].T
+        block = modes[rows, :].T
+        if keep_rows % TILE_ROWS:
+            turned[:, rows] = block
+        else:
+            for k in range(n_modes // keep_rows):
+                place = k % 2 * (n_modes // 2) + k // 2 * keep_rows
+                turned[place : place + keep_rows, rows] = block[k * keep_rows : (k + 1) * keep_rows]
     base = nb_ref[1, 0]
     last = (blocks - 1) * width
 
@@ -96,13 +103,13 @@
     p_ref[...] = both[:, :n_modes] + both[:, n_modes:]
 
 
-def own_part(neighbours, jac_blocks, modes):
+def own_part(keep_rows, neighbours, jac_blocks, modes):
     slots, width, _ = jac_blocks.shape
     rows, n_modes = modes.shape
     blocks = rows // width
     flops = 2 * n_modes * width * width * slots + 4 * rows * n_modes * n_modes
     return pl.pallas_call(
-        functools.partial(own_kernel, blocks),
+        functools.partial(own_kernel, blocks, keep_rows),
         out_shape=(
             jax.ShapeDtypeStruct((n_modes, n_modes), jnp.float32),
             jax.ShapeDtypeStruct((2, 2, n_modes, width), jnp.bfloat16),
@@ -127,45 +134,53 @@
     )(neighbours, jac_blocks, modes)
 
 
-def join_kernel(rows, p_ref, t_ref, inner_ref, outer_ref, keep_ref, give_ref):
-    total = p_ref[...]
+def regrouped(value, axis, keep_rows):
+    shape = value.shape
+    split = shape[:axis] + (shape[axis] // (2 * keep_rows), 2, keep_rows) + shape[axis + 1 :]
+    return jnp.swapaxes(value.reshape(split), axis, axis + 1).reshape(shape)
+
+
+def join_kernel(other, p_ref, t_ref, outer_ref, inner_ref, out_ref):
     core = lax.rem(lax.axis_index("cell"), 2)
+    count = out_ref.shape[0]
+    half = 1 - core if other else core
+    rows = pl.ds(pl.multiple_of(half * count, TILE_ROWS), count)
+    total = p_ref[rows, :]
     for side, halo in ((1 - core, inner_ref), (core, outer_ref)):
         for part in range(2):
-            total += dot(t_ref[side, part], halo[...])
-    first = core == 0
-    for chip in range(total.shape[0] // (2 * rows)):
-        even = total[2 * chip * rows : (2 * chip + 1) * rows]
-        odd = total[(2 * chip + 1) * rows : (2 * chip + 2) * rows]
-        place = slice(chip * rows, (chip + 1) * rows)
-        keep_ref[place, :] = jnp.where(first, even, odd)
-        give_ref[place, :] = jnp.where(first, odd, even)
+            total += dot(t_ref[side, part, rows, :], halo[...])
+    out_ref[...] = total
 
 
-def join(rows, p, t, inner, outer):
-    half = jax.ShapeDtypeStruct((p.shape[0] // 2, p.shape[1]), jnp.float32)
+def join(other, p, t, outer, inner):
+    rows = p.shape[0] // 2
     return pl.pallas_call(
-        functools.partial(join_kernel, rows),
-        out_shape=(half, half),
+        functools.partial(join_kernel, other),
+        out_shape=jax.ShapeDtypeStruct((rows, p.shape[1]), jnp.float32),
         in_specs=[pl.BlockSpec(memory_space=pltpu.VMEM)] * 4,
-        out_specs=(pl.BlockSpec(memory_space=pltpu.VMEM),) * 2,
+        out_specs=pl.BlockSpec(memory_space=pltpu.VMEM),
         compiler_params=pltpu.CompilerParams(vmem_limit_bytes=JOIN_VMEM),
-        name="join",
-    )(p, t, inner, outer)
+        cost_estimate=pl.CostEstimate(flops=8 * rows * outer.size, bytes_accessed=0, transcendentals=0),
+        name="join_give" if other else "join_keep",
+    )(p, t, outer, inner)
 
 
 def per_device(jac_blocks, modes, neighbours):
     width = jac_blocks.shape[1]
     rows, n_modes = modes.shape
     count = lax.axis_size("cell")
+    keep_rows = n_modes // count
     across = [(i, min(max(i - 1 + 2 * (i % 2), 0), count - 1)) for i in range(count)]
+    swap = [(i, i ^ 1) for i in range(count)]
     outer, inner = edges(modes, width)
     outer = lax.ppermute(outer, "cell", across)
-    inner = lax.ppermute(inner, "cell", [(i, i ^ 1) for i in range(count)])
-    p, t = own_part(neighbours.T, jac_blocks, modes)
-    keep, give = join(n_modes // count, p, t, inner, outer)
-    got = lax.ppermute(give, "cell", [(i, i ^ 1) for i in range(count)])
-    pair = (keep + got).reshape(count // 2, n_modes // count, n_modes)
+    inner = lax.ppermute(inner, "cell", swap)
+    p, t = own_part(keep_rows, neighbours.T, jac_blocks, modes)
+    if keep_rows % TILE_ROWS:
+        p, t = regrouped(p, 0, keep_rows), regrouped(t, 2, keep_rows)
+    got = lax.ppermute(join(True, p, t, outer, inner), "cell", swap)
+    keep = join(False, p, t, outer, inner)
+    pair = (keep + got).reshape(count // 2, keep_rows, n_modes)
     same_core = [list(range(core, count, 2)) for core in range(2)]
     parts = lax.all_to_all(pair, "cell", 0, 0, axis_index_groups=same_core)
     return jnp.sum(parts, axis=0)

time: 30.2 us -> 29.5 us (0.977)
  starting transfers between devices: 4.94 us -> 7.41 us
  local copies, waits for them, and re-layouts: 2.28 us -> 0.01 us
  waiting for transfers between devices: 0.99 us -> 0.63 us
    ppermute x2, starting transfers between devices: 4.14 us -> 6.6 us  [the longest x1 4.52 us: per_device(): inner = lax.ppermute(inner, 'cell', swap)]
    unnamed x6, local copies, waits for them, and re-layouts: 2.28 us -> 0.01 us
    ppermute x2, waiting for transfers between devices: 0.99 us -> 0.63 us  [the longest x1 0.62 us: per_device(): got = lax.ppermute(join(True, p, t, outer, inner), 'cell', swap)]
    pallas_call x2 -> x3, Pallas kernels: 6.39 us -> 6.11 us  [the longest x1 5.39 us: own_part(): pl.pallas_call(functools.partial(own_kernel, blocks, keep_rows), out_shap...]
  transfers between devices with their start and end apart: 3 -> 3, of which waited for: 1 -> 1; matrix products, arithmetic and copies ran while one was open for 0% -> 0% of each run, Pallas kernels for 19% -> 20%
where the time goes in v8:
time: 29.5 us; the launch traced here: 29.3 us
  blocking collectives  13.2 us (45%)
  starting transfers between devices  7.41 us (25%)
  Pallas kernels  7.34 us (25%)
  waiting for transfers between devices  0.63 us (2%)
  other arithmetic  0.63 us (2%)
    all_to_all x1, blocking collectives, per_device(): parts = lax.all_to_all(pair, 'cell', 0, 0, axis_index_groups=same_core)  13.2 us
    pallas_call x1, Pallas kernels, own_part(): pl.pallas_call(functools.partial(own_kernel, blocks, keep_rows), out_shap...  5.39 us
    ppermute x1, starting transfers between devices, per_device(): inner = lax.ppermute(inner, 'cell', swap)  4.52 us
    ppermute x1, starting transfers between devices, per_device(): got = lax.ppermute(join(True, p, t, outer, inner), 'cell', swap)  2.08 us
    pallas_call x1, Pallas kernels, edges(): pl.pallas_call(edges_kernel, out_shape=(edge, edge), in_specs=[pl.BlockSp...  1.24 us
    ppermute x1, starting transfers between devices, per_device(): outer = lax.ppermute(outer, 'cell', across)  0.81 us
    pallas_call x2, Pallas kernels, join(): pl.pallas_call(functools.partial(join_kernel, other), out_shape=jax.Shape...  0.71 us
    ppermute x1, waiting for transfers between devices, per_device(): got = lax.ppermute(join(True, p, t, outer, inner), 'cell', swap)  0.62 us
  transfers between devices with their start and end apart: 3, of which 1 were waited for; matrix products, arithmetic and copies ran while one was open for 0% of the time, Pallas kernels for 20%

profile of v8, /device:TPU:0, one launch (start us, length us, event | category | flops | bytes accessed | tf_op | source)
XLA Modules:
  0.0 29.3 jit_solution(3198396973998184104)
XLA Ops:
  0.0 0.0 copy-start.1
  0.0 0.0 copy-start.2
  0.0 0.0 copy-start
  0.0 1.2 %edges.1 = (bf16[640,256]{1,0:T(8,128)(2,1)S(1)}, bf16[640,256]{1,0:T(8,128)(2,1)S(1)}) custom-call(bf16[2560,256]{1,0:T(8,128)(2,1)} %modes_hbm.1), custom_call_target="tpu_custom_call" | custom-call | flops 10000000000 | bytes 1310720 | tf_op jit(solution)/shard_map/edges/pallas_call | solution.py:41
  1.3 0.8 %collective-permute-start = (bf16[640,256]{1,0:T(8,128)(2,1)S(1)}, bf16[640,256]{1,0:T(8,128)(2,1)S(1)}, u32[]{:S(2)}, u32[]{:S(2)}) collective-permute-start(bf16[640,256]{1,0:T(8,128)(2,1)S(1)} %get-tuple-element.11), channel_id=1, source_target_pairs={{0,0},{1,2},{2,1},{3,4},{4,3},{5,6},{6,5},{7,8},{8,7},{9,10},{10,9... | collective-permute-start | bytes 983048 | tf_op jit(solution)/shard_map/ppermute | solution.py:176
  2.1 4.5 %collective-permute-start.1 = (bf16[640,256]{1,0:T(8,128)(2,1)S(1)}, bf16[640,256]{1,0:T(8,128)(2,1)S(1)}, u32[]{:S(2)}, u32[]{:S(2)}) collective-permute-start(bf16[640,256]{1,0:T(8,128)(2,1)S(1)} %get-tuple-element.12), channel_id=1, source_target_pairs={{0,1},{1,0},{2,3},{3,2},{4,5},{5,4},{6,7},{7,6},{8,9},{9,8},{10,11... | collective-permute-start | bytes 983048 | tf_op jit(solution)/shard_map/ppermute | solution.py:177
  6.6 0.0 copy-done.1
  6.6 0.0 copy-done.2
  6.6 0.0 copy-done
  6.6 5.4 %own_part.1 = (f32[256,256]{1,0:T(8,128)S(1)}, bf16[2,2,256,640]{3,2,1,0:T(8,128)(2,1)S(1)}) custom-call(s32[2,14]{1,0:T(2,128)S(1)} %bitcast.2, bf16[14,640,640]{2,1,0:T(8,128)(2,1)S(1)} %copy-done, bf16[2560,256]{1,0:T(8,128)(2,1)S(1)} %copy-done.1), custom_call_target="tpu_custom_call" | custom-call | flops 3607101440 | bytes 12779520 | tf_op jit(solution)/shard_map/own_part/pallas_call | solution.py:111
  12.0 0.0 collective-permute-done.outer_ref
  12.0 0.0 collective-permute-done.1.inner_ref
  12.0 0.4 %join_give.1 = f32[128,256]{1,0:T(8,128)S(1)} custom-call(f32[256,256]{1,0:T(8,128)S(1)} %get-tuple-element.9.p_ref, bf16[2,2,256,640]{3,2,1,0:T(8,128)(2,1)S(1)} %get-tuple-element.10.t_ref, bf16[640,256]{1,0:T(8,128)(2,1)S(1)} %collective-permute-done.outer_ref, bf16[640,256]{1,0:T(8,128)(2,1)S(1)} %collective-permute-done.1.inner_ref), custom_call_target="tpu_custom_call" | custom-call | flops 167772160 | tf_op jit(solution)/shard_map/join_give/pallas_call | solution.py:157
  12.4 2.1 %collective-permute-start.2 = (f32[128,256]{1,0:T(8,128)S(1)}, f32[128,256]{1,0:T(8,128)S(1)}, u32[]{:S(2)}, u32[]{:S(2)}) collective-permute-start(f32[128,256]{1,0:T(8,128)S(1)} %join_give.1), channel_id=1, source_target_pairs={{0,1},{1,0},{2,3},{3,2},{4,5},{5,4},{6,7},{7,6},{8,9},{9,8},{10,11... | collective-permute-start | bytes 393224 | tf_op jit(solution)/shard_map/ppermute | solution.py:181
  14.5 0.4 %join_keep.1 = f32[128,256]{1,0:T(8,128)S(1)} custom-call(f32[256,256]{1,0:T(8,128)S(1)} %get-tuple-element.9.p_ref, bf16[2,2,256,640]{3,2,1,0:T(8,128)(2,1)S(1)} %get-tuple-element.10.t_ref, bf16[640,256]{1,0:T(8,128)(2,1)S(1)} %collective-permute-done.outer_ref, bf16[640,256]{1,0:T(8,128)(2,1)S(1)} %collective-permute-done.1.inner_ref), custom_call_target="tpu_custom_call" | custom-call | flops 167772160 | tf_op jit(solution)/shard_map/join_keep/pallas_call | solution.py:157
  14.8 0.6 %collective-permute-done.2 = f32[128,256]{1,0:T(8,128)S(1)} collective-permute-done((f32[128,256]{1,0:T(8,128)S(1)}, f32[128,256]{1,0:T(8,128)S(1)}, u32[]{:S(2)}, u32[]{:S(2)}) %collective-permute-start.2) | collective-permute-done | bytes 131104 | tf_op jit(solution)/shard_map/ppermute | solution.py:181
  15.5 13.2 %all_to_all.5 = f32[8,16,256]{2,1,0:T(8,128)S(1)} all-to-all(f32[8,16,256]{2,1,0:T(8,128)S(1)} %bitcast.3), channel_id=1, replica_groups={{0,2,4,6,8,10,12,14},{1,3,5,7,9,11,13,15},{16,18,20,22,24,26,28,30},{17..., dimensions={0} | all-to-all | bytes 262144 | tf_op jit(solution)/shard_map/all_to_all | solution.py:185
  28.7 0.6 %reduce_sum.9 = f32[16,256]{1,0:T(8,128)} reduce(f32[8,16,256]{2,1,0:T(8,128)S(1)} %all_to_all.5, f32[]{:T(128)} %constant.0.clone.1), dimensions={0}, to_apply=%region_0.0 | reduce | flops 28672 | bytes 147460 | tf_op jit(solution)/shard_map/reduce_sum | solution.py:186
  (1 shorter events, 0.0 us)
Async XLA Ops:
  0.0 6.6 %copy-start.1 = (bf16[2560,256]{1,0:T(8,128)(2,1)S(1)}, bf16[2560,256]{1,0:T(8,128)(2,1)}, u32[]{:S(2)}) copy-start(bf16[2560,256]{1,0:T(8,128)(2,1)} %modes_hbm.1) | copy-start | bytes 3932164
  0.0 6.6 %copy-start.2 = (s32[14,2]{0,1:T(2,128)S(1)}, s32[14,2]{0,1:T(2,128)}, u32[]{:S(2)}) copy-start(s32[14,2]{0,1:T(2,128)} %param.5) | copy-start | bytes 340
  0.0 6.6 %copy-start = (bf16[14,640,640]{2,1,0:T(8,128)(2,1)S(1)}, bf16[14,640,640]{2,1,0:T(8,128)(2,1)}, u32[]{:S(2)}) copy-start(bf16[14,640,640]{2,1,0:T(8,128)(2,1)} %jac.1) | copy-start | bytes 34406404
  1.3 10.8 %collective-permute-start = (bf16[640,256]{1,0:T(8,128)(2,1)S(1)}, bf16[640,256]{1,0:T(8,128)(2,1)S(1)}, u32[]{:S(2)}, u32[]{:S(2)}) collective-permute-start(bf16[640,256]{1,0:T(8,128)(2,1)S(1)} %get-tuple-element.11), channel_id=1, source_target_pairs={{0,0},{1,2},{2,1},{3,4},{4,3},{5,6},{6,5},{7,8},{8,7},{9,10},{10,9... | collective-permute-start | bytes 983048 | tf_op jit(solution)/shard_map/ppermute | solution.py:176
  2.1 9.9 %collective-permute-start.1 = (bf16[640,256]{1,0:T(8,128)(2,1)S(1)}, bf16[640,256]{1,0:T(8,128)(2,1)S(1)}, u32[]{:S(2)}, u32[]{:S(2)}) collective-permute-start(bf16[640,256]{1,0:T(8,128)(2,1)S(1)} %get-tuple-element.12), channel_id=1, source_target_pairs={{0,1},{1,0},{2,3},{3,2},{4,5},{5,4},{6,7},{7,6},{8,9},{9,8},{10,11... | collective-permute-start | bytes 983048 | tf_op jit(solution)/shard_map/ppermute | solution.py:177
  12.4 3.1 %collective-permute-start.2 = (f32[128,256]{1,0:T(8,128)S(1)}, f32[128,256]{1,0:T(8,128)S(1)}, u32[]{:S(2)}, u32[]{:S(2)}) collective-permute-start(f32[128,256]{1,0:T(8,128)S(1)} %join_give.1), channel_id=1, source_target_pairs={{0,1},{1,0},{2,3},{3,2},{4,5},{5,4},{6,7},{7,6},{8,9},{9,8},{10,11... | collective-permute-start | bytes 393224 | tf_op jit(solution)/shard_map/ppermute | solution.py:181

commit v9 on v8

--- a/solution.py
+++ b/solution.py
@@ -8,9 +8,9 @@
 from jax.sharding import PartitionSpec as P
 
 OWN_VMEM = 24 * 2**20
-JOIN_VMEM = 8 * 2**20
+SMALL_VMEM = 8 * 2**20
 TILE_ROWS = 16
-EDGES_COST = 10**10
+LOAD_COST = 5 * 10**9
 
 
 def dot(a, b):
@@ -22,32 +22,56 @@
     return upper, (value - upper.astype(jnp.float32)).astype(jnp.bfloat16)
 
 
-def edges_kernel(modes_hbm, outer_ref, inner_ref, sems):
-    width = outer_ref.shape[0]
-    last = modes_hbm.shape[0] - width
-    core = lax.rem(lax.axis_index("cell"), 2)
-    copies = []
-    for k, (side, out_ref) in enumerate(((core, outer_ref), (1 - core, inner_ref))):
-        rows = pl.ds(pl.multiple_of(side * last, 128), width)
-        copies.append(pltpu.make_async_copy(modes_hbm.at[rows, :], out_ref, sems.at[k]))
-    for copy in copies:
-        copy.start()
-    for copy in copies:
-        copy.wait()
-
-
-def edges(modes, width):
-    edge = jax.ShapeDtypeStruct((width, modes.shape[1]), modes.dtype)
-    return pl.pallas_call(
-        edges_kernel,
-        out_shape=(edge, edge),
+def outer_kernel(modes_hbm, out_ref, sem):
+    width = out_ref.shape[0]
+    start = lax.rem(lax.axis_index("cell"), 2) * (modes_hbm.shape[0] - width)
+    copy = pltpu.make_async_copy(modes_hbm.at[pl.ds(pl.multiple_of(start, 128), width), :], out_ref, sem)
+    copy.start()
+    copy.wait()
+
+
+def outer_edge(modes, width):
+    return pl.pallas_call(
+        outer_kernel,
+        out_shape=jax.ShapeDtypeStruct((width, modes.shape[1]), modes.dtype),
         in_specs=[pl.BlockSpec(memory_space=pltpu.HBM)],
-        out_specs=(pl.BlockSpec(memory_space=pltpu.VMEM),) * 2,
-        scratch_shapes=[pltpu.SemaphoreType.DMA((2,))],
-        compiler_params=pltpu.CompilerParams(vmem_limit_bytes=JOIN_VMEM),
-        cost_estimate=pl.CostEstimate(flops=EDGES_COST, bytes_accessed=4 * edge.size * 2, transcendentals=0),
-        name="edges",
+        out_specs=pl.BlockSpec(memory_space=pltpu.VMEM),
+        scratch_shapes=[pltpu.SemaphoreType.DMA],
+        compiler_params=pltpu.CompilerParams(vmem_limit_bytes=SMALL_VMEM),
+        cost_estimate=pl.CostEstimate(flops=0, bytes_accessed=4 * width * modes.shape[1], transcendentals=0),
+        name="outer_edge",
     )(pltpu.with_memory_space_constraint(modes, pltpu.HBM))
+
+
+def gate(block):
+    return pl.pallas_call(
+        lambda block_ref, out_ref: None,
+        out_shape=jax.ShapeDtypeStruct(block.shape, block.dtype),
+        in_specs=[pl.BlockSpec(memory_space=pltpu.VMEM)],
+        out_specs=pl.BlockSpec(memory_space=pltpu.VMEM),
+        input_output_aliases={0: 0},
+        compiler_params=pltpu.CompilerParams(vmem_limit_bytes=SMALL_VMEM),
+        cost_estimate=pl.CostEstimate(flops=LOAD_COST, bytes_accessed=0, transcendentals=0),
+        name="gate",
+    )(block)
+
+
+def inner_kernel(modes, out_ref):
+    width = out_ref.shape[0]
+    head = modes[:width, :]
+    tail = modes[modes.shape[0] - width :, :]
+    out_ref[...] = jnp.where(lax.rem(lax.axis_index("cell"), 2) == 0, tail, head)
+
+
+def inner_edge(modes, width):
+    return pl.pallas_call(
+        inner_kernel,
+        out_shape=jax.ShapeDtypeStruct((width, modes.shape[1]), modes.dtype),
+        in_specs=[pl.BlockSpec(memory_space=pltpu.VMEM)],
+        out_specs=pl.BlockSpec(memory_space=pltpu.VMEM),
+        compiler_params=pltpu.CompilerParams(vmem_limit_bytes=SMALL_VMEM),
+        name="inner_edge",
+    )(modes)
 
 
 def own_kernel(blocks, keep_rows, nb_ref, jac, modes, p_ref, t_ref, turned, jv, parts, face):
@@ -90,10 +114,12 @@
         return carry
 
     lax.fori_loop(blocks, slots, step, 0)
+    mid = n_modes // 2
     for side in range(2):
         upper, lower = halves(face[side])
-        t_ref[side, 0] = upper
-        t_ref[side, 1] = lower
+        for half in range(2):
+            t_ref[side, half, :mid] = upper[half * mid : (half + 1) * mid]
+            t_ref[side, half, mid:] = lower[half * mid : (half + 1) * mid]
     for s in range(blocks):
         rows = pl.ds(s * width, width)
         upper, lower = halves(jv[rows, :])
@@ -145,11 +171,8 @@
     count = out_ref.shape[0]
     half = 1 - core if other else core
     rows = pl.ds(pl.multiple_of(half * count, TILE_ROWS), count)
-    total = p_ref[rows, :]
-    for side, halo in ((1 - core, inner_ref), (core, outer_ref)):
-        for part in range(2):
-            total += dot(t_ref[side, part, rows, :], halo[...])
-    out_ref[...] = total
+    both = dot(t_ref[1 - core, half], inner_ref[...]) + dot(t_ref[core, half], outer_ref[...])
+    out_ref[...] = p_ref[rows, :] + both[:count] + both[count:]
 
 
 def join(other, p, t, outer, inner):
@@ -159,7 +182,7 @@
         out_shape=jax.ShapeDtypeStruct((rows, p.shape[1]), jnp.float32),
         in_specs=[pl.BlockSpec(memory_space=pltpu.VMEM)] * 4,
         out_specs=pl.BlockSpec(memory_space=pltpu.VMEM),
-        compiler_params=pltpu.CompilerParams(vmem_limit_bytes=JOIN_VMEM),
+        compiler_params=pltpu.CompilerParams(vmem_limit_bytes=SMALL_VMEM),
         cost_estimate=pl.CostEstimate(flops=8 * rows * outer.size, bytes_accessed=0, transcendentals=0),
         name="join_give" if other else "join_keep",
     )(p, t, outer, inner)
@@ -172,12 +195,14 @@
     keep_rows = n_modes // count
     across = [(i, min(max(i - 1 + 2 * (i % 2), 0), count - 1)) for i in range(count)]
     swap = [(i, i ^ 1) for i in range(count)]
-    outer, inner = edges(modes, width)
-    outer = lax.ppermute(outer, "cell", across)
-    inner = lax.ppermute(inner, "cell", swap)
+    outer = lax.ppermute(gate(outer_edge(modes, width)), "cell", across)
+    inner = lax.ppermute(inner_edge(modes, width), "cell", swap)
     p, t = own_part(keep_rows, neighbours.T, jac_blocks, modes)
     if keep_rows % TILE_ROWS:
-        p, t = regrouped(p, 0, keep_rows), regrouped(t, 2, keep_rows)
+        p = regrouped(p, 0, keep_rows)
+        apart = jnp.swapaxes(t.reshape(2, 2, 2, n_modes // 2, width), 1, 2).reshape(2, 2, n_modes, width)
+        apart = regrouped(apart, 2, keep_rows).reshape(2, 2, 2, n_modes // 2, width)
+        t = jnp.swapaxes(apart, 1, 2).reshape(t.shape)
     got = lax.ppermute(join(True, p, t, outer, inner), "cell", swap)
     keep = join(False, p, t, outer, inner)
     pair = (keep + got).reshape(count // 2, keep_rows, n_modes)

time: 29.5 us -> 29.8 us (1.010); the launches traced: 29.3 us -> 29.2 us
  Pallas kernels: 7.34 us -> 6.69 us
  local copies, waits for them, and re-layouts: 0.01 us -> 0.47 us
    unnamed x6, local copies, waits for them, and re-layouts: 0.01 us -> 0.47 us
    ppermute x2, starting transfers between devices: 5.33 us -> 4.88 us  [the longest x1 4.07 us: per_device(): inner = lax.ppermute(inner_edge(modes, width), 'cell', swap)]
    pallas_call x1, Pallas kernels: 5.39 us -> 4.95 us  [own_part(): pl.pallas_call(functools.partial(own_kernel, blocks, keep_rows), out_shap...]
    ppermute x1, starting transfers between devices: 2.08 us -> 2.47 us  [per_device(): got = lax.ppermute(join(True, p, t, outer, inner), 'cell', swap)]
    pallas_call x1 -> x3, Pallas kernels: 1.24 us -> 1.02 us  [the longest x1 0.98 us: outer_edge(): pl.pallas_call(outer_kernel, out_shape=jax.ShapeDtypeStruct((width, modes...]
  transfers between devices with their start and end apart: 3 -> 3, of which waited for: 1 -> 1; matrix products, arithmetic and copies ran while one was open for 0% -> 0% of each run, Pallas kernels for 20% -> 18%
where the time goes in v9:
time: 29.8 us; the launch traced here: 29.2 us
  blocking collectives  13.4 us (45%)
  starting transfers between devices  7.35 us (25%)
  Pallas kernels  6.69 us (22%)
  waiting for transfers between devices  0.63 us (2%)
  other arithmetic  0.63 us (2%)
  local copies, waits for them, and re-layouts  0.47 us (2%)
    all_to_all x1, blocking collectives, per_device(): parts = lax.all_to_all(pair, 'cell', 0, 0, axis_index_groups=same_core)  13.4 us
    pallas_call x1, Pallas kernels, own_part(): pl.pallas_call(functools.partial(own_kernel, blocks, keep_rows), out_shap...  4.95 us
    ppermute x1, starting transfers between devices, per_device(): inner = lax.ppermute(inner_edge(modes, width), 'cell', swap)  4.07 us
    ppermute x1, starting transfers between devices, per_device(): got = lax.ppermute(join(True, p, t, outer, inner), 'cell', swap)  2.47 us
    pallas_call x1, Pallas kernels, outer_edge(): pl.pallas_call(outer_kernel, out_shape=jax.ShapeDtypeStruct((width, modes...  0.98 us
    ppermute x1, starting transfers between devices, per_device(): outer = lax.ppermute(gate(outer_edge(modes, width)), 'cell', across)  0.81 us
    pallas_call x2, Pallas kernels, join(): pl.pallas_call(functools.partial(join_kernel, other), out_shape=jax.Shape...  0.72 us
    ppermute x1, waiting for transfers between devices, per_device(): got = lax.ppermute(join(True, p, t, outer, inner), 'cell', swap)  0.62 us
  transfers between devices with their start and end apart: 3, of which 1 were waited for; matrix products, arithmetic and copies ran while one was open for 0% of the time, Pallas kernels for 18%

profile of v9, /device:TPU:0, one launch (start us, length us, event | category | flops | bytes accessed | tf_op | source)
XLA Modules:
  0.0 29.2 jit_solution(3300594449998183474)
XLA Ops:
  0.0 1.0 %outer_edge.1.block_ref = bf16[640,256]{1,0:T(8,128)(2,1)S(1)} custom-call(bf16[2560,256]{1,0:T(8,128)(2,1)} %modes.3), custom_call_target="tpu_custom_call" | custom-call | bytes 655360 | tf_op jit(solution)/shard_map/outer_edge/pallas_call | solution.py:34
  1.0 0.0 copy-start
  1.0 0.0 copy-start.1
  1.0 0.0 copy-start.2
  1.0 0.8 %collective-permute-start = (bf16[640,256]{1,0:T(8,128)(2,1)S(1)}, bf16[640,256]{1,0:T(8,128)(2,1)S(1)}, u32[]{:S(2)}, u32[]{:S(2)}) collective-permute-start(bf16[640,256]{1,0:T(8,128)(2,1)S(1)} %gate.1), channel_id=1, source_target_pairs={{0,0},{1,2},{2,1},{3,4},{4,3},{5,6},{6,5},{7,8},{8,7},{9,10},{10,9... | collective-permute-start | bytes 983048 | tf_op jit(solution)/shard_map/ppermute | solution.py:198
  1.9 0.5 %copy-done = bf16[2560,256]{1,0:T(8,128)(2,1)S(1)} copy-done((bf16[2560,256]{1,0:T(8,128)(2,1)S(1)}, bf16[2560,256]{1,0:T(8,128)(2,1)}, u32[]{:S(2)}) %copy-start) | copy-done | bytes 1310744
  2.3 4.1 %collective-permute-start.1 = (bf16[640,256]{1,0:T(8,128)(2,1)S(1)}, bf16[640,256]{1,0:T(8,128)(2,1)S(1)}, u32[]{:S(2)}, u32[]{:S(2)}) collective-permute-start(bf16[640,256]{1,0:T(8,128)(2,1)S(1)} %inner_edge.1), channel_id=1, source_target_pairs={{0,1},{1,0},{2,3},{3,2},{4,5},{5,4},{6,7},{7,6},{8,9},{9,8},{10,11... | collective-permute-start | bytes 983048 | tf_op jit(solution)/shard_map/ppermute | solution.py:199
  6.4 0.0 copy-done.1
  6.4 0.0 copy-done.2
  6.4 5.0 %own_part.1 = (f32[256,256]{1,0:T(8,128)S(1)}, bf16[2,2,256,640]{3,2,1,0:T(8,128)(2,1)S(1)}) custom-call(s32[2,14]{1,0:T(2,128)S(1)} %bitcast.2, bf16[14,640,640]{2,1,0:T(8,128)(2,1)S(1)} %copy-done.1, bf16[2560,256]{1,0:T(8,128)(2,1)S(1)} %copy-done), custom_call_target="tpu_custom_call" | custom-call | flops 3607101440 | bytes 12779520 | tf_op jit(solution)/shard_map/own_part/pallas_call | solution.py:137
  11.4 0.0 collective-permute-done.outer_ref
  11.4 0.0 collective-permute-done.1.inner_ref
  11.4 0.4 %join_give.1 = f32[128,256]{1,0:T(8,128)S(1)} custom-call(f32[256,256]{1,0:T(8,128)S(1)} %get-tuple-element.7.p_ref, bf16[2,2,256,640]{3,2,1,0:T(8,128)(2,1)S(1)} %get-tuple-element.8.t_ref, bf16[640,256]{1,0:T(8,128)(2,1)S(1)} %collective-permute-done.outer_ref, bf16[640,256]{1,0:T(8,128)(2,1)S(1)} %collective-permute-done.1.inner_ref), custom_call_target="tpu_custom_call" | custom-call | flops 167772160 | tf_op jit(solution)/shard_map/join_give/pallas_call | solution.py:180
  11.8 2.5 %collective-permute-start.2 = (f32[128,256]{1,0:T(8,128)S(1)}, f32[128,256]{1,0:T(8,128)S(1)}, u32[]{:S(2)}, u32[]{:S(2)}) collective-permute-start(f32[128,256]{1,0:T(8,128)S(1)} %join_give.1), channel_id=1, source_target_pairs={{0,1},{1,0},{2,3},{3,2},{4,5},{5,4},{6,7},{7,6},{8,9},{9,8},{10,11... | collective-permute-start | bytes 393224 | tf_op jit(solution)/shard_map/ppermute | solution.py:206
  14.2 0.4 %join_keep.1 = f32[128,256]{1,0:T(8,128)S(1)} custom-call(f32[256,256]{1,0:T(8,128)S(1)} %get-tuple-element.7.p_ref, bf16[2,2,256,640]{3,2,1,0:T(8,128)(2,1)S(1)} %get-tuple-element.8.t_ref, bf16[640,256]{1,0:T(8,128)(2,1)S(1)} %collective-permute-done.outer_ref, bf16[640,256]{1,0:T(8,128)(2,1)S(1)} %collective-permute-done.1.inner_ref), custom_call_target="tpu_custom_call" | custom-call | flops 167772160 | tf_op jit(solution)/shard_map/join_keep/pallas_call | solution.py:180
  14.6 0.6 %collective-permute-done.2 = f32[128,256]{1,0:T(8,128)S(1)} collective-permute-done((f32[128,256]{1,0:T(8,128)S(1)}, f32[128,256]{1,0:T(8,128)S(1)}, u32[]{:S(2)}, u32[]{:S(2)}) %collective-permute-start.2) | collective-permute-done | bytes 131104 | tf_op jit(solution)/shard_map/ppermute | solution.py:206
  15.2 13.4 %all_to_all.5 = f32[8,16,256]{2,1,0:T(8,128)S(1)} all-to-all(f32[8,16,256]{2,1,0:T(8,128)S(1)} %bitcast.3), channel_id=1, replica_groups={{0,2,4,6,8,10,12,14},{1,3,5,7,9,11,13,15},{16,18,20,22,24,26,28,30},{17..., dimensions={0} | all-to-all | bytes 262144 | tf_op jit(solution)/shard_map/all_to_all | solution.py:210
  28.6 0.6 %reduce_sum.9 = f32[16,256]{1,0:T(8,128)} reduce(f32[8,16,256]{2,1,0:T(8,128)S(1)} %all_to_all.5, f32[]{:T(128)} %constant.0.clone.1), dimensions={0}, to_apply=%region_0.0 | reduce | flops 28672 | bytes 147460 | tf_op jit(solution)/shard_map/reduce_sum | solution.py:211
  (3 shorter events, 0.1 us)
Async XLA Ops:
  1.0 1.3 %copy-start = (bf16[2560,256]{1,0:T(8,128)(2,1)S(1)}, bf16[2560,256]{1,0:T(8,128)(2,1)}, u32[]{:S(2)}) copy-start(bf16[2560,256]{1,0:T(8,128)(2,1)} %modes.3) | copy-start | bytes 3932164
  1.0 5.4 %copy-start.1 = (bf16[14,640,640]{2,1,0:T(8,128)(2,1)S(1)}, bf16[14,640,640]{2,1,0:T(8,128)(2,1)}, u32[]{:S(2)}) copy-start(bf16[14,640,640]{2,1,0:T(8,128)(2,1)} %jac.1) | copy-start | bytes 34406404
  1.0 5.4 %copy-start.2 = (s32[14,2]{0,1:T(2,128)S(1)}, s32[14,2]{0,1:T(2,128)}, u32[]{:S(2)}) copy-start(s32[14,2]{0,1:T(2,128)} %param.5) | copy-start | bytes 340
  1.0 10.4 %collective-permute-start = (bf16[640,256]{1,0:T(8,128)(2,1)S(1)}, bf16[640,256]{1,0:T(8,128)(2,1)S(1)}, u32[]{:S(2)}, u32[]{:S(2)}) collective-permute-start(bf16[640,256]{1,0:T(8,128)(2,1)S(1)} %gate.1), channel_id=1, source_target_pairs={{0,0},{1,2},{2,1},{3,4},{4,3},{5,6},{6,5},{7,8},{8,7},{9,10},{10,9... | collective-permute-start | bytes 983048 | tf_op jit(solution)/shard_map/ppermute | solution.py:198
  2.3 9.0 %collective-permute-start.1 = (bf16[640,256]{1,0:T(8,128)(2,1)S(1)}, bf16[640,256]{1,0:T(8,128)(2,1)S(1)}, u32[]{:S(2)}, u32[]{:S(2)}) collective-permute-start(bf16[640,256]{1,0:T(8,128)(2,1)S(1)} %inner_edge.1), channel_id=1, source_target_pairs={{0,1},{1,0},{2,3},{3,2},{4,5},{5,4},{6,7},{7,6},{8,9},{9,8},{10,11... | collective-permute-start | bytes 983048 | tf_op jit(solution)/shard_map/ppermute | solution.py:199
  11.8 3.5 %collective-permute-start.2 = (f32[128,256]{1,0:T(8,128)S(1)}, f32[128,256]{1,0:T(8,128)S(1)}, u32[]{:S(2)}, u32[]{:S(2)}) collective-permute-start(f32[128,256]{1,0:T(8,128)S(1)} %join_give.1), channel_id=1, source_target_pairs={{0,1},{1,0},{2,3},{3,2},{4,5},{5,4},{6,7},{7,6},{8,9},{9,8},{10,11... | collective-permute-start | bytes 393224 | tf_op jit(solution)/shard_map/ppermute | solution.py:206

commit v10 on v9

--- a/solution.py
+++ b/solution.py
@@ -10,7 +10,7 @@
 OWN_VMEM = 24 * 2**20
 SMALL_VMEM = 8 * 2**20
 TILE_ROWS = 16
-LOAD_COST = 5 * 10**9
+LOAD_COST = 35 * 10**8
 
 
 def dot(a, b):
@@ -43,13 +43,16 @@
     )(pltpu.with_memory_space_constraint(modes, pltpu.HBM))
 
 
+def gate_kernel(block_ref, out_ref):
+    out_ref[...] = block_ref[...]
+
+
 def gate(block):
     return pl.pallas_call(
-        lambda block_ref, out_ref: None,
+        gate_kernel,
         out_shape=jax.ShapeDtypeStruct(block.shape, block.dtype),
         in_specs=[pl.BlockSpec(memory_space=pltpu.VMEM)],
         out_specs=pl.BlockSpec(memory_space=pltpu.VMEM),
-        input_output_aliases={0: 0},
         compiler_params=pltpu.CompilerParams(vmem_limit_bytes=SMALL_VMEM),
         cost_estimate=pl.CostEstimate(flops=LOAD_COST, bytes_accessed=0, transcendentals=0),
         name="gate",
@@ -74,68 +77,104 @@
     )(modes)
 
 
-def own_kernel(blocks, keep_rows, nb_ref, jac, modes, p_ref, t_ref, turned, jv, parts, face):
+def turn_kernel(keep_rows, modes, out_ref):
+    n_modes, count = out_ref.shape
+    step = count // 4
+    for start in range(0, count, step):
+        columns = slice(start, start + step)
+        block = modes[columns, :].T
+        if keep_rows % TILE_ROWS:
+            out_ref[:, columns] = block
+        else:
+            for k in range(n_modes // keep_rows):
+                place = k % 2 * (n_modes // 2) + k // 2 * keep_rows
+                out_ref[place : place + keep_rows, columns] = block[k * keep_rows : (k + 1) * keep_rows]
+
+
+def turn(modes, keep_rows):
+    count, n_modes = modes.shape
+    return pl.pallas_call(
+        functools.partial(turn_kernel, keep_rows),
+        out_shape=jax.ShapeDtypeStruct((n_modes, count), modes.dtype),
+        in_specs=[pl.BlockSpec(memory_space=pltpu.VMEM)],
+        out_specs=pl.BlockSpec(memory_space=pltpu.VMEM),
+        compiler_params=pltpu.CompilerParams(vmem_limit_bytes=SMALL_VMEM),
+        cost_estimate=pl.CostEstimate(flops=0, bytes_accessed=4 * modes.size, transcendentals=0),
+        name="turn",
+    )(modes)
+
+
+def own_kernel(blocks, nb_ref, jac, modes, turned, p_ref, t_ref, jv, parts, face, near, far):
     slots, width, _ = jac.shape
     n_modes = modes.shape[1]
 
-    face[...] = jnp.zeros_like(face)
+    def block_at(k):
+        return pl.ds(pl.multiple_of(k * width, width), width)
+
+    base = nb_ref[1, 0]
+    n_near = jnp.int32(0)
+    n_far = jnp.int32(0)
+    for s in range(blocks, slots):
+        r = nb_ref[0, s]
+        c = nb_ref[1, s] - base
+        inside = (c >= 0) & (c < blocks)
+        near[0, n_near] = s
+        near[1, n_near] = r
+        near[2, n_near] = c
+        far[0, n_far] = s
+        far[1, n_far] = jnp.where(c < 0, 0, 1)
+        n_near += ((r >= 0) & inside).astype(jnp.int32)
+        n_far += ((r >= 0) & jnp.logical_not(inside)).astype(jnp.int32)
+    near[0, n_near] = 0
+    near[1, n_near] = blocks
+    near[2, n_near] = 0
+    far[0, n_far] = 0
+    far[1, n_far] = 2
+
     for s in range(blocks):
         rows = pl.ds(s * width, width)
         jv[rows, :] = dot(jac[s], modes[rows, :])
-        block = modes[rows, :].T
-        if keep_rows % TILE_ROWS:
-            turned[:, rows] = block
-        else:
-            for k in range(n_modes // keep_rows):
-                place = k % 2 * (n_modes // 2) + k // 2 * keep_rows
-                turned[place : place + keep_rows, rows] = block[k * keep_rows : (k + 1) * keep_rows]
-    base = nb_ref[1, 0]
-    last = (blocks - 1) * width
-
-    def step(s, carry):
-        r = nb_ref[0, s]
-        c = nb_ref[1, s] - base
-        live = r >= 0
-
-        @pl.when(live & (c >= 0) & (c < blocks))
-        def _():
-            rows = pl.ds(pl.multiple_of(r * width, width), width)
-            picked = pl.ds(pl.multiple_of(c * width, width), width)
-            jv[rows, :] += dot(jac[s], modes[picked, :])
-
-        @pl.when(live & (c < 0))
-        def _():
-            face[0] += dot(turned[:, :width], jac[s])
-
-        @pl.when(live & (c >= blocks))
-        def _():
-            face[1] += dot(turned[:, last:], jac[s])
-
+    face[...] = jnp.zeros_like(face)
+
+    def near_pair(k, carry):
+        for j in (2 * k, 2 * k + 1):
+            jv[block_at(near[1, j]), :] += dot(jac[near[0, j]], modes[block_at(near[2, j]), :])
         return carry
 
-    lax.fori_loop(blocks, slots, step, 0)
+    def far_pair(k, carry):
+        for j in (2 * k, 2 * k + 1):
+            side = far[1, j]
+            edge = block_at(jnp.where(side == 1, blocks - 1, 0))
+            face[side] += dot(turned[:, edge], jac[far[0, j]])
+        return carry
+
+    lax.fori_loop(0, (n_near + 1) // 2, near_pair, 0)
+    lax.fori_loop(0, (n_far + 1) // 2, far_pair, 0)
+
     mid = n_modes // 2
     for side in range(2):
         upper, lower = halves(face[side])
         for half in range(2):
             t_ref[side, half, :mid] = upper[half * mid : (half + 1) * mid]
             t_ref[side, half, mid:] = lower[half * mid : (half + 1) * mid]
-    for s in range(blocks):
-        rows = pl.ds(s * width, width)
+    both = jnp.zeros((n_modes, 2 * n_modes), jnp.float32)
+    step = width * (2 if blocks % 2 == 0 else 1)
+    for start in range(0, blocks * width, step):
+        rows = pl.ds(start, step)
         upper, lower = halves(jv[rows, :])
         parts[rows, :n_modes] = upper
         parts[rows, n_modes:] = lower
-    both = dot(turned[...], parts[...])
+        both += dot(turned[:, rows], parts[rows, :])
     p_ref[...] = both[:, :n_modes] + both[:, n_modes:]
 
 
-def own_part(keep_rows, neighbours, jac_blocks, modes):
+def own_part(neighbours, jac_blocks, modes, turned):
     slots, width, _ = jac_blocks.shape
     rows, n_modes = modes.shape
     blocks = rows // width
     flops = 2 * n_modes * width * width * slots + 4 * rows * n_modes * n_modes
     return pl.pallas_call(
-        functools.partial(own_kernel, blocks, keep_rows),
+        functools.partial(own_kernel, blocks),
         out_shape=(
             jax.ShapeDtypeStruct((n_modes, n_modes), jnp.float32),
             jax.ShapeDtypeStruct((2, 2, n_modes, width), jnp.bfloat16),
@@ -144,20 +183,22 @@
             pl.BlockSpec(memory_space=pltpu.SMEM),
             pl.BlockSpec(memory_space=pltpu.VMEM),
             pl.BlockSpec(memory_space=pltpu.VMEM),
+            pl.BlockSpec(memory_space=pltpu.VMEM),
         ],
         out_specs=(pl.BlockSpec(memory_space=pltpu.VMEM), pl.BlockSpec(memory_space=pltpu.VMEM)),
         scratch_shapes=[
-            pltpu.VMEM((n_modes, rows), jnp.bfloat16),
-            pltpu.VMEM((rows, n_modes), jnp.float32),
+            pltpu.VMEM((rows + width, n_modes), jnp.float32),
             pltpu.VMEM((rows, 2 * n_modes), jnp.bfloat16),
-            pltpu.VMEM((2, n_modes, width), jnp.float32),
+            pltpu.VMEM((3, n_modes, width), jnp.float32),
+            pltpu.SMEM((3, slots + 1), jnp.int32),
+            pltpu.SMEM((2, slots + 1), jnp.int32),
         ],
         compiler_params=pltpu.CompilerParams(vmem_limit_bytes=OWN_VMEM),
         cost_estimate=pl.CostEstimate(
             flops=flops, bytes_accessed=slots * width * width * 2 + rows * n_modes * 2, transcendentals=0
         ),
         name="own_part",
-    )(neighbours, jac_blocks, modes)
+    )(neighbours, jac_blocks, modes, turned)
 
 
 def regrouped(value, axis, keep_rows):
@@ -197,7 +238,7 @@
     swap = [(i, i ^ 1) for i in range(count)]
     outer = lax.ppermute(gate(outer_edge(modes, width)), "cell", across)
     inner = lax.ppermute(inner_edge(modes, width), "cell", swap)
-    p, t = own_part(keep_rows, neighbours.T, jac_blocks, modes)
+    p, t = own_part(neighbours.T, jac_blocks, modes, turn(modes, keep_rows))
     if keep_rows % TILE_ROWS:
         p = regrouped(p, 0, keep_rows)
         apart = jnp.swapaxes(t.reshape(2, 2, 2, n_modes // 2, width), 1, 2).reshape(2, 2, n_modes, width)

time: 29.8 us -> 29.5 us (0.990); the launches traced: 29.2 us -> 29.4 us
    pallas_call x2 -> x3, Pallas kernels: 4.95 us -> 4.9 us  [the longest x1 4.49 us: own_part(): pl.pallas_call(functools.partial(own_kernel, blocks), out_shape=(jax.Shap...]
where the time goes in v10:
time: 29.5 us; the launch traced here: 29.4 us
  blocking collectives  13.5 us (46%)
  starting transfers between devices  7.4 us (25%)
  Pallas kernels  6.63 us (22%)
  waiting for transfers between devices  0.63 us (2%)
  other arithmetic  0.63 us (2%)
  local copies, waits for them, and re-layouts  0.46 us (2%)
    all_to_all x1, blocking collectives, per_device(): parts = lax.all_to_all(pair, 'cell', 0, 0, axis_index_groups=same_core)  13.5 us
    pallas_call x1, Pallas kernels, own_part(): pl.pallas_call(functools.partial(own_kernel, blocks), out_shape=(jax.Shap...  4.49 us
    ppermute x1, starting transfers between devices, per_device(): inner = lax.ppermute(inner_edge(modes, width), 'cell', swap)  4.08 us
    ppermute x1, starting transfers between devices, per_device(): got = lax.ppermute(join(True, p, t, outer, inner), 'cell', swap)  2.51 us
    pallas_call x1, Pallas kernels, outer_edge(): pl.pallas_call(outer_kernel, out_shape=jax.ShapeDtypeStruct((width, modes...  0.98 us
    ppermute x1, starting transfers between devices, per_device(): outer = lax.ppermute(gate(outer_edge(modes, width)), 'cell', across)  0.81 us
    pallas_call x2, Pallas kernels, join(): pl.pallas_call(functools.partial(join_kernel, other), out_shape=jax.Shape...  0.71 us
    ppermute x1, waiting for transfers between devices, per_device(): got = lax.ppermute(join(True, p, t, outer, inner), 'cell', swap)  0.63 us
  transfers between devices with their start and end apart: 3, of which 1 were waited for; matrix products, arithmetic and copies ran while one was open for 0% of the time, Pallas kernels for 18%

profile of v10, /device:TPU:0, one launch (start us, length us, event | category | flops | bytes accessed | tf_op | source)
XLA Modules:
  0.0 29.4 jit_solution(2045062685604156564)
XLA Ops:
  0.0 1.0 %outer_edge.1.block_ref = bf16[640,256]{1,0:T(8,128)(2,1)S(1)} custom-call(bf16[2560,256]{1,0:T(8,128)(2,1)} %modes.5), custom_call_target="tpu_custom_call" | custom-call | bytes 655360 | tf_op jit(solution)/shard_map/outer_edge/pallas_call | solution.py:34
  1.0 0.0 copy-start
  1.0 0.0 copy-start.1
  1.0 0.8 %collective-permute-start = (bf16[640,256]{1,0:T(8,128)(2,1)S(1)}, bf16[640,256]{1,0:T(8,128)(2,1)S(1)}, u32[]{:S(2)}, u32[]{:S(2)}) collective-permute-start(bf16[640,256]{1,0:T(8,128)(2,1)S(1)} %gate.1), channel_id=1, source_target_pairs={{0,0},{1,2},{2,1},{3,4},{4,3},{5,6},{6,5},{7,8},{8,7},{9,10},{10,9... | collective-permute-start | bytes 983048 | tf_op jit(solution)/shard_map/ppermute | solution.py:239
  1.9 0.4 %copy-done = bf16[2560,256]{1,0:T(8,128)(2,1)S(1)} copy-done((bf16[2560,256]{1,0:T(8,128)(2,1)S(1)}, bf16[2560,256]{1,0:T(8,128)(2,1)}, u32[]{:S(2)}) %copy-start) | copy-done | bytes 1310744
  2.3 0.0 copy-start.2
  2.4 4.1 %collective-permute-start.1 = (bf16[640,256]{1,0:T(8,128)(2,1)S(1)}, bf16[640,256]{1,0:T(8,128)(2,1)S(1)}, u32[]{:S(2)}, u32[]{:S(2)}) collective-permute-start(bf16[640,256]{1,0:T(8,128)(2,1)S(1)} %inner_edge.1), channel_id=1, source_target_pairs={{0,1},{1,0},{2,3},{3,2},{4,5},{5,4},{6,7},{7,6},{8,9},{9,8},{10,11... | collective-permute-start | bytes 983048 | tf_op jit(solution)/shard_map/ppermute | solution.py:240
  6.4 0.4 %turn.1.turned = bf16[256,2560]{1,0:T(8,128)(2,1)S(1)} custom-call(bf16[2560,256]{1,0:T(8,128)(2,1)S(1)} %copy-done), custom_call_target="tpu_custom_call" | custom-call | bytes 2621440 | tf_op jit(solution)/shard_map/turn/pallas_call | solution.py:96
  6.8 0.0 copy-done.1
  6.8 0.0 copy-done.2
  6.9 4.5 %own_part.1 = (f32[256,256]{1,0:T(8,128)S(1)}, bf16[2,2,256,640]{3,2,1,0:T(8,128)(2,1)S(1)}) custom-call(s32[2,14]{1,0:T(2,128)S(1)} %bitcast.2, bf16[14,640,640]{2,1,0:T(8,128)(2,1)S(1)} %copy-done.1, bf16[2560,256]{1,0:T(8,128)(2,1)S(1)} %copy-done, bf16[256,2560]{1,0:T(8,128)(2,1)S(1)} %turn.1.turned), custom_call_target="tpu_custom_call" | custom-call | flops 3607101440 | bytes 12779520 | tf_op jit(solution)/shard_map/own_part/pallas_call | solution.py:176
  11.4 0.0 collective-permute-done.outer_ref
  11.4 0.0 collective-permute-done.1.inner_ref
  11.4 0.4 %join_give.1 = f32[128,256]{1,0:T(8,128)S(1)} custom-call(f32[256,256]{1,0:T(8,128)S(1)} %get-tuple-element.7.p_ref, bf16[2,2,256,640]{3,2,1,0:T(8,128)(2,1)S(1)} %get-tuple-element.8.t_ref, bf16[640,256]{1,0:T(8,128)(2,1)S(1)} %collective-permute-done.outer_ref, bf16[640,256]{1,0:T(8,128)(2,1)S(1)} %collective-permute-done.1.inner_ref), custom_call_target="tpu_custom_call" | custom-call | flops 167772160 | tf_op jit(solution)/shard_map/join_give/pallas_call | solution.py:221
  11.7 2.5 %collective-permute-start.2 = (f32[128,256]{1,0:T(8,128)S(1)}, f32[128,256]{1,0:T(8,128)S(1)}, u32[]{:S(2)}, u32[]{:S(2)}) collective-permute-start(f32[128,256]{1,0:T(8,128)S(1)} %join_give.1), channel_id=1, source_target_pairs={{0,1},{1,0},{2,3},{3,2},{4,5},{5,4},{6,7},{7,6},{8,9},{9,8},{10,11... | collective-permute-start | bytes 393224 | tf_op jit(solution)/shard_map/ppermute | solution.py:247
  14.3 0.4 %join_keep.1 = f32[128,256]{1,0:T(8,128)S(1)} custom-call(f32[256,256]{1,0:T(8,128)S(1)} %get-tuple-element.7.p_ref, bf16[2,2,256,640]{3,2,1,0:T(8,128)(2,1)S(1)} %get-tuple-element.8.t_ref, bf16[640,256]{1,0:T(8,128)(2,1)S(1)} %collective-permute-done.outer_ref, bf16[640,256]{1,0:T(8,128)(2,1)S(1)} %collective-permute-done.1.inner_ref), custom_call_target="tpu_custom_call" | custom-call | flops 167772160 | tf_op jit(solution)/shard_map/join_keep/pallas_call | solution.py:221
  14.6 0.6 %collective-permute-done.2 = f32[128,256]{1,0:T(8,128)S(1)} collective-permute-done((f32[128,256]{1,0:T(8,128)S(1)}, f32[128,256]{1,0:T(8,128)S(1)}, u32[]{:S(2)}, u32[]{:S(2)}) %collective-permute-start.2) | collective-permute-done | bytes 131104 | tf_op jit(solution)/shard_map/ppermute | solution.py:247
  15.3 13.5 %all_to_all.5 = f32[8,16,256]{2,1,0:T(8,128)S(1)} all-to-all(f32[8,16,256]{2,1,0:T(8,128)S(1)} %bitcast.3), channel_id=1, replica_groups={{0,2,4,6,8,10,12,14},{1,3,5,7,9,11,13,15},{16,18,20,22,24,26,28,30},{17..., dimensions={0} | all-to-all | bytes 262144 | tf_op jit(solution)/shard_map/all_to_all | solution.py:251
  28.8 0.6 %reduce_sum.9 = f32[16,256]{1,0:T(8,128)} reduce(f32[8,16,256]{2,1,0:T(8,128)S(1)} %all_to_all.5, f32[]{:T(128)} %constant.0.clone.1), dimensions={0}, to_apply=%region_0.0 | reduce | flops 28672 | bytes 147460 | tf_op jit(solution)/shard_map/reduce_sum | solution.py:252
  (3 shorter events, 0.1 us)
Async XLA Ops:
  1.0 1.3 %copy-start = (bf16[2560,256]{1,0:T(8,128)(2,1)S(1)}, bf16[2560,256]{1,0:T(8,128)(2,1)}, u32[]{:S(2)}) copy-start(bf16[2560,256]{1,0:T(8,128)(2,1)} %modes.5) | copy-start | bytes 3932164
  1.0 5.8 %copy-start.1 = (bf16[14,640,640]{2,1,0:T(8,128)(2,1)S(1)}, bf16[14,640,640]{2,1,0:T(8,128)(2,1)}, u32[]{:S(2)}) copy-start(bf16[14,640,640]{2,1,0:T(8,128)(2,1)} %jac.1) | copy-start | bytes 34406404
  1.0 10.3 %collective-permute-start = (bf16[640,256]{1,0:T(8,128)(2,1)S(1)}, bf16[640,256]{1,0:T(8,128)(2,1)S(1)}, u32[]{:S(2)}, u32[]{:S(2)}) collective-permute-start(bf16[640,256]{1,0:T(8,128)(2,1)S(1)} %gate.1), channel_id=1, source_target_pairs={{0,0},{1,2},{2,1},{3,4},{4,3},{5,6},{6,5},{7,8},{8,7},{9,10},{10,9... | collective-permute-start | bytes 983048 | tf_op jit(solution)/shard_map/ppermute | solution.py:239
  2.3 4.5 %copy-start.2 = (s32[14,2]{0,1:T(2,128)S(1)}, s32[14,2]{0,1:T(2,128)}, u32[]{:S(2)}) copy-start(s32[14,2]{0,1:T(2,128)} %param.5) | copy-start | bytes 340
  2.4 9.0 %collective-permute-start.1 = (bf16[640,256]{1,0:T(8,128)(2,1)S(1)}, bf16[640,256]{1,0:T(8,128)(2,1)S(1)}, u32[]{:S(2)}, u32[]{:S(2)}) collective-permute-start(bf16[640,256]{1,0:T(8,128)(2,1)S(1)} %inner_edge.1), channel_id=1, source_target_pairs={{0,1},{1,0},{2,3},{3,2},{4,5},{5,4},{6,7},{7,6},{8,9},{9,8},{10,11... | collective-permute-start | bytes 983048 | tf_op jit(solution)/shard_map/ppermute | solution.py:240
  11.7 3.5 %collective-permute-start.2 = (f32[128,256]{1,0:T(8,128)S(1)}, f32[128,256]{1,0:T(8,128)S(1)}, u32[]{:S(2)}, u32[]{:S(2)}) collective-permute-start(f32[128,256]{1,0:T(8,128)S(1)} %join_give.1), channel_id=1, source_target_pairs={{0,1},{1,0},{2,3},{3,2},{4,5},{5,4},{6,7},{7,6},{8,9},{9,8},{10,11... | collective-permute-start | bytes 393224 | tf_op jit(solution)/shard_map/ppermute | solution.py:247

commit v11 on v10

--- a/solution.py
+++ b/solution.py
@@ -10,6 +10,7 @@
 OWN_VMEM = 24 * 2**20
 SMALL_VMEM = 8 * 2**20
 TILE_ROWS = 16
+EDGE_COPIES = 8
 LOAD_COST = 35 * 10**8
 
 
@@ -25,9 +26,15 @@
 def outer_kernel(modes_hbm, out_ref, sem):
     width = out_ref.shape[0]
     start = lax.rem(lax.axis_index("cell"), 2) * (modes_hbm.shape[0] - width)
-    copy = pltpu.make_async_copy(modes_hbm.at[pl.ds(pl.multiple_of(start, 128), width), :], out_ref, sem)
-    copy.start()
-    copy.wait()
+    step = width // EDGE_COPIES
+    copies = []
+    for k in range(EDGE_COPIES):
+        rows = pl.ds(pl.multiple_of(start + k * step, TILE_ROWS), step)
+        copies.append(pltpu.make_async_copy(modes_hbm.at[rows, :], out_ref.at[pl.ds(k * step, step), :], sem.at[k]))
+    for copy in copies:
+        copy.start()
+    for copy in copies:
+        copy.wait()
 
 
 def outer_edge(modes, width):
@@ -36,7 +43,7 @@
         out_shape=jax.ShapeDtypeStruct((width, modes.shape[1]), modes.dtype),
         in_specs=[pl.BlockSpec(memory_space=pltpu.HBM)],
         out_specs=pl.BlockSpec(memory_space=pltpu.VMEM),
-        scratch_shapes=[pltpu.SemaphoreType.DMA],
+        scratch_shapes=[pltpu.SemaphoreType.DMA((EDGE_COPIES,))],
         compiler_params=pltpu.CompilerParams(vmem_limit_bytes=SMALL_VMEM),
         cost_estimate=pl.CostEstimate(flops=0, bytes_accessed=4 * width * modes.shape[1], transcendentals=0),
         name="outer_edge",
@@ -87,7 +94,7 @@
             out_ref[:, columns] = block
         else:
             for k in range(n_modes // keep_rows):
-                place = k % 2 * (n_modes // 2) + k // 2 * keep_rows
+                place = (k ^ k // 2) % 2 * (n_modes // 2) + k // 2 * keep_rows
                 out_ref[place : place + keep_rows, columns] = block[k * keep_rows : (k + 1) * keep_rows]
 
 
@@ -201,16 +208,25 @@
     )(neighbours, jac_blocks, modes, turned)
 
 
+def teams(count):
+    return [[2 * chip + (chip + half) % 2 for chip in range(count // 2)] for half in range(2)]
+
+
+def own_team():
+    me = lax.axis_index("cell")
+    return lax.rem(me + me // 2, 2)
+
+
 def regrouped(value, axis, keep_rows):
-    shape = value.shape
-    split = shape[:axis] + (shape[axis] // (2 * keep_rows), 2, keep_rows) + shape[axis + 1 :]
-    return jnp.swapaxes(value.reshape(split), axis, axis + 1).reshape(shape)
+    first, second = teams(value.shape[axis] // keep_rows)
+    starts = [k * keep_rows for k in first + second]
+    return jnp.concatenate([lax.slice_in_dim(value, k, k + keep_rows, axis=axis) for k in starts], axis=axis)
 
 
 def join_kernel(other, p_ref, t_ref, outer_ref, inner_ref, out_ref):
     core = lax.rem(lax.axis_index("cell"), 2)
     count = out_ref.shape[0]
-    half = 1 - core if other else core
+    half = 1 - own_team() if other else own_team()
     rows = pl.ds(pl.multiple_of(half * count, TILE_ROWS), count)
     both = dot(t_ref[1 - core, half], inner_ref[...]) + dot(t_ref[core, half], outer_ref[...])
     out_ref[...] = p_ref[rows, :] + both[:count] + both[count:]
@@ -247,8 +263,7 @@
     got = lax.ppermute(join(True, p, t, outer, inner), "cell", swap)
     keep = join(False, p, t, outer, inner)
     pair = (keep + got).reshape(count // 2, keep_rows, n_modes)
-    same_core = [list(range(core, count, 2)) for core in range(2)]
-    parts = lax.all_to_all(pair, "cell", 0, 0, axis_index_groups=same_core)
+    parts = lax.all_to_all(pair, "cell", 0, 0, axis_index_groups=teams(count))
     return jnp.sum(parts, axis=0)
 
 

time: 29.5 us -> 29.1 us (0.986)
  Pallas kernels: 6.63 us -> 8.86 us
  starting transfers between devices: 7.4 us -> 5.19 us
  blocking collectives: 13.5 us -> 12.9 us
    pallas_call x1, Pallas kernels: 4.49 us -> 6.72 us  [own_part(): pl.pallas_call(functools.partial(own_kernel, blocks), out_shape=(jax.Shap...]
    ppermute x1, starting transfers between devices: 2.51 us -> 0.3 us  [per_device(): got = lax.ppermute(join(True, p, t, outer, inner), 'cell', swap)]
    all_to_all x1, blocking collectives: 13.5 us -> 12.9 us  [per_device(): parts = lax.all_to_all(pair, 'cell', 0, 0, axis_index_groups=teams(count))]
  transfers between devices with their start and end apart: 3 -> 3, of which waited for: 1 -> 1; matrix products, arithmetic and copies ran while one was open for 0% -> 0% of each run, Pallas kernels for 18% -> 26%
where the time goes in v11:
time: 29.1 us; the launch traced here: 29 us
  blocking collectives  12.9 us (44%)
  Pallas kernels  8.86 us (30%)
  starting transfers between devices  5.19 us (18%)
  waiting for transfers between devices  0.76 us (3%)
  other arithmetic  0.63 us (2%)
  local copies, waits for them, and re-layouts  0.46 us (2%)
    all_to_all x1, blocking collectives, per_device(): parts = lax.all_to_all(pair, 'cell', 0, 0, axis_index_groups=teams(count))  12.9 us
    pallas_call x1, Pallas kernels, own_part(): pl.pallas_call(functools.partial(own_kernel, blocks), out_shape=(jax.Shap...  6.72 us
    ppermute x1, starting transfers between devices, per_device(): inner = lax.ppermute(inner_edge(modes, width), 'cell', swap)  4.08 us
    pallas_call x1, Pallas kernels, outer_edge(): pl.pallas_call(outer_kernel, out_shape=jax.ShapeDtypeStruct((width, modes...  0.99 us
    ppermute x1, starting transfers between devices, per_device(): outer = lax.ppermute(gate(outer_edge(modes, width)), 'cell', across)  0.81 us
    ppermute x1, waiting for transfers between devices, per_device(): got = lax.ppermute(join(True, p, t, outer, inner), 'cell', swap)  0.75 us
    pallas_call x2, Pallas kernels, join(): pl.pallas_call(functools.partial(join_kernel, other), out_shape=jax.Shape...  0.7 us
    reduce_sum x1, other arithmetic, per_device(): return jnp.sum(parts, axis=0)  0.62 us
  transfers between devices with their start and end apart: 3, of which 1 were waited for; matrix products, arithmetic and copies ran while one was open for 0% of the time, Pallas kernels for 26%

profile of v11, /device:TPU:0, one launch (start us, length us, event | category | flops | bytes accessed | tf_op | source)
XLA Modules:
  0.0 29.0 jit_solution(2768402009590974071)
XLA Ops:
  0.0 1.0 %outer_edge.1.block_ref = bf16[640,256]{1,0:T(8,128)(2,1)S(1)} custom-call(bf16[2560,256]{1,0:T(8,128)(2,1)} %modes.5), custom_call_target="tpu_custom_call" | custom-call | bytes 655360 | tf_op jit(solution)/shard_map/outer_edge/pallas_call | solution.py:41
  1.0 0.0 copy-start
  1.0 0.0 copy-start.1
  1.0 0.8 %collective-permute-start = (bf16[640,256]{1,0:T(8,128)(2,1)S(1)}, bf16[640,256]{1,0:T(8,128)(2,1)S(1)}, u32[]{:S(2)}, u32[]{:S(2)}) collective-permute-start(bf16[640,256]{1,0:T(8,128)(2,1)S(1)} %gate.1), channel_id=1, source_target_pairs={{0,0},{1,2},{2,1},{3,4},{4,3},{5,6},{6,5},{7,8},{8,7},{9,10},{10,9... | collective-permute-start | bytes 983048 | tf_op jit(solution)/shard_map/ppermute | solution.py:255
  1.9 0.4 %copy-done = bf16[2560,256]{1,0:T(8,128)(2,1)S(1)} copy-done((bf16[2560,256]{1,0:T(8,128)(2,1)S(1)}, bf16[2560,256]{1,0:T(8,128)(2,1)}, u32[]{:S(2)}) %copy-start) | copy-done | bytes 1310744
  2.4 0.0 copy-start.2
  2.4 4.1 %collective-permute-start.1 = (bf16[640,256]{1,0:T(8,128)(2,1)S(1)}, bf16[640,256]{1,0:T(8,128)(2,1)S(1)}, u32[]{:S(2)}, u32[]{:S(2)}) collective-permute-start(bf16[640,256]{1,0:T(8,128)(2,1)S(1)} %inner_edge.1), channel_id=1, source_target_pairs={{0,1},{1,0},{2,3},{3,2},{4,5},{5,4},{6,7},{7,6},{8,9},{9,8},{10,11... | collective-permute-start | bytes 983048 | tf_op jit(solution)/shard_map/ppermute | solution.py:256
  6.4 0.4 %turn.1.turned = bf16[256,2560]{1,0:T(8,128)(2,1)S(1)} custom-call(bf16[2560,256]{1,0:T(8,128)(2,1)S(1)} %copy-done), custom_call_target="tpu_custom_call" | custom-call | bytes 2621440 | tf_op jit(solution)/shard_map/turn/pallas_call | solution.py:103
  6.8 0.0 copy-done.1
  6.8 0.0 copy-done.2
  6.9 6.7 %own_part.1 = (f32[256,256]{1,0:T(8,128)S(1)}, bf16[2,2,256,640]{3,2,1,0:T(8,128)(2,1)S(1)}) custom-call(s32[2,14]{1,0:T(2,128)S(1)} %bitcast.2, bf16[14,640,640]{2,1,0:T(8,128)(2,1)S(1)} %copy-done.1, bf16[2560,256]{1,0:T(8,128)(2,1)S(1)} %copy-done, bf16[256,2560]{1,0:T(8,128)(2,1)S(1)} %turn.1.turned), custom_call_target="tpu_custom_call" | custom-call | flops 3607101440 | bytes 12779520 | tf_op jit(solution)/shard_map/own_part/pallas_call | solution.py:183
  13.6 0.0 collective-permute-done.outer_ref
  13.6 0.0 collective-permute-done.1.inner_ref
  13.6 0.4 %join_give.1 = f32[128,256]{1,0:T(8,128)S(1)} custom-call(f32[256,256]{1,0:T(8,128)S(1)} %get-tuple-element.7.p_ref, bf16[2,2,256,640]{3,2,1,0:T(8,128)(2,1)S(1)} %get-tuple-element.8.t_ref, bf16[640,256]{1,0:T(8,128)(2,1)S(1)} %collective-permute-done.outer_ref, bf16[640,256]{1,0:T(8,128)(2,1)S(1)} %collective-permute-done.1.inner_ref), custom_call_target="tpu_custom_call" | custom-call | flops 167772160 | tf_op jit(solution)/shard_map/join_give/pallas_call | solution.py:237
  14.0 0.3 %collective-permute-start.2 = (f32[128,256]{1,0:T(8,128)S(1)}, f32[128,256]{1,0:T(8,128)S(1)}, u32[]{:S(2)}, u32[]{:S(2)}) collective-permute-start(f32[128,256]{1,0:T(8,128)S(1)} %join_give.1), channel_id=1, source_target_pairs={{0,1},{1,0},{2,3},{3,2},{4,5},{5,4},{6,7},{7,6},{8,9},{9,8},{10,11... | collective-permute-start | bytes 393224 | tf_op jit(solution)/shard_map/ppermute | solution.py:263
  14.3 0.4 %join_keep.1 = f32[128,256]{1,0:T(8,128)S(1)} custom-call(f32[256,256]{1,0:T(8,128)S(1)} %get-tuple-element.7.p_ref, bf16[2,2,256,640]{3,2,1,0:T(8,128)(2,1)S(1)} %get-tuple-element.8.t_ref, bf16[640,256]{1,0:T(8,128)(2,1)S(1)} %collective-permute-done.outer_ref, bf16[640,256]{1,0:T(8,128)(2,1)S(1)} %collective-permute-done.1.inner_ref), custom_call_target="tpu_custom_call" | custom-call | flops 167772160 | tf_op jit(solution)/shard_map/join_keep/pallas_call | solution.py:237
  14.6 0.8 %collective-permute-done.2 = f32[128,256]{1,0:T(8,128)S(1)} collective-permute-done((f32[128,256]{1,0:T(8,128)S(1)}, f32[128,256]{1,0:T(8,128)S(1)}, u32[]{:S(2)}, u32[]{:S(2)}) %collective-permute-start.2) | collective-permute-done | bytes 131104 | tf_op jit(solution)/shard_map/ppermute | solution.py:263
  15.4 12.9 %all_to_all.5 = f32[8,16,256]{2,1,0:T(8,128)S(1)} all-to-all(f32[8,16,256]{2,1,0:T(8,128)S(1)} %bitcast.3), channel_id=1, replica_groups={{0,3,4,7,8,11,12,15},{1,2,5,6,9,10,13,14},{16,19,20,23,24,27,28,31},{17..., dimensions={0} | all-to-all | bytes 262144 | tf_op jit(solution)/shard_map/all_to_all | solution.py:266
  28.3 0.6 %reduce_sum.9 = f32[16,256]{1,0:T(8,128)} reduce(f32[8,16,256]{2,1,0:T(8,128)S(1)} %all_to_all.5, f32[]{:T(128)} %constant.0.clone.1), dimensions={0}, to_apply=%region_0.0 | reduce | flops 28672 | bytes 147460 | tf_op jit(solution)/shard_map/reduce_sum | solution.py:267
  (3 shorter events, 0.1 us)
Async XLA Ops:
  1.0 1.3 %copy-start = (bf16[2560,256]{1,0:T(8,128)(2,1)S(1)}, bf16[2560,256]{1,0:T(8,128)(2,1)}, u32[]{:S(2)}) copy-start(bf16[2560,256]{1,0:T(8,128)(2,1)} %modes.5) | copy-start | bytes 3932164
  1.0 5.8 %copy-start.1 = (bf16[14,640,640]{2,1,0:T(8,128)(2,1)S(1)}, bf16[14,640,640]{2,1,0:T(8,128)(2,1)}, u32[]{:S(2)}) copy-start(bf16[14,640,640]{2,1,0:T(8,128)(2,1)} %jac.1) | copy-start | bytes 34406404
  1.0 12.5 %collective-permute-start = (bf16[640,256]{1,0:T(8,128)(2,1)S(1)}, bf16[640,256]{1,0:T(8,128)(2,1)S(1)}, u32[]{:S(2)}, u32[]{:S(2)}) collective-permute-start(bf16[640,256]{1,0:T(8,128)(2,1)S(1)} %gate.1), channel_id=1, source_target_pairs={{0,0},{1,2},{2,1},{3,4},{4,3},{5,6},{6,5},{7,8},{8,7},{9,10},{10,9... | collective-permute-start | bytes 983048 | tf_op jit(solution)/shard_map/ppermute | solution.py:255
  2.4 4.5 %copy-start.2 = (s32[14,2]{0,1:T(2,128)S(1)}, s32[14,2]{0,1:T(2,128)}, u32[]{:S(2)}) copy-start(s32[14,2]{0,1:T(2,128)} %param.5) | copy-start | bytes 340
  2.4 11.2 %collective-permute-start.1 = (bf16[640,256]{1,0:T(8,128)(2,1)S(1)}, bf16[640,256]{1,0:T(8,128)(2,1)S(1)}, u32[]{:S(2)}, u32[]{:S(2)}) collective-permute-start(bf16[640,256]{1,0:T(8,128)(2,1)S(1)} %inner_edge.1), channel_id=1, source_target_pairs={{0,1},{1,0},{2,3},{3,2},{4,5},{5,4},{6,7},{7,6},{8,9},{9,8},{10,11... | collective-permute-start | bytes 983048 | tf_op jit(solution)/shard_map/ppermute | solution.py:256
  14.0 1.4 %collective-permute-start.2 = (f32[128,256]{1,0:T(8,128)S(1)}, f32[128,256]{1,0:T(8,128)S(1)}, u32[]{:S(2)}, u32[]{:S(2)}) collective-permute-start(f32[128,256]{1,0:T(8,128)S(1)} %join_give.1), channel_id=1, source_target_pairs={{0,1},{1,0},{2,3},{3,2},{4,5},{5,4},{6,7},{7,6},{8,9},{9,8},{10,11... | collective-permute-start | bytes 393224 | tf_op jit(solution)/shard_map/ppermute | solution.py:263

commit v12 on v10

--- a/solution.py
+++ b/solution.py
@@ -87,7 +87,7 @@
             out_ref[:, columns] = block
         else:
             for k in range(n_modes // keep_rows):
-                place = k % 2 * (n_modes // 2) + k // 2 * keep_rows
+                place = (k ^ k // 2) % 2 * (n_modes // 2) + n_modes // 2 - (k // 2 + 1) * keep_rows
                 out_ref[place : place + keep_rows, columns] = block[k * keep_rows : (k + 1) * keep_rows]
 
 
@@ -201,16 +201,25 @@
     )(neighbours, jac_blocks, modes, turned)
 
 
+def teams(count):
+    return [[2 * chip + (chip + half) % 2 for chip in reversed(range(count // 2))] for half in range(2)]
+
+
+def own_team():
+    me = lax.axis_index("cell")
+    return lax.rem(me + me // 2, 2)
+
+
 def regrouped(value, axis, keep_rows):
-    shape = value.shape
-    split = shape[:axis] + (shape[axis] // (2 * keep_rows), 2, keep_rows) + shape[axis + 1 :]
-    return jnp.swapaxes(value.reshape(split), axis, axis + 1).reshape(shape)
+    first, second = teams(value.shape[axis] // keep_rows)
+    starts = [k * keep_rows for k in first + second]
+    return jnp.concatenate([lax.slice_in_dim(value, k, k + keep_rows, axis=axis) for k in starts], axis=axis)
 
 
 def join_kernel(other, p_ref, t_ref, outer_ref, inner_ref, out_ref):
     core = lax.rem(lax.axis_index("cell"), 2)
     count = out_ref.shape[0]
-    half = 1 - core if other else core
+    half = 1 - own_team() if other else own_team()
     rows = pl.ds(pl.multiple_of(half * count, TILE_ROWS), count)
     both = dot(t_ref[1 - core, half], inner_ref[...]) + dot(t_ref[core, half], outer_ref[...])
     out_ref[...] = p_ref[rows, :] + both[:count] + both[count:]
@@ -247,8 +256,7 @@
     got = lax.ppermute(join(True, p, t, outer, inner), "cell", swap)
     keep = join(False, p, t, outer, inner)
     pair = (keep + got).reshape(count // 2, keep_rows, n_modes)
-    same_core = [list(range(core, count, 2)) for core in range(2)]
-    parts = lax.all_to_all(pair, "cell", 0, 0, axis_index_groups=same_core)
+    parts = lax.all_to_all(pair, "cell", 0, 0, axis_index_groups=teams(count))
     return jnp.sum(parts, axis=0)
 
 

time: 29.5 us -> 28 us (0.949)
  blocking collectives: 13.5 us -> 12 us
    all_to_all x1, blocking collectives: 13.5 us -> 12 us  [per_device(): parts = lax.all_to_all(pair, 'cell', 0, 0, axis_index_groups=teams(count))]
  transfers between devices with their start and end apart: 3 -> 3, of which waited for: 1 -> 1; matrix products, arithmetic and copies ran while one was open for 0% -> 0% of each run, Pallas kernels for 18% -> 19%
where the time goes in v12:
time: 28 us; the launch traced here: 27.8 us
  blocking collectives  12 us (43%)
  starting transfers between devices  7.4 us (26%)
  Pallas kernels  6.62 us (24%)
  waiting for transfers between devices  0.63 us (2%)
  other arithmetic  0.63 us (2%)
  local copies, waits for them, and re-layouts  0.46 us (2%)
    all_to_all x1, blocking collectives, per_device(): parts = lax.all_to_all(pair, 'cell', 0, 0, axis_index_groups=teams(count))  12 us
    pallas_call x1, Pallas kernels, own_part(): pl.pallas_call(functools.partial(own_kernel, blocks), out_shape=(jax.Shap...  4.49 us
    ppermute x1, starting transfers between devices, per_device(): inner = lax.ppermute(inner_edge(modes, width), 'cell', swap)  4.08 us
    ppermute x1, starting transfers between devices, per_device(): got = lax.ppermute(join(True, p, t, outer, inner), 'cell', swap)  2.51 us
    pallas_call x1, Pallas kernels, outer_edge(): pl.pallas_call(outer_kernel, out_shape=jax.ShapeDtypeStruct((width, modes...  0.98 us
    ppermute x1, starting transfers between devices, per_device(): outer = lax.ppermute(gate(outer_edge(modes, width)), 'cell', across)  0.81 us
    pallas_call x2, Pallas kernels, join(): pl.pallas_call(functools.partial(join_kernel, other), out_shape=jax.Shape...  0.7 us
    ppermute x1, waiting for transfers between devices, per_device(): got = lax.ppermute(join(True, p, t, outer, inner), 'cell', swap)  0.62 us
  transfers between devices with their start and end apart: 3, of which 1 were waited for; matrix products, arithmetic and copies ran while one was open for 0% of the time, Pallas kernels for 19%

profile of v12, /device:TPU:0, one launch (start us, length us, event | category | flops | bytes accessed | tf_op | source)
XLA Modules:
  0.0 27.8 jit_solution(5946406287904586305)
XLA Ops:
  0.0 1.0 %outer_edge.1.block_ref = bf16[640,256]{1,0:T(8,128)(2,1)S(1)} custom-call(bf16[2560,256]{1,0:T(8,128)(2,1)} %modes.5), custom_call_target="tpu_custom_call" | custom-call | bytes 655360 | tf_op jit(solution)/shard_map/outer_edge/pallas_call | solution.py:34
  1.0 0.0 copy-start
  1.0 0.0 copy-start.1
  1.0 0.8 %collective-permute-start = (bf16[640,256]{1,0:T(8,128)(2,1)S(1)}, bf16[640,256]{1,0:T(8,128)(2,1)S(1)}, u32[]{:S(2)}, u32[]{:S(2)}) collective-permute-start(bf16[640,256]{1,0:T(8,128)(2,1)S(1)} %gate.1), channel_id=1, source_target_pairs={{0,0},{1,2},{2,1},{3,4},{4,3},{5,6},{6,5},{7,8},{8,7},{9,10},{10,9... | collective-permute-start | bytes 983048 | tf_op jit(solution)/shard_map/ppermute | solution.py:248
  1.9 0.4 %copy-done = bf16[2560,256]{1,0:T(8,128)(2,1)S(1)} copy-done((bf16[2560,256]{1,0:T(8,128)(2,1)S(1)}, bf16[2560,256]{1,0:T(8,128)(2,1)}, u32[]{:S(2)}) %copy-start) | copy-done | bytes 1310744
  2.3 0.0 copy-start.2
  2.4 4.1 %collective-permute-start.1 = (bf16[640,256]{1,0:T(8,128)(2,1)S(1)}, bf16[640,256]{1,0:T(8,128)(2,1)S(1)}, u32[]{:S(2)}, u32[]{:S(2)}) collective-permute-start(bf16[640,256]{1,0:T(8,128)(2,1)S(1)} %inner_edge.1), channel_id=1, source_target_pairs={{0,1},{1,0},{2,3},{3,2},{4,5},{5,4},{6,7},{7,6},{8,9},{9,8},{10,11... | collective-permute-start | bytes 983048 | tf_op jit(solution)/shard_map/ppermute | solution.py:249
  6.4 0.4 %turn.1.turned = bf16[256,2560]{1,0:T(8,128)(2,1)S(1)} custom-call(bf16[2560,256]{1,0:T(8,128)(2,1)S(1)} %copy-done), custom_call_target="tpu_custom_call" | custom-call | bytes 2621440 | tf_op jit(solution)/shard_map/turn/pallas_call | solution.py:96
  6.8 0.0 copy-done.1
  6.8 0.0 copy-done.2
  6.9 4.5 %own_part.1 = (f32[256,256]{1,0:T(8,128)S(1)}, bf16[2,2,256,640]{3,2,1,0:T(8,128)(2,1)S(1)}) custom-call(s32[2,14]{1,0:T(2,128)S(1)} %bitcast.2, bf16[14,640,640]{2,1,0:T(8,128)(2,1)S(1)} %copy-done.1, bf16[2560,256]{1,0:T(8,128)(2,1)S(1)} %copy-done, bf16[256,2560]{1,0:T(8,128)(2,1)S(1)} %turn.1.turned), custom_call_target="tpu_custom_call" | custom-call | flops 3607101440 | bytes 12779520 | tf_op jit(solution)/shard_map/own_part/pallas_call | solution.py:176
  11.4 0.0 collective-permute-done.outer_ref
  11.4 0.0 collective-permute-done.1.inner_ref
  11.4 0.3 %join_give.1 = f32[128,256]{1,0:T(8,128)S(1)} custom-call(f32[256,256]{1,0:T(8,128)S(1)} %get-tuple-element.7.p_ref, bf16[2,2,256,640]{3,2,1,0:T(8,128)(2,1)S(1)} %get-tuple-element.8.t_ref, bf16[640,256]{1,0:T(8,128)(2,1)S(1)} %collective-permute-done.outer_ref, bf16[640,256]{1,0:T(8,128)(2,1)S(1)} %collective-permute-done.1.inner_ref), custom_call_target="tpu_custom_call" | custom-call | flops 167772160 | tf_op jit(solution)/shard_map/join_give/pallas_call | solution.py:230
  11.7 2.5 %collective-permute-start.2 = (f32[128,256]{1,0:T(8,128)S(1)}, f32[128,256]{1,0:T(8,128)S(1)}, u32[]{:S(2)}, u32[]{:S(2)}) collective-permute-start(f32[128,256]{1,0:T(8,128)S(1)} %join_give.1), channel_id=1, source_target_pairs={{0,1},{1,0},{2,3},{3,2},{4,5},{5,4},{6,7},{7,6},{8,9},{9,8},{10,11... | collective-permute-start | bytes 393224 | tf_op jit(solution)/shard_map/ppermute | solution.py:256
  14.2 0.4 %join_keep.1 = f32[128,256]{1,0:T(8,128)S(1)} custom-call(f32[256,256]{1,0:T(8,128)S(1)} %get-tuple-element.7.p_ref, bf16[2,2,256,640]{3,2,1,0:T(8,128)(2,1)S(1)} %get-tuple-element.8.t_ref, bf16[640,256]{1,0:T(8,128)(2,1)S(1)} %collective-permute-done.outer_ref, bf16[640,256]{1,0:T(8,128)(2,1)S(1)} %collective-permute-done.1.inner_ref), custom_call_target="tpu_custom_call" | custom-call | flops 167772160 | tf_op jit(solution)/shard_map/join_keep/pallas_call | solution.py:230
  14.6 0.6 %collective-permute-done.2 = f32[128,256]{1,0:T(8,128)S(1)} collective-permute-done((f32[128,256]{1,0:T(8,128)S(1)}, f32[128,256]{1,0:T(8,128)S(1)}, u32[]{:S(2)}, u32[]{:S(2)}) %collective-permute-start.2) | collective-permute-done | bytes 131104 | tf_op jit(solution)/shard_map/ppermute | solution.py:256
  15.2 12.0 %all_to_all.5 = f32[8,16,256]{2,1,0:T(8,128)S(1)} all-to-all(f32[8,16,256]{2,1,0:T(8,128)S(1)} %bitcast.3), channel_id=1, replica_groups={{15,12,11,8,7,4,3,0},{14,13,10,9,6,5,2,1},{31,28,27,24,23,20,19,16},{30..., dimensions={0} | all-to-all | bytes 262144 | tf_op jit(solution)/shard_map/all_to_all | solution.py:259
  27.2 0.6 %reduce_sum.9 = f32[16,256]{1,0:T(8,128)} reduce(f32[8,16,256]{2,1,0:T(8,128)S(1)} %all_to_all.5, f32[]{:T(128)} %constant.0.clone.1), dimensions={0}, to_apply=%region_0.0 | reduce | flops 28672 | bytes 147460 | tf_op jit(solution)/shard_map/reduce_sum | solution.py:260
  (3 shorter events, 0.1 us)
Async XLA Ops:
  1.0 1.3 %copy-start = (bf16[2560,256]{1,0:T(8,128)(2,1)S(1)}, bf16[2560,256]{1,0:T(8,128)(2,1)}, u32[]{:S(2)}) copy-start(bf16[2560,256]{1,0:T(8,128)(2,1)} %modes.5) | copy-start | bytes 3932164
  1.0 5.8 %copy-start.1 = (bf16[14,640,640]{2,1,0:T(8,128)(2,1)S(1)}, bf16[14,640,640]{2,1,0:T(8,128)(2,1)}, u32[]{:S(2)}) copy-start(bf16[14,640,640]{2,1,0:T(8,128)(2,1)} %jac.1) | copy-start | bytes 34406404
  1.0 10.3 %collective-permute-start = (bf16[640,256]{1,0:T(8,128)(2,1)S(1)}, bf16[640,256]{1,0:T(8,128)(2,1)S(1)}, u32[]{:S(2)}, u32[]{:S(2)}) collective-permute-start(bf16[640,256]{1,0:T(8,128)(2,1)S(1)} %gate.1), channel_id=1, source_target_pairs={{0,0},{1,2},{2,1},{3,4},{4,3},{5,6},{6,5},{7,8},{8,7},{9,10},{10,9... | collective-permute-start | bytes 983048 | tf_op jit(solution)/shard_map/ppermute | solution.py:248
  2.3 4.5 %copy-start.2 = (s32[14,2]{0,1:T(2,128)S(1)}, s32[14,2]{0,1:T(2,128)}, u32[]{:S(2)}) copy-start(s32[14,2]{0,1:T(2,128)} %param.5) | copy-start | bytes 340
  2.4 9.0 %collective-permute-start.1 = (bf16[640,256]{1,0:T(8,128)(2,1)S(1)}, bf16[640,256]{1,0:T(8,128)(2,1)S(1)}, u32[]{:S(2)}, u32[]{:S(2)}) collective-permute-start(bf16[640,256]{1,0:T(8,128)(2,1)S(1)} %inner_edge.1), channel_id=1, source_target_pairs={{0,1},{1,0},{2,3},{3,2},{4,5},{5,4},{6,7},{7,6},{8,9},{9,8},{10,11... | collective-permute-start | bytes 983048 | tf_op jit(solution)/shard_map/ppermute | solution.py:249
  11.7 3.5 %collective-permute-start.2 = (f32[128,256]{1,0:T(8,128)S(1)}, f32[128,256]{1,0:T(8,128)S(1)}, u32[]{:S(2)}, u32[]{:S(2)}) collective-permute-start(f32[128,256]{1,0:T(8,128)S(1)} %join_give.1), channel_id=1, source_target_pairs={{0,1},{1,0},{2,3},{3,2},{4,5},{5,4},{6,7},{7,6},{8,9},{9,8},{10,11... | collective-permute-start | bytes 393224 | tf_op jit(solution)/shard_map/ppermute | solution.py:256

commit v13 on v12

--- a/solution.py
+++ b/solution.py
@@ -20,27 +20,6 @@
 def halves(value):
     upper = value.astype(jnp.bfloat16)
     return upper, (value - upper.astype(jnp.float32)).astype(jnp.bfloat16)
-
-
-def outer_kernel(modes_hbm, out_ref, sem):
-    width = out_ref.shape[0]
-    start = lax.rem(lax.axis_index("cell"), 2) * (modes_hbm.shape[0] - width)
-    copy = pltpu.make_async_copy(modes_hbm.at[pl.ds(pl.multiple_of(start, 128), width), :], out_ref, sem)
-    copy.start()
-    copy.wait()
-
-
-def outer_edge(modes, width):
-    return pl.pallas_call(
-        outer_kernel,
-        out_shape=jax.ShapeDtypeStruct((width, modes.shape[1]), modes.dtype),
-        in_specs=[pl.BlockSpec(memory_space=pltpu.HBM)],
-        out_specs=pl.BlockSpec(memory_space=pltpu.VMEM),
-        scratch_shapes=[pltpu.SemaphoreType.DMA],
-        compiler_params=pltpu.CompilerParams(vmem_limit_bytes=SMALL_VMEM),
-        cost_estimate=pl.CostEstimate(flops=0, bytes_accessed=4 * width * modes.shape[1], transcendentals=0),
-        name="outer_edge",
-    )(pltpu.with_memory_space_constraint(modes, pltpu.HBM))
 
 
 def gate_kernel(block_ref, out_ref):
@@ -238,6 +217,25 @@
     )(p, t, outer, inner)
 
 
+def sum_kernel(parts_ref, out_hbm, total, sem):
+    total[...] = jnp.sum(parts_ref[...], axis=0)
+    copy = pltpu.make_async_copy(total, out_hbm, sem)
+    copy.start()
+    copy.wait()
+
+
+def sum_parts(parts):
+    return pl.pallas_call(
+        sum_kernel,
+        out_shape=jax.ShapeDtypeStruct(parts.shape[1:], parts.dtype),
+        in_specs=[pl.BlockSpec(memory_space=pltpu.VMEM)],
+        out_specs=pl.BlockSpec(memory_space=pl.ANY),
+        scratch_shapes=[pltpu.VMEM(parts.shape[1:], parts.dtype), pltpu.SemaphoreType.DMA],
+        compiler_params=pltpu.CompilerParams(vmem_limit_bytes=SMALL_VMEM),
+        name="sum_parts",
+    )(parts)
+
+
 def per_device(jac_blocks, modes, neighbours):
     width = jac_blocks.shape[1]
     rows, n_modes = modes.shape
@@ -245,7 +243,9 @@
     keep_rows = n_modes // count
     across = [(i, min(max(i - 1 + 2 * (i % 2), 0), count - 1)) for i in range(count)]
     swap = [(i, i ^ 1) for i in range(count)]
-    outer = lax.ppermute(gate(outer_edge(modes, width)), "cell", across)
+    core = lax.rem(lax.axis_index("cell"), 2)
+    outer_edge = lax.dynamic_slice_in_dim(modes, core * (rows - width), width)
+    outer = lax.ppermute(gate(outer_edge), "cell", across)
     inner = lax.ppermute(inner_edge(modes, width), "cell", swap)
     p, t = own_part(neighbours.T, jac_blocks, modes, turn(modes, keep_rows))
     if keep_rows % TILE_ROWS:
@@ -257,7 +257,7 @@
     keep = join(False, p, t, outer, inner)
     pair = (keep + got).reshape(count // 2, keep_rows, n_modes)
     parts = lax.all_to_all(pair, "cell", 0, 0, axis_index_groups=teams(count))
-    return jnp.sum(parts, axis=0)
+    return sum_parts(parts)
 
 
 def solution(mesh):

time: 28 us -> 28 us (level)
  starting transfers between devices: 7.4 us -> 5.93 us
  Pallas kernels: 6.62 us -> 7.74 us
  local copies, waits for them, and re-layouts: 0.46 us -> 1.45 us
  other arithmetic: 0.63 us -> 0.02 us
    pallas_call x1, Pallas kernels: 4.49 us -> 5.97 us  [own_part(): pl.pallas_call(functools.partial(own_kernel, blocks), out_shape=(jax.Shap...]
    ppermute x1, starting transfers between devices: 2.51 us -> 1.04 us  [per_device(): got = lax.ppermute(join(True, p, t, outer, inner), 'cell', swap)]
    dynamic_slice x0 -> x1, local copies, waits for them, and re-layouts: none -> 0.99 us  [per_device(): outer_edge = lax.dynamic_slice_in_dim(modes, core * (rows - width), width)]
    reduce_sum x1 -> x0, other arithmetic: 0.62 us -> none  [per_device(): return jnp.sum(parts, axis=0)]
    pallas_call x1, Pallas kernels: 0.98 us -> 0.62 us  [sum_parts(): pl.pallas_call(sum_kernel, out_shape=jax.ShapeDtypeStruct(parts.shape[1:]...]
  transfers between devices with their start and end apart: 3 -> 3, of which waited for: 1 -> 1; matrix products, arithmetic and copies ran while one was open for 0% -> 0% of each run, Pallas kernels for 19% -> 24%
where the time goes in v13:
time: 28 us; the launch traced here: 27.8 us
  blocking collectives  11.9 us (42%)
  Pallas kernels  7.74 us (28%)
  starting transfers between devices  5.93 us (21%)
  local copies, waits for them, and re-layouts  1.45 us (5%)
  waiting for transfers between devices  0.63 us (2%)
    all_to_all x1, blocking collectives, per_device(): parts = lax.all_to_all(pair, 'cell', 0, 0, axis_index_groups=teams(count))  11.9 us
    pallas_call x1, Pallas kernels, own_part(): pl.pallas_call(functools.partial(own_kernel, blocks), out_shape=(jax.Shap...  5.97 us
    ppermute x1, starting transfers between devices, per_device(): inner = lax.ppermute(inner_edge(modes, width), 'cell', swap)  4.08 us
    ppermute x1, starting transfers between devices, per_device(): got = lax.ppermute(join(True, p, t, outer, inner), 'cell', swap)  1.04 us
    dynamic_slice x1, local copies, waits for them, and re-layouts, per_device(): outer_edge = lax.dynamic_slice_in_dim(modes, core * (rows - width), width)  0.99 us
    ppermute x1, starting transfers between devices, per_device(): outer = lax.ppermute(gate(outer_edge), 'cell', across)  0.81 us
    pallas_call x2, Pallas kernels, join(): pl.pallas_call(functools.partial(join_kernel, other), out_shape=jax.Shape...  0.7 us
    ppermute x1, waiting for transfers between devices, per_device(): got = lax.ppermute(join(True, p, t, outer, inner), 'cell', swap)  0.63 us
  transfers between devices with their start and end apart: 3, of which 1 were waited for; matrix products, arithmetic and copies ran while one was open for 0% of the time, Pallas kernels for 24%

profile of v13, /device:TPU:0, one launch (start us, length us, event | category | flops | bytes accessed | tf_op | source)
XLA Modules:
  0.0 27.8 jit_solution(16231624236979028135)
XLA Ops:
  0.0 1.0 %constant_dynamic-slice_fusion.block_ref = bf16[640,256]{1,0:T(8,128)(2,1)S(1)} fusion(bf16[2560,256]{1,0:T(8,128)(2,1)} %modes.5, s32[]{:T(128)S(6)} %select_n.3), kind=kLoop, calls=%fused_computation | loop fusion | bytes 655364 | tf_op jit(solution)/shard_map/dynamic_slice | solution.py:247
  1.0 0.0 copy-start
  1.0 0.0 copy-start.1
  1.1 0.8 %collective-permute-start = (bf16[640,256]{1,0:T(8,128)(2,1)S(1)}, bf16[640,256]{1,0:T(8,128)(2,1)S(1)}, u32[]{:S(2)}, u32[]{:S(2)}) collective-permute-start(bf16[640,256]{1,0:T(8,128)(2,1)S(1)} %gate.1), channel_id=1, source_target_pairs={{0,0},{1,2},{2,1},{3,4},{4,3},{5,6},{6,5},{7,8},{8,7},{9,10},{10,9... | collective-permute-start | bytes 983048 | tf_op jit(solution)/shard_map/ppermute | solution.py:248
  1.9 0.4 %copy-done = bf16[2560,256]{1,0:T(8,128)(2,1)S(1)} copy-done((bf16[2560,256]{1,0:T(8,128)(2,1)S(1)}, bf16[2560,256]{1,0:T(8,128)(2,1)}, u32[]{:S(2)}) %copy-start) | copy-done | bytes 1310744
  2.4 0.0 copy-start.2
  2.4 4.1 %collective-permute-start.1 = (bf16[640,256]{1,0:T(8,128)(2,1)S(1)}, bf16[640,256]{1,0:T(8,128)(2,1)S(1)}, u32[]{:S(2)}, u32[]{:S(2)}) collective-permute-start(bf16[640,256]{1,0:T(8,128)(2,1)S(1)} %inner_edge.1), channel_id=1, source_target_pairs={{0,1},{1,0},{2,3},{3,2},{4,5},{5,4},{6,7},{7,6},{8,9},{9,8},{10,11... | collective-permute-start | bytes 983048 | tf_op jit(solution)/shard_map/ppermute | solution.py:249
  6.4 0.4 %turn.1.turned = bf16[256,2560]{1,0:T(8,128)(2,1)S(1)} custom-call(bf16[2560,256]{1,0:T(8,128)(2,1)S(1)} %copy-done), custom_call_target="tpu_custom_call" | custom-call | bytes 2621440 | tf_op jit(solution)/shard_map/turn/pallas_call | solution.py:75
  6.8 0.0 copy-done.1
  6.9 0.0 copy-done.2
  6.9 6.0 %own_part.1 = (f32[256,256]{1,0:T(8,128)S(1)}, bf16[2,2,256,640]{3,2,1,0:T(8,128)(2,1)S(1)}) custom-call(s32[2,14]{1,0:T(2,128)S(1)} %bitcast.2, bf16[14,640,640]{2,1,0:T(8,128)(2,1)S(1)} %copy-done.1, bf16[2560,256]{1,0:T(8,128)(2,1)S(1)} %copy-done, bf16[256,2560]{1,0:T(8,128)(2,1)S(1)} %turn.1.turned), custom_call_target="tpu_custom_call" | custom-call | flops 3607101440 | bytes 12779520 | tf_op jit(solution)/shard_map/own_part/pallas_call | solution.py:155
  12.8 0.0 collective-permute-done.outer_ref
  12.9 0.0 collective-permute-done.1.inner_ref
  12.9 0.4 %join_give.1 = f32[128,256]{1,0:T(8,128)S(1)} custom-call(f32[256,256]{1,0:T(8,128)S(1)} %get-tuple-element.7.p_ref, bf16[2,2,256,640]{3,2,1,0:T(8,128)(2,1)S(1)} %get-tuple-element.8.t_ref, bf16[640,256]{1,0:T(8,128)(2,1)S(1)} %collective-permute-done.outer_ref, bf16[640,256]{1,0:T(8,128)(2,1)S(1)} %collective-permute-done.1.inner_ref), custom_call_target="tpu_custom_call" | custom-call | flops 167772160 | tf_op jit(solution)/shard_map/join_give/pallas_call | solution.py:209
  13.2 1.0 %collective-permute-start.2 = (f32[128,256]{1,0:T(8,128)S(1)}, f32[128,256]{1,0:T(8,128)S(1)}, u32[]{:S(2)}, u32[]{:S(2)}) collective-permute-start(f32[128,256]{1,0:T(8,128)S(1)} %join_give.1), channel_id=1, source_target_pairs={{0,1},{1,0},{2,3},{3,2},{4,5},{5,4},{6,7},{7,6},{8,9},{9,8},{10,11... | collective-permute-start | bytes 393224 | tf_op jit(solution)/shard_map/ppermute | solution.py:256
  14.3 0.4 %join_keep.1 = f32[128,256]{1,0:T(8,128)S(1)} custom-call(f32[256,256]{1,0:T(8,128)S(1)} %get-tuple-element.7.p_ref, bf16[2,2,256,640]{3,2,1,0:T(8,128)(2,1)S(1)} %get-tuple-element.8.t_ref, bf16[640,256]{1,0:T(8,128)(2,1)S(1)} %collective-permute-done.outer_ref, bf16[640,256]{1,0:T(8,128)(2,1)S(1)} %collective-permute-done.1.inner_ref), custom_call_target="tpu_custom_call" | custom-call | flops 167772160 | tf_op jit(solution)/shard_map/join_keep/pallas_call | solution.py:209
  14.6 0.6 %collective-permute-done.2 = f32[128,256]{1,0:T(8,128)S(1)} collective-permute-done((f32[128,256]{1,0:T(8,128)S(1)}, f32[128,256]{1,0:T(8,128)S(1)}, u32[]{:S(2)}, u32[]{:S(2)}) %collective-permute-start.2) | collective-permute-done | bytes 131104 | tf_op jit(solution)/shard_map/ppermute | solution.py:256
  15.3 11.9 %all_to_all.5.parts_ref = f32[8,16,256]{2,1,0:T(8,128)S(1)} all-to-all(f32[8,16,256]{2,1,0:T(8,128)S(1)} %bitcast.3), channel_id=1, replica_groups={{15,12,11,8,7,4,3,0},{14,13,10,9,6,5,2,1},{31,28,27,24,23,20,19,16},{30..., dimensions={0} | all-to-all | bytes 262144 | tf_op jit(solution)/shard_map/all_to_all | solution.py:259
  27.2 0.6 %sum_parts.1 = f32[16,256]{1,0:T(8,128)} custom-call(f32[8,16,256]{2,1,0:T(8,128)S(1)} %all_to_all.5.parts_ref), custom_call_target="tpu_custom_call" | custom-call | tf_op jit(solution)/shard_map/sum_parts/pallas_call | solution.py:228
  (3 shorter events, 0.1 us)
Async XLA Ops:
  1.0 1.3 %copy-start = (bf16[2560,256]{1,0:T(8,128)(2,1)S(1)}, bf16[2560,256]{1,0:T(8,128)(2,1)}, u32[]{:S(2)}) copy-start(bf16[2560,256]{1,0:T(8,128)(2,1)} %modes.5) | copy-start | bytes 3932164
  1.0 5.8 %copy-start.1 = (bf16[14,640,640]{2,1,0:T(8,128)(2,1)S(1)}, bf16[14,640,640]{2,1,0:T(8,128)(2,1)}, u32[]{:S(2)}) copy-start(bf16[14,640,640]{2,1,0:T(8,128)(2,1)} %jac.1) | copy-start | bytes 34406404
  1.1 11.8 %collective-permute-start = (bf16[640,256]{1,0:T(8,128)(2,1)S(1)}, bf16[640,256]{1,0:T(8,128)(2,1)S(1)}, u32[]{:S(2)}, u32[]{:S(2)}) collective-permute-start(bf16[640,256]{1,0:T(8,128)(2,1)S(1)} %gate.1), channel_id=1, source_target_pairs={{0,0},{1,2},{2,1},{3,4},{4,3},{5,6},{6,5},{7,8},{8,7},{9,10},{10,9... | collective-permute-start | bytes 983048 | tf_op jit(solution)/shard_map/ppermute | solution.py:248
  2.4 4.5 %copy-start.2 = (s32[14,2]{0,1:T(2,128)S(1)}, s32[14,2]{0,1:T(2,128)}, u32[]{:S(2)}) copy-start(s32[14,2]{0,1:T(2,128)} %param.5) | copy-start | bytes 340
  2.4 10.5 %collective-permute-start.1 = (bf16[640,256]{1,0:T(8,128)(2,1)S(1)}, bf16[640,256]{1,0:T(8,128)(2,1)S(1)}, u32[]{:S(2)}, u32[]{:S(2)}) collective-permute-start(bf16[640,256]{1,0:T(8,128)(2,1)S(1)} %inner_edge.1), channel_id=1, source_target_pairs={{0,1},{1,0},{2,3},{3,2},{4,5},{5,4},{6,7},{7,6},{8,9},{9,8},{10,11... | collective-permute-start | bytes 983048 | tf_op jit(solution)/shard_map/ppermute | solution.py:249
  13.2 2.0 %collective-permute-start.2 = (f32[128,256]{1,0:T(8,128)S(1)}, f32[128,256]{1,0:T(8,128)S(1)}, u32[]{:S(2)}, u32[]{:S(2)}) collective-permute-start(f32[128,256]{1,0:T(8,128)S(1)} %join_give.1), channel_id=1, source_target_pairs={{0,1},{1,0},{2,3},{3,2},{4,5},{5,4},{6,7},{7,6},{8,9},{9,8},{10,11... | collective-permute-start | bytes 393224 | tf_op jit(solution)/shard_map/ppermute | solution.py:256

commit v14 on v13

--- a/solution.py
+++ b/solution.py
@@ -83,68 +83,51 @@
     )(modes)
 
 
-def own_kernel(blocks, nb_ref, jac, modes, turned, p_ref, t_ref, jv, parts, face, near, far):
+def own_kernel(blocks, nb_ref, jac, modes, turned, p_ref, t_ref, left, parts, live):
     slots, width, _ = jac.shape
     n_modes = modes.shape[1]
-
-    def block_at(k):
-        return pl.ds(pl.multiple_of(k * width, width), width)
+    mid = n_modes // 2
 
     base = nb_ref[1, 0]
-    n_near = jnp.int32(0)
-    n_far = jnp.int32(0)
+    count = jnp.int32(0)
     for s in range(blocks, slots):
         r = nb_ref[0, s]
-        c = nb_ref[1, s] - base
-        inside = (c >= 0) & (c < blocks)
-        near[0, n_near] = s
-        near[1, n_near] = r
-        near[2, n_near] = c
-        far[0, n_far] = s
-        far[1, n_far] = jnp.where(c < 0, 0, 1)
-        n_near += ((r >= 0) & inside).astype(jnp.int32)
-        n_far += ((r >= 0) & jnp.logical_not(inside)).astype(jnp.int32)
-    near[0, n_near] = 0
-    near[1, n_near] = blocks
-    near[2, n_near] = 0
-    far[0, n_far] = 0
-    far[1, n_far] = 2
+        live[0, count] = s
+        live[1, count] = r
+        live[2, count] = nb_ref[1, s] - base + 1
+        count += (r >= 0).astype(jnp.int32)
+    live[0, count] = 0
+    live[1, count] = 0
+    live[2, count] = blocks + 2
 
     for s in range(blocks):
-        rows = pl.ds(s * width, width)
-        jv[rows, :] = dot(jac[s], modes[rows, :])
-    face[...] = jnp.zeros_like(face)
-
-    def near_pair(k, carry):
+        left[s + 1] = dot(turned[:, s * width : (s + 1) * width], jac[s])
+    left[0] = jnp.zeros((n_modes, width), jnp.float32)
+    left[blocks + 1] = jnp.zeros((n_modes, width), jnp.float32)
+
+    def pair(k, carry):
         for j in (2 * k, 2 * k + 1):
-            jv[block_at(near[1, j]), :] += dot(jac[near[0, j]], modes[block_at(near[2, j]), :])
+            columns = pl.ds(pl.multiple_of(live[1, j] * width, width), width)
+            left[live[2, j]] += dot(turned[:, columns], jac[live[0, j]])
         return carry
 
-    def far_pair(k, carry):
-        for j in (2 * k, 2 * k + 1):
-            side = far[1, j]
-            edge = block_at(jnp.where(side == 1, blocks - 1, 0))
-            face[side] += dot(turned[:, edge], jac[far[0, j]])
-        return carry
-
-    lax.fori_loop(0, (n_near + 1) // 2, near_pair, 0)
-    lax.fori_loop(0, (n_far + 1) // 2, far_pair, 0)
-
-    mid = n_modes // 2
-    for side in range(2):
-        upper, lower = halves(face[side])
+    lax.fori_loop(0, (count + 1) // 2, pair, 0)
+
+    both = jnp.zeros((2 * n_modes, n_modes), jnp.float32)
+    step = 2 if blocks % 2 == 0 else 1
+    for first in range(0, blocks, step):
+        for c in range(first, first + step):
+            upper, lower = halves(left[c + 1])
+            parts[:n_modes, c * width : (c + 1) * width] = upper
+            parts[n_modes:, c * width : (c + 1) * width] = lower
+        inner = slice(first * width, (first + step) * width)
+        both += dot(parts[:, inner], modes[inner, :])
+    p_ref[...] = both[:n_modes] + both[n_modes:]
+    for side, c in enumerate((0, blocks + 1)):
+        upper, lower = halves(left[c])
         for half in range(2):
             t_ref[side, half, :mid] = upper[half * mid : (half + 1) * mid]
             t_ref[side, half, mid:] = lower[half * mid : (half + 1) * mid]
-    both = jnp.zeros((n_modes, 2 * n_modes), jnp.float32)
-    step = width * (2 if blocks % 2 == 0 else 1)
-    for start in range(0, blocks * width, step):
-        rows = pl.ds(start, step)
-        upper, lower = halves(jv[rows, :])
-        parts[rows, :n_modes] = upper
-        parts[rows, n_modes:] = lower
-        both += dot(turned[:, rows], parts[rows, :])
-    p_ref[...] = both[:, :n_modes] + both[:, n_modes:]
 
 
 def own_part(neighbours, jac_blocks, modes, turned):
@@ -166,11 +149,9 @@
         ],
         out_specs=(pl.BlockSpec(memory_space=pltpu.VMEM), pl.BlockSpec(memory_space=pltpu.VMEM)),
         scratch_shapes=[
-            pltpu.VMEM((rows + width, n_modes), jnp.float32),
-            pltpu.VMEM((rows, 2 * n_modes), jnp.bfloat16),
-            pltpu.VMEM((3, n_modes, width), jnp.float32),
+            pltpu.VMEM((blocks + 3, n_modes, width), jnp.float32),
+            pltpu.VMEM((2 * n_modes, rows), jnp.bfloat16),
             pltpu.SMEM((3, slots + 1), jnp.int32),
-            pltpu.SMEM((2, slots + 1), jnp.int32),
         ],
         compiler_params=pltpu.CompilerParams(vmem_limit_bytes=OWN_VMEM),
         cost_estimate=pl.CostEstimate(

time: 28 us -> 28 us (level)
  starting transfers between devices: 5.93 us -> 6.72 us
  Pallas kernels: 7.74 us -> 7.23 us
    ppermute x1, starting transfers between devices: 1.04 us -> 1.83 us  [per_device(): got = lax.ppermute(join(True, p, t, outer, inner), 'cell', swap)]
    pallas_call x1, Pallas kernels: 5.97 us -> 5.46 us  [own_part(): pl.pallas_call(functools.partial(own_kernel, blocks), out_shape=(jax.Shap...]
  transfers between devices with their start and end apart: 3 -> 3, of which waited for: 1 -> 1; matrix products, arithmetic and copies ran while one was open for 0% -> 0% of each run, Pallas kernels for 24% -> 22%
where the time goes in v14:
time: 28 us; the launch traced here: 27.8 us
  blocking collectives  11.7 us (42%)
  Pallas kernels  7.23 us (26%)
  starting transfers between devices  6.72 us (24%)
  local copies, waits for them, and re-layouts  1.45 us (5%)
  waiting for transfers between devices  0.63 us (2%)
    all_to_all x1, blocking collectives, per_device(): parts = lax.all_to_all(pair, 'cell', 0, 0, axis_index_groups=teams(count))  11.7 us
    pallas_call x1, Pallas kernels, own_part(): pl.pallas_call(functools.partial(own_kernel, blocks), out_shape=(jax.Shap...  5.46 us
    ppermute x1, starting transfers between devices, per_device(): inner = lax.ppermute(inner_edge(modes, width), 'cell', swap)  4.08 us
    ppermute x1, starting transfers between devices, per_device(): got = lax.ppermute(join(True, p, t, outer, inner), 'cell', swap)  1.83 us
    dynamic_slice x1, local copies, waits for them, and re-layouts, per_device(): outer_edge = lax.dynamic_slice_in_dim(modes, core * (rows - width), width)  0.99 us
    ppermute x1, starting transfers between devices, per_device(): outer = lax.ppermute(gate(outer_edge), 'cell', across)  0.81 us
    pallas_call x2, Pallas kernels, join(): pl.pallas_call(functools.partial(join_kernel, other), out_shape=jax.Shape...  0.7 us
    ppermute x1, waiting for transfers between devices, per_device(): got = lax.ppermute(join(True, p, t, outer, inner), 'cell', swap)  0.63 us
  transfers between devices with their start and end apart: 3, of which 1 were waited for; matrix products, arithmetic and copies ran while one was open for 0% of the time, Pallas kernels for 22%

profile of v14, /device:TPU:0, one launch (start us, length us, event | category | flops | bytes accessed | tf_op | source)
XLA Modules:
  0.0 27.8 jit_solution(1701977200444078347)
XLA Ops:
  0.0 1.0 %constant_dynamic-slice_fusion.block_ref = bf16[640,256]{1,0:T(8,128)(2,1)S(1)} fusion(bf16[2560,256]{1,0:T(8,128)(2,1)} %modes.5, s32[]{:T(128)S(6)} %select_n.3), kind=kLoop, calls=%fused_computation | loop fusion | bytes 655364 | tf_op jit(solution)/shard_map/dynamic_slice | solution.py:228
  1.0 0.0 copy-start
  1.0 0.0 copy-start.1
  1.1 0.8 %collective-permute-start = (bf16[640,256]{1,0:T(8,128)(2,1)S(1)}, bf16[640,256]{1,0:T(8,128)(2,1)S(1)}, u32[]{:S(2)}, u32[]{:S(2)}) collective-permute-start(bf16[640,256]{1,0:T(8,128)(2,1)S(1)} %gate.1), channel_id=1, source_target_pairs={{0,0},{1,2},{2,1},{3,4},{4,3},{5,6},{6,5},{7,8},{8,7},{9,10},{10,9... | collective-permute-start | bytes 983048 | tf_op jit(solution)/shard_map/ppermute | solution.py:229
  1.9 0.4 %copy-done = bf16[2560,256]{1,0:T(8,128)(2,1)S(1)} copy-done((bf16[2560,256]{1,0:T(8,128)(2,1)S(1)}, bf16[2560,256]{1,0:T(8,128)(2,1)}, u32[]{:S(2)}) %copy-start) | copy-done | bytes 1310744
  2.4 0.0 copy-start.2
  2.4 4.1 %collective-permute-start.1 = (bf16[640,256]{1,0:T(8,128)(2,1)S(1)}, bf16[640,256]{1,0:T(8,128)(2,1)S(1)}, u32[]{:S(2)}, u32[]{:S(2)}) collective-permute-start(bf16[640,256]{1,0:T(8,128)(2,1)S(1)} %inner_edge.1), channel_id=1, source_target_pairs={{0,1},{1,0},{2,3},{3,2},{4,5},{5,4},{6,7},{7,6},{8,9},{9,8},{10,11... | collective-permute-start | bytes 983048 | tf_op jit(solution)/shard_map/ppermute | solution.py:230
  6.4 0.4 %turn.1.turned = bf16[256,2560]{1,0:T(8,128)(2,1)S(1)} custom-call(bf16[2560,256]{1,0:T(8,128)(2,1)S(1)} %copy-done), custom_call_target="tpu_custom_call" | custom-call | bytes 2621440 | tf_op jit(solution)/shard_map/turn/pallas_call | solution.py:75
  6.8 0.0 copy-done.1
  6.9 0.0 copy-done.2
  6.9 5.5 %own_part.1 = (f32[256,256]{1,0:T(8,128)S(1)}, bf16[2,2,256,640]{3,2,1,0:T(8,128)(2,1)S(1)}) custom-call(s32[2,14]{1,0:T(2,128)S(1)} %bitcast.2, bf16[14,640,640]{2,1,0:T(8,128)(2,1)S(1)} %copy-done.1, bf16[2560,256]{1,0:T(8,128)(2,1)S(1)} %copy-done, bf16[256,2560]{1,0:T(8,128)(2,1)S(1)} %turn.1.turned), custom_call_target="tpu_custom_call" | custom-call | flops 3607101440 | bytes 12779520 | tf_op jit(solution)/shard_map/own_part/pallas_call | solution.py:138
  12.3 0.0 collective-permute-done.outer_ref
  12.3 0.0 collective-permute-done.1.inner_ref
  12.3 0.4 %join_give.1 = f32[128,256]{1,0:T(8,128)S(1)} custom-call(f32[256,256]{1,0:T(8,128)S(1)} %get-tuple-element.7.p_ref, bf16[2,2,256,640]{3,2,1,0:T(8,128)(2,1)S(1)} %get-tuple-element.8.t_ref, bf16[640,256]{1,0:T(8,128)(2,1)S(1)} %collective-permute-done.outer_ref, bf16[640,256]{1,0:T(8,128)(2,1)S(1)} %collective-permute-done.1.inner_ref), custom_call_target="tpu_custom_call" | custom-call | flops 167772160 | tf_op jit(solution)/shard_map/join_give/pallas_call | solution.py:190
  12.7 1.8 %collective-permute-start.2 = (f32[128,256]{1,0:T(8,128)S(1)}, f32[128,256]{1,0:T(8,128)S(1)}, u32[]{:S(2)}, u32[]{:S(2)}) collective-permute-start(f32[128,256]{1,0:T(8,128)S(1)} %join_give.1), channel_id=1, source_target_pairs={{0,1},{1,0},{2,3},{3,2},{4,5},{5,4},{6,7},{7,6},{8,9},{9,8},{10,11... | collective-permute-start | bytes 393224 | tf_op jit(solution)/shard_map/ppermute | solution.py:237
  14.5 0.4 %join_keep.1 = f32[128,256]{1,0:T(8,128)S(1)} custom-call(f32[256,256]{1,0:T(8,128)S(1)} %get-tuple-element.7.p_ref, bf16[2,2,256,640]{3,2,1,0:T(8,128)(2,1)S(1)} %get-tuple-element.8.t_ref, bf16[640,256]{1,0:T(8,128)(2,1)S(1)} %collective-permute-done.outer_ref, bf16[640,256]{1,0:T(8,128)(2,1)S(1)} %collective-permute-done.1.inner_ref), custom_call_target="tpu_custom_call" | custom-call | flops 167772160 | tf_op jit(solution)/shard_map/join_keep/pallas_call | solution.py:190
  14.9 0.6 %collective-permute-done.2 = f32[128,256]{1,0:T(8,128)S(1)} collective-permute-done((f32[128,256]{1,0:T(8,128)S(1)}, f32[128,256]{1,0:T(8,128)S(1)}, u32[]{:S(2)}, u32[]{:S(2)}) %collective-permute-start.2) | collective-permute-done | bytes 131104 | tf_op jit(solution)/shard_map/ppermute | solution.py:237
  15.5 11.7 %all_to_all.5.parts_ref = f32[8,16,256]{2,1,0:T(8,128)S(1)} all-to-all(f32[8,16,256]{2,1,0:T(8,128)S(1)} %bitcast.3), channel_id=1, replica_groups={{15,12,11,8,7,4,3,0},{14,13,10,9,6,5,2,1},{31,28,27,24,23,20,19,16},{30..., dimensions={0} | all-to-all | bytes 262144 | tf_op jit(solution)/shard_map/all_to_all | solution.py:240
  27.2 0.6 %sum_parts.1 = f32[16,256]{1,0:T(8,128)} custom-call(f32[8,16,256]{2,1,0:T(8,128)S(1)} %all_to_all.5.parts_ref), custom_call_target="tpu_custom_call" | custom-call | tf_op jit(solution)/shard_map/sum_parts/pallas_call | solution.py:209
  (3 shorter events, 0.1 us)
Async XLA Ops:
  1.0 1.3 %copy-start = (bf16[2560,256]{1,0:T(8,128)(2,1)S(1)}, bf16[2560,256]{1,0:T(8,128)(2,1)}, u32[]{:S(2)}) copy-start(bf16[2560,256]{1,0:T(8,128)(2,1)} %modes.5) | copy-start | bytes 3932164
  1.0 5.8 %copy-start.1 = (bf16[14,640,640]{2,1,0:T(8,128)(2,1)S(1)}, bf16[14,640,640]{2,1,0:T(8,128)(2,1)}, u32[]{:S(2)}) copy-start(bf16[14,640,640]{2,1,0:T(8,128)(2,1)} %jac.1) | copy-start | bytes 34406404
  1.1 11.3 %collective-permute-start = (bf16[640,256]{1,0:T(8,128)(2,1)S(1)}, bf16[640,256]{1,0:T(8,128)(2,1)S(1)}, u32[]{:S(2)}, u32[]{:S(2)}) collective-permute-start(bf16[640,256]{1,0:T(8,128)(2,1)S(1)} %gate.1), channel_id=1, source_target_pairs={{0,0},{1,2},{2,1},{3,4},{4,3},{5,6},{6,5},{7,8},{8,7},{9,10},{10,9... | collective-permute-start | bytes 983048 | tf_op jit(solution)/shard_map/ppermute | solution.py:229
  2.4 4.5 %copy-start.2 = (s32[14,2]{0,1:T(2,128)S(1)}, s32[14,2]{0,1:T(2,128)}, u32[]{:S(2)}) copy-start(s32[14,2]{0,1:T(2,128)} %param.5) | copy-start | bytes 340
  2.4 10.0 %collective-permute-start.1 = (bf16[640,256]{1,0:T(8,128)(2,1)S(1)}, bf16[640,256]{1,0:T(8,128)(2,1)S(1)}, u32[]{:S(2)}, u32[]{:S(2)}) collective-permute-start(bf16[640,256]{1,0:T(8,128)(2,1)S(1)} %inner_edge.1), channel_id=1, source_target_pairs={{0,1},{1,0},{2,3},{3,2},{4,5},{5,4},{6,7},{7,6},{8,9},{9,8},{10,11... | collective-permute-start | bytes 983048 | tf_op jit(solution)/shard_map/ppermute | solution.py:230
  12.7 2.8 %collective-permute-start.2 = (f32[128,256]{1,0:T(8,128)S(1)}, f32[128,256]{1,0:T(8,128)S(1)}, u32[]{:S(2)}, u32[]{:S(2)}) collective-permute-start(f32[128,256]{1,0:T(8,128)S(1)} %join_give.1), channel_id=1, source_target_pairs={{0,1},{1,0},{2,3},{3,2},{4,5},{5,4},{6,7},{7,6},{8,9},{9,8},{10,11... | collective-permute-start | bytes 393224 | tf_op jit(solution)/shard_map/ppermute | solution.py:237

commit v15 on v14

--- a/solution.py
+++ b/solution.py
@@ -65,9 +65,9 @@
         if keep_rows % TILE_ROWS:
             out_ref[:, columns] = block
         else:
-            for k in range(n_modes // keep_rows):
-                place = (k ^ k // 2) % 2 * (n_modes // 2) + n_modes // 2 - (k // 2 + 1) * keep_rows
-                out_ref[place : place + keep_rows, columns] = block[k * keep_rows : (k + 1) * keep_rows]
+            for place, k in enumerate(sum(teams(n_modes // keep_rows), [])):
+                rows = slice(place * keep_rows, (place + 1) * keep_rows)
+                out_ref[rows, columns] = block[k * keep_rows : (k + 1) * keep_rows]
 
 
 def turn(modes, keep_rows):
@@ -161,8 +161,13 @@
     )(neighbours, jac_blocks, modes, turned)
 
 
+def chip_order(chips):
+    ring = [0, 2, 3, 1] + list(range(4, chips)) if chips >= 4 else list(range(chips))
+    return ring[::-1]
+
+
 def teams(count):
-    return [[2 * chip + (chip + half) % 2 for chip in reversed(range(count // 2))] for half in range(2)]
+    return [[2 * chip + (chip + half) % 2 for chip in chip_order(count // 2)] for half in range(2)]
 
 
 def own_team():

time: 28 us -> 28 us (level)
  starting transfers between devices: 6.72 us -> 5.88 us
  Pallas kernels: 7.23 us -> 8.05 us
    ppermute x1, starting transfers between devices: 1.83 us -> 0.99 us  [per_device(): got = lax.ppermute(join(True, p, t, outer, inner), 'cell', swap)]
    pallas_call x1, Pallas kernels: 5.46 us -> 6.28 us  [own_part(): pl.pallas_call(functools.partial(own_kernel, blocks), out_shape=(jax.Shap...]
  transfers between devices with their start and end apart: 3 -> 3, of which waited for: 1 -> 1; matrix products, arithmetic and copies ran while one was open for 0% -> 0% of each run, Pallas kernels for 22% -> 25%
where the time goes in v15:
time: 28 us; the launch traced here: 27.8 us
  blocking collectives  11.7 us (42%)
  Pallas kernels  8.05 us (29%)
  starting transfers between devices  5.88 us (21%)
  local copies, waits for them, and re-layouts  1.45 us (5%)
  waiting for transfers between devices  0.63 us (2%)
    all_to_all x1, blocking collectives, per_device(): parts = lax.all_to_all(pair, 'cell', 0, 0, axis_index_groups=teams(count))  11.7 us
    pallas_call x1, Pallas kernels, own_part(): pl.pallas_call(functools.partial(own_kernel, blocks), out_shape=(jax.Shap...  6.28 us
    ppermute x1, starting transfers between devices, per_device(): inner = lax.ppermute(inner_edge(modes, width), 'cell', swap)  4.08 us
    dynamic_slice x1, local copies, waits for them, and re-layouts, per_device(): outer_edge = lax.dynamic_slice_in_dim(modes, core * (rows - width), width)  0.99 us
    ppermute x1, starting transfers between devices, per_device(): got = lax.ppermute(join(True, p, t, outer, inner), 'cell', swap)  0.99 us
    ppermute x1, starting transfers between devices, per_device(): outer = lax.ppermute(gate(outer_edge), 'cell', across)  0.81 us
    pallas_call x2, Pallas kernels, join(): pl.pallas_call(functools.partial(join_kernel, other), out_shape=jax.Shape...  0.7 us
    ppermute x1, waiting for transfers between devices, per_device(): got = lax.ppermute(join(True, p, t, outer, inner), 'cell', swap)  0.63 us
  transfers between devices with their start and end apart: 3, of which 1 were waited for; matrix products, arithmetic and copies ran while one was open for 0% of the time, Pallas kernels for 25%

profile of v15, /device:TPU:0, one launch (start us, length us, event | category | flops | bytes accessed | tf_op | source)
XLA Modules:
  0.0 27.8 jit_solution(3784891896116389070)
XLA Ops:
  0.0 1.0 %constant_dynamic-slice_fusion.block_ref = bf16[640,256]{1,0:T(8,128)(2,1)S(1)} fusion(bf16[2560,256]{1,0:T(8,128)(2,1)} %modes.5, s32[]{:T(128)S(6)} %select_n.3), kind=kLoop, calls=%fused_computation | loop fusion | bytes 655364 | tf_op jit(solution)/shard_map/dynamic_slice | solution.py:233
  1.0 0.0 copy-start
  1.0 0.0 copy-start.1
  1.1 0.8 %collective-permute-start = (bf16[640,256]{1,0:T(8,128)(2,1)S(1)}, bf16[640,256]{1,0:T(8,128)(2,1)S(1)}, u32[]{:S(2)}, u32[]{:S(2)}) collective-permute-start(bf16[640,256]{1,0:T(8,128)(2,1)S(1)} %gate.1), channel_id=1, source_target_pairs={{0,0},{1,2},{2,1},{3,4},{4,3},{5,6},{6,5},{7,8},{8,7},{9,10},{10,9... | collective-permute-start | bytes 983048 | tf_op jit(solution)/shard_map/ppermute | solution.py:234
  1.9 0.4 %copy-done = bf16[2560,256]{1,0:T(8,128)(2,1)S(1)} copy-done((bf16[2560,256]{1,0:T(8,128)(2,1)S(1)}, bf16[2560,256]{1,0:T(8,128)(2,1)}, u32[]{:S(2)}) %copy-start) | copy-done | bytes 1310744
  2.4 0.0 copy-start.2
  2.4 4.1 %collective-permute-start.1 = (bf16[640,256]{1,0:T(8,128)(2,1)S(1)}, bf16[640,256]{1,0:T(8,128)(2,1)S(1)}, u32[]{:S(2)}, u32[]{:S(2)}) collective-permute-start(bf16[640,256]{1,0:T(8,128)(2,1)S(1)} %inner_edge.1), channel_id=1, source_target_pairs={{0,1},{1,0},{2,3},{3,2},{4,5},{5,4},{6,7},{7,6},{8,9},{9,8},{10,11... | collective-permute-start | bytes 983048 | tf_op jit(solution)/shard_map/ppermute | solution.py:235
  6.4 0.4 %turn.1.turned = bf16[256,2560]{1,0:T(8,128)(2,1)S(1)} custom-call(bf16[2560,256]{1,0:T(8,128)(2,1)S(1)} %copy-done), custom_call_target="tpu_custom_call" | custom-call | bytes 2621440 | tf_op jit(solution)/shard_map/turn/pallas_call | solution.py:75
  6.8 0.0 copy-done.1
  6.9 0.0 copy-done.2
  6.9 6.3 %own_part.1 = (f32[256,256]{1,0:T(8,128)S(1)}, bf16[2,2,256,640]{3,2,1,0:T(8,128)(2,1)S(1)}) custom-call(s32[2,14]{1,0:T(2,128)S(1)} %bitcast.2, bf16[14,640,640]{2,1,0:T(8,128)(2,1)S(1)} %copy-done.1, bf16[2560,256]{1,0:T(8,128)(2,1)S(1)} %copy-done, bf16[256,2560]{1,0:T(8,128)(2,1)S(1)} %turn.1.turned), custom_call_target="tpu_custom_call" | custom-call | flops 3607101440 | bytes 12779520 | tf_op jit(solution)/shard_map/own_part/pallas_call | solution.py:138
  13.1 0.0 collective-permute-done.outer_ref
  13.2 0.0 collective-permute-done.1.inner_ref
  13.2 0.4 %join_give.1 = f32[128,256]{1,0:T(8,128)S(1)} custom-call(f32[256,256]{1,0:T(8,128)S(1)} %get-tuple-element.7.p_ref, bf16[2,2,256,640]{3,2,1,0:T(8,128)(2,1)S(1)} %get-tuple-element.8.t_ref, bf16[640,256]{1,0:T(8,128)(2,1)S(1)} %collective-permute-done.outer_ref, bf16[640,256]{1,0:T(8,128)(2,1)S(1)} %collective-permute-done.1.inner_ref), custom_call_target="tpu_custom_call" | custom-call | flops 167772160 | tf_op jit(solution)/shard_map/join_give/pallas_call | solution.py:195
  13.5 1.0 %collective-permute-start.2 = (f32[128,256]{1,0:T(8,128)S(1)}, f32[128,256]{1,0:T(8,128)S(1)}, u32[]{:S(2)}, u32[]{:S(2)}) collective-permute-start(f32[128,256]{1,0:T(8,128)S(1)} %join_give.1), channel_id=1, source_target_pairs={{0,1},{1,0},{2,3},{3,2},{4,5},{5,4},{6,7},{7,6},{8,9},{9,8},{10,11... | collective-permute-start | bytes 393224 | tf_op jit(solution)/shard_map/ppermute | solution.py:242
  14.5 0.4 %join_keep.1 = f32[128,256]{1,0:T(8,128)S(1)} custom-call(f32[256,256]{1,0:T(8,128)S(1)} %get-tuple-element.7.p_ref, bf16[2,2,256,640]{3,2,1,0:T(8,128)(2,1)S(1)} %get-tuple-element.8.t_ref, bf16[640,256]{1,0:T(8,128)(2,1)S(1)} %collective-permute-done.outer_ref, bf16[640,256]{1,0:T(8,128)(2,1)S(1)} %collective-permute-done.1.inner_ref), custom_call_target="tpu_custom_call" | custom-call | flops 167772160 | tf_op jit(solution)/shard_map/join_keep/pallas_call | solution.py:195
  14.9 0.6 %collective-permute-done.2 = f32[128,256]{1,0:T(8,128)S(1)} collective-permute-done((f32[128,256]{1,0:T(8,128)S(1)}, f32[128,256]{1,0:T(8,128)S(1)}, u32[]{:S(2)}, u32[]{:S(2)}) %collective-permute-start.2) | collective-permute-done | bytes 131104 | tf_op jit(solution)/shard_map/ppermute | solution.py:242
  15.5 11.7 %all_to_all.5.parts_ref = f32[8,16,256]{2,1,0:T(8,128)S(1)} all-to-all(f32[8,16,256]{2,1,0:T(8,128)S(1)} %bitcast.3), channel_id=1, replica_groups={{15,12,11,8,3,7,4,0},{14,13,10,9,2,6,5,1},{31,28,27,24,19,23,20,16},{30..., dimensions={0} | all-to-all | bytes 262144 | tf_op jit(solution)/shard_map/all_to_all | solution.py:245
  27.2 0.6 %sum_parts.1 = f32[16,256]{1,0:T(8,128)} custom-call(f32[8,16,256]{2,1,0:T(8,128)S(1)} %all_to_all.5.parts_ref), custom_call_target="tpu_custom_call" | custom-call | tf_op jit(solution)/shard_map/sum_parts/pallas_call | solution.py:214
  (3 shorter events, 0.1 us)
Async XLA Ops:
  1.0 1.3 %copy-start = (bf16[2560,256]{1,0:T(8,128)(2,1)S(1)}, bf16[2560,256]{1,0:T(8,128)(2,1)}, u32[]{:S(2)}) copy-start(bf16[2560,256]{1,0:T(8,128)(2,1)} %modes.5) | copy-start | bytes 3932164
  1.0 5.8 %copy-start.1 = (bf16[14,640,640]{2,1,0:T(8,128)(2,1)S(1)}, bf16[14,640,640]{2,1,0:T(8,128)(2,1)}, u32[]{:S(2)}) copy-start(bf16[14,640,640]{2,1,0:T(8,128)(2,1)} %jac.1) | copy-start | bytes 34406404
  1.1 12.1 %collective-permute-start = (bf16[640,256]{1,0:T(8,128)(2,1)S(1)}, bf16[640,256]{1,0:T(8,128)(2,1)S(1)}, u32[]{:S(2)}, u32[]{:S(2)}) collective-permute-start(bf16[640,256]{1,0:T(8,128)(2,1)S(1)} %gate.1), channel_id=1, source_target_pairs={{0,0},{1,2},{2,1},{3,4},{4,3},{5,6},{6,5},{7,8},{8,7},{9,10},{10,9... | collective-permute-start | bytes 983048 | tf_op jit(solution)/shard_map/ppermute | solution.py:234
  2.4 4.5 %copy-start.2 = (s32[14,2]{0,1:T(2,128)S(1)}, s32[14,2]{0,1:T(2,128)}, u32[]{:S(2)}) copy-start(s32[14,2]{0,1:T(2,128)} %param.5) | copy-start | bytes 340
  2.4 10.8 %collective-permute-start.1 = (bf16[640,256]{1,0:T(8,128)(2,1)S(1)}, bf16[640,256]{1,0:T(8,128)(2,1)S(1)}, u32[]{:S(2)}, u32[]{:S(2)}) collective-permute-start(bf16[640,256]{1,0:T(8,128)(2,1)S(1)} %inner_edge.1), channel_id=1, source_target_pairs={{0,1},{1,0},{2,3},{3,2},{4,5},{5,4},{6,7},{7,6},{8,9},{9,8},{10,11... | collective-permute-start | bytes 983048 | tf_op jit(solution)/shard_map/ppermute | solution.py:235
  13.5 2.0 %collective-permute-start.2 = (f32[128,256]{1,0:T(8,128)S(1)}, f32[128,256]{1,0:T(8,128)S(1)}, u32[]{:S(2)}, u32[]{:S(2)}) collective-permute-start(f32[128,256]{1,0:T(8,128)S(1)} %join_give.1), channel_id=1, source_target_pairs={{0,1},{1,0},{2,3},{3,2},{4,5},{5,4},{6,7},{7,6},{8,9},{9,8},{10,11... | collective-permute-start | bytes 393224 | tf_op jit(solution)/shard_map/ppermute | solution.py:242

commit v16 on v15

--- a/solution.py
+++ b/solution.py
@@ -162,8 +162,8 @@
 
 
 def chip_order(chips):
-    ring = [0, 2, 3, 1] + list(range(4, chips)) if chips >= 4 else list(range(chips))
-    return ring[::-1]
+    far = 5 * chips // 8
+    return ([0, far] + [chip for chip in range(1, chips) if chip != far] if far else [0])[::-1]
 
 
 def teams(count):

time: 28 us -> 27.8 us (level)
  Pallas kernels: 8.05 us -> 7.23 us
  starting transfers between devices: 5.88 us -> 6.43 us
    pallas_call x1, Pallas kernels: 6.28 us -> 5.46 us  [own_part(): pl.pallas_call(functools.partial(own_kernel, blocks), out_shape=(jax.Shap...]
    ppermute x1, starting transfers between devices: 0.99 us -> 1.54 us  [per_device(): got = lax.ppermute(join(True, p, t, outer, inner), 'cell', swap)]
  transfers between devices with their start and end apart: 3 -> 3, of which waited for: 1 -> 1; matrix products, arithmetic and copies ran while one was open for 0% -> 0% of each run, Pallas kernels for 25% -> 22%
where the time goes in v16:
time: 27.8 us
  blocking collectives  11.9 us (43%)
  Pallas kernels  7.23 us (26%)
  starting transfers between devices  6.43 us (23%)
  local copies, waits for them, and re-layouts  1.45 us (5%)
  waiting for transfers between devices  0.63 us (2%)
    all_to_all x1, blocking collectives, per_device(): parts = lax.all_to_all(pair, 'cell', 0, 0, axis_index_groups=teams(count))  11.9 us
    pallas_call x1, Pallas kernels, own_part(): pl.pallas_call(functools.partial(own_kernel, blocks), out_shape=(jax.Shap...  5.46 us
    ppermute x1, starting transfers between devices, per_device(): inner = lax.ppermute(inner_edge(modes, width), 'cell', swap)  4.08 us
    ppermute x1, starting transfers between devices, per_device(): got = lax.ppermute(join(True, p, t, outer, inner), 'cell', swap)  1.54 us
    dynamic_slice x1, local copies, waits for them, and re-layouts, per_device(): outer_edge = lax.dynamic_slice_in_dim(modes, core * (rows - width), width)  0.99 us
    ppermute x1, starting transfers between devices, per_device(): outer = lax.ppermute(gate(outer_edge), 'cell', across)  0.81 us
    pallas_call x2, Pallas kernels, join(): pl.pallas_call(functools.partial(join_kernel, other), out_shape=jax.Shape...  0.7 us
    ppermute x1, waiting for transfers between devices, per_device(): got = lax.ppermute(join(True, p, t, outer, inner), 'cell', swap)  0.63 us
  transfers between devices with their start and end apart: 3, of which 1 were waited for; matrix products, arithmetic and copies ran while one was open for 0% of the time, Pallas kernels for 22%

profile of v16, /device:TPU:0, one launch (start us, length us, event | category | flops | bytes accessed | tf_op | source)
XLA Modules:
  0.0 27.8 jit_solution(7230344834038499673)
XLA Ops:
  0.0 1.0 %constant_dynamic-slice_fusion.block_ref = bf16[640,256]{1,0:T(8,128)(2,1)S(1)} fusion(bf16[2560,256]{1,0:T(8,128)(2,1)} %modes.5, s32[]{:T(128)S(6)} %select_n.3), kind=kLoop, calls=%fused_computation | loop fusion | bytes 655364 | tf_op jit(solution)/shard_map/dynamic_slice | solution.py:233
  1.0 0.0 copy-start
  1.0 0.0 copy-start.1
  1.1 0.8 %collective-permute-start = (bf16[640,256]{1,0:T(8,128)(2,1)S(1)}, bf16[640,256]{1,0:T(8,128)(2,1)S(1)}, u32[]{:S(2)}, u32[]{:S(2)}) collective-permute-start(bf16[640,256]{1,0:T(8,128)(2,1)S(1)} %gate.1), channel_id=1, source_target_pairs={{0,0},{1,2},{2,1},{3,4},{4,3},{5,6},{6,5},{7,8},{8,7},{9,10},{10,9... | collective-permute-start | bytes 983048 | tf_op jit(solution)/shard_map/ppermute | solution.py:234
  1.9 0.4 %copy-done = bf16[2560,256]{1,0:T(8,128)(2,1)S(1)} copy-done((bf16[2560,256]{1,0:T(8,128)(2,1)S(1)}, bf16[2560,256]{1,0:T(8,128)(2,1)}, u32[]{:S(2)}) %copy-start) | copy-done | bytes 1310744
  2.4 0.0 copy-start.2
  2.4 4.1 %collective-permute-start.1 = (bf16[640,256]{1,0:T(8,128)(2,1)S(1)}, bf16[640,256]{1,0:T(8,128)(2,1)S(1)}, u32[]{:S(2)}, u32[]{:S(2)}) collective-permute-start(bf16[640,256]{1,0:T(8,128)(2,1)S(1)} %inner_edge.1), channel_id=1, source_target_pairs={{0,1},{1,0},{2,3},{3,2},{4,5},{5,4},{6,7},{7,6},{8,9},{9,8},{10,11... | collective-permute-start | bytes 983048 | tf_op jit(solution)/shard_map/ppermute | solution.py:235
  6.4 0.4 %turn.1.turned = bf16[256,2560]{1,0:T(8,128)(2,1)S(1)} custom-call(bf16[2560,256]{1,0:T(8,128)(2,1)S(1)} %copy-done), custom_call_target="tpu_custom_call" | custom-call | bytes 2621440 | tf_op jit(solution)/shard_map/turn/pallas_call | solution.py:75
  6.8 0.0 copy-done.1
  6.9 0.0 copy-done.2
  6.9 5.5 %own_part.1 = (f32[256,256]{1,0:T(8,128)S(1)}, bf16[2,2,256,640]{3,2,1,0:T(8,128)(2,1)S(1)}) custom-call(s32[2,14]{1,0:T(2,128)S(1)} %bitcast.2, bf16[14,640,640]{2,1,0:T(8,128)(2,1)S(1)} %copy-done.1, bf16[2560,256]{1,0:T(8,128)(2,1)S(1)} %copy-done, bf16[256,2560]{1,0:T(8,128)(2,1)S(1)} %turn.1.turned), custom_call_target="tpu_custom_call" | custom-call | flops 3607101440 | bytes 12779520 | tf_op jit(solution)/shard_map/own_part/pallas_call | solution.py:138
  12.3 0.0 collective-permute-done.outer_ref
  12.3 0.0 collective-permute-done.1.inner_ref
  12.4 0.4 %join_give.1 = f32[128,256]{1,0:T(8,128)S(1)} custom-call(f32[256,256]{1,0:T(8,128)S(1)} %get-tuple-element.7.p_ref, bf16[2,2,256,640]{3,2,1,0:T(8,128)(2,1)S(1)} %get-tuple-element.8.t_ref, bf16[640,256]{1,0:T(8,128)(2,1)S(1)} %collective-permute-done.outer_ref, bf16[640,256]{1,0:T(8,128)(2,1)S(1)} %collective-permute-done.1.inner_ref), custom_call_target="tpu_custom_call" | custom-call | flops 167772160 | tf_op jit(solution)/shard_map/join_give/pallas_call | solution.py:195
  12.7 1.5 %collective-permute-start.2 = (f32[128,256]{1,0:T(8,128)S(1)}, f32[128,256]{1,0:T(8,128)S(1)}, u32[]{:S(2)}, u32[]{:S(2)}) collective-permute-start(f32[128,256]{1,0:T(8,128)S(1)} %join_give.1), channel_id=1, source_target_pairs={{0,1},{1,0},{2,3},{3,2},{4,5},{5,4},{6,7},{7,6},{8,9},{9,8},{10,11... | collective-permute-start | bytes 393224 | tf_op jit(solution)/shard_map/ppermute | solution.py:242
  14.3 0.4 %join_keep.1 = f32[128,256]{1,0:T(8,128)S(1)} custom-call(f32[256,256]{1,0:T(8,128)S(1)} %get-tuple-element.7.p_ref, bf16[2,2,256,640]{3,2,1,0:T(8,128)(2,1)S(1)} %get-tuple-element.8.t_ref, bf16[640,256]{1,0:T(8,128)(2,1)S(1)} %collective-permute-done.outer_ref, bf16[640,256]{1,0:T(8,128)(2,1)S(1)} %collective-permute-done.1.inner_ref), custom_call_target="tpu_custom_call" | custom-call | flops 167772160 | tf_op jit(solution)/shard_map/join_keep/pallas_call | solution.py:195
  14.6 0.6 %collective-permute-done.2 = f32[128,256]{1,0:T(8,128)S(1)} collective-permute-done((f32[128,256]{1,0:T(8,128)S(1)}, f32[128,256]{1,0:T(8,128)S(1)}, u32[]{:S(2)}, u32[]{:S(2)}) %collective-permute-start.2) | collective-permute-done | bytes 131104 | tf_op jit(solution)/shard_map/ppermute | solution.py:242
  15.3 11.9 %all_to_all.5.parts_ref = f32[8,16,256]{2,1,0:T(8,128)S(1)} all-to-all(f32[8,16,256]{2,1,0:T(8,128)S(1)} %bitcast.3), channel_id=1, replica_groups={{15,12,8,7,4,3,11,0},{14,13,9,6,5,2,10,1},{31,28,24,23,20,19,27,16},{30..., dimensions={0} | all-to-all | bytes 262144 | tf_op jit(solution)/shard_map/all_to_all | solution.py:245
  27.1 0.6 %sum_parts.1 = f32[16,256]{1,0:T(8,128)} custom-call(f32[8,16,256]{2,1,0:T(8,128)S(1)} %all_to_all.5.parts_ref), custom_call_target="tpu_custom_call" | custom-call | tf_op jit(solution)/shard_map/sum_parts/pallas_call | solution.py:214
  (3 shorter events, 0.1 us)
Async XLA Ops:
  1.0 1.3 %copy-start = (bf16[2560,256]{1,0:T(8,128)(2,1)S(1)}, bf16[2560,256]{1,0:T(8,128)(2,1)}, u32[]{:S(2)}) copy-start(bf16[2560,256]{1,0:T(8,128)(2,1)} %modes.5) | copy-start | bytes 3932164
  1.0 5.8 %copy-start.1 = (bf16[14,640,640]{2,1,0:T(8,128)(2,1)S(1)}, bf16[14,640,640]{2,1,0:T(8,128)(2,1)}, u32[]{:S(2)}) copy-start(bf16[14,640,640]{2,1,0:T(8,128)(2,1)} %jac.1) | copy-start | bytes 34406404
  1.1 11.3 %collective-permute-start = (bf16[640,256]{1,0:T(8,128)(2,1)S(1)}, bf16[640,256]{1,0:T(8,128)(2,1)S(1)}, u32[]{:S(2)}, u32[]{:S(2)}) collective-permute-start(bf16[640,256]{1,0:T(8,128)(2,1)S(1)} %gate.1), channel_id=1, source_target_pairs={{0,0},{1,2},{2,1},{3,4},{4,3},{5,6},{6,5},{7,8},{8,7},{9,10},{10,9... | collective-permute-start | bytes 983048 | tf_op jit(solution)/shard_map/ppermute | solution.py:234
  2.4 4.5 %copy-start.2 = (s32[14,2]{0,1:T(2,128)S(1)}, s32[14,2]{0,1:T(2,128)}, u32[]{:S(2)}) copy-start(s32[14,2]{0,1:T(2,128)} %param.5) | copy-start | bytes 340
  2.4 10.0 %collective-permute-start.1 = (bf16[640,256]{1,0:T(8,128)(2,1)S(1)}, bf16[640,256]{1,0:T(8,128)(2,1)S(1)}, u32[]{:S(2)}, u32[]{:S(2)}) collective-permute-start(bf16[640,256]{1,0:T(8,128)(2,1)S(1)} %inner_edge.1), channel_id=1, source_target_pairs={{0,1},{1,0},{2,3},{3,2},{4,5},{5,4},{6,7},{7,6},{8,9},{9,8},{10,11... | collective-permute-start | bytes 983048 | tf_op jit(solution)/shard_map/ppermute | solution.py:235
  12.7 2.5 %collective-permute-start.2 = (f32[128,256]{1,0:T(8,128)S(1)}, f32[128,256]{1,0:T(8,128)S(1)}, u32[]{:S(2)}, u32[]{:S(2)}) collective-permute-start(f32[128,256]{1,0:T(8,128)S(1)} %join_give.1), channel_id=1, source_target_pairs={{0,1},{1,0},{2,3},{3,2},{4,5},{5,4},{6,7},{7,6},{8,9},{9,8},{10,11... | collective-permute-start | bytes 393224 | tf_op jit(solution)/shard_map/ppermute | solution.py:242

commit v17 on v16

--- a/solution.py
+++ b/solution.py
@@ -161,13 +161,11 @@
     )(neighbours, jac_blocks, modes, turned)
 
 
-def chip_order(chips):
-    far = 5 * chips // 8
-    return ([0, far] + [chip for chip in range(1, chips) if chip != far] if far else [0])[::-1]
-
-
 def teams(count):
-    return [[2 * chip + (chip + half) % 2 for chip in chip_order(count // 2)] for half in range(2)]
+    chips = list(range(count // 2))
+    mid = count // 4
+    rings = [chips, [mid] + chips[:mid] + chips[mid + 1 :]]
+    return [[2 * chip + (chip + half) % 2 for chip in reversed(rings[half])] for half in range(2)]
 
 
 def own_team():

time: 27.8 us -> 28.1 us (1.011)
  starting transfers between devices: 6.43 us -> 8.02 us
  Pallas kernels: 7.23 us -> 5.65 us
  blocking collectives: 11.9 us -> 12.2 us
    ppermute x1, starting transfers between devices: 1.54 us -> 3.12 us  [per_device(): got = lax.ppermute(join(True, p, t, outer, inner), 'cell', swap)]
    pallas_call x1, Pallas kernels: 5.46 us -> 3.88 us  [own_part(): pl.pallas_call(functools.partial(own_kernel, blocks), out_shape=(jax.Shap...]
    all_to_all x1, blocking collectives: 11.9 us -> 12.2 us  [per_device(): parts = lax.all_to_all(pair, 'cell', 0, 0, axis_index_groups=teams(count))]
  transfers between devices with their start and end apart: 3 -> 3, of which waited for: 1 -> 1; matrix products, arithmetic and copies ran while one was open for 0% -> 0% of each run, Pallas kernels for 22% -> 17%
where the time goes in v17:
time: 28.1 us
  blocking collectives  12.2 us (43%)
  starting transfers between devices  8.02 us (29%)
  Pallas kernels  5.65 us (20%)
  local copies, waits for them, and re-layouts  1.45 us (5%)
  waiting for transfers between devices  0.63 us (2%)
    all_to_all x1, blocking collectives, per_device(): parts = lax.all_to_all(pair, 'cell', 0, 0, axis_index_groups=teams(count))  12.2 us
    ppermute x1, starting transfers between devices, per_device(): inner = lax.ppermute(inner_edge(modes, width), 'cell', swap)  4.08 us
    pallas_call x1, Pallas kernels, own_part(): pl.pallas_call(functools.partial(own_kernel, blocks), out_shape=(jax.Shap...  3.88 us
    ppermute x1, starting transfers between devices, per_device(): got = lax.ppermute(join(True, p, t, outer, inner), 'cell', swap)  3.12 us
    dynamic_slice x1, local copies, waits for them, and re-layouts, per_device(): outer_edge = lax.dynamic_slice_in_dim(modes, core * (rows - width), width)  0.99 us
    ppermute x1, starting transfers between devices, per_device(): outer = lax.ppermute(gate(outer_edge), 'cell', across)  0.81 us
    pallas_call x2, Pallas kernels, join(): pl.pallas_call(functools.partial(join_kernel, other), out_shape=jax.Shape...  0.7 us
    ppermute x1, waiting for transfers between devices, per_device(): got = lax.ppermute(join(True, p, t, outer, inner), 'cell', swap)  0.63 us
  transfers between devices with their start and end apart: 3, of which 1 were waited for; matrix products, arithmetic and copies ran while one was open for 0% of the time, Pallas kernels for 17%

profile of v17, /device:TPU:0, one launch (start us, length us, event | category | flops | bytes accessed | tf_op | source)
XLA Modules:
  0.0 28.1 jit_solution(11266191497285769911)
XLA Ops:
  0.0 1.0 %constant_dynamic-slice_fusion.block_ref = bf16[640,256]{1,0:T(8,128)(2,1)S(1)} fusion(bf16[2560,256]{1,0:T(8,128)(2,1)} %modes.5, s32[]{:T(128)S(6)} %select_n.3), kind=kLoop, calls=%fused_computation | loop fusion | bytes 655364 | tf_op jit(solution)/shard_map/dynamic_slice | solution.py:231
  1.0 0.0 copy-start
  1.0 0.0 copy-start.1
  1.1 0.8 %collective-permute-start = (bf16[640,256]{1,0:T(8,128)(2,1)S(1)}, bf16[640,256]{1,0:T(8,128)(2,1)S(1)}, u32[]{:S(2)}, u32[]{:S(2)}) collective-permute-start(bf16[640,256]{1,0:T(8,128)(2,1)S(1)} %gate.1), channel_id=1, source_target_pairs={{0,0},{1,2},{2,1},{3,4},{4,3},{5,6},{6,5},{7,8},{8,7},{9,10},{10,9... | collective-permute-start | bytes 983048 | tf_op jit(solution)/shard_map/ppermute | solution.py:232
  1.9 0.4 %copy-done = bf16[2560,256]{1,0:T(8,128)(2,1)S(1)} copy-done((bf16[2560,256]{1,0:T(8,128)(2,1)S(1)}, bf16[2560,256]{1,0:T(8,128)(2,1)}, u32[]{:S(2)}) %copy-start) | copy-done | bytes 1310744
  2.4 0.0 copy-start.2
  2.4 4.1 %collective-permute-start.1 = (bf16[640,256]{1,0:T(8,128)(2,1)S(1)}, bf16[640,256]{1,0:T(8,128)(2,1)S(1)}, u32[]{:S(2)}, u32[]{:S(2)}) collective-permute-start(bf16[640,256]{1,0:T(8,128)(2,1)S(1)} %inner_edge.1), channel_id=1, source_target_pairs={{0,1},{1,0},{2,3},{3,2},{4,5},{5,4},{6,7},{7,6},{8,9},{9,8},{10,11... | collective-permute-start | bytes 983048 | tf_op jit(solution)/shard_map/ppermute | solution.py:233
  6.4 0.4 %turn.1.turned = bf16[256,2560]{1,0:T(8,128)(2,1)S(1)} custom-call(bf16[2560,256]{1,0:T(8,128)(2,1)S(1)} %copy-done), custom_call_target="tpu_custom_call" | custom-call | bytes 2621440 | tf_op jit(solution)/shard_map/turn/pallas_call | solution.py:75
  6.8 0.0 copy-done.1
  6.9 0.0 copy-done.2
  6.9 3.9 %own_part.1 = (f32[256,256]{1,0:T(8,128)S(1)}, bf16[2,2,256,640]{3,2,1,0:T(8,128)(2,1)S(1)}) custom-call(s32[2,14]{1,0:T(2,128)S(1)} %bitcast.2, bf16[14,640,640]{2,1,0:T(8,128)(2,1)S(1)} %copy-done.1, bf16[2560,256]{1,0:T(8,128)(2,1)S(1)} %copy-done, bf16[256,2560]{1,0:T(8,128)(2,1)S(1)} %turn.1.turned), custom_call_target="tpu_custom_call" | custom-call | flops 3607101440 | bytes 12779520 | tf_op jit(solution)/shard_map/own_part/pallas_call | solution.py:138
  10.7 0.0 collective-permute-done.outer_ref
  10.8 0.0 collective-permute-done.1.inner_ref
  10.8 0.3 %join_give.1 = f32[128,256]{1,0:T(8,128)S(1)} custom-call(f32[256,256]{1,0:T(8,128)S(1)} %get-tuple-element.7.p_ref, bf16[2,2,256,640]{3,2,1,0:T(8,128)(2,1)S(1)} %get-tuple-element.8.t_ref, bf16[640,256]{1,0:T(8,128)(2,1)S(1)} %collective-permute-done.outer_ref, bf16[640,256]{1,0:T(8,128)(2,1)S(1)} %collective-permute-done.1.inner_ref), custom_call_target="tpu_custom_call" | custom-call | flops 167772160 | tf_op jit(solution)/shard_map/join_give/pallas_call | solution.py:193
  11.1 3.1 %collective-permute-start.2 = (f32[128,256]{1,0:T(8,128)S(1)}, f32[128,256]{1,0:T(8,128)S(1)}, u32[]{:S(2)}, u32[]{:S(2)}) collective-permute-start(f32[128,256]{1,0:T(8,128)S(1)} %join_give.1), channel_id=1, source_target_pairs={{0,1},{1,0},{2,3},{3,2},{4,5},{5,4},{6,7},{7,6},{8,9},{9,8},{10,11... | collective-permute-start | bytes 393224 | tf_op jit(solution)/shard_map/ppermute | solution.py:240
  14.3 0.4 %join_keep.1 = f32[128,256]{1,0:T(8,128)S(1)} custom-call(f32[256,256]{1,0:T(8,128)S(1)} %get-tuple-element.7.p_ref, bf16[2,2,256,640]{3,2,1,0:T(8,128)(2,1)S(1)} %get-tuple-element.8.t_ref, bf16[640,256]{1,0:T(8,128)(2,1)S(1)} %collective-permute-done.outer_ref, bf16[640,256]{1,0:T(8,128)(2,1)S(1)} %collective-permute-done.1.inner_ref), custom_call_target="tpu_custom_call" | custom-call | flops 167772160 | tf_op jit(solution)/shard_map/join_keep/pallas_call | solution.py:193
  14.6 0.6 %collective-permute-done.2 = f32[128,256]{1,0:T(8,128)S(1)} collective-permute-done((f32[128,256]{1,0:T(8,128)S(1)}, f32[128,256]{1,0:T(8,128)S(1)}, u32[]{:S(2)}, u32[]{:S(2)}) %collective-permute-start.2) | collective-permute-done | bytes 131104 | tf_op jit(solution)/shard_map/ppermute | solution.py:240
  15.3 12.2 %all_to_all.5.parts_ref = f32[8,16,256]{2,1,0:T(8,128)S(1)} all-to-all(f32[8,16,256]{2,1,0:T(8,128)S(1)} %bitcast.3), channel_id=1, replica_groups={{15,12,11,8,7,4,3,0},{14,13,10,6,5,2,1,9},{31,28,27,24,23,20,19,16},{30..., dimensions={0} | all-to-all | bytes 262144 | tf_op jit(solution)/shard_map/all_to_all | solution.py:243
  27.4 0.6 %sum_parts.1 = f32[16,256]{1,0:T(8,128)} custom-call(f32[8,16,256]{2,1,0:T(8,128)S(1)} %all_to_all.5.parts_ref), custom_call_target="tpu_custom_call" | custom-call | tf_op jit(solution)/shard_map/sum_parts/pallas_call | solution.py:212
  (3 shorter events, 0.1 us)
Async XLA Ops:
  1.0 1.3 %copy-start = (bf16[2560,256]{1,0:T(8,128)(2,1)S(1)}, bf16[2560,256]{1,0:T(8,128)(2,1)}, u32[]{:S(2)}) copy-start(bf16[2560,256]{1,0:T(8,128)(2,1)} %modes.5) | copy-start | bytes 3932164
  1.0 5.8 %copy-start.1 = (bf16[14,640,640]{2,1,0:T(8,128)(2,1)S(1)}, bf16[14,640,640]{2,1,0:T(8,128)(2,1)}, u32[]{:S(2)}) copy-start(bf16[14,640,640]{2,1,0:T(8,128)(2,1)} %jac.1) | copy-start | bytes 34406404
  1.1 9.7 %collective-permute-start = (bf16[640,256]{1,0:T(8,128)(2,1)S(1)}, bf16[640,256]{1,0:T(8,128)(2,1)S(1)}, u32[]{:S(2)}, u32[]{:S(2)}) collective-permute-start(bf16[640,256]{1,0:T(8,128)(2,1)S(1)} %gate.1), channel_id=1, source_target_pairs={{0,0},{1,2},{2,1},{3,4},{4,3},{5,6},{6,5},{7,8},{8,7},{9,10},{10,9... | collective-permute-start | bytes 983048 | tf_op jit(solution)/shard_map/ppermute | solution.py:232
  2.4 4.5 %copy-start.2 = (s32[14,2]{0,1:T(2,128)S(1)}, s32[14,2]{0,1:T(2,128)}, u32[]{:S(2)}) copy-start(s32[14,2]{0,1:T(2,128)} %param.5) | copy-start | bytes 340
  2.4 8.4 %collective-permute-start.1 = (bf16[640,256]{1,0:T(8,128)(2,1)S(1)}, bf16[640,256]{1,0:T(8,128)(2,1)S(1)}, u32[]{:S(2)}, u32[]{:S(2)}) collective-permute-start(bf16[640,256]{1,0:T(8,128)(2,1)S(1)} %inner_edge.1), channel_id=1, source_target_pairs={{0,1},{1,0},{2,3},{3,2},{4,5},{5,4},{6,7},{7,6},{8,9},{9,8},{10,11... | collective-permute-start | bytes 983048 | tf_op jit(solution)/shard_map/ppermute | solution.py:233
  11.1 4.1 %collective-permute-start.2 = (f32[128,256]{1,0:T(8,128)S(1)}, f32[128,256]{1,0:T(8,128)S(1)}, u32[]{:S(2)}, u32[]{:S(2)}) collective-permute-start(f32[128,256]{1,0:T(8,128)S(1)} %join_give.1), channel_id=1, source_target_pairs={{0,1},{1,0},{2,3},{3,2},{4,5},{5,4},{6,7},{7,6},{8,9},{9,8},{10,11... | collective-permute-start | bytes 393224 | tf_op jit(solution)/shard_map/ppermute | solution.py:240

commit v18 on v17

--- a/solution.py
+++ b/solution.py
@@ -162,9 +162,10 @@
 
 
 def teams(count):
-    chips = list(range(count // 2))
-    mid = count // 4
-    rings = [chips, [mid] + chips[:mid] + chips[mid + 1 :]]
+    chips = range(count // 2)
+    middle = [chip for chip in (count // 4, count // 4 + 1) if 0 < chip < count // 2]
+    rest = [chip for chip in chips if chip not in middle]
+    rings = [middle[::-1] + rest, middle + rest]
     return [[2 * chip + (chip + half) % 2 for chip in reversed(rings[half])] for half in range(2)]
 
 

time: 28.1 us -> 27.3 us (0.972)
  starting transfers between devices: 8.02 us -> 6.41 us
  Pallas kernels: 5.65 us -> 7.25 us
  blocking collectives: 12.2 us -> 11.3 us
    ppermute x1, starting transfers between devices: 3.12 us -> 1.52 us  [per_device(): got = lax.ppermute(join(True, p, t, outer, inner), 'cell', swap)]
    pallas_call x1, Pallas kernels: 3.88 us -> 5.48 us  [own_part(): pl.pallas_call(functools.partial(own_kernel, blocks), out_shape=(jax.Shap...]
    all_to_all x1, blocking collectives: 12.2 us -> 11.3 us  [per_device(): parts = lax.all_to_all(pair, 'cell', 0, 0, axis_index_groups=teams(count))]
  transfers between devices with their start and end apart: 3 -> 3, of which waited for: 1 -> 1; matrix products, arithmetic and copies ran while one was open for 0% -> 0% of each run, Pallas kernels for 17% -> 23%
where the time goes in v18:
time: 27.3 us; the launch traced here: 27.1 us
  blocking collectives  11.3 us (41%)
  Pallas kernels  7.25 us (27%)
  starting transfers between devices  6.41 us (23%)
  local copies, waits for them, and re-layouts  1.45 us (5%)
  waiting for transfers between devices  0.63 us (2%)
    all_to_all x1, blocking collectives, per_device(): parts = lax.all_to_all(pair, 'cell', 0, 0, axis_index_groups=teams(count))  11.3 us
    pallas_call x1, Pallas kernels, own_part(): pl.pallas_call(functools.partial(own_kernel, blocks), out_shape=(jax.Shap...  5.48 us
    ppermute x1, starting transfers between devices, per_device(): inner = lax.ppermute(inner_edge(modes, width), 'cell', swap)  4.08 us
    ppermute x1, starting transfers between devices, per_device(): got = lax.ppermute(join(True, p, t, outer, inner), 'cell', swap)  1.52 us
    dynamic_slice x1, local copies, waits for them, and re-layouts, per_device(): outer_edge = lax.dynamic_slice_in_dim(modes, core * (rows - width), width)  0.99 us
    ppermute x1, starting transfers between devices, per_device(): outer = lax.ppermute(gate(outer_edge), 'cell', across)  0.81 us
    pallas_call x2, Pallas kernels, join(): pl.pallas_call(functools.partial(join_kernel, other), out_shape=jax.Shape...  0.7 us
    ppermute x1, waiting for transfers between devices, per_device(): got = lax.ppermute(join(True, p, t, outer, inner), 'cell', swap)  0.63 us
  transfers between devices with their start and end apart: 3, of which 1 were waited for; matrix products, arithmetic and copies ran while one was open for 0% of the time, Pallas kernels for 23%

profile of v18, /device:TPU:0, one launch (start us, length us, event | category | flops | bytes accessed | tf_op | source)
XLA Modules:
  0.0 27.1 jit_solution(15291301222874757688)
XLA Ops:
  0.0 1.0 %constant_dynamic-slice_fusion.block_ref = bf16[640,256]{1,0:T(8,128)(2,1)S(1)} fusion(bf16[2560,256]{1,0:T(8,128)(2,1)} %modes.5, s32[]{:T(128)S(6)} %select_n.3), kind=kLoop, calls=%fused_computation | loop fusion | bytes 655364 | tf_op jit(solution)/shard_map/dynamic_slice | solution.py:232
  1.0 0.0 copy-start
  1.0 0.0 copy-start.1
  1.1 0.8 %collective-permute-start = (bf16[640,256]{1,0:T(8,128)(2,1)S(1)}, bf16[640,256]{1,0:T(8,128)(2,1)S(1)}, u32[]{:S(2)}, u32[]{:S(2)}) collective-permute-start(bf16[640,256]{1,0:T(8,128)(2,1)S(1)} %gate.1), channel_id=1, source_target_pairs={{0,0},{1,2},{2,1},{3,4},{4,3},{5,6},{6,5},{7,8},{8,7},{9,10},{10,9... | collective-permute-start | bytes 983048 | tf_op jit(solution)/shard_map/ppermute | solution.py:233
  1.9 0.4 %copy-done = bf16[2560,256]{1,0:T(8,128)(2,1)S(1)} copy-done((bf16[2560,256]{1,0:T(8,128)(2,1)S(1)}, bf16[2560,256]{1,0:T(8,128)(2,1)}, u32[]{:S(2)}) %copy-start) | copy-done | bytes 1310744
  2.4 0.0 copy-start.2
  2.4 4.1 %collective-permute-start.1 = (bf16[640,256]{1,0:T(8,128)(2,1)S(1)}, bf16[640,256]{1,0:T(8,128)(2,1)S(1)}, u32[]{:S(2)}, u32[]{:S(2)}) collective-permute-start(bf16[640,256]{1,0:T(8,128)(2,1)S(1)} %inner_edge.1), channel_id=1, source_target_pairs={{0,1},{1,0},{2,3},{3,2},{4,5},{5,4},{6,7},{7,6},{8,9},{9,8},{10,11... | collective-permute-start | bytes 983048 | tf_op jit(solution)/shard_map/ppermute | solution.py:234
  6.4 0.4 %turn.1.turned = bf16[256,2560]{1,0:T(8,128)(2,1)S(1)} custom-call(bf16[2560,256]{1,0:T(8,128)(2,1)S(1)} %copy-done), custom_call_target="tpu_custom_call" | custom-call | bytes 2621440 | tf_op jit(solution)/shard_map/turn/pallas_call | solution.py:75
  6.8 0.0 copy-done.1
  6.9 0.0 copy-done.2
  6.9 5.5 %own_part.1 = (f32[256,256]{1,0:T(8,128)S(1)}, bf16[2,2,256,640]{3,2,1,0:T(8,128)(2,1)S(1)}) custom-call(s32[2,14]{1,0:T(2,128)S(1)} %bitcast.2, bf16[14,640,640]{2,1,0:T(8,128)(2,1)S(1)} %copy-done.1, bf16[2560,256]{1,0:T(8,128)(2,1)S(1)} %copy-done, bf16[256,2560]{1,0:T(8,128)(2,1)S(1)} %turn.1.turned), custom_call_target="tpu_custom_call" | custom-call | flops 3607101440 | bytes 12779520 | tf_op jit(solution)/shard_map/own_part/pallas_call | solution.py:138
  12.3 0.0 collective-permute-done.outer_ref
  12.4 0.0 collective-permute-done.1.inner_ref
  12.4 0.4 %join_give.1 = f32[128,256]{1,0:T(8,128)S(1)} custom-call(f32[256,256]{1,0:T(8,128)S(1)} %get-tuple-element.7.p_ref, bf16[2,2,256,640]{3,2,1,0:T(8,128)(2,1)S(1)} %get-tuple-element.8.t_ref, bf16[640,256]{1,0:T(8,128)(2,1)S(1)} %collective-permute-done.outer_ref, bf16[640,256]{1,0:T(8,128)(2,1)S(1)} %collective-permute-done.1.inner_ref), custom_call_target="tpu_custom_call" | custom-call | flops 167772160 | tf_op jit(solution)/shard_map/join_give/pallas_call | solution.py:194
  12.7 1.5 %collective-permute-start.2 = (f32[128,256]{1,0:T(8,128)S(1)}, f32[128,256]{1,0:T(8,128)S(1)}, u32[]{:S(2)}, u32[]{:S(2)}) collective-permute-start(f32[128,256]{1,0:T(8,128)S(1)} %join_give.1), channel_id=1, source_target_pairs={{0,1},{1,0},{2,3},{3,2},{4,5},{5,4},{6,7},{7,6},{8,9},{9,8},{10,11... | collective-permute-start | bytes 393224 | tf_op jit(solution)/shard_map/ppermute | solution.py:241
  14.3 0.4 %join_keep.1 = f32[128,256]{1,0:T(8,128)S(1)} custom-call(f32[256,256]{1,0:T(8,128)S(1)} %get-tuple-element.7.p_ref, bf16[2,2,256,640]{3,2,1,0:T(8,128)(2,1)S(1)} %get-tuple-element.8.t_ref, bf16[640,256]{1,0:T(8,128)(2,1)S(1)} %collective-permute-done.outer_ref, bf16[640,256]{1,0:T(8,128)(2,1)S(1)} %collective-permute-done.1.inner_ref), custom_call_target="tpu_custom_call" | custom-call | flops 167772160 | tf_op jit(solution)/shard_map/join_keep/pallas_call | solution.py:194
  14.6 0.6 %collective-permute-done.2 = f32[128,256]{1,0:T(8,128)S(1)} collective-permute-done((f32[128,256]{1,0:T(8,128)S(1)}, f32[128,256]{1,0:T(8,128)S(1)}, u32[]{:S(2)}, u32[]{:S(2)}) %collective-permute-start.2) | collective-permute-done | bytes 131104 | tf_op jit(solution)/shard_map/ppermute | solution.py:241
  15.3 11.3 %all_to_all.5.parts_ref = f32[8,16,256]{2,1,0:T(8,128)S(1)} all-to-all(f32[8,16,256]{2,1,0:T(8,128)S(1)} %bitcast.3), channel_id=1, replica_groups={{15,12,7,4,3,0,8,11},{14,13,6,5,2,1,10,9},{31,28,23,20,19,16,24,27},{30..., dimensions={0} | all-to-all | bytes 262144 | tf_op jit(solution)/shard_map/all_to_all | solution.py:244
  26.5 0.6 %sum_parts.1 = f32[16,256]{1,0:T(8,128)} custom-call(f32[8,16,256]{2,1,0:T(8,128)S(1)} %all_to_all.5.parts_ref), custom_call_target="tpu_custom_call" | custom-call | tf_op jit(solution)/shard_map/sum_parts/pallas_call | solution.py:213
  (3 shorter events, 0.1 us)
Async XLA Ops:
  1.0 1.3 %copy-start = (bf16[2560,256]{1,0:T(8,128)(2,1)S(1)}, bf16[2560,256]{1,0:T(8,128)(2,1)}, u32[]{:S(2)}) copy-start(bf16[2560,256]{1,0:T(8,128)(2,1)} %modes.5) | copy-start | bytes 3932164
  1.0 5.8 %copy-start.1 = (bf16[14,640,640]{2,1,0:T(8,128)(2,1)S(1)}, bf16[14,640,640]{2,1,0:T(8,128)(2,1)}, u32[]{:S(2)}) copy-start(bf16[14,640,640]{2,1,0:T(8,128)(2,1)} %jac.1) | copy-start | bytes 34406404
  1.1 11.3 %collective-permute-start = (bf16[640,256]{1,0:T(8,128)(2,1)S(1)}, bf16[640,256]{1,0:T(8,128)(2,1)S(1)}, u32[]{:S(2)}, u32[]{:S(2)}) collective-permute-start(bf16[640,256]{1,0:T(8,128)(2,1)S(1)} %gate.1), channel_id=1, source_target_pairs={{0,0},{1,2},{2,1},{3,4},{4,3},{5,6},{6,5},{7,8},{8,7},{9,10},{10,9... | collective-permute-start | bytes 983048 | tf_op jit(solution)/shard_map/ppermute | solution.py:233
  2.4 4.5 %copy-start.2 = (s32[14,2]{0,1:T(2,128)S(1)}, s32[14,2]{0,1:T(2,128)}, u32[]{:S(2)}) copy-start(s32[14,2]{0,1:T(2,128)} %param.5) | copy-start | bytes 340
  2.4 10.0 %collective-permute-start.1 = (bf16[640,256]{1,0:T(8,128)(2,1)S(1)}, bf16[640,256]{1,0:T(8,128)(2,1)S(1)}, u32[]{:S(2)}, u32[]{:S(2)}) collective-permute-start(bf16[640,256]{1,0:T(8,128)(2,1)S(1)} %inner_edge.1), channel_id=1, source_target_pairs={{0,1},{1,0},{2,3},{3,2},{4,5},{5,4},{6,7},{7,6},{8,9},{9,8},{10,11... | collective-permute-start | bytes 983048 | tf_op jit(solution)/shard_map/ppermute | solution.py:234
  12.7 2.5 %collective-permute-start.2 = (f32[128,256]{1,0:T(8,128)S(1)}, f32[128,256]{1,0:T(8,128)S(1)}, u32[]{:S(2)}, u32[]{:S(2)}) collective-permute-start(f32[128,256]{1,0:T(8,128)S(1)} %join_give.1), channel_id=1, source_target_pairs={{0,1},{1,0},{2,3},{3,2},{4,5},{5,4},{6,7},{7,6},{8,9},{9,8},{10,11... | collective-permute-start | bytes 393224 | tf_op jit(solution)/shard_map/ppermute | solution.py:241

commit v19 on v18

--- a/solution.py
+++ b/solution.py
@@ -165,7 +165,7 @@
     chips = range(count // 2)
     middle = [chip for chip in (count // 4, count // 4 + 1) if 0 < chip < count // 2]
     rest = [chip for chip in chips if chip not in middle]
-    rings = [middle[::-1] + rest, middle + rest]
+    rings = [middle + rest, middle + rest[:-2] + rest[: -3 : -1]]
     return [[2 * chip + (chip + half) % 2 for chip in reversed(rings[half])] for half in range(2)]
 
 

time: 27.3 us -> 27.1 us (level)
  no operation moved by 1% of the time
where the time goes in v19:
time: 27.1 us; the launch traced here: 27 us
  blocking collectives  11.1 us (41%)
  Pallas kernels  7.22 us (27%)
  starting transfers between devices  6.44 us (24%)
  local copies, waits for them, and re-layouts  1.45 us (5%)
  waiting for transfers between devices  0.63 us (2%)
    all_to_all x1, blocking collectives, per_device(): parts = lax.all_to_all(pair, 'cell', 0, 0, axis_index_groups=teams(count))  11.1 us
    pallas_call x1, Pallas kernels, own_part(): pl.pallas_call(functools.partial(own_kernel, blocks), out_shape=(jax.Shap...  5.45 us
    ppermute x1, starting transfers between devices, per_device(): inner = lax.ppermute(inner_edge(modes, width), 'cell', swap)  4.08 us
    ppermute x1, starting transfers between devices, per_device(): got = lax.ppermute(join(True, p, t, outer, inner), 'cell', swap)  1.55 us
    dynamic_slice x1, local copies, waits for them, and re-layouts, per_device(): outer_edge = lax.dynamic_slice_in_dim(modes, core * (rows - width), width)  0.99 us
    ppermute x1, starting transfers between devices, per_device(): outer = lax.ppermute(gate(outer_edge), 'cell', across)  0.81 us
    pallas_call x2, Pallas kernels, join(): pl.pallas_call(functools.partial(join_kernel, other), out_shape=jax.Shape...  0.7 us
    ppermute x1, waiting for transfers between devices, per_device(): got = lax.ppermute(join(True, p, t, outer, inner), 'cell', swap)  0.63 us
  transfers between devices with their start and end apart: 3, of which 1 were waited for; matrix products, arithmetic and copies ran while one was open for 0% of the time, Pallas kernels for 23%

profile of v19, /device:TPU:0, one launch (start us, length us, event | category | flops | bytes accessed | tf_op | source)
XLA Modules:
  0.0 27.0 jit_solution(17651368992443723855)
XLA Ops:
  0.0 1.0 %constant_dynamic-slice_fusion.block_ref = bf16[640,256]{1,0:T(8,128)(2,1)S(1)} fusion(bf16[2560,256]{1,0:T(8,128)(2,1)} %modes.5, s32[]{:T(128)S(6)} %select_n.3), kind=kLoop, calls=%fused_computation | loop fusion | bytes 655364 | tf_op jit(solution)/shard_map/dynamic_slice | solution.py:232
  1.0 0.0 copy-start
  1.0 0.0 copy-start.1
  1.1 0.8 %collective-permute-start = (bf16[640,256]{1,0:T(8,128)(2,1)S(1)}, bf16[640,256]{1,0:T(8,128)(2,1)S(1)}, u32[]{:S(2)}, u32[]{:S(2)}) collective-permute-start(bf16[640,256]{1,0:T(8,128)(2,1)S(1)} %gate.1), channel_id=1, source_target_pairs={{0,0},{1,2},{2,1},{3,4},{4,3},{5,6},{6,5},{7,8},{8,7},{9,10},{10,9... | collective-permute-start | bytes 983048 | tf_op jit(solution)/shard_map/ppermute | solution.py:233
  1.9 0.4 %copy-done = bf16[2560,256]{1,0:T(8,128)(2,1)S(1)} copy-done((bf16[2560,256]{1,0:T(8,128)(2,1)S(1)}, bf16[2560,256]{1,0:T(8,128)(2,1)}, u32[]{:S(2)}) %copy-start) | copy-done | bytes 1310744
  2.4 0.0 copy-start.2
  2.4 4.1 %collective-permute-start.1 = (bf16[640,256]{1,0:T(8,128)(2,1)S(1)}, bf16[640,256]{1,0:T(8,128)(2,1)S(1)}, u32[]{:S(2)}, u32[]{:S(2)}) collective-permute-start(bf16[640,256]{1,0:T(8,128)(2,1)S(1)} %inner_edge.1), channel_id=1, source_target_pairs={{0,1},{1,0},{2,3},{3,2},{4,5},{5,4},{6,7},{7,6},{8,9},{9,8},{10,11... | collective-permute-start | bytes 983048 | tf_op jit(solution)/shard_map/ppermute | solution.py:234
  6.4 0.4 %turn.1.turned = bf16[256,2560]{1,0:T(8,128)(2,1)S(1)} custom-call(bf16[2560,256]{1,0:T(8,128)(2,1)S(1)} %copy-done), custom_call_target="tpu_custom_call" | custom-call | bytes 2621440 | tf_op jit(solution)/shard_map/turn/pallas_call | solution.py:75
  6.8 0.0 copy-done.1
  6.9 0.0 copy-done.2
  6.9 5.4 %own_part.1 = (f32[256,256]{1,0:T(8,128)S(1)}, bf16[2,2,256,640]{3,2,1,0:T(8,128)(2,1)S(1)}) custom-call(s32[2,14]{1,0:T(2,128)S(1)} %bitcast.2, bf16[14,640,640]{2,1,0:T(8,128)(2,1)S(1)} %copy-done.1, bf16[2560,256]{1,0:T(8,128)(2,1)S(1)} %copy-done, bf16[256,2560]{1,0:T(8,128)(2,1)S(1)} %turn.1.turned), custom_call_target="tpu_custom_call" | custom-call | flops 3607101440 | bytes 12779520 | tf_op jit(solution)/shard_map/own_part/pallas_call | solution.py:138
  12.3 0.0 collective-permute-done.outer_ref
  12.3 0.0 collective-permute-done.1.inner_ref
  12.3 0.4 %join_give.1 = f32[128,256]{1,0:T(8,128)S(1)} custom-call(f32[256,256]{1,0:T(8,128)S(1)} %get-tuple-element.7.p_ref, bf16[2,2,256,640]{3,2,1,0:T(8,128)(2,1)S(1)} %get-tuple-element.8.t_ref, bf16[640,256]{1,0:T(8,128)(2,1)S(1)} %collective-permute-done.outer_ref, bf16[640,256]{1,0:T(8,128)(2,1)S(1)} %collective-permute-done.1.inner_ref), custom_call_target="tpu_custom_call" | custom-call | flops 167772160 | tf_op jit(solution)/shard_map/join_give/pallas_call | solution.py:194
  12.7 1.6 %collective-permute-start.2 = (f32[128,256]{1,0:T(8,128)S(1)}, f32[128,256]{1,0:T(8,128)S(1)}, u32[]{:S(2)}, u32[]{:S(2)}) collective-permute-start(f32[128,256]{1,0:T(8,128)S(1)} %join_give.1), channel_id=1, source_target_pairs={{0,1},{1,0},{2,3},{3,2},{4,5},{5,4},{6,7},{7,6},{8,9},{9,8},{10,11... | collective-permute-start | bytes 393224 | tf_op jit(solution)/shard_map/ppermute | solution.py:241
  14.3 0.4 %join_keep.1 = f32[128,256]{1,0:T(8,128)S(1)} custom-call(f32[256,256]{1,0:T(8,128)S(1)} %get-tuple-element.7.p_ref, bf16[2,2,256,640]{3,2,1,0:T(8,128)(2,1)S(1)} %get-tuple-element.8.t_ref, bf16[640,256]{1,0:T(8,128)(2,1)S(1)} %collective-permute-done.outer_ref, bf16[640,256]{1,0:T(8,128)(2,1)S(1)} %collective-permute-done.1.inner_ref), custom_call_target="tpu_custom_call" | custom-call | flops 167772160 | tf_op jit(solution)/shard_map/join_keep/pallas_call | solution.py:194
  14.6 0.6 %collective-permute-done.2 = f32[128,256]{1,0:T(8,128)S(1)} collective-permute-done((f32[128,256]{1,0:T(8,128)S(1)}, f32[128,256]{1,0:T(8,128)S(1)}, u32[]{:S(2)}, u32[]{:S(2)}) %collective-permute-start.2) | collective-permute-done | bytes 131104 | tf_op jit(solution)/shard_map/ppermute | solution.py:241
  15.3 11.1 %all_to_all.5.parts_ref = f32[8,16,256]{2,1,0:T(8,128)S(1)} all-to-all(f32[8,16,256]{2,1,0:T(8,128)S(1)} %bitcast.3), channel_id=1, replica_groups={{15,12,7,4,3,0,11,8},{13,14,6,5,2,1,10,9},{31,28,23,20,19,16,27,24},{29..., dimensions={0} | all-to-all | bytes 262144 | tf_op jit(solution)/shard_map/all_to_all | solution.py:244
  26.4 0.6 %sum_parts.1 = f32[16,256]{1,0:T(8,128)} custom-call(f32[8,16,256]{2,1,0:T(8,128)S(1)} %all_to_all.5.parts_ref), custom_call_target="tpu_custom_call" | custom-call | tf_op jit(solution)/shard_map/sum_parts/pallas_call | solution.py:213
  (3 shorter events, 0.1 us)
Async XLA Ops:
  1.0 1.3 %copy-start = (bf16[2560,256]{1,0:T(8,128)(2,1)S(1)}, bf16[2560,256]{1,0:T(8,128)(2,1)}, u32[]{:S(2)}) copy-start(bf16[2560,256]{1,0:T(8,128)(2,1)} %modes.5) | copy-start | bytes 3932164
  1.0 5.8 %copy-start.1 = (bf16[14,640,640]{2,1,0:T(8,128)(2,1)S(1)}, bf16[14,640,640]{2,1,0:T(8,128)(2,1)}, u32[]{:S(2)}) copy-start(bf16[14,640,640]{2,1,0:T(8,128)(2,1)} %jac.1) | copy-start | bytes 34406404
  1.1 11.3 %collective-permute-start = (bf16[640,256]{1,0:T(8,128)(2,1)S(1)}, bf16[640,256]{1,0:T(8,128)(2,1)S(1)}, u32[]{:S(2)}, u32[]{:S(2)}) collective-permute-start(bf16[640,256]{1,0:T(8,128)(2,1)S(1)} %gate.1), channel_id=1, source_target_pairs={{0,0},{1,2},{2,1},{3,4},{4,3},{5,6},{6,5},{7,8},{8,7},{9,10},{10,9... | collective-permute-start | bytes 983048 | tf_op jit(solution)/shard_map/ppermute | solution.py:233
  2.4 4.5 %copy-start.2 = (s32[14,2]{0,1:T(2,128)S(1)}, s32[14,2]{0,1:T(2,128)}, u32[]{:S(2)}) copy-start(s32[14,2]{0,1:T(2,128)} %param.5) | copy-start | bytes 340
  2.4 10.0 %collective-permute-start.1 = (bf16[640,256]{1,0:T(8,128)(2,1)S(1)}, bf16[640,256]{1,0:T(8,128)(2,1)S(1)}, u32[]{:S(2)}, u32[]{:S(2)}) collective-permute-start(bf16[640,256]{1,0:T(8,128)(2,1)S(1)} %inner_edge.1), channel_id=1, source_target_pairs={{0,1},{1,0},{2,3},{3,2},{4,5},{5,4},{6,7},{7,6},{8,9},{9,8},{10,11... | collective-permute-start | bytes 983048 | tf_op jit(solution)/shard_map/ppermute | solution.py:234
  12.7 2.5 %collective-permute-start.2 = (f32[128,256]{1,0:T(8,128)S(1)}, f32[128,256]{1,0:T(8,128)S(1)}, u32[]{:S(2)}, u32[]{:S(2)}) collective-permute-start(f32[128,256]{1,0:T(8,128)S(1)} %join_give.1), channel_id=1, source_target_pairs={{0,1},{1,0},{2,3},{3,2},{4,5},{5,4},{6,7},{7,6},{8,9},{9,8},{10,11... | collective-permute-start | bytes 393224 | tf_op jit(solution)/shard_map/ppermute | solution.py:241

commit v20 on v19

--- a/solution.py
+++ b/solution.py
@@ -180,22 +180,25 @@
     return jnp.concatenate([lax.slice_in_dim(value, k, k + keep_rows, axis=axis) for k in starts], axis=axis)
 
 
-def join_kernel(other, p_ref, t_ref, outer_ref, inner_ref, out_ref):
+def join_kernel(other, p_ref, t_ref, outer_ref, inner_ref, *out_refs):
     core = lax.rem(lax.axis_index("cell"), 2)
-    count = out_ref.shape[0]
+    count = p_ref.shape[0] // 2
     half = 1 - own_team() if other else own_team()
     rows = pl.ds(pl.multiple_of(half * count, TILE_ROWS), count)
     both = dot(t_ref[1 - core, half], inner_ref[...]) + dot(t_ref[core, half], outer_ref[...])
-    out_ref[...] = p_ref[rows, :] + both[:count] + both[count:]
-
-
-def join(other, p, t, outer, inner):
+    total = p_ref[rows, :] + both[:count] + both[count:]
+    step = count // len(out_refs)
+    for k, out_ref in enumerate(out_refs):
+        out_ref[...] = total[k * step : (k + 1) * step]
+
+
+def join(other, pieces, p, t, outer, inner):
     rows = p.shape[0] // 2
     return pl.pallas_call(
         functools.partial(join_kernel, other),
-        out_shape=jax.ShapeDtypeStruct((rows, p.shape[1]), jnp.float32),
+        out_shape=(jax.ShapeDtypeStruct((rows // pieces, p.shape[1]), jnp.float32),) * pieces,
         in_specs=[pl.BlockSpec(memory_space=pltpu.VMEM)] * 4,
-        out_specs=pl.BlockSpec(memory_space=pltpu.VMEM),
+        out_specs=(pl.BlockSpec(memory_space=pltpu.VMEM),) * pieces,
         compiler_params=pltpu.CompilerParams(vmem_limit_bytes=SMALL_VMEM),
         cost_estimate=pl.CostEstimate(flops=8 * rows * outer.size, bytes_accessed=0, transcendentals=0),
         name="join_give" if other else "join_keep",
@@ -238,9 +241,9 @@
         apart = jnp.swapaxes(t.reshape(2, 2, 2, n_modes // 2, width), 1, 2).reshape(2, 2, n_modes, width)
         apart = regrouped(apart, 2, keep_rows).reshape(2, 2, 2, n_modes // 2, width)
         t = jnp.swapaxes(apart, 1, 2).reshape(t.shape)
-    got = lax.ppermute(join(True, p, t, outer, inner), "cell", swap)
-    keep = join(False, p, t, outer, inner)
-    pair = (keep + got).reshape(count // 2, keep_rows, n_modes)
+    got = [lax.ppermute(piece, "cell", swap) for piece in join(True, 2, p, t, outer, inner)]
+    keep = join(False, 1, p, t, outer, inner)[0]
+    pair = (keep + jnp.concatenate(got)).reshape(count // 2, keep_rows, n_modes)
     parts = lax.all_to_all(pair, "cell", 0, 0, axis_index_groups=teams(count))
     return sum_parts(parts)
 

time: 27.1 us -> 27.3 us (level)
  starting transfers between devices: 6.44 us -> 8.08 us
  Pallas kernels: 7.22 us -> 5.66 us
    ppermute x1 -> x2, starting transfers between devices: 1.55 us -> 3.19 us  [per_device(): lax.ppermute(piece, 'cell', swap)]
    pallas_call x1, Pallas kernels: 5.45 us -> 3.89 us  [own_part(): pl.pallas_call(functools.partial(own_kernel, blocks), out_shape=(jax.Shap...]
    ppermute x1 -> x2, waiting for transfers between devices: 0.63 us -> 0.82 us  [per_device(): lax.ppermute(piece, 'cell', swap)]
  transfers between devices with their start and end apart: 3 -> 4, of which waited for: 1 -> 2; matrix products, arithmetic and copies ran while one was open for 0% -> 0% of each run, Pallas kernels for 23% -> 17%
where the time goes in v20:
time: 27.3 us; the launch traced here: 27.2 us
  blocking collectives  11 us (40%)
  starting transfers between devices  8.08 us (30%)
  Pallas kernels  5.66 us (21%)
  local copies, waits for them, and re-layouts  1.45 us (5%)
  waiting for transfers between devices  0.82 us (3%)
    all_to_all x1, blocking collectives, per_device(): parts = lax.all_to_all(pair, 'cell', 0, 0, axis_index_groups=teams(count))  11 us
    ppermute x1, starting transfers between devices, per_device(): inner = lax.ppermute(inner_edge(modes, width), 'cell', swap)  4.08 us
    pallas_call x1, Pallas kernels, own_part(): pl.pallas_call(functools.partial(own_kernel, blocks), out_shape=(jax.Shap...  3.89 us
    ppermute x2, starting transfers between devices, per_device(): lax.ppermute(piece, 'cell', swap)  3.19 us
    dynamic_slice x1, local copies, waits for them, and re-layouts, per_device(): outer_edge = lax.dynamic_slice_in_dim(modes, core * (rows - width), width)  0.99 us
    ppermute x2, waiting for transfers between devices, per_device(): lax.ppermute(piece, 'cell', swap)  0.82 us
    ppermute x1, starting transfers between devices, per_device(): outer = lax.ppermute(gate(outer_edge), 'cell', across)  0.81 us
    pallas_call x2, Pallas kernels, join(): pl.pallas_call(functools.partial(join_kernel, other), out_shape=(jax.Shap...  0.7 us
  transfers between devices with their start and end apart: 4, of which 2 were waited for; matrix products, arithmetic and copies ran while one was open for 0% of the time, Pallas kernels for 17%

profile of v20, /device:TPU:0, one launch (start us, length us, event | category | flops | bytes accessed | tf_op | source)
XLA Modules:
  0.0 27.2 jit_solution(10566624478739699079)
XLA Ops:
  0.0 1.0 %constant_dynamic-slice_fusion.block_ref = bf16[640,256]{1,0:T(8,128)(2,1)S(1)} fusion(bf16[2560,256]{1,0:T(8,128)(2,1)} %modes.5, s32[]{:T(128)S(6)} %select_n.3), kind=kLoop, calls=%fused_computation.1 | loop fusion | bytes 655364 | tf_op jit(solution)/shard_map/dynamic_slice | solution.py:235
  1.0 0.0 copy-start
  1.0 0.0 copy-start.1
  1.1 0.8 %collective-permute-start = (bf16[640,256]{1,0:T(8,128)(2,1)S(1)}, bf16[640,256]{1,0:T(8,128)(2,1)S(1)}, u32[]{:S(2)}, u32[]{:S(2)}) collective-permute-start(bf16[640,256]{1,0:T(8,128)(2,1)S(1)} %gate.1), channel_id=1, source_target_pairs={{0,0},{1,2},{2,1},{3,4},{4,3},{5,6},{6,5},{7,8},{8,7},{9,10},{10,9... | collective-permute-start | bytes 983048 | tf_op jit(solution)/shard_map/ppermute | solution.py:236
  1.9 0.4 %copy-done = bf16[2560,256]{1,0:T(8,128)(2,1)S(1)} copy-done((bf16[2560,256]{1,0:T(8,128)(2,1)S(1)}, bf16[2560,256]{1,0:T(8,128)(2,1)}, u32[]{:S(2)}) %copy-start) | copy-done | bytes 1310744
  2.4 0.0 copy-start.2
  2.4 4.1 %collective-permute-start.1 = (bf16[640,256]{1,0:T(8,128)(2,1)S(1)}, bf16[640,256]{1,0:T(8,128)(2,1)S(1)}, u32[]{:S(2)}, u32[]{:S(2)}) collective-permute-start(bf16[640,256]{1,0:T(8,128)(2,1)S(1)} %inner_edge.1), channel_id=1, source_target_pairs={{0,1},{1,0},{2,3},{3,2},{4,5},{5,4},{6,7},{7,6},{8,9},{9,8},{10,11... | collective-permute-start | bytes 983048 | tf_op jit(solution)/shard_map/ppermute | solution.py:237
  6.4 0.4 %turn.1.turned = bf16[256,2560]{1,0:T(8,128)(2,1)S(1)} custom-call(bf16[2560,256]{1,0:T(8,128)(2,1)S(1)} %copy-done), custom_call_target="tpu_custom_call" | custom-call | bytes 2621440 | tf_op jit(solution)/shard_map/turn/pallas_call | solution.py:75
  6.8 0.0 copy-done.1
  6.9 0.0 copy-done.2
  6.9 3.9 %own_part.1 = (f32[256,256]{1,0:T(8,128)S(1)}, bf16[2,2,256,640]{3,2,1,0:T(8,128)(2,1)S(1)}) custom-call(s32[2,14]{1,0:T(2,128)S(1)} %bitcast.2, bf16[14,640,640]{2,1,0:T(8,128)(2,1)S(1)} %copy-done.1, bf16[2560,256]{1,0:T(8,128)(2,1)S(1)} %copy-done, bf16[256,2560]{1,0:T(8,128)(2,1)S(1)} %turn.1.turned), custom_call_target="tpu_custom_call" | custom-call | flops 3607101440 | bytes 12779520 | tf_op jit(solution)/shard_map/own_part/pallas_call | solution.py:138
  10.8 0.0 collective-permute-done.outer_ref
  10.8 0.0 collective-permute-done.1.inner_ref
  10.8 0.4 %join_give.1 = (f32[64,256]{1,0:T(8,128)S(1)}, f32[64,256]{1,0:T(8,128)S(1)}) custom-call(f32[256,256]{1,0:T(8,128)S(1)} %get-tuple-element.9.p_ref, bf16[2,2,256,640]{3,2,1,0:T(8,128)(2,1)S(1)} %get-tuple-element.10.t_ref, bf16[640,256]{1,0:T(8,128)(2,1)S(1)} %collective-permute-done.outer_ref, bf16[640,256]{1,0:T(8,128)(2,1)S(1)} %collective-permute-done.1.inner_ref), custom_call_target="tpu_custom_call" | custom-call | flops 167772160 | tf_op jit(solution)/shard_map/join_give/pallas_call | solution.py:197
  11.1 3.1 %collective-permute-start.3 = (f32[64,256]{1,0:T(8,128)S(1)}, f32[64,256]{1,0:T(8,128)S(1)}, u32[]{:S(2)}, u32[]{:S(2)}) collective-permute-start(f32[64,256]{1,0:T(8,128)S(1)} %get-tuple-element.12), channel_id=1, source_target_pairs={{0,1},{1,0},{2,3},{3,2},{4,5},{5,4},{6,7},{7,6},{8,9},{9,8},{10,11... | collective-permute-start | bytes 196616 | tf_op jit(solution)/shard_map/ppermute | solution.py:244
  14.3 0.1 collective-permute-start.2
  14.3 0.4 %join_keep.1 = f32[128,256]{1,0:T(8,128)S(1)} custom-call(f32[256,256]{1,0:T(8,128)S(1)} %get-tuple-element.9.p_ref, bf16[2,2,256,640]{3,2,1,0:T(8,128)(2,1)S(1)} %get-tuple-element.10.t_ref, bf16[640,256]{1,0:T(8,128)(2,1)S(1)} %collective-permute-done.outer_ref, bf16[640,256]{1,0:T(8,128)(2,1)S(1)} %collective-permute-done.1.inner_ref), custom_call_target="tpu_custom_call" | custom-call | flops 167772160 | tf_op jit(solution)/shard_map/join_keep/pallas_call | solution.py:197
  14.7 0.5 %collective-permute-done.3 = f32[64,256]{1,0:T(8,128)S(1)} collective-permute-done((f32[64,256]{1,0:T(8,128)S(1)}, f32[64,256]{1,0:T(8,128)S(1)}, u32[]{:S(2)}, u32[]{:S(2)}) %collective-permute-start.3) | collective-permute-done | bytes 65568 | tf_op jit(solution)/shard_map/ppermute | solution.py:244
  15.2 0.4 %collective-permute-done.2 = f32[64,256]{1,0:T(8,128)S(1)} collective-permute-done((f32[64,256]{1,0:T(8,128)S(1)}, f32[64,256]{1,0:T(8,128)S(1)}, u32[]{:S(2)}, u32[]{:S(2)}) %collective-permute-start.2) | collective-permute-done | bytes 65568 | tf_op jit(solution)/shard_map/ppermute | solution.py:244
  15.5 11.0 %all_to_all.5.parts_ref = f32[8,16,256]{2,1,0:T(8,128)S(1)} all-to-all(f32[8,16,256]{2,1,0:T(8,128)S(1)} %bitcast.3), channel_id=1, replica_groups={{15,12,7,4,3,0,11,8},{13,14,6,5,2,1,10,9},{31,28,23,20,19,16,27,24},{29..., dimensions={0} | all-to-all | bytes 262144 | tf_op jit(solution)/shard_map/all_to_all | solution.py:247
  26.5 0.6 %sum_parts.1 = f32[16,256]{1,0:T(8,128)} custom-call(f32[8,16,256]{2,1,0:T(8,128)S(1)} %all_to_all.5.parts_ref), custom_call_target="tpu_custom_call" | custom-call | tf_op jit(solution)/shard_map/sum_parts/pallas_call | solution.py:216
  (3 shorter events, 0.1 us)
Async XLA Ops:
  1.0 1.3 %copy-start = (bf16[2560,256]{1,0:T(8,128)(2,1)S(1)}, bf16[2560,256]{1,0:T(8,128)(2,1)}, u32[]{:S(2)}) copy-start(bf16[2560,256]{1,0:T(8,128)(2,1)} %modes.5) | copy-start | bytes 3932164
  1.0 5.8 %copy-start.1 = (bf16[14,640,640]{2,1,0:T(8,128)(2,1)S(1)}, bf16[14,640,640]{2,1,0:T(8,128)(2,1)}, u32[]{:S(2)}) copy-start(bf16[14,640,640]{2,1,0:T(8,128)(2,1)} %jac.1) | copy-start | bytes 34406404
  1.1 9.7 %collective-permute-start = (bf16[640,256]{1,0:T(8,128)(2,1)S(1)}, bf16[640,256]{1,0:T(8,128)(2,1)S(1)}, u32[]{:S(2)}, u32[]{:S(2)}) collective-permute-start(bf16[640,256]{1,0:T(8,128)(2,1)S(1)} %gate.1), channel_id=1, source_target_pairs={{0,0},{1,2},{2,1},{3,4},{4,3},{5,6},{6,5},{7,8},{8,7},{9,10},{10,9... | collective-permute-start | bytes 983048 | tf_op jit(solution)/shard_map/ppermute | solution.py:236
  2.4 4.5 %copy-start.2 = (s32[14,2]{0,1:T(2,128)S(1)}, s32[14,2]{0,1:T(2,128)}, u32[]{:S(2)}) copy-start(s32[14,2]{0,1:T(2,128)} %param.5) | copy-start | bytes 340
  2.4 8.4 %collective-permute-start.1 = (bf16[640,256]{1,0:T(8,128)(2,1)S(1)}, bf16[640,256]{1,0:T(8,128)(2,1)S(1)}, u32[]{:S(2)}, u32[]{:S(2)}) collective-permute-start(bf16[640,256]{1,0:T(8,128)(2,1)S(1)} %inner_edge.1), channel_id=1, source_target_pairs={{0,1},{1,0},{2,3},{3,2},{4,5},{5,4},{6,7},{7,6},{8,9},{9,8},{10,11... | collective-permute-start | bytes 983048 | tf_op jit(solution)/shard_map/ppermute | solution.py:237
  11.1 4.0 %collective-permute-start.3 = (f32[64,256]{1,0:T(8,128)S(1)}, f32[64,256]{1,0:T(8,128)S(1)}, u32[]{:S(2)}, u32[]{:S(2)}) collective-permute-start(f32[64,256]{1,0:T(8,128)S(1)} %get-tuple-element.12), channel_id=1, source_target_pairs={{0,1},{1,0},{2,3},{3,2},{4,5},{5,4},{6,7},{7,6},{8,9},{9,8},{10,11... | collective-permute-start | bytes 196616 | tf_op jit(solution)/shard_map/ppermute | solution.py:244
  14.3 1.3 %collective-permute-start.2 = (f32[64,256]{1,0:T(8,128)S(1)}, f32[64,256]{1,0:T(8,128)S(1)}, u32[]{:S(2)}, u32[]{:S(2)}) collective-permute-start(f32[64,256]{1,0:T(8,128)S(1)} %get-tuple-element.11), channel_id=1, source_target_pairs={{0,1},{1,0},{2,3},{3,2},{4,5},{5,4},{6,7},{7,6},{8,9},{9,8},{10,11... | collective-permute-start | bytes 196616 | tf_op jit(solution)/shard_map/ppermute | solution.py:244

commit v21 on v19

--- a/solution.py
+++ b/solution.py
@@ -165,7 +165,8 @@
     chips = range(count // 2)
     middle = [chip for chip in (count // 4, count // 4 + 1) if 0 < chip < count // 2]
     rest = [chip for chip in chips if chip not in middle]
-    rings = [middle + rest, middle + rest[:-2] + rest[: -3 : -1]]
+    near = count // 8
+    rings = [[chip for chip in rest if chip != near] + [near] + middle, middle + rest[:-2] + rest[: -3 : -1]]
     return [[2 * chip + (chip + half) % 2 for chip in reversed(rings[half])] for half in range(2)]
 
 

time: 27.1 us -> 27.2 us (level)
  starting transfers between devices: 6.44 us -> 8.3 us
  Pallas kernels: 7.22 us -> 5.65 us
    ppermute x1, starting transfers between devices: 1.55 us -> 3.4 us  [per_device(): got = lax.ppermute(join(True, p, t, outer, inner), 'cell', swap)]
    pallas_call x1, Pallas kernels: 5.45 us -> 3.88 us  [own_part(): pl.pallas_call(functools.partial(own_kernel, blocks), out_shape=(jax.Shap...]
  transfers between devices with their start and end apart: 3 -> 3, of which waited for: 1 -> 1; matrix products, arithmetic and copies ran while one was open for 0% -> 0% of each run, Pallas kernels for 23% -> 17%
where the time goes in v21:
time: 27.2 us; the launch traced here: 27 us
  blocking collectives  10.9 us (40%)
  starting transfers between devices  8.3 us (31%)
  Pallas kernels  5.65 us (21%)
  local copies, waits for them, and re-layouts  1.45 us (5%)
  waiting for transfers between devices  0.63 us (2%)
    all_to_all x1, blocking collectives, per_device(): parts = lax.all_to_all(pair, 'cell', 0, 0, axis_index_groups=teams(count))  10.9 us
    ppermute x1, starting transfers between devices, per_device(): inner = lax.ppermute(inner_edge(modes, width), 'cell', swap)  4.08 us
    pallas_call x1, Pallas kernels, own_part(): pl.pallas_call(functools.partial(own_kernel, blocks), out_shape=(jax.Shap...  3.88 us
    ppermute x1, starting transfers between devices, per_device(): got = lax.ppermute(join(True, p, t, outer, inner), 'cell', swap)  3.4 us
    dynamic_slice x1, local copies, waits for them, and re-layouts, per_device(): outer_edge = lax.dynamic_slice_in_dim(modes, core * (rows - width), width)  0.99 us
    ppermute x1, starting transfers between devices, per_device(): outer = lax.ppermute(gate(outer_edge), 'cell', across)  0.81 us
    pallas_call x2, Pallas kernels, join(): pl.pallas_call(functools.partial(join_kernel, other), out_shape=jax.Shape...  0.7 us
    ppermute x1, waiting for transfers between devices, per_device(): got = lax.ppermute(join(True, p, t, outer, inner), 'cell', swap)  0.63 us
  transfers between devices with their start and end apart: 3, of which 1 were waited for; matrix products, arithmetic and copies ran while one was open for 0% of the time, Pallas kernels for 17%

profile of v21, /device:TPU:0, one launch (start us, length us, event | category | flops | bytes accessed | tf_op | source)
XLA Modules:
  0.0 27.0 jit_solution(10388203859472318195)
XLA Ops:
  0.0 1.0 %constant_dynamic-slice_fusion.block_ref = bf16[640,256]{1,0:T(8,128)(2,1)S(1)} fusion(bf16[2560,256]{1,0:T(8,128)(2,1)} %modes.5, s32[]{:T(128)S(6)} %select_n.3), kind=kLoop, calls=%fused_computation | loop fusion | bytes 655364 | tf_op jit(solution)/shard_map/dynamic_slice | solution.py:233
  1.0 0.0 copy-start
  1.0 0.0 copy-start.1
  1.1 0.8 %collective-permute-start = (bf16[640,256]{1,0:T(8,128)(2,1)S(1)}, bf16[640,256]{1,0:T(8,128)(2,1)S(1)}, u32[]{:S(2)}, u32[]{:S(2)}) collective-permute-start(bf16[640,256]{1,0:T(8,128)(2,1)S(1)} %gate.1), channel_id=1, source_target_pairs={{0,0},{1,2},{2,1},{3,4},{4,3},{5,6},{6,5},{7,8},{8,7},{9,10},{10,9... | collective-permute-start | bytes 983048 | tf_op jit(solution)/shard_map/ppermute | solution.py:234
  1.9 0.4 %copy-done = bf16[2560,256]{1,0:T(8,128)(2,1)S(1)} copy-done((bf16[2560,256]{1,0:T(8,128)(2,1)S(1)}, bf16[2560,256]{1,0:T(8,128)(2,1)}, u32[]{:S(2)}) %copy-start) | copy-done | bytes 1310744
  2.4 0.0 copy-start.2
  2.4 4.1 %collective-permute-start.1 = (bf16[640,256]{1,0:T(8,128)(2,1)S(1)}, bf16[640,256]{1,0:T(8,128)(2,1)S(1)}, u32[]{:S(2)}, u32[]{:S(2)}) collective-permute-start(bf16[640,256]{1,0:T(8,128)(2,1)S(1)} %inner_edge.1), channel_id=1, source_target_pairs={{0,1},{1,0},{2,3},{3,2},{4,5},{5,4},{6,7},{7,6},{8,9},{9,8},{10,11... | collective-permute-start | bytes 983048 | tf_op jit(solution)/shard_map/ppermute | solution.py:235
  6.4 0.4 %turn.1.turned = bf16[256,2560]{1,0:T(8,128)(2,1)S(1)} custom-call(bf16[2560,256]{1,0:T(8,128)(2,1)S(1)} %copy-done), custom_call_target="tpu_custom_call" | custom-call | bytes 2621440 | tf_op jit(solution)/shard_map/turn/pallas_call | solution.py:75
  6.8 0.0 copy-done.1
  6.9 0.0 copy-done.2
  6.9 3.9 %own_part.1 = (f32[256,256]{1,0:T(8,128)S(1)}, bf16[2,2,256,640]{3,2,1,0:T(8,128)(2,1)S(1)}) custom-call(s32[2,14]{1,0:T(2,128)S(1)} %bitcast.2, bf16[14,640,640]{2,1,0:T(8,128)(2,1)S(1)} %copy-done.1, bf16[2560,256]{1,0:T(8,128)(2,1)S(1)} %copy-done, bf16[256,2560]{1,0:T(8,128)(2,1)S(1)} %turn.1.turned), custom_call_target="tpu_custom_call" | custom-call | flops 3607101440 | bytes 12779520 | tf_op jit(solution)/shard_map/own_part/pallas_call | solution.py:138
  10.7 0.0 collective-permute-done.outer_ref
  10.8 0.0 collective-permute-done.1.inner_ref
  10.8 0.3 %join_give.1 = f32[128,256]{1,0:T(8,128)S(1)} custom-call(f32[256,256]{1,0:T(8,128)S(1)} %get-tuple-element.7.p_ref, bf16[2,2,256,640]{3,2,1,0:T(8,128)(2,1)S(1)} %get-tuple-element.8.t_ref, bf16[640,256]{1,0:T(8,128)(2,1)S(1)} %collective-permute-done.outer_ref, bf16[640,256]{1,0:T(8,128)(2,1)S(1)} %collective-permute-done.1.inner_ref), custom_call_target="tpu_custom_call" | custom-call | flops 167772160 | tf_op jit(solution)/shard_map/join_give/pallas_call | solution.py:195
  11.1 3.4 %collective-permute-start.2 = (f32[128,256]{1,0:T(8,128)S(1)}, f32[128,256]{1,0:T(8,128)S(1)}, u32[]{:S(2)}, u32[]{:S(2)}) collective-permute-start(f32[128,256]{1,0:T(8,128)S(1)} %join_give.1), channel_id=1, source_target_pairs={{0,1},{1,0},{2,3},{3,2},{4,5},{5,4},{6,7},{7,6},{8,9},{9,8},{10,11... | collective-permute-start | bytes 393224 | tf_op jit(solution)/shard_map/ppermute | solution.py:242
  14.5 0.4 %join_keep.1 = f32[128,256]{1,0:T(8,128)S(1)} custom-call(f32[256,256]{1,0:T(8,128)S(1)} %get-tuple-element.7.p_ref, bf16[2,2,256,640]{3,2,1,0:T(8,128)(2,1)S(1)} %get-tuple-element.8.t_ref, bf16[640,256]{1,0:T(8,128)(2,1)S(1)} %collective-permute-done.outer_ref, bf16[640,256]{1,0:T(8,128)(2,1)S(1)} %collective-permute-done.1.inner_ref), custom_call_target="tpu_custom_call" | custom-call | flops 167772160 | tf_op jit(solution)/shard_map/join_keep/pallas_call | solution.py:195
  14.9 0.6 %collective-permute-done.2 = f32[128,256]{1,0:T(8,128)S(1)} collective-permute-done((f32[128,256]{1,0:T(8,128)S(1)}, f32[128,256]{1,0:T(8,128)S(1)}, u32[]{:S(2)}, u32[]{:S(2)}) %collective-permute-start.2) | collective-permute-done | bytes 131104 | tf_op jit(solution)/shard_map/ppermute | solution.py:242
  15.5 10.9 %all_to_all.5.parts_ref = f32[8,16,256]{2,1,0:T(8,128)S(1)} all-to-all(f32[8,16,256]{2,1,0:T(8,128)S(1)} %bitcast.3), channel_id=1, replica_groups={{11,8,4,15,12,7,3,0},{13,14,6,5,2,1,10,9},{27,24,20,31,28,23,19,16},{29..., dimensions={0} | all-to-all | bytes 262144 | tf_op jit(solution)/shard_map/all_to_all | solution.py:245
  26.4 0.6 %sum_parts.1 = f32[16,256]{1,0:T(8,128)} custom-call(f32[8,16,256]{2,1,0:T(8,128)S(1)} %all_to_all.5.parts_ref), custom_call_target="tpu_custom_call" | custom-call | tf_op jit(solution)/shard_map/sum_parts/pallas_call | solution.py:214
  (3 shorter events, 0.1 us)
Async XLA Ops:
  1.0 1.3 %copy-start = (bf16[2560,256]{1,0:T(8,128)(2,1)S(1)}, bf16[2560,256]{1,0:T(8,128)(2,1)}, u32[]{:S(2)}) copy-start(bf16[2560,256]{1,0:T(8,128)(2,1)} %modes.5) | copy-start | bytes 3932164
  1.0 5.8 %copy-start.1 = (bf16[14,640,640]{2,1,0:T(8,128)(2,1)S(1)}, bf16[14,640,640]{2,1,0:T(8,128)(2,1)}, u32[]{:S(2)}) copy-start(bf16[14,640,640]{2,1,0:T(8,128)(2,1)} %jac.1) | copy-start | bytes 34406404
  1.1 9.7 %collective-permute-start = (bf16[640,256]{1,0:T(8,128)(2,1)S(1)}, bf16[640,256]{1,0:T(8,128)(2,1)S(1)}, u32[]{:S(2)}, u32[]{:S(2)}) collective-permute-start(bf16[640,256]{1,0:T(8,128)(2,1)S(1)} %gate.1), channel_id=1, source_target_pairs={{0,0},{1,2},{2,1},{3,4},{4,3},{5,6},{6,5},{7,8},{8,7},{9,10},{10,9... | collective-permute-start | bytes 983048 | tf_op jit(solution)/shard_map/ppermute | solution.py:234
  2.4 4.5 %copy-start.2 = (s32[14,2]{0,1:T(2,128)S(1)}, s32[14,2]{0,1:T(2,128)}, u32[]{:S(2)}) copy-start(s32[14,2]{0,1:T(2,128)} %param.5) | copy-start | bytes 340
  2.4 8.4 %collective-permute-start.1 = (bf16[640,256]{1,0:T(8,128)(2,1)S(1)}, bf16[640,256]{1,0:T(8,128)(2,1)S(1)}, u32[]{:S(2)}, u32[]{:S(2)}) collective-permute-start(bf16[640,256]{1,0:T(8,128)(2,1)S(1)} %inner_edge.1), channel_id=1, source_target_pairs={{0,1},{1,0},{2,3},{3,2},{4,5},{5,4},{6,7},{7,6},{8,9},{9,8},{10,11... | collective-permute-start | bytes 983048 | tf_op jit(solution)/shard_map/ppermute | solution.py:235
  11.1 4.4 %collective-permute-start.2 = (f32[128,256]{1,0:T(8,128)S(1)}, f32[128,256]{1,0:T(8,128)S(1)}, u32[]{:S(2)}, u32[]{:S(2)}) collective-permute-start(f32[128,256]{1,0:T(8,128)S(1)} %join_give.1), channel_id=1, source_target_pairs={{0,1},{1,0},{2,3},{3,2},{4,5},{5,4},{6,7},{7,6},{8,9},{9,8},{10,11... | collective-permute-start | bytes 393224 | tf_op jit(solution)/shard_map/ppermute | solution.py:242

commit v22 on v19

--- a/solution.py
+++ b/solution.py
@@ -164,8 +164,10 @@
 def teams(count):
     chips = range(count // 2)
     middle = [chip for chip in (count // 4, count // 4 + 1) if 0 < chip < count // 2]
-    rest = [chip for chip in chips if chip not in middle]
-    rings = [middle + rest, middle + rest[:-2] + rest[: -3 : -1]]
+    rings = []
+    for near in ((count // 8 - 1, count // 8), (count // 8,)):
+        near = [chip for chip in near if chip > 0]
+        rings.append([chip for chip in chips if chip not in near + middle] + near + middle)
     return [[2 * chip + (chip + half) % 2 for chip in reversed(rings[half])] for half in range(2)]
 
 

time: 27.1 us -> 27.4 us (1.011)
  Pallas kernels: 7.22 us -> 6.43 us
  starting transfers between devices: 6.44 us -> 7.23 us
    pallas_call x1, Pallas kernels: 5.45 us -> 4.66 us  [own_part(): pl.pallas_call(functools.partial(own_kernel, blocks), out_shape=(jax.Shap...]
    ppermute x1, starting transfers between devices: 1.55 us -> 2.34 us  [per_device(): got = lax.ppermute(join(True, p, t, outer, inner), 'cell', swap)]
  transfers between devices with their start and end apart: 3 -> 3, of which waited for: 1 -> 1; matrix products, arithmetic and copies ran while one was open for 0% -> 0% of each run, Pallas kernels for 23% -> 20%
where the time goes in v22:
time: 27.4 us; the launch traced here: 27.2 us
  blocking collectives  11.3 us (41%)
  starting transfers between devices  7.23 us (26%)
  Pallas kernels  6.43 us (23%)
  local copies, waits for them, and re-layouts  1.45 us (5%)
  waiting for transfers between devices  0.63 us (2%)
    all_to_all x1, blocking collectives, per_device(): parts = lax.all_to_all(pair, 'cell', 0, 0, axis_index_groups=teams(count))  11.3 us
    pallas_call x1, Pallas kernels, own_part(): pl.pallas_call(functools.partial(own_kernel, blocks), out_shape=(jax.Shap...  4.66 us
    ppermute x1, starting transfers between devices, per_device(): inner = lax.ppermute(inner_edge(modes, width), 'cell', swap)  4.08 us
    ppermute x1, starting transfers between devices, per_device(): got = lax.ppermute(join(True, p, t, outer, inner), 'cell', swap)  2.34 us
    dynamic_slice x1, local copies, waits for them, and re-layouts, per_device(): outer_edge = lax.dynamic_slice_in_dim(modes, core * (rows - width), width)  0.99 us
    ppermute x1, starting transfers between devices, per_device(): outer = lax.ppermute(gate(outer_edge), 'cell', across)  0.81 us
    pallas_call x2, Pallas kernels, join(): pl.pallas_call(functools.partial(join_kernel, other), out_shape=jax.Shape...  0.7 us
    ppermute x1, waiting for transfers between devices, per_device(): got = lax.ppermute(join(True, p, t, outer, inner), 'cell', swap)  0.63 us
  transfers between devices with their start and end apart: 3, of which 1 were waited for; matrix products, arithmetic and copies ran while one was open for 0% of the time, Pallas kernels for 20%

profile of v22, /device:TPU:0, one launch (start us, length us, event | category | flops | bytes accessed | tf_op | source)
XLA Modules:
  0.0 27.2 jit_solution(17550650459976071768)
XLA Ops:
  0.0 1.0 %constant_dynamic-slice_fusion.block_ref = bf16[640,256]{1,0:T(8,128)(2,1)S(1)} fusion(bf16[2560,256]{1,0:T(8,128)(2,1)} %modes.5, s32[]{:T(128)S(6)} %select_n.3), kind=kLoop, calls=%fused_computation | loop fusion | bytes 655364 | tf_op jit(solution)/shard_map/dynamic_slice | solution.py:234
  1.0 0.0 copy-start
  1.0 0.0 copy-start.1
  1.1 0.8 %collective-permute-start = (bf16[640,256]{1,0:T(8,128)(2,1)S(1)}, bf16[640,256]{1,0:T(8,128)(2,1)S(1)}, u32[]{:S(2)}, u32[]{:S(2)}) collective-permute-start(bf16[640,256]{1,0:T(8,128)(2,1)S(1)} %gate.1), channel_id=1, source_target_pairs={{0,0},{1,2},{2,1},{3,4},{4,3},{5,6},{6,5},{7,8},{8,7},{9,10},{10,9... | collective-permute-start | bytes 983048 | tf_op jit(solution)/shard_map/ppermute | solution.py:235
  1.9 0.4 %copy-done = bf16[2560,256]{1,0:T(8,128)(2,1)S(1)} copy-done((bf16[2560,256]{1,0:T(8,128)(2,1)S(1)}, bf16[2560,256]{1,0:T(8,128)(2,1)}, u32[]{:S(2)}) %copy-start) | copy-done | bytes 1310744
  2.4 0.0 copy-start.2
  2.4 4.1 %collective-permute-start.1 = (bf16[640,256]{1,0:T(8,128)(2,1)S(1)}, bf16[640,256]{1,0:T(8,128)(2,1)S(1)}, u32[]{:S(2)}, u32[]{:S(2)}) collective-permute-start(bf16[640,256]{1,0:T(8,128)(2,1)S(1)} %inner_edge.1), channel_id=1, source_target_pairs={{0,1},{1,0},{2,3},{3,2},{4,5},{5,4},{6,7},{7,6},{8,9},{9,8},{10,11... | collective-permute-start | bytes 983048 | tf_op jit(solution)/shard_map/ppermute | solution.py:236
  6.4 0.4 %turn.1.turned = bf16[256,2560]{1,0:T(8,128)(2,1)S(1)} custom-call(bf16[2560,256]{1,0:T(8,128)(2,1)S(1)} %copy-done), custom_call_target="tpu_custom_call" | custom-call | bytes 2621440 | tf_op jit(solution)/shard_map/turn/pallas_call | solution.py:75
  6.8 0.0 copy-done.1
  6.9 0.0 copy-done.2
  6.9 4.7 %own_part.1 = (f32[256,256]{1,0:T(8,128)S(1)}, bf16[2,2,256,640]{3,2,1,0:T(8,128)(2,1)S(1)}) custom-call(s32[2,14]{1,0:T(2,128)S(1)} %bitcast.2, bf16[14,640,640]{2,1,0:T(8,128)(2,1)S(1)} %copy-done.1, bf16[2560,256]{1,0:T(8,128)(2,1)S(1)} %copy-done, bf16[256,2560]{1,0:T(8,128)(2,1)S(1)} %turn.1.turned), custom_call_target="tpu_custom_call" | custom-call | flops 3607101440 | bytes 12779520 | tf_op jit(solution)/shard_map/own_part/pallas_call | solution.py:138
  11.5 0.0 collective-permute-done.outer_ref
  11.5 0.0 collective-permute-done.1.inner_ref
  11.6 0.4 %join_give.1 = f32[128,256]{1,0:T(8,128)S(1)} custom-call(f32[256,256]{1,0:T(8,128)S(1)} %get-tuple-element.7.p_ref, bf16[2,2,256,640]{3,2,1,0:T(8,128)(2,1)S(1)} %get-tuple-element.8.t_ref, bf16[640,256]{1,0:T(8,128)(2,1)S(1)} %collective-permute-done.outer_ref, bf16[640,256]{1,0:T(8,128)(2,1)S(1)} %collective-permute-done.1.inner_ref), custom_call_target="tpu_custom_call" | custom-call | flops 167772160 | tf_op jit(solution)/shard_map/join_give/pallas_call | solution.py:196
  11.9 2.3 %collective-permute-start.2 = (f32[128,256]{1,0:T(8,128)S(1)}, f32[128,256]{1,0:T(8,128)S(1)}, u32[]{:S(2)}, u32[]{:S(2)}) collective-permute-start(f32[128,256]{1,0:T(8,128)S(1)} %join_give.1), channel_id=1, source_target_pairs={{0,1},{1,0},{2,3},{3,2},{4,5},{5,4},{6,7},{7,6},{8,9},{9,8},{10,11... | collective-permute-start | bytes 393224 | tf_op jit(solution)/shard_map/ppermute | solution.py:243
  14.3 0.4 %join_keep.1 = f32[128,256]{1,0:T(8,128)S(1)} custom-call(f32[256,256]{1,0:T(8,128)S(1)} %get-tuple-element.7.p_ref, bf16[2,2,256,640]{3,2,1,0:T(8,128)(2,1)S(1)} %get-tuple-element.8.t_ref, bf16[640,256]{1,0:T(8,128)(2,1)S(1)} %collective-permute-done.outer_ref, bf16[640,256]{1,0:T(8,128)(2,1)S(1)} %collective-permute-done.1.inner_ref), custom_call_target="tpu_custom_call" | custom-call | flops 167772160 | tf_op jit(solution)/shard_map/join_keep/pallas_call | solution.py:196
  14.6 0.6 %collective-permute-done.2 = f32[128,256]{1,0:T(8,128)S(1)} collective-permute-done((f32[128,256]{1,0:T(8,128)S(1)}, f32[128,256]{1,0:T(8,128)S(1)}, u32[]{:S(2)}, u32[]{:S(2)}) %collective-permute-start.2) | collective-permute-done | bytes 131104 | tf_op jit(solution)/shard_map/ppermute | solution.py:243
  15.3 11.3 %all_to_all.5.parts_ref = f32[8,16,256]{2,1,0:T(8,128)S(1)} all-to-all(f32[8,16,256]{2,1,0:T(8,128)S(1)} %bitcast.3), channel_id=1, replica_groups={{11,8,4,3,15,12,7,0},{10,9,5,14,13,6,2,1},{27,24,20,19,31,28,23,16},{26..., dimensions={0} | all-to-all | bytes 262144 | tf_op jit(solution)/shard_map/all_to_all | solution.py:246
  26.6 0.6 %sum_parts.1 = f32[16,256]{1,0:T(8,128)} custom-call(f32[8,16,256]{2,1,0:T(8,128)S(1)} %all_to_all.5.parts_ref), custom_call_target="tpu_custom_call" | custom-call | tf_op jit(solution)/shard_map/sum_parts/pallas_call | solution.py:215
  (3 shorter events, 0.1 us)
Async XLA Ops:
  1.0 1.3 %copy-start = (bf16[2560,256]{1,0:T(8,128)(2,1)S(1)}, bf16[2560,256]{1,0:T(8,128)(2,1)}, u32[]{:S(2)}) copy-start(bf16[2560,256]{1,0:T(8,128)(2,1)} %modes.5) | copy-start | bytes 3932164
  1.0 5.8 %copy-start.1 = (bf16[14,640,640]{2,1,0:T(8,128)(2,1)S(1)}, bf16[14,640,640]{2,1,0:T(8,128)(2,1)}, u32[]{:S(2)}) copy-start(bf16[14,640,640]{2,1,0:T(8,128)(2,1)} %jac.1) | copy-start | bytes 34406404
  1.1 10.5 %collective-permute-start = (bf16[640,256]{1,0:T(8,128)(2,1)S(1)}, bf16[640,256]{1,0:T(8,128)(2,1)S(1)}, u32[]{:S(2)}, u32[]{:S(2)}) collective-permute-start(bf16[640,256]{1,0:T(8,128)(2,1)S(1)} %gate.1), channel_id=1, source_target_pairs={{0,0},{1,2},{2,1},{3,4},{4,3},{5,6},{6,5},{7,8},{8,7},{9,10},{10,9... | collective-permute-start | bytes 983048 | tf_op jit(solution)/shard_map/ppermute | solution.py:235
  2.4 4.5 %copy-start.2 = (s32[14,2]{0,1:T(2,128)S(1)}, s32[14,2]{0,1:T(2,128)}, u32[]{:S(2)}) copy-start(s32[14,2]{0,1:T(2,128)} %param.5) | copy-start | bytes 340
  2.4 9.2 %collective-permute-start.1 = (bf16[640,256]{1,0:T(8,128)(2,1)S(1)}, bf16[640,256]{1,0:T(8,128)(2,1)S(1)}, u32[]{:S(2)}, u32[]{:S(2)}) collective-permute-start(bf16[640,256]{1,0:T(8,128)(2,1)S(1)} %inner_edge.1), channel_id=1, source_target_pairs={{0,1},{1,0},{2,3},{3,2},{4,5},{5,4},{6,7},{7,6},{8,9},{9,8},{10,11... | collective-permute-start | bytes 983048 | tf_op jit(solution)/shard_map/ppermute | solution.py:236
  11.9 3.3 %collective-permute-start.2 = (f32[128,256]{1,0:T(8,128)S(1)}, f32[128,256]{1,0:T(8,128)S(1)}, u32[]{:S(2)}, u32[]{:S(2)}) collective-permute-start(f32[128,256]{1,0:T(8,128)S(1)} %join_give.1), channel_id=1, source_target_pairs={{0,1},{1,0},{2,3},{3,2},{4,5},{5,4},{6,7},{7,6},{8,9},{9,8},{10,11... | collective-permute-start | bytes 393224 | tf_op jit(solution)/shard_map/ppermute | solution.py:243

commit v23 on v21

--- a/solution.py
+++ b/solution.py
@@ -167,12 +167,11 @@
     rest = [chip for chip in chips if chip not in middle]
     near = count // 8
     rings = [[chip for chip in rest if chip != near] + [near] + middle, middle + rest[:-2] + rest[: -3 : -1]]
-    return [[2 * chip + (chip + half) % 2 for chip in reversed(rings[half])] for half in range(2)]
+    return [[2 * chip + half for chip in reversed(rings[half])] for half in range(2)]
 
 
 def own_team():
-    me = lax.axis_index("cell")
-    return lax.rem(me + me // 2, 2)
+    return lax.rem(lax.axis_index("cell"), 2)
 
 
 def regrouped(value, axis, keep_rows):

time: 27.2 us -> 27.7 us (1.018)
  Pallas kernels: 5.65 us -> 7.25 us
  starting transfers between devices: 8.3 us -> 6.75 us
  blocking collectives: 10.9 us -> 11.3 us
    pallas_call x1, Pallas kernels: 3.88 us -> 5.47 us  [own_part(): pl.pallas_call(functools.partial(own_kernel, blocks), out_shape=(jax.Shap...]
    ppermute x1, starting transfers between devices: 3.4 us -> 1.86 us  [per_device(): got = lax.ppermute(join(True, p, t, outer, inner), 'cell', swap)]
    all_to_all x1, blocking collectives: 10.9 us -> 11.3 us  [per_device(): parts = lax.all_to_all(pair, 'cell', 0, 0, axis_index_groups=teams(count))]
  transfers between devices with their start and end apart: 3 -> 3, of which waited for: 1 -> 1; matrix products, arithmetic and copies ran while one was open for 0% -> 0% of each run, Pallas kernels for 17% -> 23%
where the time goes in v23:
time: 27.7 us; the launch traced here: 27.5 us
  blocking collectives  11.3 us (41%)
  Pallas kernels  7.25 us (26%)
  starting transfers between devices  6.75 us (24%)
  local copies, waits for them, and re-layouts  1.45 us (5%)
  waiting for transfers between devices  0.63 us (2%)
    all_to_all x1, blocking collectives, per_device(): parts = lax.all_to_all(pair, 'cell', 0, 0, axis_index_groups=teams(count))  11.3 us
    pallas_call x1, Pallas kernels, own_part(): pl.pallas_call(functools.partial(own_kernel, blocks), out_shape=(jax.Shap...  5.47 us
    ppermute x1, starting transfers between devices, per_device(): inner = lax.ppermute(inner_edge(modes, width), 'cell', swap)  4.08 us
    ppermute x1, starting transfers between devices, per_device(): got = lax.ppermute(join(True, p, t, outer, inner), 'cell', swap)  1.86 us
    dynamic_slice x1, local copies, waits for them, and re-layouts, per_device(): outer_edge = lax.dynamic_slice_in_dim(modes, core * (rows - width), width)  0.99 us
    ppermute x1, starting transfers between devices, per_device(): outer = lax.ppermute(gate(outer_edge), 'cell', across)  0.81 us
    pallas_call x2, Pallas kernels, join(): pl.pallas_call(functools.partial(join_kernel, other), out_shape=jax.Shape...  0.71 us
    ppermute x1, waiting for transfers between devices, per_device(): got = lax.ppermute(join(True, p, t, outer, inner), 'cell', swap)  0.63 us
  transfers between devices with their start and end apart: 3, of which 1 were waited for; matrix products, arithmetic and copies ran while one was open for 0% of the time, Pallas kernels for 23%

profile of v23, /device:TPU:0, one launch (start us, length us, event | category | flops | bytes accessed | tf_op | source)
XLA Modules:
  0.0 27.5 jit_solution(16778628375844069210)
XLA Ops:
  0.0 1.0 %constant_dynamic-slice_fusion.block_ref = bf16[640,256]{1,0:T(8,128)(2,1)S(1)} fusion(bf16[2560,256]{1,0:T(8,128)(2,1)} %modes.5, s32[]{:T(128)S(6)} %select_n.3), kind=kLoop, calls=%fused_computation | loop fusion | bytes 655364 | tf_op jit(solution)/shard_map/dynamic_slice | solution.py:232
  1.0 0.0 copy-start
  1.0 0.0 copy-start.1
  1.1 0.8 %collective-permute-start = (bf16[640,256]{1,0:T(8,128)(2,1)S(1)}, bf16[640,256]{1,0:T(8,128)(2,1)S(1)}, u32[]{:S(2)}, u32[]{:S(2)}) collective-permute-start(bf16[640,256]{1,0:T(8,128)(2,1)S(1)} %gate.1), channel_id=1, source_target_pairs={{0,0},{1,2},{2,1},{3,4},{4,3},{5,6},{6,5},{7,8},{8,7},{9,10},{10,9... | collective-permute-start | bytes 983048 | tf_op jit(solution)/shard_map/ppermute | solution.py:233
  1.9 0.4 %copy-done = bf16[2560,256]{1,0:T(8,128)(2,1)S(1)} copy-done((bf16[2560,256]{1,0:T(8,128)(2,1)S(1)}, bf16[2560,256]{1,0:T(8,128)(2,1)}, u32[]{:S(2)}) %copy-start) | copy-done | bytes 1310744
  2.4 0.0 copy-start.2
  2.4 4.1 %collective-permute-start.1 = (bf16[640,256]{1,0:T(8,128)(2,1)S(1)}, bf16[640,256]{1,0:T(8,128)(2,1)S(1)}, u32[]{:S(2)}, u32[]{:S(2)}) collective-permute-start(bf16[640,256]{1,0:T(8,128)(2,1)S(1)} %inner_edge.1), channel_id=1, source_target_pairs={{0,1},{1,0},{2,3},{3,2},{4,5},{5,4},{6,7},{7,6},{8,9},{9,8},{10,11... | collective-permute-start | bytes 983048 | tf_op jit(solution)/shard_map/ppermute | solution.py:234
  6.4 0.4 %turn.1.turned = bf16[256,2560]{1,0:T(8,128)(2,1)S(1)} custom-call(bf16[2560,256]{1,0:T(8,128)(2,1)S(1)} %copy-done), custom_call_target="tpu_custom_call" | custom-call | bytes 2621440 | tf_op jit(solution)/shard_map/turn/pallas_call | solution.py:75
  6.8 0.0 copy-done.1
  6.9 0.0 copy-done.2
  6.9 5.5 %own_part.1 = (f32[256,256]{1,0:T(8,128)S(1)}, bf16[2,2,256,640]{3,2,1,0:T(8,128)(2,1)S(1)}) custom-call(s32[2,14]{1,0:T(2,128)S(1)} %bitcast.2, bf16[14,640,640]{2,1,0:T(8,128)(2,1)S(1)} %copy-done.1, bf16[2560,256]{1,0:T(8,128)(2,1)S(1)} %copy-done, bf16[256,2560]{1,0:T(8,128)(2,1)S(1)} %turn.1.turned), custom_call_target="tpu_custom_call" | custom-call | flops 3607101440 | bytes 12779520 | tf_op jit(solution)/shard_map/own_part/pallas_call | solution.py:138
  12.3 0.0 collective-permute-done.outer_ref
  12.4 0.0 collective-permute-done.1.inner_ref
  12.4 0.4 %join_give.1 = f32[128,256]{1,0:T(8,128)S(1)} custom-call(f32[256,256]{1,0:T(8,128)S(1)} %get-tuple-element.7.p_ref, bf16[2,2,256,640]{3,2,1,0:T(8,128)(2,1)S(1)} %get-tuple-element.8.t_ref, bf16[640,256]{1,0:T(8,128)(2,1)S(1)} %collective-permute-done.outer_ref, bf16[640,256]{1,0:T(8,128)(2,1)S(1)} %collective-permute-done.1.inner_ref), custom_call_target="tpu_custom_call" | custom-call | flops 167772160 | tf_op jit(solution)/shard_map/join_give/pallas_call | solution.py:194
  12.7 1.9 %collective-permute-start.2 = (f32[128,256]{1,0:T(8,128)S(1)}, f32[128,256]{1,0:T(8,128)S(1)}, u32[]{:S(2)}, u32[]{:S(2)}) collective-permute-start(f32[128,256]{1,0:T(8,128)S(1)} %join_give.1), channel_id=1, source_target_pairs={{0,1},{1,0},{2,3},{3,2},{4,5},{5,4},{6,7},{7,6},{8,9},{9,8},{10,11... | collective-permute-start | bytes 393224 | tf_op jit(solution)/shard_map/ppermute | solution.py:241
  14.6 0.4 %join_keep.1 = f32[128,256]{1,0:T(8,128)S(1)} custom-call(f32[256,256]{1,0:T(8,128)S(1)} %get-tuple-element.7.p_ref, bf16[2,2,256,640]{3,2,1,0:T(8,128)(2,1)S(1)} %get-tuple-element.8.t_ref, bf16[640,256]{1,0:T(8,128)(2,1)S(1)} %collective-permute-done.outer_ref, bf16[640,256]{1,0:T(8,128)(2,1)S(1)} %collective-permute-done.1.inner_ref), custom_call_target="tpu_custom_call" | custom-call | flops 167772160 | tf_op jit(solution)/shard_map/join_keep/pallas_call | solution.py:194
  14.9 0.6 %collective-permute-done.2 = f32[128,256]{1,0:T(8,128)S(1)} collective-permute-done((f32[128,256]{1,0:T(8,128)S(1)}, f32[128,256]{1,0:T(8,128)S(1)}, u32[]{:S(2)}, u32[]{:S(2)}) %collective-permute-start.2) | collective-permute-done | bytes 131104 | tf_op jit(solution)/shard_map/ppermute | solution.py:241
  15.6 11.3 %all_to_all.5.parts_ref = f32[8,16,256]{2,1,0:T(8,128)S(1)} all-to-all(f32[8,16,256]{2,1,0:T(8,128)S(1)} %bitcast.3), channel_id=1, replica_groups={{10,8,4,14,12,6,2,0},{13,15,7,5,3,1,11,9},{26,24,20,30,28,22,18,16},{29..., dimensions={0} | all-to-all | bytes 262144 | tf_op jit(solution)/shard_map/all_to_all | solution.py:244
  26.9 0.6 %sum_parts.1 = f32[16,256]{1,0:T(8,128)} custom-call(f32[8,16,256]{2,1,0:T(8,128)S(1)} %all_to_all.5.parts_ref), custom_call_target="tpu_custom_call" | custom-call | tf_op jit(solution)/shard_map/sum_parts/pallas_call | solution.py:213
  (3 shorter events, 0.1 us)
Async XLA Ops:
  1.0 1.3 %copy-start = (bf16[2560,256]{1,0:T(8,128)(2,1)S(1)}, bf16[2560,256]{1,0:T(8,128)(2,1)}, u32[]{:S(2)}) copy-start(bf16[2560,256]{1,0:T(8,128)(2,1)} %modes.5) | copy-start | bytes 3932164
  1.0 5.8 %copy-start.1 = (bf16[14,640,640]{2,1,0:T(8,128)(2,1)S(1)}, bf16[14,640,640]{2,1,0:T(8,128)(2,1)}, u32[]{:S(2)}) copy-start(bf16[14,640,640]{2,1,0:T(8,128)(2,1)} %jac.1) | copy-start | bytes 34406404
  1.1 11.3 %collective-permute-start = (bf16[640,256]{1,0:T(8,128)(2,1)S(1)}, bf16[640,256]{1,0:T(8,128)(2,1)S(1)}, u32[]{:S(2)}, u32[]{:S(2)}) collective-permute-start(bf16[640,256]{1,0:T(8,128)(2,1)S(1)} %gate.1), channel_id=1, source_target_pairs={{0,0},{1,2},{2,1},{3,4},{4,3},{5,6},{6,5},{7,8},{8,7},{9,10},{10,9... | collective-permute-start | bytes 983048 | tf_op jit(solution)/shard_map/ppermute | solution.py:233
  2.4 4.5 %copy-start.2 = (s32[14,2]{0,1:T(2,128)S(1)}, s32[14,2]{0,1:T(2,128)}, u32[]{:S(2)}) copy-start(s32[14,2]{0,1:T(2,128)} %param.5) | copy-start | bytes 340
  2.4 10.0 %collective-permute-start.1 = (bf16[640,256]{1,0:T(8,128)(2,1)S(1)}, bf16[640,256]{1,0:T(8,128)(2,1)S(1)}, u32[]{:S(2)}, u32[]{:S(2)}) collective-permute-start(bf16[640,256]{1,0:T(8,128)(2,1)S(1)} %inner_edge.1), channel_id=1, source_target_pairs={{0,1},{1,0},{2,3},{3,2},{4,5},{5,4},{6,7},{7,6},{8,9},{9,8},{10,11... | collective-permute-start | bytes 983048 | tf_op jit(solution)/shard_map/ppermute | solution.py:234
  12.7 2.8 %collective-permute-start.2 = (f32[128,256]{1,0:T(8,128)S(1)}, f32[128,256]{1,0:T(8,128)S(1)}, u32[]{:S(2)}, u32[]{:S(2)}) collective-permute-start(f32[128,256]{1,0:T(8,128)S(1)} %join_give.1), channel_id=1, source_target_pairs={{0,1},{1,0},{2,3},{3,2},{4,5},{5,4},{6,7},{7,6},{8,9},{9,8},{10,11... | collective-permute-start | bytes 393224 | tf_op jit(solution)/shard_map/ppermute | solution.py:241

commit v24 on v19

--- a/solution.py
+++ b/solution.py
@@ -22,16 +22,13 @@
     return upper, (value - upper.astype(jnp.float32)).astype(jnp.bfloat16)
 
 
-def gate_kernel(block_ref, out_ref):
-    out_ref[...] = block_ref[...]
-
-
 def gate(block):
     return pl.pallas_call(
-        gate_kernel,
+        lambda block_ref, out_ref: None,
         out_shape=jax.ShapeDtypeStruct(block.shape, block.dtype),
-        in_specs=[pl.BlockSpec(memory_space=pltpu.VMEM)],
-        out_specs=pl.BlockSpec(memory_space=pltpu.VMEM),
+        in_specs=[pl.BlockSpec(memory_space=pl.ANY)],
+        out_specs=pl.BlockSpec(memory_space=pl.ANY),
+        input_output_aliases={0: 0},
         compiler_params=pltpu.CompilerParams(vmem_limit_bytes=SMALL_VMEM),
         cost_estimate=pl.CostEstimate(flops=LOAD_COST, bytes_accessed=0, transcendentals=0),
         name="gate",
@@ -185,7 +182,8 @@
     count = out_ref.shape[0]
     half = 1 - own_team() if other else own_team()
     rows = pl.ds(pl.multiple_of(half * count, TILE_ROWS), count)
-    both = dot(t_ref[1 - core, half], inner_ref[...]) + dot(t_ref[core, half], outer_ref[...])
+    left = jnp.concatenate([t_ref[1 - core, half], t_ref[core, half]], axis=1)
+    both = dot(left, jnp.concatenate([inner_ref[...], outer_ref[...]], axis=0))
     out_ref[...] = p_ref[rows, :] + both[:count] + both[count:]
 
 

time: 27.1 us -> 27.1 us (level)
  Pallas kernels: 7.22 us -> 6.41 us
  starting transfers between devices: 6.44 us -> 7.2 us
    ppermute x1, starting transfers between devices: 1.55 us -> 2.33 us  [per_device(): got = lax.ppermute(join(True, p, t, outer, inner), 'cell', swap)]
    pallas_call x1, Pallas kernels: 5.45 us -> 4.68 us  [own_part(): pl.pallas_call(functools.partial(own_kernel, blocks), out_shape=(jax.Shap...]
  transfers between devices with their start and end apart: 3 -> 3, of which waited for: 1 -> 1; matrix products, arithmetic and copies ran while one was open for 0% -> 0% of each run, Pallas kernels for 23% -> 20%
where the time goes in v24:
time: 27.1 us; the launch traced here: 26.9 us
  blocking collectives  11 us (41%)
  starting transfers between devices  7.2 us (27%)
  Pallas kernels  6.41 us (24%)
  local copies, waits for them, and re-layouts  1.47 us (5%)
  waiting for transfers between devices  0.64 us (2%)
    all_to_all x1, blocking collectives, per_device(): parts = lax.all_to_all(pair, 'cell', 0, 0, axis_index_groups=teams(count))  11 us
    pallas_call x1, Pallas kernels, own_part(): pl.pallas_call(functools.partial(own_kernel, blocks), out_shape=(jax.Shap...  4.68 us
    ppermute x1, starting transfers between devices, per_device(): inner = lax.ppermute(inner_edge(modes, width), 'cell', swap)  4.06 us
    ppermute x1, starting transfers between devices, per_device(): got = lax.ppermute(join(True, p, t, outer, inner), 'cell', swap)  2.33 us
    dynamic_slice x1, local copies, waits for them, and re-layouts, per_device(): outer_edge = lax.dynamic_slice_in_dim(modes, core * (rows - width), width)  0.99 us
    ppermute x1, starting transfers between devices, per_device(): outer = lax.ppermute(gate(outer_edge), 'cell', across)  0.81 us
    pallas_call x2, Pallas kernels, join(): pl.pallas_call(functools.partial(join_kernel, other), out_shape=jax.Shape...  0.69 us
    ppermute x1, waiting for transfers between devices, per_device(): got = lax.ppermute(join(True, p, t, outer, inner), 'cell', swap)  0.63 us
  transfers between devices with their start and end apart: 3, of which 1 were waited for; matrix products, arithmetic and copies ran while one was open for 0% of the time, Pallas kernels for 20%

profile of v24, /device:TPU:0, one launch (start us, length us, event | category | flops | bytes accessed | tf_op | source)
XLA Modules:
  0.0 26.9 jit_solution(1109850049798673095)
XLA Ops:
  0.0 1.0 %constant_dynamic-slice_fusion.block_ref = bf16[640,256]{1,0:T(8,128)(2,1)S(1)} fusion(bf16[2560,256]{1,0:T(8,128)(2,1)} %modes.5, s32[]{:T(128)S(6)} %select_n.3), kind=kLoop, calls=%fused_computation | loop fusion | bytes 655364 | tf_op jit(solution)/shard_map/dynamic_slice | solution.py:230
  1.0 0.0 copy-start
  1.0 0.0 copy-start.1
  1.0 0.8 %collective-permute-start = (bf16[640,256]{1,0:T(8,128)(2,1)S(1)}, bf16[640,256]{1,0:T(8,128)(2,1)S(1)}, u32[]{:S(2)}, u32[]{:S(2)}) collective-permute-start(bf16[640,256]{1,0:T(8,128)(2,1)S(1)} %gate.1), channel_id=1, source_target_pairs={{0,0},{1,2},{2,1},{3,4},{4,3},{5,6},{6,5},{7,8},{8,7},{9,10},{10,9... | collective-permute-start | bytes 983048 | tf_op jit(solution)/shard_map/ppermute | solution.py:231
  1.9 0.5 %copy-done = bf16[2560,256]{1,0:T(8,128)(2,1)S(1)} copy-done((bf16[2560,256]{1,0:T(8,128)(2,1)S(1)}, bf16[2560,256]{1,0:T(8,128)(2,1)}, u32[]{:S(2)}) %copy-start) | copy-done | bytes 1310744
  2.4 0.0 copy-start.2
  2.4 4.1 %collective-permute-start.1 = (bf16[640,256]{1,0:T(8,128)(2,1)S(1)}, bf16[640,256]{1,0:T(8,128)(2,1)S(1)}, u32[]{:S(2)}, u32[]{:S(2)}) collective-permute-start(bf16[640,256]{1,0:T(8,128)(2,1)S(1)} %inner_edge.1), channel_id=1, source_target_pairs={{0,1},{1,0},{2,3},{3,2},{4,5},{5,4},{6,7},{7,6},{8,9},{9,8},{10,11... | collective-permute-start | bytes 983048 | tf_op jit(solution)/shard_map/ppermute | solution.py:232
  6.4 0.4 %turn.1.turned = bf16[256,2560]{1,0:T(8,128)(2,1)S(1)} custom-call(bf16[2560,256]{1,0:T(8,128)(2,1)S(1)} %copy-done), custom_call_target="tpu_custom_call" | custom-call | bytes 2621440 | tf_op jit(solution)/shard_map/turn/pallas_call | solution.py:72
  6.8 0.0 copy-done.1
  6.8 0.0 copy-done.2
  6.8 4.7 %own_part.1 = (f32[256,256]{1,0:T(8,128)S(1)}, bf16[2,2,256,640]{3,2,1,0:T(8,128)(2,1)S(1)}) custom-call(s32[2,14]{1,0:T(2,128)S(1)} %bitcast.2, bf16[14,640,640]{2,1,0:T(8,128)(2,1)S(1)} %copy-done.1, bf16[2560,256]{1,0:T(8,128)(2,1)S(1)} %copy-done, bf16[256,2560]{1,0:T(8,128)(2,1)S(1)} %turn.1.turned), custom_call_target="tpu_custom_call" | custom-call | flops 3607101440 | bytes 12779520 | tf_op jit(solution)/shard_map/own_part/pallas_call | solution.py:135
  11.5 0.0 collective-permute-done.outer_ref
  11.5 0.0 collective-permute-done.1.inner_ref
  11.5 0.3 %join_give.1 = f32[128,256]{1,0:T(8,128)S(1)} custom-call(f32[256,256]{1,0:T(8,128)S(1)} %get-tuple-element.7.p_ref, bf16[2,2,256,640]{3,2,1,0:T(8,128)(2,1)S(1)} %get-tuple-element.8.t_ref, bf16[640,256]{1,0:T(8,128)(2,1)S(1)} %collective-permute-done.outer_ref, bf16[640,256]{1,0:T(8,128)(2,1)S(1)} %collective-permute-done.1.inner_ref), custom_call_target="tpu_custom_call" | custom-call | flops 167772160 | tf_op jit(solution)/shard_map/join_give/pallas_call | solution.py:192
  11.9 2.3 %collective-permute-start.2 = (f32[128,256]{1,0:T(8,128)S(1)}, f32[128,256]{1,0:T(8,128)S(1)}, u32[]{:S(2)}, u32[]{:S(2)}) collective-permute-start(f32[128,256]{1,0:T(8,128)S(1)} %join_give.1), channel_id=1, source_target_pairs={{0,1},{1,0},{2,3},{3,2},{4,5},{5,4},{6,7},{7,6},{8,9},{9,8},{10,11... | collective-permute-start | bytes 393224 | tf_op jit(solution)/shard_map/ppermute | solution.py:239
  14.2 0.3 %join_keep.1 = f32[128,256]{1,0:T(8,128)S(1)} custom-call(f32[256,256]{1,0:T(8,128)S(1)} %get-tuple-element.7.p_ref, bf16[2,2,256,640]{3,2,1,0:T(8,128)(2,1)S(1)} %get-tuple-element.8.t_ref, bf16[640,256]{1,0:T(8,128)(2,1)S(1)} %collective-permute-done.outer_ref, bf16[640,256]{1,0:T(8,128)(2,1)S(1)} %collective-permute-done.1.inner_ref), custom_call_target="tpu_custom_call" | custom-call | flops 167772160 | tf_op jit(solution)/shard_map/join_keep/pallas_call | solution.py:192
  14.6 0.6 %collective-permute-done.2 = f32[128,256]{1,0:T(8,128)S(1)} collective-permute-done((f32[128,256]{1,0:T(8,128)S(1)}, f32[128,256]{1,0:T(8,128)S(1)}, u32[]{:S(2)}, u32[]{:S(2)}) %collective-permute-start.2) | collective-permute-done | bytes 131104 | tf_op jit(solution)/shard_map/ppermute | solution.py:239
  15.2 11.0 %all_to_all.5.parts_ref = f32[8,16,256]{2,1,0:T(8,128)S(1)} all-to-all(f32[8,16,256]{2,1,0:T(8,128)S(1)} %bitcast.3), channel_id=1, replica_groups={{15,12,7,4,3,0,11,8},{13,14,6,5,2,1,10,9},{31,28,23,20,19,16,27,24},{29..., dimensions={0} | all-to-all | bytes 262144 | tf_op jit(solution)/shard_map/all_to_all | solution.py:242
  26.3 0.6 %sum_parts.1 = f32[16,256]{1,0:T(8,128)} custom-call(f32[8,16,256]{2,1,0:T(8,128)S(1)} %all_to_all.5.parts_ref), custom_call_target="tpu_custom_call" | custom-call | tf_op jit(solution)/shard_map/sum_parts/pallas_call | solution.py:211
  (3 shorter events, 0.1 us)
Async XLA Ops:
  1.0 1.3 %copy-start = (bf16[2560,256]{1,0:T(8,128)(2,1)S(1)}, bf16[2560,256]{1,0:T(8,128)(2,1)}, u32[]{:S(2)}) copy-start(bf16[2560,256]{1,0:T(8,128)(2,1)} %modes.5) | copy-start | bytes 3932164
  1.0 5.8 %copy-start.1 = (bf16[14,640,640]{2,1,0:T(8,128)(2,1)S(1)}, bf16[14,640,640]{2,1,0:T(8,128)(2,1)}, u32[]{:S(2)}) copy-start(bf16[14,640,640]{2,1,0:T(8,128)(2,1)} %jac.1) | copy-start | bytes 34406404
  1.0 10.5 %collective-permute-start = (bf16[640,256]{1,0:T(8,128)(2,1)S(1)}, bf16[640,256]{1,0:T(8,128)(2,1)S(1)}, u32[]{:S(2)}, u32[]{:S(2)}) collective-permute-start(bf16[640,256]{1,0:T(8,128)(2,1)S(1)} %gate.1), channel_id=1, source_target_pairs={{0,0},{1,2},{2,1},{3,4},{4,3},{5,6},{6,5},{7,8},{8,7},{9,10},{10,9... | collective-permute-start | bytes 983048 | tf_op jit(solution)/shard_map/ppermute | solution.py:231
  2.4 4.5 %copy-start.2 = (s32[14,2]{0,1:T(2,128)S(1)}, s32[14,2]{0,1:T(2,128)}, u32[]{:S(2)}) copy-start(s32[14,2]{0,1:T(2,128)} %param.5) | copy-start | bytes 340
  2.4 9.2 %collective-permute-start.1 = (bf16[640,256]{1,0:T(8,128)(2,1)S(1)}, bf16[640,256]{1,0:T(8,128)(2,1)S(1)}, u32[]{:S(2)}, u32[]{:S(2)}) collective-permute-start(bf16[640,256]{1,0:T(8,128)(2,1)S(1)} %inner_edge.1), channel_id=1, source_target_pairs={{0,1},{1,0},{2,3},{3,2},{4,5},{5,4},{6,7},{7,6},{8,9},{9,8},{10,11... | collective-permute-start | bytes 983048 | tf_op jit(solution)/shard_map/ppermute | solution.py:232
  11.9 3.3 %collective-permute-start.2 = (f32[128,256]{1,0:T(8,128)S(1)}, f32[128,256]{1,0:T(8,128)S(1)}, u32[]{:S(2)}, u32[]{:S(2)}) collective-permute-start(f32[128,256]{1,0:T(8,128)S(1)} %join_give.1), channel_id=1, source_target_pairs={{0,1},{1,0},{2,3},{3,2},{4,5},{5,4},{6,7},{7,6},{8,9},{9,8},{10,11... | collective-permute-start | bytes 393224 | tf_op jit(solution)/shard_map/ppermute | solution.py:239

commit v25 on v24

--- a/solution.py
+++ b/solution.py
@@ -110,21 +110,22 @@
 
     lax.fori_loop(0, (count + 1) // 2, pair, 0)
 
-    both = jnp.zeros((2 * n_modes, n_modes), jnp.float32)
-    step = 2 if blocks % 2 == 0 else 1
-    for first in range(0, blocks, step):
-        for c in range(first, first + step):
-            upper, lower = halves(left[c + 1])
-            parts[:n_modes, c * width : (c + 1) * width] = upper
-            parts[n_modes:, c * width : (c + 1) * width] = lower
-        inner = slice(first * width, (first + step) * width)
-        both += dot(parts[:, inner], modes[inner, :])
-    p_ref[...] = both[:n_modes] + both[n_modes:]
-    for side, c in enumerate((0, blocks + 1)):
+    def split_outside(side, c):
         upper, lower = halves(left[c])
         for half in range(2):
             t_ref[side, half, :mid] = upper[half * mid : (half + 1) * mid]
             t_ref[side, half, mid:] = lower[half * mid : (half + 1) * mid]
+
+    both = jnp.zeros((2 * n_modes, n_modes), jnp.float32)
+    for c in range(blocks):
+        columns = slice(c * width, (c + 1) * width)
+        upper, lower = halves(left[c + 1])
+        parts[:n_modes, columns] = upper
+        parts[n_modes:, columns] = lower
+        both += dot(parts[:, columns], modes[columns, :])
+        if c < 2:
+            split_outside(c, c * (blocks + 1))
+    p_ref[...] = both[:n_modes] + both[n_modes:]
 
 
 def own_part(neighbours, jac_blocks, modes, turned):

time: 27.1 us -> 27.2 us (level)
  starting transfers between devices: 7.2 us -> 8.28 us
  Pallas kernels: 6.41 us -> 5.79 us
  blocking collectives: 11 us -> 10.6 us
    ppermute x1, starting transfers between devices: 2.33 us -> 3.41 us  [per_device(): got = lax.ppermute(join(True, p, t, outer, inner), 'cell', swap)]
    pallas_call x1, Pallas kernels: 4.68 us -> 4.05 us  [own_part(): pl.pallas_call(functools.partial(own_kernel, blocks), out_shape=(jax.Shap...]
    all_to_all x1, blocking collectives: 11 us -> 10.6 us  [per_device(): parts = lax.all_to_all(pair, 'cell', 0, 0, axis_index_groups=teams(count))]
  transfers between devices with their start and end apart: 3 -> 3, of which waited for: 1 -> 1; matrix products, arithmetic and copies ran while one was open for 0% -> 0% of each run, Pallas kernels for 20% -> 18%
where the time goes in v25:
time: 27.2 us; the launch traced here: 26.9 us
  blocking collectives  10.6 us (39%)
  starting transfers between devices  8.28 us (30%)
  Pallas kernels  5.79 us (21%)
  local copies, waits for them, and re-layouts  1.47 us (5%)
  waiting for transfers between devices  0.64 us (2%)
    all_to_all x1, blocking collectives, per_device(): parts = lax.all_to_all(pair, 'cell', 0, 0, axis_index_groups=teams(count))  10.6 us
    ppermute x1, starting transfers between devices, per_device(): inner = lax.ppermute(inner_edge(modes, width), 'cell', swap)  4.06 us
    pallas_call x1, Pallas kernels, own_part(): pl.pallas_call(functools.partial(own_kernel, blocks), out_shape=(jax.Shap...  4.05 us
    ppermute x1, starting transfers between devices, per_device(): got = lax.ppermute(join(True, p, t, outer, inner), 'cell', swap)  3.41 us
    dynamic_slice x1, local copies, waits for them, and re-layouts, per_device(): outer_edge = lax.dynamic_slice_in_dim(modes, core * (rows - width), width)  0.99 us
    ppermute x1, starting transfers between devices, per_device(): outer = lax.ppermute(gate(outer_edge), 'cell', across)  0.81 us
    pallas_call x2, Pallas kernels, join(): pl.pallas_call(functools.partial(join_kernel, other), out_shape=jax.Shape...  0.69 us
    ppermute x1, waiting for transfers between devices, per_device(): got = lax.ppermute(join(True, p, t, outer, inner), 'cell', swap)  0.64 us
  transfers between devices with their start and end apart: 3, of which 1 were waited for; matrix products, arithmetic and copies ran while one was open for 0% of the time, Pallas kernels for 18%

profile of v25, /device:TPU:0, one launch (start us, length us, event | category | flops | bytes accessed | tf_op | source)
XLA Modules:
  0.0 26.9 jit_solution(13054553371123122107)
XLA Ops:
  0.0 1.0 %constant_dynamic-slice_fusion.block_ref = bf16[640,256]{1,0:T(8,128)(2,1)S(1)} fusion(bf16[2560,256]{1,0:T(8,128)(2,1)} %modes.5, s32[]{:T(128)S(6)} %select_n.3), kind=kLoop, calls=%fused_computation | loop fusion | bytes 655364 | tf_op jit(solution)/shard_map/dynamic_slice | solution.py:231
  1.0 0.0 copy-start
  1.0 0.0 copy-start.1
  1.0 0.8 %collective-permute-start = (bf16[640,256]{1,0:T(8,128)(2,1)S(1)}, bf16[640,256]{1,0:T(8,128)(2,1)S(1)}, u32[]{:S(2)}, u32[]{:S(2)}) collective-permute-start(bf16[640,256]{1,0:T(8,128)(2,1)S(1)} %gate.1), channel_id=1, source_target_pairs={{0,0},{1,2},{2,1},{3,4},{4,3},{5,6},{6,5},{7,8},{8,7},{9,10},{10,9... | collective-permute-start | bytes 983048 | tf_op jit(solution)/shard_map/ppermute | solution.py:232
  1.9 0.5 %copy-done = bf16[2560,256]{1,0:T(8,128)(2,1)S(1)} copy-done((bf16[2560,256]{1,0:T(8,128)(2,1)S(1)}, bf16[2560,256]{1,0:T(8,128)(2,1)}, u32[]{:S(2)}) %copy-start) | copy-done | bytes 1310744
  2.4 0.0 copy-start.2
  2.4 4.1 %collective-permute-start.1 = (bf16[640,256]{1,0:T(8,128)(2,1)S(1)}, bf16[640,256]{1,0:T(8,128)(2,1)S(1)}, u32[]{:S(2)}, u32[]{:S(2)}) collective-permute-start(bf16[640,256]{1,0:T(8,128)(2,1)S(1)} %inner_edge.1), channel_id=1, source_target_pairs={{0,1},{1,0},{2,3},{3,2},{4,5},{5,4},{6,7},{7,6},{8,9},{9,8},{10,11... | collective-permute-start | bytes 983048 | tf_op jit(solution)/shard_map/ppermute | solution.py:233
  6.4 0.4 %turn.1.turned = bf16[256,2560]{1,0:T(8,128)(2,1)S(1)} custom-call(bf16[2560,256]{1,0:T(8,128)(2,1)S(1)} %copy-done), custom_call_target="tpu_custom_call" | custom-call | bytes 2621440 | tf_op jit(solution)/shard_map/turn/pallas_call | solution.py:72
  6.8 0.0 copy-done.1
  6.8 0.0 copy-done.2
  6.8 4.1 %own_part.1 = (f32[256,256]{1,0:T(8,128)S(1)}, bf16[2,2,256,640]{3,2,1,0:T(8,128)(2,1)S(1)}) custom-call(s32[2,14]{1,0:T(2,128)S(1)} %bitcast.2, bf16[14,640,640]{2,1,0:T(8,128)(2,1)S(1)} %copy-done.1, bf16[2560,256]{1,0:T(8,128)(2,1)S(1)} %copy-done, bf16[256,2560]{1,0:T(8,128)(2,1)S(1)} %turn.1.turned), custom_call_target="tpu_custom_call" | custom-call | flops 3607101440 | bytes 12779520 | tf_op jit(solution)/shard_map/own_part/pallas_call | solution.py:136
  10.9 0.0 collective-permute-done.outer_ref
  10.9 0.0 collective-permute-done.1.inner_ref
  10.9 0.3 %join_give.1 = f32[128,256]{1,0:T(8,128)S(1)} custom-call(f32[256,256]{1,0:T(8,128)S(1)} %get-tuple-element.7.p_ref, bf16[2,2,256,640]{3,2,1,0:T(8,128)(2,1)S(1)} %get-tuple-element.8.t_ref, bf16[640,256]{1,0:T(8,128)(2,1)S(1)} %collective-permute-done.outer_ref, bf16[640,256]{1,0:T(8,128)(2,1)S(1)} %collective-permute-done.1.inner_ref), custom_call_target="tpu_custom_call" | custom-call | flops 167772160 | tf_op jit(solution)/shard_map/join_give/pallas_call | solution.py:193
  11.3 3.4 %collective-permute-start.2 = (f32[128,256]{1,0:T(8,128)S(1)}, f32[128,256]{1,0:T(8,128)S(1)}, u32[]{:S(2)}, u32[]{:S(2)}) collective-permute-start(f32[128,256]{1,0:T(8,128)S(1)} %join_give.1), channel_id=1, source_target_pairs={{0,1},{1,0},{2,3},{3,2},{4,5},{5,4},{6,7},{7,6},{8,9},{9,8},{10,11... | collective-permute-start | bytes 393224 | tf_op jit(solution)/shard_map/ppermute | solution.py:240
  14.7 0.3 %join_keep.1 = f32[128,256]{1,0:T(8,128)S(1)} custom-call(f32[256,256]{1,0:T(8,128)S(1)} %get-tuple-element.7.p_ref, bf16[2,2,256,640]{3,2,1,0:T(8,128)(2,1)S(1)} %get-tuple-element.8.t_ref, bf16[640,256]{1,0:T(8,128)(2,1)S(1)} %collective-permute-done.outer_ref, bf16[640,256]{1,0:T(8,128)(2,1)S(1)} %collective-permute-done.1.inner_ref), custom_call_target="tpu_custom_call" | custom-call | flops 167772160 | tf_op jit(solution)/shard_map/join_keep/pallas_call | solution.py:193
  15.0 0.6 %collective-permute-done.2 = f32[128,256]{1,0:T(8,128)S(1)} collective-permute-done((f32[128,256]{1,0:T(8,128)S(1)}, f32[128,256]{1,0:T(8,128)S(1)}, u32[]{:S(2)}, u32[]{:S(2)}) %collective-permute-start.2) | collective-permute-done | bytes 131104 | tf_op jit(solution)/shard_map/ppermute | solution.py:240
  15.7 10.6 %all_to_all.5.parts_ref = f32[8,16,256]{2,1,0:T(8,128)S(1)} all-to-all(f32[8,16,256]{2,1,0:T(8,128)S(1)} %bitcast.3), channel_id=1, replica_groups={{15,12,7,4,3,0,11,8},{13,14,6,5,2,1,10,9},{31,28,23,20,19,16,27,24},{29..., dimensions={0} | all-to-all | bytes 262144 | tf_op jit(solution)/shard_map/all_to_all | solution.py:243
  26.3 0.6 %sum_parts.1 = f32[16,256]{1,0:T(8,128)} custom-call(f32[8,16,256]{2,1,0:T(8,128)S(1)} %all_to_all.5.parts_ref), custom_call_target="tpu_custom_call" | custom-call | tf_op jit(solution)/shard_map/sum_parts/pallas_call | solution.py:212
  (3 shorter events, 0.1 us)
Async XLA Ops:
  1.0 1.3 %copy-start = (bf16[2560,256]{1,0:T(8,128)(2,1)S(1)}, bf16[2560,256]{1,0:T(8,128)(2,1)}, u32[]{:S(2)}) copy-start(bf16[2560,256]{1,0:T(8,128)(2,1)} %modes.5) | copy-start | bytes 3932164
  1.0 5.8 %copy-start.1 = (bf16[14,640,640]{2,1,0:T(8,128)(2,1)S(1)}, bf16[14,640,640]{2,1,0:T(8,128)(2,1)}, u32[]{:S(2)}) copy-start(bf16[14,640,640]{2,1,0:T(8,128)(2,1)} %jac.1) | copy-start | bytes 34406404
  1.0 9.9 %collective-permute-start = (bf16[640,256]{1,0:T(8,128)(2,1)S(1)}, bf16[640,256]{1,0:T(8,128)(2,1)S(1)}, u32[]{:S(2)}, u32[]{:S(2)}) collective-permute-start(bf16[640,256]{1,0:T(8,128)(2,1)S(1)} %gate.1), channel_id=1, source_target_pairs={{0,0},{1,2},{2,1},{3,4},{4,3},{5,6},{6,5},{7,8},{8,7},{9,10},{10,9... | collective-permute-start | bytes 983048 | tf_op jit(solution)/shard_map/ppermute | solution.py:232
  2.4 4.5 %copy-start.2 = (s32[14,2]{0,1:T(2,128)S(1)}, s32[14,2]{0,1:T(2,128)}, u32[]{:S(2)}) copy-start(s32[14,2]{0,1:T(2,128)} %param.5) | copy-start | bytes 340
  2.4 8.5 %collective-permute-start.1 = (bf16[640,256]{1,0:T(8,128)(2,1)S(1)}, bf16[640,256]{1,0:T(8,128)(2,1)S(1)}, u32[]{:S(2)}, u32[]{:S(2)}) collective-permute-start(bf16[640,256]{1,0:T(8,128)(2,1)S(1)} %inner_edge.1), channel_id=1, source_target_pairs={{0,1},{1,0},{2,3},{3,2},{4,5},{5,4},{6,7},{7,6},{8,9},{9,8},{10,11... | collective-permute-start | bytes 983048 | tf_op jit(solution)/shard_map/ppermute | solution.py:233
  11.3 4.4 %collective-permute-start.2 = (f32[128,256]{1,0:T(8,128)S(1)}, f32[128,256]{1,0:T(8,128)S(1)}, u32[]{:S(2)}, u32[]{:S(2)}) collective-permute-start(f32[128,256]{1,0:T(8,128)S(1)} %join_give.1), channel_id=1, source_target_pairs={{0,1},{1,0},{2,3},{3,2},{4,5},{5,4},{6,7},{7,6},{8,9},{9,8},{10,11... | collective-permute-start | bytes 393224 | tf_op jit(solution)/shard_map/ppermute | solution.py:240

commit v26 on v24

--- a/solution.py
+++ b/solution.py
@@ -110,15 +110,11 @@
 
     lax.fori_loop(0, (count + 1) // 2, pair, 0)
 
-    both = jnp.zeros((2 * n_modes, n_modes), jnp.float32)
-    step = 2 if blocks % 2 == 0 else 1
-    for first in range(0, blocks, step):
-        for c in range(first, first + step):
-            upper, lower = halves(left[c + 1])
-            parts[:n_modes, c * width : (c + 1) * width] = upper
-            parts[n_modes:, c * width : (c + 1) * width] = lower
-        inner = slice(first * width, (first + step) * width)
-        both += dot(parts[:, inner], modes[inner, :])
+    for c in range(blocks):
+        upper, lower = halves(left[c + 1])
+        parts[:n_modes, c * width : (c + 1) * width] = upper
+        parts[n_modes:, c * width : (c + 1) * width] = lower
+    both = dot(parts[...], modes[...])
     p_ref[...] = both[:n_modes] + both[n_modes:]
     for side, c in enumerate((0, blocks + 1)):
         upper, lower = halves(left[c])

time: 27.1 us -> 27.1 us (level)
  Pallas kernels: 6.41 us -> 7.19 us
  starting transfers between devices: 7.2 us -> 6.73 us
  blocking collectives: 11 us -> 10.7 us
    pallas_call x1, Pallas kernels: 4.68 us -> 5.45 us  [own_part(): pl.pallas_call(functools.partial(own_kernel, blocks), out_shape=(jax.Shap...]
    ppermute x1, starting transfers between devices: 2.33 us -> 1.86 us  [per_device(): got = lax.ppermute(join(True, p, t, outer, inner), 'cell', swap)]
    all_to_all x1, blocking collectives: 11 us -> 10.7 us  [per_device(): parts = lax.all_to_all(pair, 'cell', 0, 0, axis_index_groups=teams(count))]
  transfers between devices with their start and end apart: 3 -> 3, of which waited for: 1 -> 1; matrix products, arithmetic and copies ran while one was open for 0% -> 0% of each run, Pallas kernels for 20% -> 23%
where the time goes in v26:
time: 27.1 us; the launch traced here: 26.9 us
  blocking collectives  10.7 us (39%)
  Pallas kernels  7.19 us (27%)
  starting transfers between devices  6.73 us (25%)
  local copies, waits for them, and re-layouts  1.47 us (5%)
  waiting for transfers between devices  0.64 us (2%)
    all_to_all x1, blocking collectives, per_device(): parts = lax.all_to_all(pair, 'cell', 0, 0, axis_index_groups=teams(count))  10.7 us
    pallas_call x1, Pallas kernels, own_part(): pl.pallas_call(functools.partial(own_kernel, blocks), out_shape=(jax.Shap...  5.45 us
    ppermute x1, starting transfers between devices, per_device(): inner = lax.ppermute(inner_edge(modes, width), 'cell', swap)  4.06 us
    ppermute x1, starting transfers between devices, per_device(): got = lax.ppermute(join(True, p, t, outer, inner), 'cell', swap)  1.86 us
    dynamic_slice x1, local copies, waits for them, and re-layouts, per_device(): outer_edge = lax.dynamic_slice_in_dim(modes, core * (rows - width), width)  0.99 us
    ppermute x1, starting transfers between devices, per_device(): outer = lax.ppermute(gate(outer_edge), 'cell', across)  0.81 us
    pallas_call x2, Pallas kernels, join(): pl.pallas_call(functools.partial(join_kernel, other), out_shape=jax.Shape...  0.69 us
    ppermute x1, waiting for transfers between devices, per_device(): got = lax.ppermute(join(True, p, t, outer, inner), 'cell', swap)  0.63 us
  transfers between devices with their start and end apart: 3, of which 1 were waited for; matrix products, arithmetic and copies ran while one was open for 0% of the time, Pallas kernels for 23%

profile of v26, /device:TPU:0, one launch (start us, length us, event | category | flops | bytes accessed | tf_op | source)
XLA Modules:
  0.0 26.9 jit_solution(9985784930283089717)
XLA Ops:
  0.0 1.0 %constant_dynamic-slice_fusion.block_ref = bf16[640,256]{1,0:T(8,128)(2,1)S(1)} fusion(bf16[2560,256]{1,0:T(8,128)(2,1)} %modes.5, s32[]{:T(128)S(6)} %select_n.3), kind=kLoop, calls=%fused_computation | loop fusion | bytes 655364 | tf_op jit(solution)/shard_map/dynamic_slice | solution.py:226
  1.0 0.0 copy-start
  1.0 0.0 copy-start.1
  1.0 0.8 %collective-permute-start = (bf16[640,256]{1,0:T(8,128)(2,1)S(1)}, bf16[640,256]{1,0:T(8,128)(2,1)S(1)}, u32[]{:S(2)}, u32[]{:S(2)}) collective-permute-start(bf16[640,256]{1,0:T(8,128)(2,1)S(1)} %gate.1), channel_id=1, source_target_pairs={{0,0},{1,2},{2,1},{3,4},{4,3},{5,6},{6,5},{7,8},{8,7},{9,10},{10,9... | collective-permute-start | bytes 983048 | tf_op jit(solution)/shard_map/ppermute | solution.py:227
  1.9 0.5 %copy-done = bf16[2560,256]{1,0:T(8,128)(2,1)S(1)} copy-done((bf16[2560,256]{1,0:T(8,128)(2,1)S(1)}, bf16[2560,256]{1,0:T(8,128)(2,1)}, u32[]{:S(2)}) %copy-start) | copy-done | bytes 1310744
  2.4 0.0 copy-start.2
  2.4 4.1 %collective-permute-start.1 = (bf16[640,256]{1,0:T(8,128)(2,1)S(1)}, bf16[640,256]{1,0:T(8,128)(2,1)S(1)}, u32[]{:S(2)}, u32[]{:S(2)}) collective-permute-start(bf16[640,256]{1,0:T(8,128)(2,1)S(1)} %inner_edge.1), channel_id=1, source_target_pairs={{0,1},{1,0},{2,3},{3,2},{4,5},{5,4},{6,7},{7,6},{8,9},{9,8},{10,11... | collective-permute-start | bytes 983048 | tf_op jit(solution)/shard_map/ppermute | solution.py:228
  6.4 0.4 %turn.1.turned = bf16[256,2560]{1,0:T(8,128)(2,1)S(1)} custom-call(bf16[2560,256]{1,0:T(8,128)(2,1)S(1)} %copy-done), custom_call_target="tpu_custom_call" | custom-call | bytes 2621440 | tf_op jit(solution)/shard_map/turn/pallas_call | solution.py:72
  6.8 0.0 copy-done.1
  6.8 0.0 copy-done.2
  6.8 5.5 %own_part.1 = (f32[256,256]{1,0:T(8,128)S(1)}, bf16[2,2,256,640]{3,2,1,0:T(8,128)(2,1)S(1)}) custom-call(s32[2,14]{1,0:T(2,128)S(1)} %bitcast.2, bf16[14,640,640]{2,1,0:T(8,128)(2,1)S(1)} %copy-done.1, bf16[2560,256]{1,0:T(8,128)(2,1)S(1)} %copy-done, bf16[256,2560]{1,0:T(8,128)(2,1)S(1)} %turn.1.turned), custom_call_target="tpu_custom_call" | custom-call | flops 3607101440 | bytes 12779520 | tf_op jit(solution)/shard_map/own_part/pallas_call | solution.py:131
  12.3 0.0 collective-permute-done.outer_ref
  12.3 0.0 collective-permute-done.1.inner_ref
  12.3 0.3 %join_give.1 = f32[128,256]{1,0:T(8,128)S(1)} custom-call(f32[256,256]{1,0:T(8,128)S(1)} %get-tuple-element.7.p_ref, bf16[2,2,256,640]{3,2,1,0:T(8,128)(2,1)S(1)} %get-tuple-element.8.t_ref, bf16[640,256]{1,0:T(8,128)(2,1)S(1)} %collective-permute-done.outer_ref, bf16[640,256]{1,0:T(8,128)(2,1)S(1)} %collective-permute-done.1.inner_ref), custom_call_target="tpu_custom_call" | custom-call | flops 167772160 | tf_op jit(solution)/shard_map/join_give/pallas_call | solution.py:188
  12.7 1.9 %collective-permute-start.2 = (f32[128,256]{1,0:T(8,128)S(1)}, f32[128,256]{1,0:T(8,128)S(1)}, u32[]{:S(2)}, u32[]{:S(2)}) collective-permute-start(f32[128,256]{1,0:T(8,128)S(1)} %join_give.1), channel_id=1, source_target_pairs={{0,1},{1,0},{2,3},{3,2},{4,5},{5,4},{6,7},{7,6},{8,9},{9,8},{10,11... | collective-permute-start | bytes 393224 | tf_op jit(solution)/shard_map/ppermute | solution.py:235
  14.5 0.3 %join_keep.1 = f32[128,256]{1,0:T(8,128)S(1)} custom-call(f32[256,256]{1,0:T(8,128)S(1)} %get-tuple-element.7.p_ref, bf16[2,2,256,640]{3,2,1,0:T(8,128)(2,1)S(1)} %get-tuple-element.8.t_ref, bf16[640,256]{1,0:T(8,128)(2,1)S(1)} %collective-permute-done.outer_ref, bf16[640,256]{1,0:T(8,128)(2,1)S(1)} %collective-permute-done.1.inner_ref), custom_call_target="tpu_custom_call" | custom-call | flops 167772160 | tf_op jit(solution)/shard_map/join_keep/pallas_call | solution.py:188
  14.9 0.6 %collective-permute-done.2 = f32[128,256]{1,0:T(8,128)S(1)} collective-permute-done((f32[128,256]{1,0:T(8,128)S(1)}, f32[128,256]{1,0:T(8,128)S(1)}, u32[]{:S(2)}, u32[]{:S(2)}) %collective-permute-start.2) | collective-permute-done | bytes 131104 | tf_op jit(solution)/shard_map/ppermute | solution.py:235
  15.5 10.7 %all_to_all.5.parts_ref = f32[8,16,256]{2,1,0:T(8,128)S(1)} all-to-all(f32[8,16,256]{2,1,0:T(8,128)S(1)} %bitcast.3), channel_id=1, replica_groups={{15,12,7,4,3,0,11,8},{13,14,6,5,2,1,10,9},{31,28,23,20,19,16,27,24},{29..., dimensions={0} | all-to-all | bytes 262144 | tf_op jit(solution)/shard_map/all_to_all | solution.py:238
  26.3 0.6 %sum_parts.1 = f32[16,256]{1,0:T(8,128)} custom-call(f32[8,16,256]{2,1,0:T(8,128)S(1)} %all_to_all.5.parts_ref), custom_call_target="tpu_custom_call" | custom-call | tf_op jit(solution)/shard_map/sum_parts/pallas_call | solution.py:207
  (3 shorter events, 0.1 us)
Async XLA Ops:
  1.0 1.3 %copy-start = (bf16[2560,256]{1,0:T(8,128)(2,1)S(1)}, bf16[2560,256]{1,0:T(8,128)(2,1)}, u32[]{:S(2)}) copy-start(bf16[2560,256]{1,0:T(8,128)(2,1)} %modes.5) | copy-start | bytes 3932164
  1.0 5.8 %copy-start.1 = (bf16[14,640,640]{2,1,0:T(8,128)(2,1)S(1)}, bf16[14,640,640]{2,1,0:T(8,128)(2,1)}, u32[]{:S(2)}) copy-start(bf16[14,640,640]{2,1,0:T(8,128)(2,1)} %jac.1) | copy-start | bytes 34406404
  1.0 11.3 %collective-permute-start = (bf16[640,256]{1,0:T(8,128)(2,1)S(1)}, bf16[640,256]{1,0:T(8,128)(2,1)S(1)}, u32[]{:S(2)}, u32[]{:S(2)}) collective-permute-start(bf16[640,256]{1,0:T(8,128)(2,1)S(1)} %gate.1), channel_id=1, source_target_pairs={{0,0},{1,2},{2,1},{3,4},{4,3},{5,6},{6,5},{7,8},{8,7},{9,10},{10,9... | collective-permute-start | bytes 983048 | tf_op jit(solution)/shard_map/ppermute | solution.py:227
  2.4 4.5 %copy-start.2 = (s32[14,2]{0,1:T(2,128)S(1)}, s32[14,2]{0,1:T(2,128)}, u32[]{:S(2)}) copy-start(s32[14,2]{0,1:T(2,128)} %param.5) | copy-start | bytes 340
  2.4 9.9 %collective-permute-start.1 = (bf16[640,256]{1,0:T(8,128)(2,1)S(1)}, bf16[640,256]{1,0:T(8,128)(2,1)S(1)}, u32[]{:S(2)}, u32[]{:S(2)}) collective-permute-start(bf16[640,256]{1,0:T(8,128)(2,1)S(1)} %inner_edge.1), channel_id=1, source_target_pairs={{0,1},{1,0},{2,3},{3,2},{4,5},{5,4},{6,7},{7,6},{8,9},{9,8},{10,11... | collective-permute-start | bytes 983048 | tf_op jit(solution)/shard_map/ppermute | solution.py:228
  12.7 2.8 %collective-permute-start.2 = (f32[128,256]{1,0:T(8,128)S(1)}, f32[128,256]{1,0:T(8,128)S(1)}, u32[]{:S(2)}, u32[]{:S(2)}) collective-permute-start(f32[128,256]{1,0:T(8,128)S(1)} %join_give.1), channel_id=1, source_target_pairs={{0,1},{1,0},{2,3},{3,2},{4,5},{5,4},{6,7},{7,6},{8,9},{9,8},{10,11... | collective-permute-start | bytes 393224 | tf_op jit(solution)/shard_map/ppermute | solution.py:235

commit v27 on v24

--- a/solution.py
+++ b/solution.py
@@ -80,11 +80,19 @@
     )(modes)
 
 
-def own_kernel(blocks, nb_ref, jac, modes, turned, p_ref, t_ref, left, parts, live):
+def own_kernel(blocks, nb_hbm, jac, modes, turned, p_ref, t_ref, left, parts, live, nb_ref, sem):
     slots, width, _ = jac.shape
     n_modes = modes.shape[1]
     mid = n_modes // 2
 
+    fetch = pltpu.make_async_copy(nb_hbm, nb_ref, sem)
+    fetch.start()
+    for s in range(blocks):
+        left[s + 1] = dot(turned[:, s * width : (s + 1) * width], jac[s])
+    left[0] = jnp.zeros((n_modes, width), jnp.float32)
+    left[blocks + 1] = jnp.zeros((n_modes, width), jnp.float32)
+
+    fetch.wait()
     base = nb_ref[1, 0]
     count = jnp.int32(0)
     for s in range(blocks, slots):
@@ -96,11 +104,6 @@
     live[0, count] = 0
     live[1, count] = 0
     live[2, count] = blocks + 2
-
-    for s in range(blocks):
-        left[s + 1] = dot(turned[:, s * width : (s + 1) * width], jac[s])
-    left[0] = jnp.zeros((n_modes, width), jnp.float32)
-    left[blocks + 1] = jnp.zeros((n_modes, width), jnp.float32)
 
     def pair(k, carry):
         for j in (2 * k, 2 * k + 1):
@@ -139,7 +142,7 @@
             jax.ShapeDtypeStruct((2, 2, n_modes, width), jnp.bfloat16),
         ),
         in_specs=[
-            pl.BlockSpec(memory_space=pltpu.SMEM),
+            pl.BlockSpec(memory_space=pltpu.HBM),
             pl.BlockSpec(memory_space=pltpu.VMEM),
             pl.BlockSpec(memory_space=pltpu.VMEM),
             pl.BlockSpec(memory_space=pltpu.VMEM),
@@ -149,13 +152,15 @@
             pltpu.VMEM((blocks + 3, n_modes, width), jnp.float32),
             pltpu.VMEM((2 * n_modes, rows), jnp.bfloat16),
             pltpu.SMEM((3, slots + 1), jnp.int32),
+            pltpu.SMEM(neighbours.shape, jnp.int32),
+            pltpu.SemaphoreType.DMA,
         ],
         compiler_params=pltpu.CompilerParams(vmem_limit_bytes=OWN_VMEM),
         cost_estimate=pl.CostEstimate(
             flops=flops, bytes_accessed=slots * width * width * 2 + rows * n_modes * 2, transcendentals=0
         ),
         name="own_part",
-    )(neighbours, jac_blocks, modes, turned)
+    )(pltpu.with_memory_space_constraint(neighbours, pltpu.HBM), jac_blocks, modes, turned)
 
 
 def teams(count):

time: 27.1 us -> 27.1 us (level)
  starting transfers between devices: 7.2 us -> 8.58 us
  Pallas kernels: 6.41 us -> 5.04 us
    ppermute x1, starting transfers between devices: 2.33 us -> 3.71 us  [per_device(): got = lax.ppermute(join(True, p, t, outer, inner), 'cell', swap)]
    pallas_call x1, Pallas kernels: 4.68 us -> 3.31 us  [own_part(): pl.pallas_call(functools.partial(own_kernel, blocks), out_shape=(jax.Shap...]
  transfers between devices with their start and end apart: 3 -> 3, of which waited for: 1 -> 1; matrix products, arithmetic and copies ran while one was open for 0% -> 0% of each run, Pallas kernels for 20% -> 15%
where the time goes in v27:
time: 27.1 us; the launch traced here: 26.9 us
  blocking collectives  11 us (41%)
  starting transfers between devices  8.58 us (32%)
  Pallas kernels  5.04 us (19%)
  local copies, waits for them, and re-layouts  1.47 us (5%)
  waiting for transfers between devices  0.65 us (2%)
    all_to_all x1, blocking collectives, per_device(): parts = lax.all_to_all(pair, 'cell', 0, 0, axis_index_groups=teams(count))  11 us
    ppermute x1, starting transfers between devices, per_device(): inner = lax.ppermute(inner_edge(modes, width), 'cell', swap)  4.06 us
    ppermute x1, starting transfers between devices, per_device(): got = lax.ppermute(join(True, p, t, outer, inner), 'cell', swap)  3.71 us
    pallas_call x1, Pallas kernels, own_part(): pl.pallas_call(functools.partial(own_kernel, blocks), out_shape=(jax.Shap...  3.31 us
    dynamic_slice x1, local copies, waits for them, and re-layouts, per_device(): outer_edge = lax.dynamic_slice_in_dim(modes, core * (rows - width), width)  0.99 us
    ppermute x1, starting transfers between devices, per_device(): outer = lax.ppermute(gate(outer_edge), 'cell', across)  0.81 us
    pallas_call x2, Pallas kernels, join(): pl.pallas_call(functools.partial(join_kernel, other), out_shape=jax.Shape...  0.68 us
    ppermute x1, waiting for transfers between devices, per_device(): got = lax.ppermute(join(True, p, t, outer, inner), 'cell', swap)  0.64 us
  transfers between devices with their start and end apart: 3, of which 1 were waited for; matrix products, arithmetic and copies ran while one was open for 0% of the time, Pallas kernels for 15%

profile of v27, /device:TPU:0, one launch (start us, length us, event | category | flops | bytes accessed | tf_op | source)
XLA Modules:
  0.0 26.9 jit_solution(11634704854604953858)
XLA Ops:
  0.0 1.0 %constant_dynamic-slice_fusion.block_ref = bf16[640,256]{1,0:T(8,128)(2,1)S(1)} fusion(bf16[2560,256]{1,0:T(8,128)(2,1)} %modes.5, s32[]{:T(128)S(6)} %select_n.3), kind=kLoop, calls=%fused_computation | loop fusion | bytes 655364 | tf_op jit(solution)/shard_map/dynamic_slice | solution.py:235
  1.0 0.0 copy-start
  1.0 0.0 copy-start.1
  1.0 0.8 %collective-permute-start = (bf16[640,256]{1,0:T(8,128)(2,1)S(1)}, bf16[640,256]{1,0:T(8,128)(2,1)S(1)}, u32[]{:S(2)}, u32[]{:S(2)}) collective-permute-start(bf16[640,256]{1,0:T(8,128)(2,1)S(1)} %gate.1), channel_id=1, source_target_pairs={{0,0},{1,2},{2,1},{3,4},{4,3},{5,6},{6,5},{7,8},{8,7},{9,10},{10,9... | collective-permute-start | bytes 983048 | tf_op jit(solution)/shard_map/ppermute | solution.py:236
  1.9 0.5 %copy-done = bf16[2560,256]{1,0:T(8,128)(2,1)S(1)} copy-done((bf16[2560,256]{1,0:T(8,128)(2,1)S(1)}, bf16[2560,256]{1,0:T(8,128)(2,1)}, u32[]{:S(2)}) %copy-start) | copy-done | bytes 1310744
  2.4 4.1 %collective-permute-start.1 = (bf16[640,256]{1,0:T(8,128)(2,1)S(1)}, bf16[640,256]{1,0:T(8,128)(2,1)S(1)}, u32[]{:S(2)}, u32[]{:S(2)}) collective-permute-start(bf16[640,256]{1,0:T(8,128)(2,1)S(1)} %inner_edge.1), channel_id=1, source_target_pairs={{0,1},{1,0},{2,3},{3,2},{4,5},{5,4},{6,7},{7,6},{8,9},{9,8},{10,11... | collective-permute-start | bytes 983048 | tf_op jit(solution)/shard_map/ppermute | solution.py:237
  6.4 0.4 %turn.1.turned = bf16[256,2560]{1,0:T(8,128)(2,1)S(1)} custom-call(bf16[2560,256]{1,0:T(8,128)(2,1)S(1)} %copy-done), custom_call_target="tpu_custom_call" | custom-call | bytes 2621440 | tf_op jit(solution)/shard_map/turn/pallas_call | solution.py:72
  6.8 0.0 copy-done.1
  6.8 3.3 %own_part.1 = (f32[256,256]{1,0:T(8,128)S(1)}, bf16[2,2,256,640]{3,2,1,0:T(8,128)(2,1)S(1)}) custom-call(s32[2,14]{1,0:T(2,128)} %bitcast.3, bf16[14,640,640]{2,1,0:T(8,128)(2,1)S(1)} %copy-done.1, bf16[2560,256]{1,0:T(8,128)(2,1)S(1)} %copy-done, bf16[256,2560]{1,0:T(8,128)(2,1)S(1)} %turn.1.turned), custom_call_target="tpu_custom_call" | custom-call | flops 3607101440 | bytes 12779520 | tf_op jit(solution)/shard_map/own_part/pallas_call | solution.py:138
  10.1 0.0 collective-permute-done.outer_ref
  10.1 0.0 collective-permute-done.1.inner_ref
  10.2 0.3 %join_give.1 = f32[128,256]{1,0:T(8,128)S(1)} custom-call(f32[256,256]{1,0:T(8,128)S(1)} %get-tuple-element.7.p_ref, bf16[2,2,256,640]{3,2,1,0:T(8,128)(2,1)S(1)} %get-tuple-element.8.t_ref, bf16[640,256]{1,0:T(8,128)(2,1)S(1)} %collective-permute-done.outer_ref, bf16[640,256]{1,0:T(8,128)(2,1)S(1)} %collective-permute-done.1.inner_ref), custom_call_target="tpu_custom_call" | custom-call | flops 167772160 | tf_op jit(solution)/shard_map/join_give/pallas_call | solution.py:197
  10.5 3.7 %collective-permute-start.2 = (f32[128,256]{1,0:T(8,128)S(1)}, f32[128,256]{1,0:T(8,128)S(1)}, u32[]{:S(2)}, u32[]{:S(2)}) collective-permute-start(f32[128,256]{1,0:T(8,128)S(1)} %join_give.1), channel_id=1, source_target_pairs={{0,1},{1,0},{2,3},{3,2},{4,5},{5,4},{6,7},{7,6},{8,9},{9,8},{10,11... | collective-permute-start | bytes 393224 | tf_op jit(solution)/shard_map/ppermute | solution.py:244
  14.2 0.3 %join_keep.1 = f32[128,256]{1,0:T(8,128)S(1)} custom-call(f32[256,256]{1,0:T(8,128)S(1)} %get-tuple-element.7.p_ref, bf16[2,2,256,640]{3,2,1,0:T(8,128)(2,1)S(1)} %get-tuple-element.8.t_ref, bf16[640,256]{1,0:T(8,128)(2,1)S(1)} %collective-permute-done.outer_ref, bf16[640,256]{1,0:T(8,128)(2,1)S(1)} %collective-permute-done.1.inner_ref), custom_call_target="tpu_custom_call" | custom-call | flops 167772160 | tf_op jit(solution)/shard_map/join_keep/pallas_call | solution.py:197
  14.6 0.6 %collective-permute-done.2 = f32[128,256]{1,0:T(8,128)S(1)} collective-permute-done((f32[128,256]{1,0:T(8,128)S(1)}, f32[128,256]{1,0:T(8,128)S(1)}, u32[]{:S(2)}, u32[]{:S(2)}) %collective-permute-start.2) | collective-permute-done | bytes 131104 | tf_op jit(solution)/shard_map/ppermute | solution.py:244
  15.2 11.0 %all_to_all.5.parts_ref = f32[8,16,256]{2,1,0:T(8,128)S(1)} all-to-all(f32[8,16,256]{2,1,0:T(8,128)S(1)} %bitcast.2), channel_id=1, replica_groups={{15,12,7,4,3,0,11,8},{13,14,6,5,2,1,10,9},{31,28,23,20,19,16,27,24},{29..., dimensions={0} | all-to-all | bytes 262144 | tf_op jit(solution)/shard_map/all_to_all | solution.py:247
  26.3 0.6 %sum_parts.1 = f32[16,256]{1,0:T(8,128)} custom-call(f32[8,16,256]{2,1,0:T(8,128)S(1)} %all_to_all.5.parts_ref), custom_call_target="tpu_custom_call" | custom-call | tf_op jit(solution)/shard_map/sum_parts/pallas_call | solution.py:216
  (3 shorter events, 0.1 us)
Async XLA Ops:
  1.0 1.3 %copy-start = (bf16[2560,256]{1,0:T(8,128)(2,1)S(1)}, bf16[2560,256]{1,0:T(8,128)(2,1)}, u32[]{:S(2)}) copy-start(bf16[2560,256]{1,0:T(8,128)(2,1)} %modes.5) | copy-start | bytes 3932164
  1.0 5.8 %copy-start.1 = (bf16[14,640,640]{2,1,0:T(8,128)(2,1)S(1)}, bf16[14,640,640]{2,1,0:T(8,128)(2,1)}, u32[]{:S(2)}) copy-start(bf16[14,640,640]{2,1,0:T(8,128)(2,1)} %jac.1) | copy-start | bytes 34406404
  1.0 9.1 %collective-permute-start = (bf16[640,256]{1,0:T(8,128)(2,1)S(1)}, bf16[640,256]{1,0:T(8,128)(2,1)S(1)}, u32[]{:S(2)}, u32[]{:S(2)}) collective-permute-start(bf16[640,256]{1,0:T(8,128)(2,1)S(1)} %gate.1), channel_id=1, source_target_pairs={{0,0},{1,2},{2,1},{3,4},{4,3},{5,6},{6,5},{7,8},{8,7},{9,10},{10,9... | collective-permute-start | bytes 983048 | tf_op jit(solution)/shard_map/ppermute | solution.py:236
  2.4 7.8 %collective-permute-start.1 = (bf16[640,256]{1,0:T(8,128)(2,1)S(1)}, bf16[640,256]{1,0:T(8,128)(2,1)S(1)}, u32[]{:S(2)}, u32[]{:S(2)}) collective-permute-start(bf16[640,256]{1,0:T(8,128)(2,1)S(1)} %inner_edge.1), channel_id=1, source_target_pairs={{0,1},{1,0},{2,3},{3,2},{4,5},{5,4},{6,7},{7,6},{8,9},{9,8},{10,11... | collective-permute-start | bytes 983048 | tf_op jit(solution)/shard_map/ppermute | solution.py:237
  10.5 4.7 %collective-permute-start.2 = (f32[128,256]{1,0:T(8,128)S(1)}, f32[128,256]{1,0:T(8,128)S(1)}, u32[]{:S(2)}, u32[]{:S(2)}) collective-permute-start(f32[128,256]{1,0:T(8,128)S(1)} %join_give.1), channel_id=1, source_target_pairs={{0,1},{1,0},{2,3},{3,2},{4,5},{5,4},{6,7},{7,6},{8,9},{9,8},{10,11... | collective-permute-start | bytes 393224 | tf_op jit(solution)/shard_map/ppermute | solution.py:244

commit v28 on v27

--- a/solution.py
+++ b/solution.py
@@ -167,7 +167,8 @@
     chips = range(count // 2)
     middle = [chip for chip in (count // 4, count // 4 + 1) if 0 < chip < count // 2]
     rest = [chip for chip in chips if chip not in middle]
-    rings = [middle + rest, middle + rest[:-2] + rest[: -3 : -1]]
+    near = count // 8
+    rings = [[chip for chip in rest if chip != near] + [near] + middle, middle + rest[:-2] + rest[: -3 : -1]]
     return [[2 * chip + (chip + half) % 2 for chip in reversed(rings[half])] for half in range(2)]
 
 

time: 27.1 us -> 27.2 us (level)
  Pallas kernels: 5.04 us -> 6.59 us
  starting transfers between devices: 8.58 us -> 7.04 us
    ppermute x1, starting transfers between devices: 3.71 us -> 2.17 us  [per_device(): got = lax.ppermute(join(True, p, t, outer, inner), 'cell', swap)]
    pallas_call x1, Pallas kernels: 3.31 us -> 4.86 us  [own_part(): pl.pallas_call(functools.partial(own_kernel, blocks), out_shape=(jax.Shap...]
  transfers between devices with their start and end apart: 3 -> 3, of which waited for: 1 -> 1; matrix products, arithmetic and copies ran while one was open for 0% -> 0% of each run, Pallas kernels for 15% -> 21%
where the time goes in v28:
time: 27.2 us; the launch traced here: 27 us
  blocking collectives  11.2 us (41%)
  starting transfers between devices  7.04 us (26%)
  Pallas kernels  6.59 us (24%)
  local copies, waits for them, and re-layouts  1.47 us (5%)
  waiting for transfers between devices  0.65 us (2%)
    all_to_all x1, blocking collectives, per_device(): parts = lax.all_to_all(pair, 'cell', 0, 0, axis_index_groups=teams(count))  11.2 us
    pallas_call x1, Pallas kernels, own_part(): pl.pallas_call(functools.partial(own_kernel, blocks), out_shape=(jax.Shap...  4.86 us
    ppermute x1, starting transfers between devices, per_device(): inner = lax.ppermute(inner_edge(modes, width), 'cell', swap)  4.06 us
    ppermute x1, starting transfers between devices, per_device(): got = lax.ppermute(join(True, p, t, outer, inner), 'cell', swap)  2.17 us
    dynamic_slice x1, local copies, waits for them, and re-layouts, per_device(): outer_edge = lax.dynamic_slice_in_dim(modes, core * (rows - width), width)  0.99 us
    ppermute x1, starting transfers between devices, per_device(): outer = lax.ppermute(gate(outer_edge), 'cell', across)  0.81 us
    pallas_call x2, Pallas kernels, join(): pl.pallas_call(functools.partial(join_kernel, other), out_shape=jax.Shape...  0.68 us
    ppermute x1, waiting for transfers between devices, per_device(): got = lax.ppermute(join(True, p, t, outer, inner), 'cell', swap)  0.64 us
  transfers between devices with their start and end apart: 3, of which 1 were waited for; matrix products, arithmetic and copies ran while one was open for 0% of the time, Pallas kernels for 21%

profile of v28, /device:TPU:0, one launch (start us, length us, event | category | flops | bytes accessed | tf_op | source)
XLA Modules:
  0.0 27.0 jit_solution(3400138710754428459)
XLA Ops:
  0.0 1.0 %constant_dynamic-slice_fusion.block_ref = bf16[640,256]{1,0:T(8,128)(2,1)S(1)} fusion(bf16[2560,256]{1,0:T(8,128)(2,1)} %modes.5, s32[]{:T(128)S(6)} %select_n.3), kind=kLoop, calls=%fused_computation | loop fusion | bytes 655364 | tf_op jit(solution)/shard_map/dynamic_slice | solution.py:236
  1.0 0.0 copy-start
  1.0 0.0 copy-start.1
  1.0 0.8 %collective-permute-start = (bf16[640,256]{1,0:T(8,128)(2,1)S(1)}, bf16[640,256]{1,0:T(8,128)(2,1)S(1)}, u32[]{:S(2)}, u32[]{:S(2)}) collective-permute-start(bf16[640,256]{1,0:T(8,128)(2,1)S(1)} %gate.1), channel_id=1, source_target_pairs={{0,0},{1,2},{2,1},{3,4},{4,3},{5,6},{6,5},{7,8},{8,7},{9,10},{10,9... | collective-permute-start | bytes 983048 | tf_op jit(solution)/shard_map/ppermute | solution.py:237
  1.9 0.5 %copy-done = bf16[2560,256]{1,0:T(8,128)(2,1)S(1)} copy-done((bf16[2560,256]{1,0:T(8,128)(2,1)S(1)}, bf16[2560,256]{1,0:T(8,128)(2,1)}, u32[]{:S(2)}) %copy-start) | copy-done | bytes 1310744
  2.4 4.1 %collective-permute-start.1 = (bf16[640,256]{1,0:T(8,128)(2,1)S(1)}, bf16[640,256]{1,0:T(8,128)(2,1)S(1)}, u32[]{:S(2)}, u32[]{:S(2)}) collective-permute-start(bf16[640,256]{1,0:T(8,128)(2,1)S(1)} %inner_edge.1), channel_id=1, source_target_pairs={{0,1},{1,0},{2,3},{3,2},{4,5},{5,4},{6,7},{7,6},{8,9},{9,8},{10,11... | collective-permute-start | bytes 983048 | tf_op jit(solution)/shard_map/ppermute | solution.py:238
  6.4 0.4 %turn.1.turned = bf16[256,2560]{1,0:T(8,128)(2,1)S(1)} custom-call(bf16[2560,256]{1,0:T(8,128)(2,1)S(1)} %copy-done), custom_call_target="tpu_custom_call" | custom-call | bytes 2621440 | tf_op jit(solution)/shard_map/turn/pallas_call | solution.py:72
  6.8 0.0 copy-done.1
  6.8 4.9 %own_part.1 = (f32[256,256]{1,0:T(8,128)S(1)}, bf16[2,2,256,640]{3,2,1,0:T(8,128)(2,1)S(1)}) custom-call(s32[2,14]{1,0:T(2,128)} %bitcast.3, bf16[14,640,640]{2,1,0:T(8,128)(2,1)S(1)} %copy-done.1, bf16[2560,256]{1,0:T(8,128)(2,1)S(1)} %copy-done, bf16[256,2560]{1,0:T(8,128)(2,1)S(1)} %turn.1.turned), custom_call_target="tpu_custom_call" | custom-call | flops 3607101440 | bytes 12779520 | tf_op jit(solution)/shard_map/own_part/pallas_call | solution.py:138
  11.7 0.0 collective-permute-done.outer_ref
  11.7 0.0 collective-permute-done.1.inner_ref
  11.7 0.3 %join_give.1 = f32[128,256]{1,0:T(8,128)S(1)} custom-call(f32[256,256]{1,0:T(8,128)S(1)} %get-tuple-element.7.p_ref, bf16[2,2,256,640]{3,2,1,0:T(8,128)(2,1)S(1)} %get-tuple-element.8.t_ref, bf16[640,256]{1,0:T(8,128)(2,1)S(1)} %collective-permute-done.outer_ref, bf16[640,256]{1,0:T(8,128)(2,1)S(1)} %collective-permute-done.1.inner_ref), custom_call_target="tpu_custom_call" | custom-call | flops 167772160 | tf_op jit(solution)/shard_map/join_give/pallas_call | solution.py:198
  12.1 2.2 %collective-permute-start.2 = (f32[128,256]{1,0:T(8,128)S(1)}, f32[128,256]{1,0:T(8,128)S(1)}, u32[]{:S(2)}, u32[]{:S(2)}) collective-permute-start(f32[128,256]{1,0:T(8,128)S(1)} %join_give.1), channel_id=1, source_target_pairs={{0,1},{1,0},{2,3},{3,2},{4,5},{5,4},{6,7},{7,6},{8,9},{9,8},{10,11... | collective-permute-start | bytes 393224 | tf_op jit(solution)/shard_map/ppermute | solution.py:245
  14.2 0.3 %join_keep.1 = f32[128,256]{1,0:T(8,128)S(1)} custom-call(f32[256,256]{1,0:T(8,128)S(1)} %get-tuple-element.7.p_ref, bf16[2,2,256,640]{3,2,1,0:T(8,128)(2,1)S(1)} %get-tuple-element.8.t_ref, bf16[640,256]{1,0:T(8,128)(2,1)S(1)} %collective-permute-done.outer_ref, bf16[640,256]{1,0:T(8,128)(2,1)S(1)} %collective-permute-done.1.inner_ref), custom_call_target="tpu_custom_call" | custom-call | flops 167772160 | tf_op jit(solution)/shard_map/join_keep/pallas_call | solution.py:198
  14.6 0.6 %collective-permute-done.2 = f32[128,256]{1,0:T(8,128)S(1)} collective-permute-done((f32[128,256]{1,0:T(8,128)S(1)}, f32[128,256]{1,0:T(8,128)S(1)}, u32[]{:S(2)}, u32[]{:S(2)}) %collective-permute-start.2) | collective-permute-done | bytes 131104 | tf_op jit(solution)/shard_map/ppermute | solution.py:245
  15.2 11.2 %all_to_all.5.parts_ref = f32[8,16,256]{2,1,0:T(8,128)S(1)} all-to-all(f32[8,16,256]{2,1,0:T(8,128)S(1)} %bitcast.2), channel_id=1, replica_groups={{11,8,4,15,12,7,3,0},{13,14,6,5,2,1,10,9},{27,24,20,31,28,23,19,16},{29..., dimensions={0} | all-to-all | bytes 262144 | tf_op jit(solution)/shard_map/all_to_all | solution.py:248
  26.4 0.6 %sum_parts.1 = f32[16,256]{1,0:T(8,128)} custom-call(f32[8,16,256]{2,1,0:T(8,128)S(1)} %all_to_all.5.parts_ref), custom_call_target="tpu_custom_call" | custom-call | tf_op jit(solution)/shard_map/sum_parts/pallas_call | solution.py:217
  (3 shorter events, 0.1 us)
Async XLA Ops:
  1.0 1.3 %copy-start = (bf16[2560,256]{1,0:T(8,128)(2,1)S(1)}, bf16[2560,256]{1,0:T(8,128)(2,1)}, u32[]{:S(2)}) copy-start(bf16[2560,256]{1,0:T(8,128)(2,1)} %modes.5) | copy-start | bytes 3932164
  1.0 5.8 %copy-start.1 = (bf16[14,640,640]{2,1,0:T(8,128)(2,1)S(1)}, bf16[14,640,640]{2,1,0:T(8,128)(2,1)}, u32[]{:S(2)}) copy-start(bf16[14,640,640]{2,1,0:T(8,128)(2,1)} %jac.1) | copy-start | bytes 34406404
  1.0 10.7 %collective-permute-start = (bf16[640,256]{1,0:T(8,128)(2,1)S(1)}, bf16[640,256]{1,0:T(8,128)(2,1)S(1)}, u32[]{:S(2)}, u32[]{:S(2)}) collective-permute-start(bf16[640,256]{1,0:T(8,128)(2,1)S(1)} %gate.1), channel_id=1, source_target_pairs={{0,0},{1,2},{2,1},{3,4},{4,3},{5,6},{6,5},{7,8},{8,7},{9,10},{10,9... | collective-permute-start | bytes 983048 | tf_op jit(solution)/shard_map/ppermute | solution.py:237
  2.4 9.3 %collective-permute-start.1 = (bf16[640,256]{1,0:T(8,128)(2,1)S(1)}, bf16[640,256]{1,0:T(8,128)(2,1)S(1)}, u32[]{:S(2)}, u32[]{:S(2)}) collective-permute-start(bf16[640,256]{1,0:T(8,128)(2,1)S(1)} %inner_edge.1), channel_id=1, source_target_pairs={{0,1},{1,0},{2,3},{3,2},{4,5},{5,4},{6,7},{7,6},{8,9},{9,8},{10,11... | collective-permute-start | bytes 983048 | tf_op jit(solution)/shard_map/ppermute | solution.py:238
  12.1 3.2 %collective-permute-start.2 = (f32[128,256]{1,0:T(8,128)S(1)}, f32[128,256]{1,0:T(8,128)S(1)}, u32[]{:S(2)}, u32[]{:S(2)}) collective-permute-start(f32[128,256]{1,0:T(8,128)S(1)} %join_give.1), channel_id=1, source_target_pairs={{0,1},{1,0},{2,3},{3,2},{4,5},{5,4},{6,7},{7,6},{8,9},{9,8},{10,11... | collective-permute-start | bytes 393224 | tf_op jit(solution)/shard_map/ppermute | solution.py:245
